TPU v7x, 32 devices: a whole 2x2x4 slice. The times are simulated.
32 devices in a mesh: tiles: 2 (over y), cols: 4 (over z), lines: 2 (over x), view: 2 (over core).
Axes of the slice: x: 2, y: 2, z: 4, core: 2. Of those that a mesh axis runs over, the one named last changes fastest.
Arguments:
- features: bfloat16 [2, 64, 64, 1024], P('view', ('tiles', 'lines'), None, 'cols'), parts along dimension 1, as said below
- valid_cols: int32 [2, 2048], P(None, ('tiles', 'cols')), parts along dimension 1, may hold values 0 or 1
- offsets: int32 [64], P(('tiles', 'lines')), parts along dimension 0, may hold values from 0 to 32
- guide_weight: bfloat16 [64, 108], replicated, may hold values from -0.75 to 0.75
Outputs:
- disparity: float32 [4, 16, 1024], P(('tiles', 'lines'), 'cols'), parts along dimension 0
There are 2 independent parts, one for each index of `tiles`. A program takes and returns all parts, laid end to end along the dimension named above; an argument that names none is the same for every part. Nothing has to cross between parts.
Inputs may be any that keep to these rules, and one draw needn't show every extreme that they name: `features`: features of one tile's two views.
All inputs are finite; a program needn't handle non-finite values. No bound on the sum of `valid_cols` on one device may be relied on, other than what follows from the above.
Results may differ from a plain program's by a relative error of at most 0.0066.
Values may be sent and summed in bfloat16 or wider, within the bound.
No kernel may reach another device: no remote copies, remote signals or barrier semaphores. Data moves between devices by JAX's collectives and lax.ppermute only.
A program may use at most 64 MiB of HBM per device.

v0:
```python
import math

import jax
import jax.numpy as jnp
from jax import lax
from jax.sharding import PartitionSpec as P

DISP = 192
DGROUP = 16
LAYERS = 3
RIM = 224


SHARPNESS = 2.0


def combined_all(part, axis, combine):
    gathered = jax.tree.map(lambda a: lax.all_gather(a, axis), part)

    def take(source):
        return jax.tree.map(lambda a: lax.dynamic_index_in_dim(a, source, 0, False), gathered)

    return lax.fori_loop(
        1, lax.axis_size(axis), lambda source, state: combine(state, take(source)), take(0)
    )


def partner(x, axis, distance):
    return lax.ppermute(x, axis, [(i, i ^ 1 << distance) for i in range(lax.axis_size(axis))])


def combine_halves(first, second):
    largest = jnp.maximum(first[0], second[0])
    factor_a = jnp.exp(first[0] - largest)
    factor_b = jnp.exp(second[0] - largest)
    return (
        largest,
        first[1] * factor_a + second[1] * factor_b,
        first[2] * factor_a + second[2] * factor_b,
    )


def widen(volume, dilation):
    return jnp.pad(volume, ((0, 0), (0, 0), (0, 0), (dilation, dilation)))


def soft_disparity(costs, gate_maps, line_offsets, view_index):
    rows, half_disp, columns = costs.shape
    group_half = half_disp // DGROUP
    volume = costs.astype(jnp.float32).reshape(rows, group_half, DGROUP, columns)
    weights = gate_maps.astype(jnp.float32).reshape(rows, LAYERS, 3, group_half, 1, columns)
    for layer_index in range(LAYERS):
        dilation = 3**layer_index
        padded = widen(volume, dilation)
        left_part = padded[..., :columns]
        right_part = padded[..., 2 * dilation :]
        first = weights[:, layer_index, 0]
        middle = weights[:, layer_index, 1]
        last = weights[:, layer_index, 2]
        volume = (first * left_part + middle * volume + last * right_part) / (first + middle + last)
    logits = SHARPNESS * volume.reshape(rows, half_disp, columns)
    disp_values = (view_index * half_disp + jnp.arange(half_disp)).astype(jnp.float32)
    maxima = jnp.max(logits, axis=1)
    exponent = jnp.exp(logits - maxima[:, None, :])
    totals = jnp.sum(exponent, axis=1)
    moments = jnp.sum(exponent * disp_values[None, :, None], axis=1)
    maxima, totals, moments = combined_all((maxima, totals, moments), "view", combine_halves)
    return moments / totals / DISP + line_offsets.astype(jnp.float32)[:, None] / DISP


def on_device(features, valid_cols, offsets, guide_weight):
    view_index = lax.axis_index("view")
    own_view = features[0]
    block_rows = own_view.shape[0]
    channels = own_view.shape[1]
    half_disp = DISP // 2
    group_half = half_disp // DGROUP
    mask_sec = valid_cols[1].astype(jnp.bfloat16)
    own_view = jnp.where(view_index == 1, own_view * mask_sec[None, None, :], own_view)
    sub_rows = block_rows // lax.axis_size("cols")
    line_offsets = lax.dynamic_slice_in_dim(offsets, lax.axis_index("cols") * sub_rows, sub_rows, 0)
    own_view = lax.all_to_all(own_view, "cols", split_axis=0, concat_axis=2, tiled=True)
    mask_ref = lax.all_gather(valid_cols[0], "cols", axis=0, tiled=True).astype(jnp.float32)
    row_count, channels, shard_cols = own_view.shape
    opposite = partner(own_view, "view", 0)
    ref_view = jnp.where(view_index == 0, own_view, opposite)
    sec_view = jnp.where(view_index == 0, opposite, own_view)
    left_rim = jnp.zeros((row_count, channels, RIM), sec_view.dtype)
    extended = jnp.concatenate([left_rim, sec_view], axis=2)
    window_len = shard_cols + half_disp - 1
    starts = left_rim.shape[2] - view_index * half_disp - line_offsets - (half_disp - 1)
    windows = jax.vmap(
        lambda one_row, start_col: lax.dynamic_slice_in_dim(one_row, start_col, window_len, 1)
    )(extended, starts)
    tile_cols = min(128, shard_cols)
    tile_count = shard_cols // tile_cols
    tile_reach = tile_cols + half_disp - 1
    corr_scale = 1.0 / math.sqrt(channels)

    def correlate(packed):
        ref_row, win_row = packed
        ref_tiles = ref_row.reshape(channels, tile_count, tile_cols)
        win_tiles = jnp.stack(
            [
                win_row[:, tile_index * tile_cols : tile_index * tile_cols + tile_reach]
                for tile_index in range(tile_count)
            ],
            axis=1,
        )
        products = jnp.einsum(
            "cta,ctb->tab", ref_tiles, win_tiles, preferred_element_type=jnp.float32
        )
        flattened = products.reshape(tile_count, tile_cols * tile_reach)
        flattened = jnp.pad(flattened, ((0, 0), (0, tile_cols)))
        diagonals = flattened.reshape(tile_count, tile_cols, tile_reach + 1)[:, :, :half_disp]
        raw_cost = jnp.transpose(diagonals[:, :, ::-1], (2, 0, 1)).reshape(half_disp, shard_cols)
        return (raw_cost * corr_scale * mask_ref[None, :]).astype(jnp.bfloat16)

    costs = lax.map(correlate, (ref_view, windows))
    selected = lax.dynamic_slice_in_dim(
        guide_weight.reshape(channels, LAYERS * 3, -1), view_index * group_half, group_half, 2
    ).reshape(channels, -1)
    logits_gate = jnp.einsum("hcw,ck->hkw", ref_view, selected, preferred_element_type=jnp.float32)
    gate_maps = (0.1 + 0.9 * jax.nn.sigmoid(logits_gate)).astype(jnp.bfloat16)
    result = soft_disparity(costs, gate_maps, line_offsets, view_index)
    return result[None].astype(jnp.float32)


def solution(mesh):
    return jax.shard_map(
        on_device,
        mesh=mesh,
        in_specs=(
            P("view", ("tiles", "lines"), None, "cols"),
            P(None, ("tiles", "cols")),
            P(("tiles", "lines")),
            P(),
        ),
        out_specs=P(("tiles", "lines"), "cols", None),
        check_vma=False,
    )
```

profile of v0, /device:TPU:0, one launch (start us, length us, event | category | flops | bytes accessed | tf_op | source)
XLA Modules:
  0.0 79.1 jit_solution(14868269091857640258)
XLA Ops:
  0.7 1.9 %multiply_select_fusion = bf16[16,64,256]{2,1,0:T(8,128)(2,1)} fusion(bf16[1,16,64,256]{3,2,1,0:T(8,128)(2,1)} %param.6, pred[]{:T(512)S(6)} %eq.8, bf16[256]{0:T(256)(128)(2,1)S(1)} %fusion.41), kind=kLoop, calls=%fused_computation.60 | loop fusion | flops 524288 | bytes 1049089 | tf_op jit(solution)/shard_map/jit(_where)/select_n | solution.py:79
  2.6 6.4 %all-to-all-start = ((bf16[16,64,256]{2,1,0:T(8,128)(2,1)}), bf16[16,64,256]{2,1,0:T(8,128)(2,1)S(1)}, u32[]{:S(2)}, u32[]{:S(2)}) async-start(bf16[16,64,256]{2,1,0:T(8,128)(2,1)} %multiply_select_fusion), calls=%async_computation | async-start | bytes 1048576 | tf_op jit(solution)/shard_map/all_to_all | solution.py:82
  9.0 14.5 %all-to-all-done = bf16[16,64,256]{2,1,0:T(8,128)(2,1)S(1)} async-done(((bf16[16,64,256]{2,1,0:T(8,128)(2,1)}), bf16[16,64,256]{2,1,0:T(8,128)(2,1)S(1)}, u32[]{:S(2)}, u32[]{:S(2)}) %all-to-all-start) | async-done | bytes 524320 | tf_op jit(solution)/shard_map/all_to_all | solution.py:82
  24.6 9.0 %all-gather = s32[1,1024]{1,0:T(1,128)S(1)} all-gather(s32[1,256]{1,0:T(1,128)S(1)} %slice-done), channel_id=2, replica_groups=mesh['tiles'=2,'cols'=4,'lines'=2,'view'=2] {'cols'}, dimensions={1}, use_global_device_ids=true | all-gather | bytes 5120 | tf_op jit(solution)/shard_map/all_gather | solution.py:83
  35.7 0.8 %add_add_fusion.1 = (f32[4,6,1024]{2,0,1:T(4,128)}, f32[4,6,1024]{2,0,1:T(4,128)}, f32[4,6,1024]{2,0,1:T(4,128)}) fusion(f32[4,3,3,6,1,1024]{5,0,3,4,2,1:T(4,128)S(1)} %bitcast.145, f32[4,3,3,6,1,1024]{5,0,3,2,1,4:T(4,128)S(1)} %bitcast.146), kind=kLoop, calls=%fused_computation.74 | loop fusion | flops 147456 | bytes 1179648 | tf_op jit(solution)/shard_map/add | solution.py:60
  36.5 0.8 %slice_bitcast_fusion.16 = (f32[4,6,1024]{2,0,1:T(4,128)}, f32[4,6,1024]{2,0,1:T(4,128)}, f32[4,6,1024]{2,0,1:T(4,128)}, f32[4,6,1024]{2,0,1:T(4,128)}, f32[4,6,1024]{2,0,1:T(4,128)}, /*index=5*/f32[4,6,1024]{2,0,1:T(4,128)S(1)}) fusion(f32[4,3,3,6,1,1024]{5,0,3,4,2,1:T(4,128)S(1)} %bitcast.147), kind=kLoop, calls=%fused_computation.72 | loop fusion | bytes 1179648 | tf_op jit(solution)/shard_map/mul | solution.py:60
  37.5 11.3 %while.10 = (s32[]{:T(128)}, bf16[4,64,1248]{2,1,0:T(8,128)(2,1)S(1)}, s32[4,3]{1,0:T(4,128)S(1)}, bf16[4,64,1119]{2,1,0:T(8,128)(2,1)}, s32[]{:T(128)}) while((s32[]{:T(128)}, bf16[4,64,1248]{2,1,0:T(8,128)(2,1)S(1)}, s32[4,3]{1,0:T(4,128)S(1)}, bf16[4,64,1119]{2,1,0:T(8,128)(2,1)}, s32[]{:T(128)}) %tuple.58), condition=%wide.while_cond, body=%wide.while_body.sunk | while | flops 2 | bytes 291829 | solution.py:93
  38.2 2.1 %dynamic-slice_dynamic-update-slice_fusion.2 = bf16[4,64,1119]{2,1,0:T(8,128)(2,1)} fusion(bf16[4,64,1119]{2,1,0:T(8,128)(2,1)} %get-tuple-element.225, s32[]{:T(128)S(6)} %copy.114, bf16[4,64,1248]{2,1,0:T(8,128)(2,1)S(1)} %get-tuple-element.228, s32[]{:T(128)} %bitcast.141, s32[]{:T(128)} %bitcast.142), kind=kLoop, calls=%fused_computation.24.clone.1 | loop fusion | bytes 291716 | tf_op jit(solution)/shard_map/vmap()/gather
  41.0 2.1 %dynamic-slice_dynamic-update-slice_fusion.2 = bf16[4,64,1119]{2,1,0:T(8,128)(2,1)} fusion(bf16[4,64,1119]{2,1,0:T(8,128)(2,1)} %get-tuple-element.225, s32[]{:T(128)S(6)} %copy.114, bf16[4,64,1248]{2,1,0:T(8,128)(2,1)S(1)} %get-tuple-element.228, s32[]{:T(128)} %bitcast.141, s32[]{:T(128)} %bitcast.142), kind=kLoop, calls=%fused_computation.24.clone.1 | loop fusion | bytes 291716 | tf_op jit(solution)/shard_map/vmap()/gather
  43.8 2.1 %dynamic-slice_dynamic-update-slice_fusion.2 = bf16[4,64,1119]{2,1,0:T(8,128)(2,1)} fusion(bf16[4,64,1119]{2,1,0:T(8,128)(2,1)} %get-tuple-element.225, s32[]{:T(128)S(6)} %copy.114, bf16[4,64,1248]{2,1,0:T(8,128)(2,1)S(1)} %get-tuple-element.228, s32[]{:T(128)} %bitcast.141, s32[]{:T(128)} %bitcast.142), kind=kLoop, calls=%fused_computation.24.clone.1 | loop fusion | bytes 291716 | tf_op jit(solution)/shard_map/vmap()/gather
  46.7 2.1 %dynamic-slice_dynamic-update-slice_fusion.2 = bf16[4,64,1119]{2,1,0:T(8,128)(2,1)} fusion(bf16[4,64,1119]{2,1,0:T(8,128)(2,1)} %get-tuple-element.225, s32[]{:T(128)S(6)} %copy.114, bf16[4,64,1248]{2,1,0:T(8,128)(2,1)S(1)} %get-tuple-element.228, s32[]{:T(128)} %bitcast.141, s32[]{:T(128)} %bitcast.142), kind=kLoop, calls=%fused_computation.24.clone.1 | loop fusion | bytes 291716 | tf_op jit(solution)/shard_map/vmap()/gather
  48.8 18.2 %while.9 = (s32[]{:T(128)}, bf16[4,96,1024]{2,1,0:T(8,128)(2,1)}, bf16[4,64,1024]{2,1,0:T(8,128)(2,1)S(1)}, bf16[4,64,1119]{2,1,0:T(8,128)(2,1)}, f32[1024]{0:T(1024)S(1)}, /*index=5*/s32[]{:T(128)}, f32[]{:T(128)}) while((s32[]{:T(128)}, bf16[4,96,1024]{2,1,0:T(8,128)(2,1)}, bf16[4,64,1024]{2,1,0:T(8,128)(2,1)S(1)}, ...), condition=%wide.region_1.2_spmd, body=%wide.region_0.1_spmd.sunk | while | flops 29426688 | bytes 11057893 | solution.py:119
  48.8 0.9 %dynamic-slice_bitcast_fusion.4 = bf16[64,1119]{1,0:T(8,128)(2,1)S(1)} fusion(bf16[4,64,1119]{2,1,0:T(8,128)(2,1)} %get-tuple-element.249, s32[]{:T(128)S(6)} %copy.120), kind=kLoop, calls=%fused_computation.2.clone.1 | loop fusion | bytes 286468 | tf_op jit(solution)/shard_map/while/body/jit(dynamic_index_in_dim)/squeeze | solution.py:119
  51.6 0.7 rev.7
  53.4 0.9 %dynamic-slice_bitcast_fusion.4 = bf16[64,1119]{1,0:T(8,128)(2,1)S(1)} fusion(bf16[4,64,1119]{2,1,0:T(8,128)(2,1)} %get-tuple-element.249, s32[]{:T(128)S(6)} %copy.120), kind=kLoop, calls=%fused_computation.2.clone.1 | loop fusion | bytes 286468 | tf_op jit(solution)/shard_map/while/body/jit(dynamic_index_in_dim)/squeeze | solution.py:119
  57.9 0.9 %dynamic-slice_bitcast_fusion.4 = bf16[64,1119]{1,0:T(8,128)(2,1)S(1)} fusion(bf16[4,64,1119]{2,1,0:T(8,128)(2,1)} %get-tuple-element.249, s32[]{:T(128)S(6)} %copy.120), kind=kLoop, calls=%fused_computation.2.clone.1 | loop fusion | bytes 286468 | tf_op jit(solution)/shard_map/while/body/jit(dynamic_index_in_dim)/squeeze | solution.py:119
  62.5 0.9 %dynamic-slice_bitcast_fusion.4 = bf16[64,1119]{1,0:T(8,128)(2,1)S(1)} fusion(bf16[4,64,1119]{2,1,0:T(8,128)(2,1)} %get-tuple-element.249, s32[]{:T(128)S(6)} %copy.120), kind=kLoop, calls=%fused_computation.2.clone.1 | loop fusion | bytes 286468 | tf_op jit(solution)/shard_map/while/body/jit(dynamic_index_in_dim)/squeeze | solution.py:119
  67.1 1.4 %convert.6 = f32[4,6,16,1024]{3,2,1,0:T(8,128)S(1)} convert(bf16[4,6,16,1024]{3,2,1,0:T(8,128)(2,1)} %bitcast.150) | non-fusion elementwise | flops 393216 | bytes 2359296 | tf_op jit(solution)/shard_map/reshape | solution.py:50
  69.6 1.0 %fusion.14 = f32[4,6,16,1024]{3,2,1,0:T(8,128)S(1)} fusion(f32[4,6,16,1024]{3,2,1,0:T(8,128)S(1)} %convert.6, f32[4,6,1024]{2,1,0:T(8,128)S(1)} %copy.79, f32[4,6,1024]{2,1,0:T(8,128)S(1)} %copy.78, f32[4,6,1024]{2,1,0:T(8,128)S(1)} %copy.77, f32[4,6,1024]{2,1,0:T(8,128)S(1)} %copy.73), kind=kLoop, calls=%fused_computation.35 | loop fusion | flops 2359296 | bytes 3538944 | tf_op jit(solution)/shard_map/div | solution.py:60
  70.6 1.0 %fusion.19 = f32[4,6,16,1024]{3,2,1,0:T(8,128)S(1)} fusion(f32[4,6,16,1024]{3,2,1,0:T(8,128)S(1)} %fusion.14, f32[4,6,1024]{2,1,0:T(8,128)S(1)} %copy.83, f32[4,6,1024]{2,1,0:T(8,128)S(1)} %copy.82, f32[4,6,1024]{2,1,0:T(8,128)S(1)} %copy.81, f32[4,6,1024]{2,1,0:T(8,128)S(1)} %copy.71), kind=kLoop, calls=%fused_computation.40 | loop fusion | flops 2359296 | bytes 3538944 | tf_op jit(solution)/shard_map/div | solution.py:60
  71.5 1.0 %fusion.43 = (f32[4,1024]{1,0:T(4,128)S(1)}, f32[4,6,16,1024]{3,2,1,0:T(8,128)S(1)}) fusion(f32[4,6,1024]{2,1,0:T(8,128)S(1)} %copy.87, f32[4,6,1024]{2,1,0:T(8,128)S(1)} %copy.86, f32[4,6,16,1024]{3,2,1,0:T(8,128)S(1)} %fusion.19, f32[4,6,1024]{2,1,0:T(8,128)S(1)} %copy.85, f32[4,6,1024]{2,1,0:T(8,128)S(1)} %copy.69), kind=kLoop, calls=%fused_computation.96 | loop fusion | flops 3141632 | bytes 3555328 | tf_op jit(solution)/shard_map/reduce_max | solution.py:63
  72.6 1.8 %all-gather.5 = f32[2,4,1024]{2,1,0:T(4,128)S(1)} all-gather(f32[1,4,1024]{2,1,0:T(4,128)S(1)} %bitcast.151), channel_id=4, replica_groups=mesh['tiles'=2,'cols'=4,'lines'=2,'view'=2] {'view'}, dimensions={0}, use_global_device_ids=true | all-gather | bytes 49152 | tf_op jit(solution)/shard_map/all_gather | solution.py:18
  74.8 1.8 %all-gather.6 = f32[2,4,1024]{2,1,0:T(4,128)S(1)} all-gather(f32[1,4,1024]{2,1,0:T(4,128)S(1)} %bitcast.154), channel_id=5, replica_groups=mesh['tiles'=2,'cols'=4,'lines'=2,'view'=2] {'view'}, dimensions={0}, use_global_device_ids=true | all-gather | bytes 49152 | tf_op jit(solution)/shard_map/all_gather | solution.py:18
  76.6 1.8 %all-gather.4 = f32[2,4,1024]{2,1,0:T(4,128)S(1)} all-gather(f32[1,4,1024]{2,1,0:T(4,128)S(1)} %bitcast.153), channel_id=3, replica_groups=mesh['tiles'=2,'cols'=4,'lines'=2,'view'=2] {'view'}, dimensions={0}, use_global_device_ids=true | all-gather | bytes 49152 | tf_op jit(solution)/shard_map/all_gather | solution.py:18
  (152 shorter events, 22.0 us)
Async XLA Ops:
  2.6 21.8 %copy-start.12 = (s32[16]{0:T(128)S(1)}, s32[16]{0:T(128)}, u32[]{:S(2)}) copy-start(s32[16]{0:T(128)} %param.8) | copy-start | bytes 196
  2.6 22.0 %slice-start = ((s32[2,256]{1,0:T(2,128)}), s32[1,256]{1,0:T(1,128)S(1)}, s32[]{:S(2)}) async-start(s32[2,256]{1,0:T(2,128)} %param.7), calls=%async_computation.1 | async-start | bytes 2048 | tf_op jit(solution)/shard_map/slice | solution.py:83
  2.6 31.0 %copy-start.11 = (bf16[64,108]{1,0:T(8,128)(2,1)S(1)}, bf16[64,108]{1,0:T(8,128)(2,1)}, u32[]{:S(2)}) copy-start(bf16[64,108]{1,0:T(8,128)(2,1)} %param.9) | copy-start | bytes 41476
  2.6 20.9 %all-to-all-start = ((bf16[16,64,256]{2,1,0:T(8,128)(2,1)}), bf16[16,64,256]{2,1,0:T(8,128)(2,1)S(1)}, u32[]{:S(2)}, u32[]{:S(2)}) async-start(bf16[16,64,256]{2,1,0:T(8,128)(2,1)} %multiply_select_fusion), calls=%async_computation | async-start | bytes 1048576 | tf_op jit(solution)/shard_map/all_to_all | solution.py:82
  24.3 9.6 %collective-permute-start = (bf16[4,64,1024]{2,1,0:T(8,128)(2,1)S(1)}, bf16[4,64,1024]{2,1,0:T(8,128)(2,1)S(1)}, u32[]{:S(2)}, u32[]{:S(2)}) collective-permute-start(bf16[4,64,1024]{2,1,0:T(8,128)(2,1)S(1)} %all_to_all.16), channel_id=1, source_target_pairs={{0,1},{1,0},{2,3},{3,2},{4,5},{5,4},{6,7},{7,6},{8,9},{9,8},{10,11... | collective-permute-start | bytes 1572872 | tf_op jit(solution)/shard_map/ppermute | solution.py:29
  67.0 1.5 %copy-start.10 = (f32[4,6,1024]{2,0,1:T(4,128)S(1)}, f32[4,6,1024]{2,0,1:T(4,128)}, u32[]{:S(2)}) copy-start(f32[4,6,1024]{2,0,1:T(4,128)} %get-tuple-element.143) | copy-start | bytes 294916
  67.0 1.6 %copy-start.9 = (f32[4,6,1024]{2,0,1:T(4,128)S(1)}, f32[4,6,1024]{2,0,1:T(4,128)}, u32[]{:S(2)}) copy-start(f32[4,6,1024]{2,0,1:T(4,128)} %get-tuple-element.144) | copy-start | bytes 294916
  67.0 1.6 %copy-start.8 = (f32[4,6,1024]{2,0,1:T(4,128)S(1)}, f32[4,6,1024]{2,0,1:T(4,128)}, u32[]{:S(2)}) copy-start(f32[4,6,1024]{2,0,1:T(4,128)} %get-tuple-element.145) | copy-start | bytes 294916
  67.0 1.7 %copy-start.5 = (f32[4,6,1024]{2,0,1:T(4,128)S(1)}, f32[4,6,1024]{2,0,1:T(4,128)}, u32[]{:S(2)}) copy-start(f32[4,6,1024]{2,0,1:T(4,128)} %get-tuple-element.154) | copy-start | bytes 294916
  67.0 1.8 %copy-start.3 = (f32[4,6,1024]{2,0,1:T(4,128)S(1)}, f32[4,6,1024]{2,0,1:T(4,128)}, u32[]{:S(2)}) copy-start(f32[4,6,1024]{2,0,1:T(4,128)} %get-tuple-element.155) | copy-start | bytes 294916
  67.0 1.9 %copy-start.1 = (f32[4,6,1024]{2,0,1:T(4,128)S(1)}, f32[4,6,1024]{2,0,1:T(4,128)}, u32[]{:S(2)}) copy-start(f32[4,6,1024]{2,0,1:T(4,128)} %get-tuple-element.156) | copy-start | bytes 294916
  67.0 1.9 %copy-start.7 = (f32[4,6,1024]{2,0,1:T(4,128)S(1)}, f32[4,6,1024]{2,0,1:T(4,128)}, u32[]{:S(2)}) copy-start(f32[4,6,1024]{2,0,1:T(4,128)} %get-tuple-element.148) | copy-start | bytes 294916
  67.0 2.0 %copy-start.6 = (f32[4,6,1024]{2,0,1:T(4,128)S(1)}, f32[4,6,1024]{2,0,1:T(4,128)}, u32[]{:S(2)}) copy-start(f32[4,6,1024]{2,0,1:T(4,128)} %get-tuple-element.149) | copy-start | bytes 294916
  67.0 2.1 %copy-start.4 = (f32[4,6,1024]{2,0,1:T(4,128)S(1)}, f32[4,6,1024]{2,0,1:T(4,128)}, u32[]{:S(2)}) copy-start(f32[4,6,1024]{2,0,1:T(4,128)} %get-tuple-element.150) | copy-start | bytes 294916
  68.5 0.9 %copy-start.2 = (f32[4,6,1024]{2,0,1:T(4,128)S(1)}, f32[4,6,1024]{2,0,1:T(4,128)}, u32[]{:S(2)}) copy-start(f32[4,6,1024]{2,0,1:T(4,128)} %get-tuple-element.151) | copy-start | bytes 294916
  68.5 1.0 %copy-start = (f32[4,6,1024]{2,0,1:T(4,128)S(1)}, f32[4,6,1024]{2,0,1:T(4,128)}, u32[]{:S(2)}) copy-start(f32[4,6,1024]{2,0,1:T(4,128)} %get-tuple-element.152) | copy-start | bytes 294916
where the time goes:
time: 79.6 us; the launch traced here: 79.1 us
  local copies, waits for them, and re-layouts  31.1 us (39%)
  waiting for transfers between devices  14.5 us (18%)
  blocking collectives  14.5 us (18%)
  other arithmetic  9.92 us (12%)
  starting transfers between devices  6.52 us (8%)
  matrix products  1.77 us (2%)
    all_to_all x1, waiting for transfers between devices, on_device(): lax.all_to_all(own_view, 'cols', split_axis=0, concat_axis=2, tiled=True)  14.5 us
    gather x12, local copies, waits for them, and re-layouts  11.2 us
    all_gather x1, blocking collectives, on_device(): lax.all_gather(valid_cols[0], 'cols', axis=0, tiled=True)  9.01 us
    all_to_all x1, starting transfers between devices, on_device(): lax.all_to_all(own_view, 'cols', split_axis=0, concat_axis=2, tiled=True)  6.45 us
    all_gather x3, blocking collectives, combined_all(): gathered = jax.tree.map(lambda a: lax.all_gather(a, axis), part)  5.48 us
    squeeze x4, local copies, waits for them, and re-layouts, on_device(): costs = lax.map(correlate, (ref_view, windows))  3.71 us
    dynamic_update_slice x8, local copies, waits for them, and re-layouts, on_device(): costs = lax.map(correlate, (ref_view, windows))  3.33 us
    rev x4, local copies, waits for them, and re-layouts, correlate(): diagonals[:, :, ::-1]  2.86 us
  transfers between devices with their start and end apart: 2, of which 1 were waited for; matrix products, arithmetic and copies ran while one was open for 1% of the time, Pallas kernels for 0%

commit v1 on v0

v1 whole, which is shorter than its diff:
```python
import functools
import math

import jax
import jax.numpy as jnp
from jax import lax
from jax.experimental import pallas as pl
from jax.experimental.pallas import tpu as pltpu
from jax.sharding import PartitionSpec as P

DISP = 192
DGROUP = 16
GROUPS = DISP // DGROUP
LAYERS = 3
SHARPNESS = 2.0
HALO = 32
CUT = 16
STEP = 3
LANES = 128
LINES = 8
CHANNELS = 64
BLOCK = 256
SPAN = BLOCK + HALO
USED = SPAN // STEP
KEYS = 112
PACK = LANES // HALO
OUT = BLOCK + LANES

BF = jnp.bfloat16
F32 = jnp.float32


def iota(shape, dim):
    return lax.broadcasted_iota(jnp.int32, shape, dim)


def dot_t(a, b, precision=None):
    return lax.dot_general(
        a, b, (((1,), (1,)), ((), ())), preferred_element_type=F32, precision=precision
    )


def column_of(n_shape, lane_dim):
    lane = iota(n_shape, lane_dim)
    return SPAN - 1 - STEP * (lane & (LANES - 1)) - (lane >> 7), (lane & (LANES - 1)) < USED


def kernel(
    scal, kept, swapped, sec_a, sec_b, halo_a, halo_b, mask_own, mask_left, guide, out, vol, gate, ref_rows
):
    first_view = scal[0] == 0
    first_block = scal[1] == 0

    def pick(a, b):
        return jnp.where(first_view, a, b)

    for line in range(LINES):
        lo = line * CHANNELS
        ref_rows[lo : lo + CHANNELS, LANES:] = pick(kept[line], swapped[line])
        packed = pick(halo_a[line // PACK], halo_b[line // PACK]).astype(F32)
        turn = (LANES - HALO) - HALO * (line % PACK)
        if turn:
            packed = pltpu.roll(packed, turn, 1)
        ref_rows[lo : lo + CHANNELS, :LANES] = packed.astype(BF)

    wide = STEP * LANES
    col, real = column_of((wide, wide), 0)
    place = iota((wide, wide), 1)
    perm = jnp.where(real & (place == col + (LANES - HALO)), 1.0, 0.0).astype(BF)
    ref_mask = jnp.concatenate([mask_left[0:1, BLOCK - LANES :], mask_own[0:1, :]], axis=1).astype(F32)
    ref_mask = ref_mask * (1.0 / math.sqrt(CHANNELS))
    mask_cols = dot_t(perm, jnp.broadcast_to(ref_mask, (BLOCK, wide)).astype(BF))
    sec_mask = jnp.concatenate([mask_left[1:2, :], mask_own[1:2, :]], axis=1).astype(F32)

    eye = jnp.where(iota((KEYS, KEYS), 0) == iota((KEYS, KEYS), 1), 1.0, 0.0).astype(BF)
    keys = LAYERS * 3 * GROUPS
    guide_t = dot_t(eye[:, :keys], guide[...]).astype(BF)
    zero_guide = jnp.zeros((KEYS, CHANNELS), BF)

    disp_row = iota((DISP, 2 * LANES), 0)
    flip = jnp.where(iota((DISP, 2 * LANES), 1) == 2 * LANES - 1 - disp_row, 1.0, 0.0).astype(BF)

    lane = iota((8, LANES), 1)
    skewed = lane - STEP * iota((8, LANES), 0)

    for quad in range(LINES // 4):
        rows = ref_rows[quad * 4 * CHANNELS : (quad + 1) * 4 * CHANNELS, :]
        ref_t = dot_t(perm, rows)
        guides = jnp.concatenate(
            [
                jnp.concatenate([guide_t if a == b else zero_guide for a in range(4)], axis=1)
                for b in range(4)
            ],
            axis=0,
        )
        logits = dot_t(guides, ref_t.astype(BF))
        ref_t = (ref_t * mask_cols).astype(BF)
        for q in range(4):
            line = quad * 4 + q
            for t in range(STEP):
                gate[t, pl.ds(line, KEYS, stride=8), :] = logits[
                    q * KEYS : (q + 1) * KEYS, t * LANES : (t + 1) * LANES
                ]
            off = scal[2 + line]
            left = pick(sec_b[line], sec_a[line]).astype(F32) * sec_mask[:, :BLOCK]
            own = pick(swapped[line], kept[line]).astype(F32) * sec_mask[:, BLOCK:]
            tiles = [left[:, :LANES], left[:, LANES:], own[:, :LANES], own[:, LANES:]]
            tiles = [pltpu.roll(tile, off, 1) for tile in tiles]
            ch_lane = iota((CHANNELS, LANES), 1)
            shifted = [
                jnp.where(ch_lane < off, tiles[max(i - 1, 0)], tiles[i]).astype(BF) for i in range(4)
            ]
            shifted = jnp.concatenate(shifted, axis=1)
            lhs = ref_t[:, q * CHANNELS : (q + 1) * CHANNELS]
            blocks = []
            for t in range(STEP):
                products = jnp.dot(
                    lhs[t * LANES : t * LANES + USED], shifted, preferred_element_type=F32
                )
                parts = []
                for j in range(USED // 8):
                    base = 8 * STEP * j + t
                    rolled = {}

                    def turned(i):
                        if i not in rolled:
                            tile = products[8 * j : 8 * j + 8, i * LANES : (i + 1) * LANES]
                            turn = base % LANES
                            if turn + 7 * STEP >= LANES:
                                tile = pltpu.roll(tile, turn, 1)
                                turn = 0
                            rolled[i] = pltpu.roll(tile, turn, 1, stride=STEP, stride_axis=0)
                        return rolled[i]

                    pair = []
                    for v in (2, 3):
                        lowest = max(v + (-7 * STEP - base) // LANES, 0)
                        highest = v + (LANES - 1 - base) // LANES
                        value = turned(lowest)
                        for i in range(lowest + 1, highest + 1):
                            value = jnp.where(skewed >= base + LANES * (i - v), turned(i), value)
                        pair.append(value)
                    parts.append(jnp.concatenate(pair, axis=1))
                parts.append(jnp.zeros((LANES - USED, 2 * LANES), F32))
                blocks.append(jnp.concatenate(parts, axis=0).astype(BF))
            costs = dot_t(flip, jnp.concatenate(blocks, axis=0))
            for t in range(STEP):
                vol[t, pl.ds(line, DISP, stride=8), :] = costs[:, t * LANES : (t + 1) * LANES]

    inside = []
    for t in range(STEP):
        col_t = SPAN - 1 - t - STEP * lane
        keep = (lane < USED) & ((col_t >= HALO) | jnp.logical_not(first_block))
        inside.append(jnp.where(keep, 1.0, 0.0))

    def aggregate(group, largest):
        weights = []
        for layer in range(LAYERS):
            per_tile = []
            for t in range(STEP):
                taps = []
                for tap in range(3):
                    at = pl.multiple_of(((3 * layer + tap) * GROUPS + group) * 8, 8)
                    z = gate[t, pl.ds(at, 8), :]
                    taps.append((0.55 + 0.45 * jnp.tanh(0.5 * z)).astype(BF).astype(F32))
                scale = inside[t] / (taps[0] + taps[1] + taps[2])
                per_tile.append([tap * scale for tap in taps])
            weights.append(per_tile)
        largest = list(largest)
        for d in range(DGROUP):
            at = pl.multiple_of((group * DGROUP + d) * 8, 8)
            v = [vol[t, pl.ds(at, 8), :] for t in range(STEP)]
            before = [v[1], v[2], pltpu.roll(v[0], LANES - 1, 1)]
            after = [pltpu.roll(v[2], 1, 1), v[0], v[1]]
            for layer in range(LAYERS):
                if layer:
                    turn = 3 ** (layer - 1)
                    before = [pltpu.roll(a, LANES - turn, 1) for a in v]
                    after = [pltpu.roll(a, turn, 1) for a in v]
                w = weights[layer]
                v = [
                    w[t][0] * before[t] + w[t][1] * v[t] + w[t][2] * after[t] for t in range(STEP)
                ]
            for t in range(STEP):
                vol[t, pl.ds(at, 8), :] = v[t]
                largest[t] = jnp.maximum(largest[t], v[t])
        return tuple(largest)

    lowest = jnp.full((8, LANES), -jnp.inf, F32)
    largest = lax.fori_loop(0, GROUPS, aggregate, (lowest,) * STEP)

    def accumulate(group, state):
        totals, moments = list(state[:STEP]), list(state[STEP:])
        base = (group * DGROUP).astype(F32)
        for t in range(STEP):
            part = jnp.zeros((8, LANES), F32)
            first = jnp.zeros((8, LANES), F32)
            for d in range(DGROUP):
                at = pl.multiple_of((group * DGROUP + d) * 8, 8)
                e = jnp.exp(SHARPNESS * (vol[t, pl.ds(at, 8), :] - largest[t]))
                part = part + e
                if d:
                    first = first + e * float(d)
            totals[t] = totals[t] + part
            moments[t] = moments[t] + (first + base * part)
        return tuple(totals + moments)

    zero = jnp.zeros((8, LANES), F32)
    state = lax.fori_loop(0, GROUPS, accumulate, (zero,) * (2 * STEP))
    offs = zero
    for line in range(LINES):
        offs = jnp.where(iota((8, LANES), 0) == line, scal[2 + line].astype(F32), offs)
    flat = jnp.concatenate(
        [(state[STEP + t] / state[t] + offs) * (1.0 / DISP) for t in range(STEP)], axis=1
    )
    col, real = column_of((wide, OUT), 0)
    place = iota((wide, OUT), 1)
    want = jnp.where(
        place < BLOCK - CUT,
        place + HALO,
        jnp.where(place < BLOCK, place - (BLOCK - CUT) + CUT, place + (SPAN - CUT - BLOCK)),
    )
    spread = jnp.where(real & (want == col), 1.0, 0.0)
    out[...] = jnp.dot(flat, spread, preferred_element_type=F32, precision=lax.Precision.HIGHEST)


def disparities(scal, *arrays):
    specs = [pl.BlockSpec(memory_space=pltpu.SMEM)] + [pl.BlockSpec(memory_space=pltpu.VMEM)] * 9
    return pl.pallas_call(
        kernel,
        out_shape=jax.ShapeDtypeStruct((LINES, OUT), F32),
        in_specs=specs,
        out_specs=pl.BlockSpec(memory_space=pltpu.VMEM),
        scratch_shapes=[
            pltpu.VMEM((STEP, DISP * 8, LANES), F32),
            pltpu.VMEM((STEP, KEYS * 8, LANES), F32),
            pltpu.VMEM((LINES * CHANNELS, STEP * LANES), BF),
        ],
        compiler_params=pltpu.CompilerParams(vmem_limit_bytes=32 * 1024 * 1024),
        cost_estimate=pl.CostEstimate(flops=4_000_000_000, bytes_accessed=2_000_000, transcendentals=1_000_000),
    )(scal, *arrays)


def pack_halo(block):
    tail = block[:, :, BLOCK - HALO :].reshape(LINES // PACK, PACK, CHANNELS, HALO)
    return jnp.concatenate([tail[:, p] for p in range(PACK)], axis=2)


def on_device(features, valid_cols, offsets, guide_weight):
    own = features[0]
    n = lax.axis_size("cols")
    view = lax.axis_index("view")
    block = lax.axis_index("cols")
    both = ("cols", "view")

    def send(x, moves):
        return lax.ppermute(x, both, [(2 * a + b, 2 * c + d) for a, b, c, d in moves])

    kept = lax.dynamic_slice_in_dim(own, view * LINES, LINES, 0)
    given = lax.dynamic_slice_in_dim(own, (1 - view) * LINES, LINES, 0)
    steps = range(n - 1)
    sec_a = send(kept, [(c, 1, c + 1, 1) for c in steps])
    sec_b = send(given, [(c, 1, c + 1, 0) for c in steps])
    swapped = send(given, [(c, v, c, 1 - v) for c in range(n) for v in range(2)])
    halo_a = send(pack_halo(kept), [(c, 0, c + 1, 0) for c in steps])
    halo_b = send(pack_halo(given), [(c, 0, c + 1, 1) for c in steps])
    mask_left = send(valid_cols, [(c, v, c + 1, v) for c in steps for v in range(2)])
    my_offsets = lax.dynamic_slice_in_dim(offsets, view * LINES, LINES, 0)
    scal = jnp.concatenate([jnp.stack([view, block]).astype(jnp.int32), my_offsets])
    result = disparities(
        scal, kept, swapped, sec_a, sec_b, halo_a, halo_b, valid_cols, mask_left, guide_weight
    )

    sub = own.shape[0] // n
    pieces = []
    for k in range(n):
        target = lax.rem(block + k, n) // 2
        piece = lax.dynamic_slice_in_dim(result, target * sub, sub, 0)
        moves = []
        for c in range(n):
            for v in range(2):
                a, b = divmod((c + k) % n, 2)
                moves.append((c, v, n // 2 * v + a, b))
        pieces.append(send(piece, moves))
    mine = 2 * lax.rem(block, n // 2) + view
    ring = jnp.stack(pieces[::-1])
    ring = jnp.concatenate([ring, ring], axis=0)
    ordered = lax.dynamic_slice_in_dim(ring, lax.rem(2 * n - 1 - mine, n), n, 0)
    main = ordered[:, :, :BLOCK]
    tail = ordered[n - 1 :, :, BLOCK:]
    tail = jnp.concatenate([tail[:, :, CUT:], tail[:, :, :CUT]], axis=2)
    tail = jnp.concatenate([jnp.zeros_like(tail), tail], axis=2)
    following = jnp.concatenate([main[1:], tail], axis=0)
    columns = jnp.arange(BLOCK)
    joined = jnp.where(columns[None, None, :] < BLOCK - CUT, main, following)
    return jnp.transpose(joined, (1, 0, 2)).reshape(1, sub, n * BLOCK)


def solution(mesh):
    return jax.shard_map(
        on_device,
        mesh=mesh,
        in_specs=(
            P("view", ("tiles", "lines"), None, "cols"),
            P(None, ("tiles", "cols")),
            P(("tiles", "lines")),
            P(),
        ),
        out_specs=P(("tiles", "lines"), "cols", None),
        check_vma=False,
    )
```

time: 79.6 us -> 47.5 us (0.60)
  the two profiles are of different devices: /device:TPU:0 before, /device:TPU:1 now
where the time goes in v1:
time: 47.5 us; the launch traced here: 47.2 us
  starting transfers between devices  24.7 us (52%)
  Pallas kernels  12.7 us (27%)
  waiting for transfers between devices  6.3 us (13%)
  local copies, waits for them, and re-layouts  2.22 us (5%)
  other arithmetic  0.97 us (2%)
    ppermute x10, starting transfers between devices, send(): lax.ppermute(x, both, [(2 * a + b, 2 * c + d) for a, b, c, d in moves])  24.7 us
    pallas_call x1, Pallas kernels, disparities(): pl.pallas_call(kernel, out_shape=jax.ShapeDtypeStruct((LINES, OUT), F32),...  12.7 us
    ppermute x10, waiting for transfers between devices, send(): lax.ppermute(x, both, [(2 * a + b, 2 * c + d) for a, b, c, d in moves])  6.3 us
    dynamic_slice x1, local copies, waits for them, and re-layouts, on_device(): given = lax.dynamic_slice_in_dim(own, (1 - view) * LINES, LINES, 0)  1.08 us
  transfers between devices with their start and end apart: 10, of which 2 were waited for; matrix products, arithmetic and copies ran while one was open for 1% of the time, Pallas kernels for 0%

profile of v1, /device:TPU:1, one launch (start us, length us, event | category | flops | bytes accessed | tf_op | source)
XLA Modules:
  0.0 47.2 jit_solution(385922647554535679)
XLA Ops:
  0.0 1.1 %dynamic-slice_bitcast_fusion = (bf16[8,64,256]{2,1,0:T(8,128)(2,1)S(1)}, bf16[8,64,256]{2,1,0:T(8,128)(2,1)S(1)}) fusion(bf16[1,16,64,256]{3,2,1,0:T(8,128)(2,1)} %param.4, s32[]{:T(128)S(6)} %select_n.41, s32[]{:T(128)S(6)} %select_n.40), kind=kLoop, calls=%fused_computation | loop fusion | bytes 1048584 | tf_op jit(solution)/shard_map/dynamic_slice | solution.py:260
  1.1 4.6 %collective-permute-start.2 = (bf16[8,64,256]{2,1,0:T(8,128)(2,1)S(1)}, bf16[8,64,256]{2,1,0:T(8,128)(2,1)S(1)}, u32[]{:S(2)}, u32[]{:S(2)}) collective-permute-start(bf16[8,64,256]{2,1,0:T(8,128)(2,1)S(1)} %get-tuple-element.5), channel_id=1, source_target_pairs={{1,4},{5,8},{9,12},{3,6},{7,10},{11,14},{17,20},{21,24},{25,28},{1... | collective-permute-start | bytes 786440 | tf_op jit(solution)/shard_map/ppermute | solution.py:257
  5.7 0.1 collective-permute-start
  5.8 3.2 %collective-permute-start.5 = (s32[2,256]{1,0:T(2,128)S(1)}, s32[2,256]{1,0:T(2,128)S(1)}, u32[]{:S(2)}, u32[]{:S(2)}) collective-permute-start(s32[2,256]{1,0:T(2,128)S(1)} %copy-done.1), channel_id=1, source_target_pairs={{0,4},{1,5},{4,8},{5,9},{8,12},{9,13},{2,6},{3,7},{6,10},{7,11},{1... | collective-permute-start | bytes 6152 | tf_op jit(solution)/shard_map/ppermute | solution.py:257
  9.0 0.1 slice.65
  9.1 0.1 pad_maximum_fusion.1
  9.2 0.7 %collective-permute-start.4 = (bf16[2,64,128]{2,1,0:T(8,128)(2,1)S(1)}, bf16[2,64,128]{2,1,0:T(8,128)(2,1)S(1)}, u32[]{:S(2)}, u32[]{:S(2)}) collective-permute-start(bf16[2,64,128]{2,1,0:T(8,128)(2,1)S(1)} %pad_maximum_fusion.1), channel_id=1, source_target_pairs={{0,5},{4,9},{8,13},{2,7},{6,11},{10,15},{16,21},{20,25},{24,29},{1... | collective-permute-start | bytes 98312 | tf_op jit(solution)/shard_map/ppermute | solution.py:257
  9.9 3.8 %collective-permute-start.1 = (bf16[8,64,256]{2,1,0:T(8,128)(2,1)S(1)}, bf16[8,64,256]{2,1,0:T(8,128)(2,1)S(1)}, u32[]{:S(2)}, u32[]{:S(2)}) collective-permute-start(bf16[8,64,256]{2,1,0:T(8,128)(2,1)S(1)} %get-tuple-element.6.kept), channel_id=1, source_target_pairs={{1,5},{5,9},{9,13},{3,7},{7,11},{11,15},{17,21},{21,25},{25,29},{1... | collective-permute-start | bytes 786440 | tf_op jit(solution)/shard_map/ppermute | solution.py:257
  13.8 0.1 slice.60
  13.9 0.1 pad_maximum_fusion
  14.0 0.6 %copy-done.2 = s32[16]{0:T(128)S(1)} copy-done((s32[16]{0:T(128)S(1)}, s32[16]{0:T(128)}, u32[]{:S(2)}) %copy-start.2) | copy-done | bytes 88
  14.7 0.1 dynamic_slice.28
  14.7 0.7 %collective-permute-start.3 = (bf16[2,64,128]{2,1,0:T(8,128)(2,1)S(1)}, bf16[2,64,128]{2,1,0:T(8,128)(2,1)S(1)}, u32[]{:S(2)}, u32[]{:S(2)}) collective-permute-start(bf16[2,64,128]{2,1,0:T(8,128)(2,1)S(1)} %pad_maximum_fusion), channel_id=1, source_target_pairs={{0,4},{4,8},{8,12},{2,6},{6,10},{10,14},{16,20},{20,24},{24,28},{1... | collective-permute-start | bytes 98312 | tf_op jit(solution)/shard_map/ppermute | solution.py:257
  15.4 0.1 pad_add_fusion.scal
  15.5 0.0 copy-start
  15.6 1.5 %collective-permute-done.1.sec_a = bf16[8,64,256]{2,1,0:T(8,128)(2,1)S(1)} collective-permute-done((bf16[8,64,256]{2,1,0:T(8,128)(2,1)S(1)}, bf16[8,64,256]{2,1,0:T(8,128)(2,1)S(1)}, u32[]{:S(2)}, u32[]{:S(2)}) %collective-permute-start.1) | collective-permute-done | bytes 262176 | tf_op jit(solution)/shard_map/ppermute | solution.py:257
  17.0 12.7 %shard_map.46 = f32[8,384]{1,0:T(8,128)S(1)} custom-call(s32[10]{0:T(128)S(1)} %pad_add_fusion.scal, bf16[8,64,256]{2,1,0:T(8,128)(2,1)S(1)} %get-tuple-element.6.kept, bf16[8,64,256]{2,1,0:T(8,128)(2,1)S(1)} %collective-permute-done.swapped, bf16[8,64,256]{2,1,0:T(8,128)(2,1)S(1)} %collective-permute-done.1.sec_a, ...), custom_call_target="tpu_custom_call" | custom-call | flops 4000000000 | bytes 2000000 | tf_op jit(solution)/shard_map/pallas_call | solution.py:229
  29.8 3.3 %collective-permute-start.6 = (f32[4,384]{1,0:T(4,128)S(1)}, f32[4,384]{1,0:T(4,128)S(1)}, u32[]{:S(2)}, u32[]{:S(2)}) collective-permute-start(f32[4,384]{1,0:T(4,128)S(1)} %get-tuple-element.18), channel_id=1, source_target_pairs={{0,5},{1,13},{4,0},{5,8},{8,1},{9,9},{12,4},{13,12},{2,7},{3,15},{... | collective-permute-start | bytes 18440 | tf_op jit(solution)/shard_map/ppermute | solution.py:257
  33.1 3.3 %collective-permute-start.9 = (f32[4,384]{1,0:T(4,128)S(1)}, f32[4,384]{1,0:T(4,128)S(1)}, u32[]{:S(2)}, u32[]{:S(2)}) collective-permute-start(f32[4,384]{1,0:T(4,128)S(1)} %get-tuple-element.15), channel_id=1, source_target_pairs={{0,0},{1,8},{4,1},{5,9},{8,4},{9,12},{12,5},{13,13},{2,2},{3,10},{... | collective-permute-start | bytes 18440 | tf_op jit(solution)/shard_map/ppermute | solution.py:257
  36.4 5.0 %collective-permute-start.8 = (f32[4,384]{1,0:T(4,128)S(1)}, f32[4,384]{1,0:T(4,128)S(1)}, u32[]{:S(2)}, u32[]{:S(2)}) collective-permute-start(f32[4,384]{1,0:T(4,128)S(1)} %get-tuple-element.16), channel_id=1, source_target_pairs={{0,1},{1,9},{4,4},{5,12},{8,5},{9,13},{12,0},{13,8},{2,3},{3,11},{... | collective-permute-start | bytes 18440 | tf_op jit(solution)/shard_map/ppermute | solution.py:257
  41.4 0.1 collective-permute-start.7
  41.5 4.8 %collective-permute-done.7 = f32[4,384]{1,0:T(4,128)S(1)} collective-permute-done((f32[4,384]{1,0:T(4,128)S(1)}, f32[4,384]{1,0:T(4,128)S(1)}, u32[]{:S(2)}, u32[]{:S(2)}) %collective-permute-start.7) | collective-permute-done | bytes 6176 | tf_op jit(solution)/shard_map/ppermute | solution.py:257
  46.4 0.1 constant_dynamic-slice_fusion
  46.5 0.7 %dynamic-slice_select_fusion = f32[4,4,256]{2,1,0:T(4,128)} fusion(f32[8,4,384]{2,1,0:T(4,128)S(1)} %constant_dynamic-update-slice_fusion, s32[]{:T(128)S(6)} %select_n.50, f32[1,4,16]{2,1,0:T(4,128)S(1)} %constant_dynamic-slice_fusion.2, f32[1,4,112]{2,1,0:T(4,128)S(1)} %constant_dynamic-slice_fusion, f32[3,4,256]{2,1,0:T(4,128)S(1)} %constant_dynamic-slice_fusion.1, ...), kind=kLoop, calls=%fused_computation.20 | loop fusion | flops 16384 | bytes 51460 | tf_op jit(solution)/shard_map/jit(_where)/select_n | solution.py:295
  (28 shorter events, 0.2 us)
Async XLA Ops:
  0.0 5.8 %copy-start.1 = (s32[2,256]{1,0:T(2,128)S(1)}, s32[2,256]{1,0:T(2,128)}, u32[]{:S(2)}) copy-start(s32[2,256]{1,0:T(2,128)} %mask_own.1) | copy-start | bytes 6148
  1.1 14.5 %collective-permute-start.2 = (bf16[8,64,256]{2,1,0:T(8,128)(2,1)S(1)}, bf16[8,64,256]{2,1,0:T(8,128)(2,1)S(1)}, u32[]{:S(2)}, u32[]{:S(2)}) collective-permute-start(bf16[8,64,256]{2,1,0:T(8,128)(2,1)S(1)} %get-tuple-element.5), channel_id=1, source_target_pairs={{1,4},{5,8},{9,12},{3,6},{7,10},{11,14},{17,20},{21,24},{25,28},{1... | collective-permute-start | bytes 786440 | tf_op jit(solution)/shard_map/ppermute | solution.py:257
  5.7 9.9 %collective-permute-start = (bf16[8,64,256]{2,1,0:T(8,128)(2,1)S(1)}, bf16[8,64,256]{2,1,0:T(8,128)(2,1)S(1)}, u32[]{:S(2)}, u32[]{:S(2)}) collective-permute-start(bf16[8,64,256]{2,1,0:T(8,128)(2,1)S(1)} %get-tuple-element.5), channel_id=1, source_target_pairs={{0,1},{1,0},{4,5},{5,4},{8,9},{9,8},{12,13},{13,12},{2,3},{3,2},{6... | collective-permute-start | bytes 786440 | tf_op jit(solution)/shard_map/ppermute | solution.py:257
  5.8 8.9 %collective-permute-start.5 = (s32[2,256]{1,0:T(2,128)S(1)}, s32[2,256]{1,0:T(2,128)S(1)}, u32[]{:S(2)}, u32[]{:S(2)}) collective-permute-start(s32[2,256]{1,0:T(2,128)S(1)} %copy-done.1), channel_id=1, source_target_pairs={{0,4},{1,5},{4,8},{5,9},{8,12},{9,13},{2,6},{3,7},{6,10},{7,11},{1... | collective-permute-start | bytes 6152 | tf_op jit(solution)/shard_map/ppermute | solution.py:257
  9.2 6.3 %collective-permute-start.4 = (bf16[2,64,128]{2,1,0:T(8,128)(2,1)S(1)}, bf16[2,64,128]{2,1,0:T(8,128)(2,1)S(1)}, u32[]{:S(2)}, u32[]{:S(2)}) collective-permute-start(bf16[2,64,128]{2,1,0:T(8,128)(2,1)S(1)} %pad_maximum_fusion.1), channel_id=1, source_target_pairs={{0,5},{4,9},{8,13},{2,7},{6,11},{10,15},{16,21},{20,25},{24,29},{1... | collective-permute-start | bytes 98312 | tf_op jit(solution)/shard_map/ppermute | solution.py:257
  9.9 7.1 %collective-permute-start.1 = (bf16[8,64,256]{2,1,0:T(8,128)(2,1)S(1)}, bf16[8,64,256]{2,1,0:T(8,128)(2,1)S(1)}, u32[]{:S(2)}, u32[]{:S(2)}) collective-permute-start(bf16[8,64,256]{2,1,0:T(8,128)(2,1)S(1)} %get-tuple-element.6.kept), channel_id=1, source_target_pairs={{1,5},{5,9},{9,13},{3,7},{7,11},{11,15},{17,21},{21,25},{25,29},{1... | collective-permute-start | bytes 786440 | tf_op jit(solution)/shard_map/ppermute | solution.py:257
  14.0 0.7 %copy-start.2 = (s32[16]{0:T(128)S(1)}, s32[16]{0:T(128)}, u32[]{:S(2)}) copy-start(s32[16]{0:T(128)} %param.6) | copy-start | bytes 196
  14.7 0.8 %collective-permute-start.3 = (bf16[2,64,128]{2,1,0:T(8,128)(2,1)S(1)}, bf16[2,64,128]{2,1,0:T(8,128)(2,1)S(1)}, u32[]{:S(2)}, u32[]{:S(2)}) collective-permute-start(bf16[2,64,128]{2,1,0:T(8,128)(2,1)S(1)} %pad_maximum_fusion), channel_id=1, source_target_pairs={{0,4},{4,8},{8,12},{2,6},{6,10},{10,14},{16,20},{20,24},{24,28},{1... | collective-permute-start | bytes 98312 | tf_op jit(solution)/shard_map/ppermute | solution.py:257
  15.5 1.6 %copy-start = (bf16[64,108]{1,0:T(8,128)(2,1)S(1)}, bf16[64,108]{1,0:T(8,128)(2,1)}, u32[]{:S(2)}) copy-start(bf16[64,108]{1,0:T(8,128)(2,1)} %guide.1) | copy-start | bytes 41476
  29.8 11.7 %collective-permute-start.6 = (f32[4,384]{1,0:T(4,128)S(1)}, f32[4,384]{1,0:T(4,128)S(1)}, u32[]{:S(2)}, u32[]{:S(2)}) collective-permute-start(f32[4,384]{1,0:T(4,128)S(1)} %get-tuple-element.18), channel_id=1, source_target_pairs={{0,5},{1,13},{4,0},{5,8},{8,1},{9,9},{12,4},{13,12},{2,7},{3,15},{... | collective-permute-start | bytes 18440 | tf_op jit(solution)/shard_map/ppermute | solution.py:257
  33.1 13.2 %collective-permute-start.9 = (f32[4,384]{1,0:T(4,128)S(1)}, f32[4,384]{1,0:T(4,128)S(1)}, u32[]{:S(2)}, u32[]{:S(2)}) collective-permute-start(f32[4,384]{1,0:T(4,128)S(1)} %get-tuple-element.15), channel_id=1, source_target_pairs={{0,0},{1,8},{4,1},{5,9},{8,4},{9,12},{12,5},{13,13},{2,2},{3,10},{... | collective-permute-start | bytes 18440 | tf_op jit(solution)/shard_map/ppermute | solution.py:257
  36.4 10.0 %collective-permute-start.8 = (f32[4,384]{1,0:T(4,128)S(1)}, f32[4,384]{1,0:T(4,128)S(1)}, u32[]{:S(2)}, u32[]{:S(2)}) collective-permute-start(f32[4,384]{1,0:T(4,128)S(1)} %get-tuple-element.16), channel_id=1, source_target_pairs={{0,1},{1,9},{4,4},{5,12},{8,5},{9,13},{12,0},{13,8},{2,3},{3,11},{... | collective-permute-start | bytes 18440 | tf_op jit(solution)/shard_map/ppermute | solution.py:257
  41.4 4.9 %collective-permute-start.7 = (f32[4,384]{1,0:T(4,128)S(1)}, f32[4,384]{1,0:T(4,128)S(1)}, u32[]{:S(2)}, u32[]{:S(2)}) collective-permute-start(f32[4,384]{1,0:T(4,128)S(1)} %get-tuple-element.17), channel_id=1, source_target_pairs={{0,4},{1,12},{4,5},{5,13},{8,0},{9,8},{12,1},{13,9},{2,6},{3,14},{... | collective-permute-start | bytes 18440 | tf_op jit(solution)/shard_map/ppermute | solution.py:257

commit v2 on v0

v2 whole, which is shorter than its diff:
```python
import math

import jax
import jax.numpy as jnp
from jax import lax
from jax.experimental import pallas as pl
from jax.experimental.pallas import tpu as pltpu
from jax.sharding import PartitionSpec as P

DISP = 192
DGROUP = 16
GROUPS = DISP // DGROUP
LAYERS = 3
SHARPNESS = 2.0
HALO = 32
LANES = 128
LINES = 8
CHANNELS = 64
BLOCK = 256
SPAN = BLOCK + HALO
PARTS = LANES // LINES
RUN = SPAN // PARTS
KEYS = 40
WIDE = BLOCK + LANES
SEC_ROWS = LINES * CHANNELS
PAYLOAD = SEC_ROWS + CHANNELS + 16
PACK = LANES // HALO
CUT = 16

BF = jnp.bfloat16
F32 = jnp.float32


def iota(shape, dim):
    return lax.broadcasted_iota(jnp.int32, shape, dim)


def dot_t(a, b):
    return lax.dot_general(a, b, (((1,), (1,)), ((), ())), preferred_element_type=F32)


def payload_kernel(own, other, valid, out):
    view = lax.axis_index("view")
    first_view = view == 0
    sec_mask = valid[1:2, :].astype(F32).astype(BF)
    lane = iota((CHANNELS, LANES), 1)
    tails = []
    for line in range(LINES):
        at = view * LINES + line
        mine, theirs = own[at], other[at]
        out[line * CHANNELS : (line + 1) * CHANNELS, :] = jnp.where(first_view, theirs, mine) * sec_mask
        tail = jnp.where(first_view, mine[:, BLOCK - LANES :], theirs[:, BLOCK - LANES :]).astype(F32)
        slot = line % PACK
        turn = (HALO * (slot + 1)) % LANES
        if turn:
            tail = pltpu.roll(tail, turn, 1)
        if slot:
            tail = jnp.where(lane >= HALO * slot, tail, tails[-1])
            tails[-1] = tail
        else:
            tails.append(tail)
    for i, tail in enumerate(tails):
        out[SEC_ROWS : SEC_ROWS + CHANNELS, i * LANES : (i + 1) * LANES] = tail.astype(BF)
    ref_mask = jnp.broadcast_to(valid[0:1, :].astype(F32), (16, BLOCK))
    out[SEC_ROWS + CHANNELS :, :] = ref_mask.astype(BF)


def payload(own, other, valid):
    return pl.pallas_call(
        payload_kernel,
        out_shape=jax.ShapeDtypeStruct((PAYLOAD, BLOCK), BF),
        in_specs=[pl.BlockSpec(memory_space=pltpu.VMEM)] * 3,
        out_specs=pl.BlockSpec(memory_space=pltpu.VMEM),
        compiler_params=pltpu.CompilerParams(vmem_limit_bytes=16 * 1024 * 1024),
    )(own, other, valid)


def main_kernel(
    offsets, own, other, mine, left, valid, guide, out,
    ref_rows, ref_cols, skew, cost_rows, gate_rows, vol, wts, vals, turned
):
    view = lax.axis_index("view")
    first_view = view == 0
    low = jnp.where(lax.axis_index("cols") == 0, HALO, 0)
    base = view * LINES

    for line in range(LINES):
        lo = line * CHANNELS
        ref_rows[lo : lo + CHANNELS, LANES:] = jnp.where(first_view, own[base + line], other[base + line])
        half = line // PACK
        packed = left[SEC_ROWS : SEC_ROWS + CHANNELS, half * LANES : (half + 1) * LANES].astype(F32)
        turn = (LANES - HALO) - HALO * (line % PACK)
        if turn:
            packed = pltpu.roll(packed, turn, 1)
        ref_rows[lo : lo + CHANNELS, :LANES] = packed.astype(BF)

    perm = jnp.where(iota((SPAN, WIDE), 1) == WIDE - 1 - iota((SPAN, WIDE), 0), 1.0, 0.0).astype(BF)
    mask_left = left[SEC_ROWS + CHANNELS : SEC_ROWS + CHANNELS + 1, BLOCK - LANES :].astype(F32)
    ref_mask = jnp.concatenate([mask_left, valid[0:1, :].astype(F32)], axis=1)
    ref_mask = jnp.broadcast_to(ref_mask * (1.0 / math.sqrt(CHANNELS)), (LANES, WIDE))
    mask_cols = dot_t(perm, ref_mask.astype(BF))

    keys = LAYERS * 3 * GROUPS
    row = iota((3 * KEYS, keys), 0)
    tap = jnp.where(row >= KEYS, 1, 0) + jnp.where(row >= 2 * KEYS, 1, 0)
    row = row - KEYS * tap
    layer = jnp.where(row >= GROUPS, 1, 0) + jnp.where(row >= 2 * GROUPS, 1, 0)
    key = 2 * GROUPS * layer + GROUPS * tap + row
    chosen = jnp.where((iota((3 * KEYS, keys), 1) == key) & (row < 3 * GROUPS), 1.0, 0.0).astype(BF)
    guide_t = dot_t(chosen, guide[...]).astype(BF)
    guide_t = jnp.concatenate([guide_t, guide_t], axis=1)

    flip = 2 * LANES - 1 - iota((DISP, 2 * LANES), 0)
    flip = jnp.where(iota((DISP, 2 * LANES), 1) == flip, 1.0, 0.0).astype(BF)

    ch_lane = iota((CHANNELS, LANES), 1)
    diagonal = iota((8, LANES), 1) - iota((8, LANES), 0)
    half_lane = iota((PARTS, LANES), 1) < CHANNELS
    span_lane = iota((SPAN, LANES), 1) < CHANNELS

    def shifted(line):
        off = offsets[base + line]
        lo = line * CHANNELS
        tiles = [
            src[lo : lo + CHANNELS, i * LANES : (i + 1) * LANES].astype(F32)
            for src in (left, mine)
            for i in range(2)
        ]
        tiles = [pltpu.roll(tile, off, 1) for tile in tiles]
        tiles = [jnp.where(ch_lane < off, tiles[max(i - 1, 0)], tiles[i]).astype(BF) for i in range(4)]
        return jnp.concatenate(tiles, axis=1)

    for quad in range(LINES // 4):
        ref_t = dot_t(perm, ref_rows[quad * 4 * CHANNELS : (quad + 1) * 4 * CHANNELS, :])
        for pair in range(2):
            cols = ref_t[:, pair * LANES : (pair + 1) * LANES]
            slot = quad * 2 + pair
            ref_cols[slot] = cols
            masked = cols * mask_cols
            rhs = jnp.concatenate([shifted(2 * slot), shifted(2 * slot + 1)], axis=0)
            for side in range(2):
                line = 2 * slot + side
                for t in range(RUN):
                    picked = ref_cols[slot, pl.ds(t, PARTS, stride=RUN), :]
                    picked = jnp.where(half_lane if side == 0 else ~half_lane, picked, 0.0)
                    at = t * LANES + line * PARTS
                    gate_rows[at : at + PARTS, :] = picked.astype(BF)
                lhs = jnp.where(span_lane if side == 0 else ~span_lane, masked, 0.0).astype(BF)
                for chunk in range(3):
                    rows = min(LANES, SPAN - chunk * LANES)
                    first = max(1 - chunk, 0)
                    last = 3 - chunk
                    products = jnp.dot(
                        lhs[chunk * LANES : chunk * LANES + rows],
                        rhs[:, first * LANES : (last + 1) * LANES],
                        preferred_element_type=F32,
                    )
                    for j in range(rows // 8):
                        tiles = [
                            pltpu.roll(
                                products[8 * j : 8 * j + 8, i * LANES : (i + 1) * LANES],
                                8 * j, 1, stride=1, stride_axis=0,
                            )
                            for i in range(last + 1 - first)
                        ]
                        if len(tiles) < 3:
                            tiles = [tiles[0]] + tiles
                        beyond = diagonal >= 8 * j
                        at = chunk * LANES + 8 * j
                        skew[line, 0, at : at + 8, :] = jnp.where(beyond, tiles[1], tiles[0])
                        skew[line, 1, at : at + 8, :] = jnp.where(beyond, tiles[2], tiles[1])
                for t in range(RUN):
                    at = t * LANES + line * PARTS
                    for v in range(2):
                        cost_rows[at : at + PARTS, v * LANES : (v + 1) * LANES] = skew[
                            line, v, pl.ds(t, PARTS, stride=RUN), :
                        ].astype(BF)

    place = iota((KEYS, LANES), 1)
    x_base = SPAN - 1 - RUN * (place & (PARTS - 1))
    row = iota((KEYS, LANES), 0)
    reach = jnp.where(row >= 2 * GROUPS, 9, jnp.where(row >= GROUPS, 3, 1))
    room_left = x_base - reach - low
    room_right = x_base + reach - SPAN

    for two in range(RUN // 2):
        at = 2 * two * LANES
        costs = dot_t(flip, cost_rows[at : at + 2 * LANES, :])
        logits = dot_t(guide_t, gate_rows[at : at + 2 * LANES, :])
        for i in range(2):
            t = 2 * two + i
            vol[t] = costs[:, i * LANES : (i + 1) * LANES]
            z = logits[:, i * LANES : (i + 1) * LANES]
            z = (0.55 + 0.45 * jnp.tanh(0.5 * z)).astype(BF).astype(F32)
            taps = [z[k * KEYS : (k + 1) * KEYS] for k in range(3)]
            scale = 1.0 / (taps[0] + taps[1] + taps[2])
            wts[t, 0:KEYS, :] = jnp.where(room_left >= t, taps[0] * scale, 0.0)
            wts[t, KEYS : 2 * KEYS, :] = taps[1] * scale
            wts[t, 2 * KEYS : 3 * KEYS, :] = jnp.where(room_right < t, taps[2] * scale, 0.0)

    def aggregate(group, carry):
        for half in range(2):
            at = pl.multiple_of(group * DGROUP + half * 8, 8)
            v = [vol[t, pl.ds(at, 8), :] for t in range(RUN)]
            for layer in range(LAYERS):
                s = 3**layer
                before = [v[t + s] if t + s < RUN else pltpu.roll(v[t + s - RUN], LANES - 1, 1) for t in range(RUN)]
                after = [v[t - s] if t >= s else pltpu.roll(v[t - s + RUN], 1, 1) for t in range(RUN)]
                fresh = []
                for t in range(RUN):
                    w = [wts[t, pl.ds(k * KEYS + layer * GROUPS + group, 1), :] for k in range(3)]
                    fresh.append(w[0] * before[t] + w[1] * v[t] + w[2] * after[t])
                v = fresh
            for t in range(RUN):
                vol[t, pl.ds(at, 8), :] = v[t]
        return carry

    lax.fori_loop(0, GROUPS, aggregate, 0)

    vals[...] = jnp.zeros((LANES, LANES), F32)
    sub = iota((8, LANES), 0).astype(F32)
    line_of = iota((1, LANES), 1) >> 4
    offs = jnp.zeros((1, LANES), F32)
    for line in range(LINES):
        offs = jnp.where(line_of == line, offsets[base + line].astype(F32), offs)

    def softmax(t, carry):
        v = [vol[t, 8 * i : 8 * i + 8, :] for i in range(DISP // 8)]
        top = v
        while len(top) > 1:
            top = [jnp.maximum(a, b) for a, b in zip(top[::2], top[1::2])] + top[len(top) & ~1 :]
        top = jnp.max(top[0], axis=0, keepdims=True)
        e = [jnp.exp(SHARPNESS * (a - top)) for a in v]
        total = e[0]
        moment = jnp.zeros((8, LANES), F32)
        for i in range(1, DISP // 8):
            total = total + e[i]
            moment = moment + float(8 * i) * e[i]
        moment = jnp.sum(moment + sub * total, axis=0, keepdims=True)
        total = jnp.sum(total, axis=0, keepdims=True)
        vals[pl.ds(RUN - 1 - t, 1), :] = (moment / total + offs) * (1.0 / DISP)
        return carry

    lax.fori_loop(0, RUN, softmax, 0)

    turned[...] = jnp.transpose(vals[...])
    lane = iota((8, LANES), 1)
    result = [jnp.zeros((8, LANES), F32) for _ in range(WIDE // LANES)]
    for part in range(PARTS):
        piece = turned[pl.ds(part, LINES, stride=PARTS), :]
        start = (RUN * (PARTS - 1 - part) - HALO) % WIDE
        tile, turn = divmod(start, LANES)
        if turn:
            piece = pltpu.roll(piece, turn, 1)
        if turn + RUN > LANES:
            after = (tile + 1) % len(result)
            result[after] = result[after] + jnp.where(lane < turn, piece, 0.0)
            piece = jnp.where(lane >= turn, piece, 0.0)
        result[tile] = result[tile] + piece
    for i in range(out.shape[0]):
        for tile, value in enumerate(result):
            out[i, :, tile * LANES : (tile + 1) * LANES] = value


def disparities(copies, offsets, *arrays):
    specs = [pl.BlockSpec(memory_space=pltpu.SMEM)] + [pl.BlockSpec(memory_space=pltpu.VMEM)] * 6
    return pl.pallas_call(
        main_kernel,
        out_shape=jax.ShapeDtypeStruct((copies, LINES, WIDE), F32),
        in_specs=specs,
        out_specs=pl.BlockSpec(memory_space=pltpu.VMEM),
        scratch_shapes=[
            pltpu.VMEM((SEC_ROWS, WIDE), BF),
            pltpu.VMEM((LINES // 2, SPAN, LANES), F32),
            pltpu.VMEM((LINES, 2, SPAN, LANES), F32),
            pltpu.VMEM((RUN * LANES, 2 * LANES), BF),
            pltpu.VMEM((RUN * LANES, LANES), BF),
            pltpu.VMEM((RUN, DISP, LANES), F32),
            pltpu.VMEM((RUN, 3 * KEYS, LANES), F32),
            pltpu.VMEM((LANES, LANES), F32),
            pltpu.VMEM((LANES, LANES), F32),
        ],
        compiler_params=pltpu.CompilerParams(vmem_limit_bytes=40 * 1024 * 1024),
    )(offsets, *arrays)


def join_kernel(pieces, out):
    n = out.shape[2] // BLOCK
    sub = out.shape[1]
    block = lax.axis_index("cols")
    view = block // (n // 2)
    at = (block % (n // 2)) * sub
    keep = iota((sub, LANES), 1) < LANES - CUT

    def rows(b, lo):
        whole = pieces[2 * b + view, :, lo : lo + LANES]
        picked = whole[:sub]
        for start in range(sub, LINES, sub):
            picked = jnp.where(at == start, whole[start : start + sub], picked)
        return picked

    for b in range(n):
        lo = b * BLOCK
        out[0, :, lo : lo + LANES] = rows(b, 0)
        second = rows(b, LANES)
        if b + 1 < n:
            second = jnp.where(keep, second, rows(b + 1, BLOCK))
        out[0, :, lo + LANES : lo + BLOCK] = second


def join(pieces, sub, n):
    return pl.pallas_call(
        join_kernel,
        out_shape=jax.ShapeDtypeStruct((1, sub, n * BLOCK), F32),
        in_specs=[pl.BlockSpec(memory_space=pltpu.VMEM)],
        out_specs=pl.BlockSpec(memory_space=pltpu.VMEM),
    )(pieces)


def on_device(features, valid_cols, offsets, guide_weight):
    own = features[0]
    n = lax.axis_size("cols")
    other = lax.ppermute(own, "view", [(0, 1), (1, 0)])
    mine = payload(own, other, valid_cols)
    left = lax.ppermute(mine, "cols", [(c, c + 1) for c in range(n - 1)])
    result = disparities(2 * n, offsets, own, other, mine, left, valid_cols, guide_weight)
    pieces = lax.all_to_all(result, ("cols", "view"), split_axis=0, concat_axis=0, tiled=True)
    return join(pieces, own.shape[0] // n, n)


def solution(mesh):
    return jax.shard_map(
        on_device,
        mesh=mesh,
        in_specs=(
            P("view", ("tiles", "lines"), None, "cols"),
            P(None, ("tiles", "cols")),
            P(("tiles", "lines")),
            P(),
        ),
        out_specs=P(("tiles", "lines"), "cols", None),
        check_vma=False,
    )
```

time: 79.6 us -> 36.6 us (0.46)
  local copies, waits for them, and re-layouts: 31.1 us -> 1.73 us
  other arithmetic: 9.92 us -> 0 us
  Pallas kernels: 0 us -> 8.64 us
  waiting for transfers between devices: 14.5 us -> 8.45 us
  blocking collectives: 14.5 us -> 12 us
  matrix products: 1.77 us -> 0 us
  starting transfers between devices: 6.52 us -> 5.45 us
    all_gather x4 -> x0, blocking collectives: 14.5 us -> none  [the longest x1 9.01 us: on_device(): lax.all_gather(valid_cols[0], 'cols', axis=0, tiled=True)]
    all_to_all x1 -> x0, waiting for transfers between devices: 14.5 us -> none  [on_device(): lax.all_to_all(own_view, 'cols', split_axis=0, concat_axis=2, tiled=True)]
    all_to_all x0 -> x1, blocking collectives: none -> 12 us  [on_device(): lax.all_to_all(result, ('cols', 'view'), split_axis=0, concat_axis=0, til...]
    gather x12 -> x0, local copies, waits for them, and re-layouts: 11.2 us -> none
    pallas_call x0 -> x3, Pallas kernels: none -> 8.64 us  [the longest x1 7.01 us: disparities(): pl.pallas_call(main_kernel, out_shape=jax.ShapeDtypeStruct((copies, LINES...]
    ppermute x1 -> x2, waiting for transfers between devices: 0.01 us -> 8.45 us  [the longest x1 6.71 us: on_device(): left = lax.ppermute(mine, 'cols', [(c, c + 1) for c in range(n - 1)])]
    all_to_all x1 -> x0, starting transfers between devices: 6.45 us -> none  [on_device(): lax.all_to_all(own_view, 'cols', split_axis=0, concat_axis=2, tiled=True)]
    reshape x11 -> x0, local copies, waits for them, and re-layouts: 5.54 us -> none  [the longest x4 2.63 us: correlate(): flattened.reshape(tile_count, tile_cols, tile_reach + 1)[:, :, :half_disp]]
  transfers between devices with their start and end apart: 2 -> 2, of which waited for: 1 -> 2; matrix products, arithmetic and copies ran while one was open for 1% -> 0% of each run, Pallas kernels for 0% -> 0%
where the time goes in v2:
time: 36.6 us; the launch traced here: 36.3 us
  blocking collectives  12 us (33%)
  Pallas kernels  8.64 us (24%)
  waiting for transfers between devices  8.45 us (23%)
  starting transfers between devices  5.45 us (15%)
  local copies, waits for them, and re-layouts  1.73 us (5%)
    all_to_all x1, blocking collectives, on_device(): lax.all_to_all(result, ('cols', 'view'), split_axis=0, concat_axis=0, til...  12 us
    pallas_call x1, Pallas kernels, disparities(): pl.pallas_call(main_kernel, out_shape=jax.ShapeDtypeStruct((copies, LINES...  7.01 us
    ppermute x1, waiting for transfers between devices, on_device(): left = lax.ppermute(mine, 'cols', [(c, c + 1) for c in range(n - 1)])  6.71 us
    ppermute x1, starting transfers between devices, on_device(): left = lax.ppermute(mine, 'cols', [(c, c + 1) for c in range(n - 1)])  5 us
    ppermute x1, waiting for transfers between devices, on_device(): other = lax.ppermute(own, 'view', [(0, 1), (1, 0)])  1.75 us
    unnamed x10, local copies, waits for them, and re-layouts  1.73 us
    pallas_call x1, Pallas kernels, join(): pl.pallas_call(join_kernel, out_shape=jax.ShapeDtypeStruct((1, sub, n * B...  1.51 us
  transfers between devices with their start and end apart: 2, of which 2 were waited for; matrix products, arithmetic and copies ran while one was open for 0% of the time, Pallas kernels for 0%

profile of v2, /device:TPU:0, one launch (start us, length us, event | category | flops | bytes accessed | tf_op | source)
XLA Modules:
  0.0 36.3 jit_solution(15594760333212870641)
XLA Ops:
  0.0 0.0 copy-start.4
  0.0 0.5 %collective-permute-start = (bf16[16,64,256]{2,1,0:T(8,128)(2,1)}, bf16[16,64,256]{2,1,0:T(8,128)(2,1)S(1)}, u32[]{:S(2)}, u32[]{:S(2)}) collective-permute-start(bf16[16,64,256]{2,1,0:T(8,128)(2,1)} %bitcast.1), channel_id=1, source_target_pairs={{0,1},{1,0},{2,3},{3,2},{4,5},{5,4},{6,7},{7,6},{8,9},{9,8},{10,11... | collective-permute-start | bytes 1572872 | tf_op jit(solution)/shard_map/ppermute | solution.py:323
  0.5 1.7 %collective-permute-done.other = bf16[16,64,256]{2,1,0:T(8,128)(2,1)S(1)} collective-permute-done((bf16[16,64,256]{2,1,0:T(8,128)(2,1)}, bf16[16,64,256]{2,1,0:T(8,128)(2,1)S(1)}, u32[]{:S(2)}, u32[]{:S(2)}) %collective-permute-start) | collective-permute-done | bytes 524320 | tf_op jit(solution)/shard_map/ppermute | solution.py:323
  2.2 0.0 copy-start
  2.2 1.0 %copy-done = bf16[1,16,64,256]{3,2,1,0:T(8,128)(2,1)S(1)} copy-done((bf16[1,16,64,256]{3,2,1,0:T(8,128)(2,1)S(1)}, bf16[1,16,64,256]{3,2,1,0:T(8,128)(2,1)}, u32[]{:S(2)}) %copy-start) | copy-done | bytes 524312
  3.2 0.0 copy-start.3
  3.2 0.7 %copy-done.3 = s32[2,256]{1,0:T(2,128)S(1)} copy-done((s32[2,256]{1,0:T(2,128)S(1)}, s32[2,256]{1,0:T(2,128)}, u32[]{:S(2)}) %copy-start.3) | copy-done | bytes 2072
  3.9 0.0 copy-start.1
  3.9 0.0 copy-start.2
  3.9 0.1 shard_map.46.mine
  4.1 5.0 %collective-permute-start.1 = (bf16[592,256]{1,0:T(8,128)(2,1)S(1)}, bf16[592,256]{1,0:T(8,128)(2,1)S(1)}, u32[]{:S(2)}, u32[]{:S(2)}) collective-permute-start(bf16[592,256]{1,0:T(8,128)(2,1)S(1)} %shard_map.46.mine), channel_id=1, source_target_pairs={{0,4},{4,8},{8,12},{1,5},{5,9},{9,13},{2,6},{6,10},{10,14},{3,7},{... | collective-permute-start | bytes 909320 | tf_op jit(solution)/shard_map/ppermute | solution.py:325
  9.1 6.7 %collective-permute-done.1.left = bf16[592,256]{1,0:T(8,128)(2,1)S(1)} collective-permute-done((bf16[592,256]{1,0:T(8,128)(2,1)S(1)}, bf16[592,256]{1,0:T(8,128)(2,1)S(1)}, u32[]{:S(2)}, u32[]{:S(2)}) %collective-permute-start.1) | collective-permute-done | bytes 303136 | tf_op jit(solution)/shard_map/ppermute | solution.py:325
  15.8 0.0 copy-done.4
  15.8 0.0 copy-done.1
  15.8 0.0 copy-done.2
  15.8 7.0 %shard_map.47 = f32[8,8,384]{2,1,0:T(8,128)S(1)} custom-call(s32[16]{0:T(128)S(1)} %copy-done.4, bf16[16,64,256]{2,1,0:T(8,128)(2,1)S(1)} %bitcast.3, bf16[16,64,256]{2,1,0:T(8,128)(2,1)S(1)} %collective-permute-done.other, bf16[592,256]{1,0:T(8,128)(2,1)S(1)} %shard_map.46.mine, bf16[592,256]{1,0:T(8,128)(2,1)S(1)} %collective-permute-done.1.left, ...), custom_call_target="tpu_custom_call" | custom-call | tf_op jit(solution)/shard_map/pallas_call | solution.py:267
  22.8 12.0 %all_to_all.5.pieces = f32[8,8,384]{2,1,0:T(8,128)} all-to-all(f32[8,8,384]{2,1,0:T(8,128)S(1)} %shard_map.47), channel_id=1, replica_groups=mesh['tiles'=2,'cols'=4,'lines'=2,'view'=2] {'cols','view'}, dimensions={0} | all-to-all | bytes 196608 | tf_op jit(solution)/shard_map/all_to_all | solution.py:327
  34.8 1.5 %shard_map.48 = f32[1,4,1024]{2,1,0:T(4,128)} custom-call(f32[8,8,384]{2,1,0:T(8,128)} %all_to_all.5.pieces), custom_call_target="tpu_custom_call" | custom-call | tf_op jit(solution)/shard_map/pallas_call | solution.py:312
Async XLA Ops:
  0.0 15.8 %copy-start.4 = (s32[16]{0:T(128)S(1)}, s32[16]{0:T(128)}, u32[]{:S(2)}) copy-start(s32[16]{0:T(128)} %offsets.1) | copy-start | bytes 196
  0.0 2.2 %collective-permute-start = (bf16[16,64,256]{2,1,0:T(8,128)(2,1)}, bf16[16,64,256]{2,1,0:T(8,128)(2,1)S(1)}, u32[]{:S(2)}, u32[]{:S(2)}) collective-permute-start(bf16[16,64,256]{2,1,0:T(8,128)(2,1)} %bitcast.1), channel_id=1, source_target_pairs={{0,1},{1,0},{2,3},{3,2},{4,5},{5,4},{6,7},{7,6},{8,9},{9,8},{10,11... | collective-permute-start | bytes 1572872 | tf_op jit(solution)/shard_map/ppermute | solution.py:323
  2.2 1.0 %copy-start = (bf16[1,16,64,256]{3,2,1,0:T(8,128)(2,1)S(1)}, bf16[1,16,64,256]{3,2,1,0:T(8,128)(2,1)}, u32[]{:S(2)}) copy-start(bf16[1,16,64,256]{3,2,1,0:T(8,128)(2,1)} %param.4) | copy-start | bytes 1572868
  3.2 0.7 %copy-start.3 = (s32[2,256]{1,0:T(2,128)S(1)}, s32[2,256]{1,0:T(2,128)}, u32[]{:S(2)}) copy-start(s32[2,256]{1,0:T(2,128)} %valid.3) | copy-start | bytes 6148
  3.9 11.9 %copy-start.1 = (bf16[1,16,64,256]{3,2,1,0:T(8,128)(2,1)S(1)}, bf16[1,16,64,256]{3,2,1,0:T(8,128)(2,1)}, u32[]{:S(2)}) copy-start(bf16[1,16,64,256]{3,2,1,0:T(8,128)(2,1)} %param.4) | copy-start | bytes 1572868
  3.9 11.9 %copy-start.2 = (bf16[64,108]{1,0:T(8,128)(2,1)S(1)}, bf16[64,108]{1,0:T(8,128)(2,1)}, u32[]{:S(2)}) copy-start(bf16[64,108]{1,0:T(8,128)(2,1)} %guide.1) | copy-start | bytes 41476
  4.1 11.7 %collective-permute-start.1 = (bf16[592,256]{1,0:T(8,128)(2,1)S(1)}, bf16[592,256]{1,0:T(8,128)(2,1)S(1)}, u32[]{:S(2)}, u32[]{:S(2)}) collective-permute-start(bf16[592,256]{1,0:T(8,128)(2,1)S(1)} %shard_map.46.mine), channel_id=1, source_target_pairs={{0,4},{4,8},{8,12},{1,5},{5,9},{9,13},{2,6},{6,10},{10,14},{3,7},{... | collective-permute-start | bytes 909320 | tf_op jit(solution)/shard_map/ppermute | solution.py:325

commit v3 on v2

v3 whole, which is shorter than its diff:
```python
import math

import jax
import jax.numpy as jnp
from jax import lax
from jax.experimental import pallas as pl
from jax.experimental.pallas import tpu as pltpu
from jax.sharding import PartitionSpec as P

DISP = 192
DGROUP = 16
GROUPS = DISP // DGROUP
LAYERS = 3
SHARPNESS = 2.0
HALO = 32
LANES = 128
LINES = 8
CHANNELS = 64
BLOCK = 256
SPAN = BLOCK + HALO
PARTS = LANES // LINES
RUN = SPAN // PARTS
KEYS = 40
WIDE = BLOCK + LANES
SEC_ROWS = LINES * CHANNELS
QUAD_ROWS = SEC_ROWS // 2
MASK_AT = QUAD_ROWS + CHANNELS
PAYLOAD = MASK_AT + 16
QUAD = LINES // 2
QUAD_LANES = LANES // 2
PACK = LANES // HALO
CUT = 16

BF = jnp.bfloat16
F32 = jnp.float32


def iota(shape, dim):
    return lax.broadcasted_iota(jnp.int32, shape, dim)


def dot_t(a, b):
    return lax.dot_general(a, b, (((1,), (1,)), ((), ())), preferred_element_type=F32)


def call(kernel, outs, scratch, smem, args, flops=0, space=pltpu.VMEM):
    specs = [pl.BlockSpec(memory_space=pltpu.SMEM)] * smem
    specs += [pl.BlockSpec(memory_space=space)] * (len(args) - smem)
    return pl.pallas_call(
        kernel,
        out_shape=[jax.ShapeDtypeStruct(shape, dtype) for shape, dtype in outs],
        in_specs=specs,
        out_specs=[pl.BlockSpec(memory_space=pltpu.VMEM)] * len(outs),
        scratch_shapes=scratch,
        compiler_params=pltpu.CompilerParams(vmem_limit_bytes=24 * 1024 * 1024),
        cost_estimate=pl.CostEstimate(flops=flops, bytes_accessed=1_000_000, transcendentals=0),
    )(*args)


def prefetch_kernel(own, valid, guide, own_out, masks, perm, flip, guide_out, valid_in, guide_in, sems):
    copies = [
        pltpu.make_async_copy(src, dst, sems.at[i])
        for i, (src, dst) in enumerate([(own, own_out), (guide, guide_in), (valid, valid_in)])
    ]
    for copy in copies:
        copy.start()
    perm[...] = jnp.where(
        iota((SPAN, WIDE), 1) == WIDE - 1 - iota((SPAN, WIDE), 0), 1.0, 0.0
    ).astype(BF)
    back = 2 * LANES - 1 - iota((DISP, 2 * LANES), 0)
    flip[...] = jnp.where(iota((DISP, 2 * LANES), 1) == back, 1.0, 0.0).astype(BF)

    keys = LAYERS * 3 * GROUPS
    row = iota((3 * KEYS, keys), 0)
    tap = jnp.where(row >= KEYS, 1, 0) + jnp.where(row >= 2 * KEYS, 1, 0)
    row = row - KEYS * tap
    layer = jnp.where(row >= GROUPS, 1, 0) + jnp.where(row >= 2 * GROUPS, 1, 0)
    key = 2 * GROUPS * layer + GROUPS * tap + row
    chosen = jnp.where((iota((3 * KEYS, keys), 1) == key) & (row < 3 * GROUPS), 1.0, 0.0).astype(BF)
    copies[1].wait()
    guide_t = dot_t(chosen, guide_in[...]).astype(BF)
    guide_out[...] = jnp.concatenate([guide_t, guide_t], axis=1)
    copies[2].wait()
    masks[...] = valid_in[...].astype(F32)
    copies[0].wait()


def payload_kernel(own, other, masks, first, second, ref_own):
    view = lax.axis_index("view")
    first_view = view == 0
    sec_mask = masks[1:2, :].astype(BF)
    lane = iota((CHANNELS, LANES), 1)
    tails = []
    for line in range(LINES):
        at = view * LINES + line
        mine, theirs = own[at], other[at]
        lo = line * CHANNELS
        dest, start = (first, lo) if line < QUAD else (second, lo - QUAD_ROWS)
        dest[start : start + CHANNELS, :] = jnp.where(first_view, theirs, mine) * sec_mask
        ref = jnp.where(first_view, mine, theirs)
        ref_own[lo : lo + CHANNELS, :] = ref
        tail = ref[:, BLOCK - LANES :].astype(F32)
        slot = line % PACK
        turn = (HALO * (slot + 1)) % LANES
        if turn:
            tail = pltpu.roll(tail, turn, 1)
        if slot:
            tails[-1] = jnp.where(lane >= HALO * slot, tail, tails[-1])
        else:
            tails.append(tail)
    for i, tail in enumerate(tails):
        first[QUAD_ROWS:MASK_AT, i * LANES : (i + 1) * LANES] = tail.astype(BF)
    first[MASK_AT:, :] = jnp.broadcast_to(masks[0:1, :], (16, BLOCK)).astype(BF)


def shifted(left, mine, lo, off):
    ch_lane = iota((CHANNELS, LANES), 1)
    tiles = [
        src[lo : lo + CHANNELS, i * LANES : (i + 1) * LANES].astype(F32)
        for src in (left, mine)
        for i in range(2)
    ]
    tiles = [pltpu.roll(tile, off, 1) for tile in tiles]
    tiles = [jnp.where(ch_lane < off, tiles[max(i - 1, 0)], tiles[i]).astype(BF) for i in range(4)]
    return jnp.concatenate(tiles, axis=1)


def line_costs(lhs, rhs, slot, skew, cost_rows):
    diagonal = iota((8, LANES), 1) - iota((8, LANES), 0)
    for chunk in range(3):
        rows = min(LANES, SPAN - chunk * LANES)
        first = max(1 - chunk, 0)
        last = 3 - chunk
        products = jnp.dot(
            lhs[chunk * LANES : chunk * LANES + rows],
            rhs[:, first * LANES : (last + 1) * LANES],
            preferred_element_type=F32,
        )
        for j in range(rows // 8):
            tiles = [
                pltpu.roll(
                    products[8 * j : 8 * j + 8, i * LANES : (i + 1) * LANES],
                    8 * j, 1, stride=1, stride_axis=0,
                )
                for i in range(last + 1 - first)
            ]
            if len(tiles) < 3:
                tiles = [tiles[0]] + tiles
            beyond = diagonal >= 8 * j
            at = chunk * LANES + 8 * j
            skew[slot, 0, at : at + 8, :] = jnp.where(beyond, tiles[1], tiles[0])
            skew[slot, 1, at : at + 8, :] = jnp.where(beyond, tiles[2], tiles[1])
    for t in range(RUN):
        at = t * QUAD_LANES + slot * PARTS
        for v in range(2):
            cost_rows[at : at + PARTS, v * LANES : (v + 1) * LANES] = skew[
                slot, v, pl.ds(t, PARTS, stride=RUN), :
            ].astype(BF)


def early_kernel(
    offsets, ref_own, mine, left, masks, perm, guide, wts, cost_rows, lhs_out,
    ref_rows, ref_cols, gate_rows, skew
):
    base = lax.axis_index("view") * LINES
    low = jnp.where(lax.axis_index("cols") == 0, HALO, 0)
    for line in range(LINES):
        lo = line * CHANNELS
        ref_rows[lo : lo + CHANNELS, LANES:] = ref_own[lo : lo + CHANNELS, :]
        half = line // PACK
        packed = left[QUAD_ROWS:MASK_AT, half * LANES : (half + 1) * LANES].astype(F32)
        turn = (LANES - HALO) - HALO * (line % PACK)
        if turn:
            packed = pltpu.roll(packed, turn, 1)
        ref_rows[lo : lo + CHANNELS, :LANES] = packed.astype(BF)

    mask_left = left[MASK_AT : MASK_AT + 1, BLOCK - LANES :].astype(F32)
    ref_mask = jnp.concatenate([mask_left, masks[0:1, :]], axis=1)
    ref_mask = jnp.broadcast_to(ref_mask * (1.0 / math.sqrt(CHANNELS)), (LANES, WIDE))
    mask_cols = dot_t(perm[...], ref_mask.astype(BF))
    half_lane = iota((PARTS, LANES), 1) < CHANNELS
    span_lane = iota((SPAN, LANES), 1) < CHANNELS

    for quad in range(LINES // QUAD):
        ref_t = dot_t(perm[...], ref_rows[quad * QUAD_ROWS : (quad + 1) * QUAD_ROWS, :])
        for pair in range(QUAD // 2):
            cols = ref_t[:, pair * LANES : (pair + 1) * LANES]
            slot = quad * 2 + pair
            ref_cols[slot] = cols
            masked = cols * mask_cols
            if quad == 0:
                rhs = jnp.concatenate(
                    [
                        shifted(left, mine, line * CHANNELS, offsets[base + line])
                        for line in (2 * slot, 2 * slot + 1)
                    ],
                    axis=0,
                )
            for side in range(2):
                line = 2 * slot + side
                for t in range(RUN):
                    picked = ref_cols[slot, pl.ds(t, PARTS, stride=RUN), :]
                    picked = jnp.where(half_lane if side == 0 else ~half_lane, picked, 0.0)
                    at = t * LANES + line * PARTS
                    gate_rows[at : at + PARTS, :] = picked.astype(BF)
                lhs = jnp.where(span_lane if side == 0 else ~span_lane, masked, 0.0).astype(BF)
                if quad == 0:
                    line_costs(lhs, rhs, line, skew, cost_rows)
                else:
                    lhs_out[line - QUAD] = lhs

    place = iota((KEYS, LANES), 1)
    x_base = SPAN - 1 - RUN * (place & (PARTS - 1))
    row = iota((KEYS, LANES), 0)
    reach = jnp.where(row >= 2 * GROUPS, 9, jnp.where(row >= GROUPS, 3, 1))
    room_left = x_base - reach - low
    room_right = x_base + reach - SPAN
    for two in range(RUN // 2):
        at = 2 * two * LANES
        logits = dot_t(guide[...], gate_rows[at : at + 2 * LANES, :])
        for i in range(2):
            t = 2 * two + i
            z = logits[:, i * LANES : (i + 1) * LANES]
            z = (0.55 + 0.45 * jnp.tanh(0.5 * z)).astype(BF).astype(F32)
            taps = [z[k * KEYS : (k + 1) * KEYS] for k in range(3)]
            scale = 1.0 / (taps[0] + taps[1] + taps[2])
            wts[t, 0:KEYS, :] = jnp.where(room_left >= t, taps[0] * scale, 0.0)
            wts[t, KEYS : 2 * KEYS, :] = taps[1] * scale
            wts[t, 2 * KEYS : 3 * KEYS, :] = jnp.where(room_right < t, taps[2] * scale, 0.0)


def late_kernel(
    offsets, mine, left, lhs, early_rows, wts, flip, out, skew, cost_rows, vol, vals, turned
):
    base = lax.axis_index("view") * LINES
    for pair in range(QUAD // 2):
        rhs = jnp.concatenate(
            [
                shifted(left, mine, line * CHANNELS, offsets[base + QUAD + line])
                for line in (2 * pair, 2 * pair + 1)
            ],
            axis=0,
        )
        for line in (2 * pair, 2 * pair + 1):
            line_costs(lhs[line], rhs, line, skew, cost_rows)

    for two in range(RUN // 2):
        rows = []
        for t in (2 * two, 2 * two + 1):
            for part in (early_rows, cost_rows):
                rows.append(part[t * QUAD_LANES : (t + 1) * QUAD_LANES, :])
        costs = dot_t(flip[...], jnp.concatenate(rows, axis=0))
        vol[2 * two] = costs[:, :LANES]
        vol[2 * two + 1] = costs[:, LANES:]

    def aggregate(group, carry):
        for half in range(2):
            at = pl.multiple_of(group * DGROUP + half * 8, 8)
            v = [vol[t, pl.ds(at, 8), :] for t in range(RUN)]
            for layer in range(LAYERS):
                s = 3**layer
                before = [v[t + s] if t + s < RUN else pltpu.roll(v[t + s - RUN], LANES - 1, 1) for t in range(RUN)]
                after = [v[t - s] if t >= s else pltpu.roll(v[t - s + RUN], 1, 1) for t in range(RUN)]
                fresh = []
                for t in range(RUN):
                    w = [wts[t, pl.ds(k * KEYS + layer * GROUPS + group, 1), :] for k in range(3)]
                    fresh.append(w[0] * before[t] + w[1] * v[t] + w[2] * after[t])
                v = fresh
            for t in range(RUN):
                vol[t, pl.ds(at, 8), :] = v[t]
        return carry

    lax.fori_loop(0, GROUPS, aggregate, 0)

    vals[...] = jnp.zeros((LANES, LANES), F32)
    sub = iota((8, LANES), 0).astype(F32)
    line_of = iota((1, LANES), 1) >> 4
    offs = jnp.zeros((1, LANES), F32)
    for line in range(LINES):
        offs = jnp.where(line_of == line, offsets[base + line].astype(F32), offs)

    def softmax(t, carry):
        v = [vol[t, 8 * i : 8 * i + 8, :] for i in range(DISP // 8)]
        top = v
        while len(top) > 1:
            top = [jnp.maximum(a, b) for a, b in zip(top[::2], top[1::2])] + top[len(top) & ~1 :]
        top = jnp.max(top[0], axis=0, keepdims=True)
        e = [jnp.exp(SHARPNESS * (a - top)) for a in v]
        total = e[0]
        moment = jnp.zeros((8, LANES), F32)
        for i in range(1, DISP // 8):
            total = total + e[i]
            moment = moment + float(8 * i) * e[i]
        moment = jnp.sum(moment + sub * total, axis=0, keepdims=True)
        total = jnp.sum(total, axis=0, keepdims=True)
        vals[pl.ds(RUN - 1 - t, 1), :] = (moment / total + offs) * (1.0 / DISP)
        return carry

    lax.fori_loop(0, RUN, softmax, 0)

    turned[...] = jnp.transpose(vals[...])
    lane = iota((8, LANES), 1)
    result = [jnp.zeros((8, LANES), F32) for _ in range(WIDE // LANES)]
    for part in range(PARTS):
        piece = turned[pl.ds(part, LINES, stride=PARTS), :]
        start = (RUN * (PARTS - 1 - part) - HALO) % WIDE
        tile, turn = divmod(start, LANES)
        if turn:
            piece = pltpu.roll(piece, turn, 1)
        if turn + RUN > LANES:
            after = (tile + 1) % len(result)
            result[after] = result[after] + jnp.where(lane < turn, piece, 0.0)
            piece = jnp.where(lane >= turn, piece, 0.0)
        result[tile] = result[tile] + piece
    for tile, value in enumerate(result):
        out[:, tile * LANES : (tile + 1) * LANES] = value


def join(pieces, sub, n):
    block = lax.axis_index("cols")
    pieces = pieces.reshape(n, 2, LINES, WIDE)
    start = (0, block // (n // 2), (block % (n // 2)) * sub, 0)
    pieces = lax.dynamic_slice(pieces, start, (n, 1, sub, WIDE))[:, 0]
    main = pieces[:, :, :BLOCK]
    tail = jnp.pad(pieces[1:, :, BLOCK:], ((0, 1), (0, 0), (LANES, 0)))
    place = (n, sub, BLOCK)
    keep = (iota(place, 2) < BLOCK - CUT) | (iota(place, 0) == n - 1)
    joined = jnp.where(keep, main, tail)
    return jnp.transpose(joined, (1, 0, 2)).reshape(1, sub, n * BLOCK)


def on_device(features, valid_cols, offsets, guide_weight):
    own = features[0]
    n = lax.axis_size("cols")
    right = [(c, c + 1) for c in range(n - 1)]
    other = lax.ppermute(own, "view", [(0, 1), (1, 0)])
    near, masks, perm, flip, guide = call(
        prefetch_kernel,
        [(own.shape, BF), (valid_cols.shape, F32), ((SPAN, WIDE), BF), ((DISP, 2 * LANES), BF), ((3 * KEYS, LANES), BF)],
        [pltpu.VMEM(valid_cols.shape, jnp.int32), pltpu.VMEM(guide_weight.shape, BF), pltpu.SemaphoreType.DMA((3,))],
        0, (own, valid_cols, guide_weight), 100_000_000, pl.ANY,
    )
    first, second, ref_own = call(
        payload_kernel,
        [((PAYLOAD, BLOCK), BF), ((QUAD_ROWS, BLOCK), BF), ((SEC_ROWS, BLOCK), BF)],
        [], 0, (near, other, masks),
    )
    left_first = lax.ppermute(first, "cols", right)
    left_second = lax.ppermute(second, "cols", right)
    quad_rows = (RUN * QUAD_LANES, 2 * LANES)
    skew = pltpu.VMEM((QUAD, 2, SPAN, LANES), F32)
    square = pltpu.VMEM((LANES, LANES), F32)
    wts, early_rows, lhs = call(
        early_kernel,
        [((RUN, 3 * KEYS, LANES), F32), (quad_rows, BF), ((QUAD, SPAN, LANES), BF)],
        [pltpu.VMEM((SEC_ROWS, WIDE), BF), pltpu.VMEM((QUAD, SPAN, LANES), F32), pltpu.VMEM((RUN * LANES, LANES), BF), skew],
        1, (offsets, ref_own, first, left_first, masks, perm, guide), 1_000_000_000,
    )
    (result,) = call(
        late_kernel,
        [((LINES, WIDE), F32)],
        [skew, pltpu.VMEM(quad_rows, BF), pltpu.VMEM((RUN, DISP, LANES), F32), square, square],
        1, (offsets, second, left_second, lhs, early_rows, wts, flip), 1_000_000_000,
    )
    pieces = lax.all_gather(result, ("cols", "view"), axis=0)
    return join(pieces, own.shape[0] // n, n)


def solution(mesh):
    return jax.shard_map(
        on_device,
        mesh=mesh,
        in_specs=(
            P("view", ("tiles", "lines"), None, "cols"),
            P(None, ("tiles", "cols")),
            P(("tiles", "lines")),
            P(),
        ),
        out_specs=P(("tiles", "lines"), "cols", None),
        check_vma=False,
    )
```

time: 36.6 us -> 36.8 us (level)
  waiting for transfers between devices: 8.45 us -> 1.32 us
  blocking collectives: 12 us -> 15.1 us
  starting transfers between devices: 5.45 us -> 8.43 us
  local copies, waits for them, and re-layouts: 1.73 us -> 2.46 us
  other arithmetic: 0 us -> 0.69 us
    all_gather x0 -> x1, blocking collectives: none -> 15.1 us  [on_device(): pieces = lax.all_gather(result, ('cols', 'view'), axis=0)]
    all_to_all x1 -> x0, blocking collectives: 12 us -> none  [on_device(): lax.all_to_all(result, ('cols', 'view'), split_axis=0, concat_axis=0, til...]
    ppermute x1 -> x2, waiting for transfers between devices: 6.71 us -> 1.32 us  [the longest x1 1.12 us: on_device(): left_first = lax.ppermute(first, 'cols', right)]
    ppermute x1 -> x2, starting transfers between devices: 5 us -> 7.98 us  [the longest x1 4.5 us: on_device(): left_first = lax.ppermute(first, 'cols', right)]
    ppermute x1, waiting for transfers between devices: 1.75 us -> 0.01 us  [on_device(): other = lax.ppermute(own, 'view', [(0, 1), (1, 0)])]
    unnamed x10 -> x8, local copies, waits for them, and re-layouts: 1.73 us -> 2.44 us
    select_n x0 -> x1, other arithmetic: none -> 0.68 us  [join(): joined = jnp.where(keep, main, tail)]
    pallas_call x3 -> x4, Pallas kernels: 8.64 us -> 8.46 us  [call(): pl.pallas_call(kernel, out_shape=[jax.ShapeDtypeStruct(shape, dtype) for...]
  transfers between devices with their start and end apart: 2 -> 3, of which waited for: 2 -> 2; matrix products, arithmetic and copies ran while one was open for 0% -> 0% of each run, Pallas kernels for 0% -> 7%
where the time goes in v3:
time: 36.8 us; the launch traced here: 36.5 us
  blocking collectives  15.1 us (41%)
  Pallas kernels  8.46 us (23%)
  starting transfers between devices  8.43 us (23%)
  local copies, waits for them, and re-layouts  2.46 us (7%)
  waiting for transfers between devices  1.32 us (4%)
  other arithmetic  0.69 us (2%)
    all_gather x1, blocking collectives, on_device(): pieces = lax.all_gather(result, ('cols', 'view'), axis=0)  15.1 us
    pallas_call x4, Pallas kernels, call(): pl.pallas_call(kernel, out_shape=[jax.ShapeDtypeStruct(shape, dtype) for...  8.46 us
    ppermute x1, starting transfers between devices, on_device(): left_first = lax.ppermute(first, 'cols', right)  4.5 us
    ppermute x1, starting transfers between devices, on_device(): left_second = lax.ppermute(second, 'cols', right)  3.48 us
    unnamed x8, local copies, waits for them, and re-layouts  2.44 us
    ppermute x1, waiting for transfers between devices, on_device(): left_first = lax.ppermute(first, 'cols', right)  1.12 us
  transfers between devices with their start and end apart: 3, of which 2 were waited for; matrix products, arithmetic and copies ran while one was open for 0% of the time, Pallas kernels for 7%

profile of v3, /device:TPU:0, one launch (start us, length us, event | category | flops | bytes accessed | tf_op | source)
XLA Modules:
  0.0 36.5 jit_solution(4557250884883994394)
XLA Ops:
  0.0 0.0 copy-start.3
  0.0 0.5 %collective-permute-start = (bf16[16,64,256]{2,1,0:T(8,128)(2,1)}, bf16[16,64,256]{2,1,0:T(8,128)(2,1)S(1)}, u32[]{:S(2)}, u32[]{:S(2)}) collective-permute-start(bf16[16,64,256]{2,1,0:T(8,128)(2,1)} %bitcast.9), channel_id=1, source_target_pairs={{0,1},{1,0},{2,3},{3,2},{4,5},{5,4},{6,7},{7,6},{8,9},{9,8},{10,11... | collective-permute-start | bytes 1572872 | tf_op jit(solution)/shard_map/ppermute | solution.py:336
  0.5 0.0 copy-start
  0.5 1.0 %copy-done = bf16[1,16,64,256]{3,2,1,0:T(8,128)(2,1)S(1)} copy-done((bf16[1,16,64,256]{3,2,1,0:T(8,128)(2,1)S(1)}, bf16[1,16,64,256]{3,2,1,0:T(8,128)(2,1)}, u32[]{:S(2)}) %copy-start) | copy-done | bytes 524312
  1.5 0.0 copy-start.1
  1.5 0.7 %copy-done.1 = bf16[64,108]{1,0:T(8,128)(2,1)S(1)} copy-done((bf16[64,108]{1,0:T(8,128)(2,1)S(1)}, bf16[64,108]{1,0:T(8,128)(2,1)}, u32[]{:S(2)}) %copy-start.1) | copy-done | bytes 13848
  2.2 0.0 copy-start.2
  2.2 0.7 %copy-done.2 = s32[2,256]{1,0:T(2,128)S(1)} copy-done((s32[2,256]{1,0:T(2,128)S(1)}, s32[2,256]{1,0:T(2,128)}, u32[]{:S(2)}) %copy-start.2) | copy-done | bytes 2072
  2.9 0.4 shard_map.46
  3.3 0.0 collective-permute-done.other
  3.3 0.1 shard_map.47
  3.4 4.5 %collective-permute-start.2 = (bf16[336,256]{1,0:T(8,128)(2,1)S(1)}, bf16[336,256]{1,0:T(8,128)(2,1)S(1)}, u32[]{:S(2)}, u32[]{:S(2)}) collective-permute-start(bf16[336,256]{1,0:T(8,128)(2,1)S(1)} %get-tuple-element.20.mine), channel_id=1, source_target_pairs={{0,4},{4,8},{8,12},{1,5},{5,9},{9,13},{2,6},{6,10},{10,14},{3,7},{... | collective-permute-start | bytes 516104 | tf_op jit(solution)/shard_map/ppermute | solution.py:348
  7.9 3.5 %collective-permute-start.1 = (bf16[256,256]{1,0:T(8,128)(2,1)S(1)}, bf16[256,256]{1,0:T(8,128)(2,1)S(1)}, u32[]{:S(2)}, u32[]{:S(2)}) collective-permute-start(bf16[256,256]{1,0:T(8,128)(2,1)S(1)} %get-tuple-element.18.mine), channel_id=1, source_target_pairs={{0,4},{4,8},{8,12},{1,5},{5,9},{9,13},{2,6},{6,10},{10,14},{3,7},{... | collective-permute-start | bytes 393224 | tf_op jit(solution)/shard_map/ppermute | solution.py:349
  11.4 1.1 %collective-permute-done.2.left = bf16[336,256]{1,0:T(8,128)(2,1)S(1)} collective-permute-done((bf16[336,256]{1,0:T(8,128)(2,1)S(1)}, bf16[336,256]{1,0:T(8,128)(2,1)S(1)}, u32[]{:S(2)}, u32[]{:S(2)}) %collective-permute-start.2) | collective-permute-done | bytes 172064 | tf_op jit(solution)/shard_map/ppermute | solution.py:348
  12.6 0.0 copy-done.3
  12.6 2.2 %shard_map.48 = (f32[18,120,128]{2,1,0:T(8,128)S(1)}, bf16[1152,256]{1,0:T(8,128)(2,1)S(1)}, bf16[4,288,128]{2,1,0:T(8,128)(2,1)S(1)}) custom-call(s32[16]{0:T(128)S(1)} %copy-done.3, bf16[512,256]{1,0:T(8,128)(2,1)S(1)} %get-tuple-element.19.ref_own, bf16[336,256]{1,0:T(8,128)(2,1)S(1)} %get-tuple-element.20.mine, ...), custom_call_target="tpu_custom_call" | custom-call | flops 1000000000 | bytes 1000000 | tf_op jit(solution)/shard_map/pallas_call | solution.py:49
  14.8 0.2 collective-permute-done.1.left
  15.0 5.8 %shard_map.49 = f32[8,384]{1,0:T(8,128)S(1)} custom-call(s32[16]{0:T(128)S(1)} %copy-done.3, bf16[256,256]{1,0:T(8,128)(2,1)S(1)} %get-tuple-element.18.mine, bf16[256,256]{1,0:T(8,128)(2,1)S(1)} %collective-permute-done.1.left, bf16[4,288,128]{2,1,0:T(8,128)(2,1)S(1)} %get-tuple-element.23.lhs, bf16[1152,256]{1,0:T(8,128)(2,1)S(1)} %get-tuple-element.24.early_rows, ...), custom_call_target="tpu_custom_call" | custom-call | flops 1000000000 | bytes 1000000 | tf_op jit(solution)/shard_map/pallas_call | solution.py:49
  20.8 15.1 %all-gather = f32[64,384]{1,0:T(8,128)S(1)} all-gather(f32[8,384]{1,0:T(8,128)S(1)} %shard_map.49), channel_id=2, replica_groups=mesh['tiles'=2,'cols'=4,'lines'=2,'view'=2] {'cols','view'}, dimensions={0}, use_global_device_ids=true | all-gather | bytes 110592 | tf_op jit(solution)/shard_map/all_gather | solution.py:365
  35.8 0.7 %slice_select_fusion = f32[4,4,256]{2,1,0:T(4,128)} fusion(f32[4,4,384]{2,1,0:T(4,128)S(1)} %dynamic-slice_bitcast_fusion, f32[3,4,128]{2,1,0:T(4,128)S(1)} %slice.9, pred[256]{0:T(512)(128)(4,1)S(1)} %iota_compare_fusion, pred[4]{0:T(512)(128)(4,1)S(1)} %iota_compare_fusion.1), kind=kLoop, calls=%fused_computation.1 | loop fusion | flops 8192 | bytes 39172 | tf_op jit(solution)/shard_map/jit(_where)/select_n | solution.py:328
  (4 shorter events, 0.0 us)
Async XLA Ops:
  0.0 12.6 %copy-start.3 = (s32[16]{0:T(128)S(1)}, s32[16]{0:T(128)}, u32[]{:S(2)}) copy-start(s32[16]{0:T(128)} %offsets.3) | copy-start | bytes 196
  0.0 3.3 %collective-permute-start = (bf16[16,64,256]{2,1,0:T(8,128)(2,1)}, bf16[16,64,256]{2,1,0:T(8,128)(2,1)S(1)}, u32[]{:S(2)}, u32[]{:S(2)}) collective-permute-start(bf16[16,64,256]{2,1,0:T(8,128)(2,1)} %bitcast.9), channel_id=1, source_target_pairs={{0,1},{1,0},{2,3},{3,2},{4,5},{5,4},{6,7},{7,6},{8,9},{9,8},{10,11... | collective-permute-start | bytes 1572872 | tf_op jit(solution)/shard_map/ppermute | solution.py:336
  0.5 1.0 %copy-start = (bf16[1,16,64,256]{3,2,1,0:T(8,128)(2,1)S(1)}, bf16[1,16,64,256]{3,2,1,0:T(8,128)(2,1)}, u32[]{:S(2)}) copy-start(bf16[1,16,64,256]{3,2,1,0:T(8,128)(2,1)} %param.4) | copy-start | bytes 1572868
  1.5 0.7 %copy-start.1 = (bf16[64,108]{1,0:T(8,128)(2,1)S(1)}, bf16[64,108]{1,0:T(8,128)(2,1)}, u32[]{:S(2)}) copy-start(bf16[64,108]{1,0:T(8,128)(2,1)} %guide.1) | copy-start | bytes 41476
  2.2 0.7 %copy-start.2 = (s32[2,256]{1,0:T(2,128)S(1)}, s32[2,256]{1,0:T(2,128)}, u32[]{:S(2)}) copy-start(s32[2,256]{1,0:T(2,128)} %valid.1) | copy-start | bytes 6148
  3.4 9.2 %collective-permute-start.2 = (bf16[336,256]{1,0:T(8,128)(2,1)S(1)}, bf16[336,256]{1,0:T(8,128)(2,1)S(1)}, u32[]{:S(2)}, u32[]{:S(2)}) collective-permute-start(bf16[336,256]{1,0:T(8,128)(2,1)S(1)} %get-tuple-element.20.mine), channel_id=1, source_target_pairs={{0,4},{4,8},{8,12},{1,5},{5,9},{9,13},{2,6},{6,10},{10,14},{3,7},{... | collective-permute-start | bytes 516104 | tf_op jit(solution)/shard_map/ppermute | solution.py:348
  7.9 7.1 %collective-permute-start.1 = (bf16[256,256]{1,0:T(8,128)(2,1)S(1)}, bf16[256,256]{1,0:T(8,128)(2,1)S(1)}, u32[]{:S(2)}, u32[]{:S(2)}) collective-permute-start(bf16[256,256]{1,0:T(8,128)(2,1)S(1)} %get-tuple-element.18.mine), channel_id=1, source_target_pairs={{0,4},{4,8},{8,12},{1,5},{5,9},{9,13},{2,6},{6,10},{10,14},{3,7},{... | collective-permute-start | bytes 393224 | tf_op jit(solution)/shard_map/ppermute | solution.py:349

commit v4 on v3

--- a/solution.py
+++ b/solution.py
@@ -1,3 +1,4 @@
+import functools
 import math
 
 import jax
@@ -57,6 +58,27 @@
     )(*args)
 
 
+def spread_guide(guide):
+    keys = LAYERS * 3 * GROUPS
+    row = iota((3 * KEYS, keys), 0)
+    tap = jnp.where(row >= KEYS, 1, 0) + jnp.where(row >= 2 * KEYS, 1, 0)
+    row = row - KEYS * tap
+    layer = jnp.where(row >= GROUPS, 1, 0) + jnp.where(row >= 2 * GROUPS, 1, 0)
+    key = 2 * GROUPS * layer + GROUPS * tap + row
+    chosen = jnp.where((iota((3 * KEYS, keys), 1) == key) & (row < 3 * GROUPS), 1.0, 0.0).astype(BF)
+    guide_t = dot_t(chosen, guide).astype(BF)
+    return jnp.concatenate([guide_t, guide_t], axis=1)
+
+
+def normalise(z, wts, t, room_left, room_right):
+    z = (0.55 + 0.45 * jnp.tanh(0.5 * z)).astype(BF).astype(F32)
+    taps = [z[k * KEYS : (k + 1) * KEYS] for k in range(3)]
+    scale = 1.0 / (taps[0] + taps[1] + taps[2])
+    wts[t, 0:KEYS, :] = jnp.where(room_left >= t, taps[0] * scale, 0.0)
+    wts[t, KEYS : 2 * KEYS, :] = taps[1] * scale
+    wts[t, 2 * KEYS : 3 * KEYS, :] = jnp.where(room_right < t, taps[2] * scale, 0.0)
+
+
 def prefetch_kernel(own, valid, guide, own_out, masks, perm, flip, guide_out, valid_in, guide_in, sems):
     copies = [
         pltpu.make_async_copy(src, dst, sems.at[i])
@@ -70,16 +92,8 @@
     back = 2 * LANES - 1 - iota((DISP, 2 * LANES), 0)
     flip[...] = jnp.where(iota((DISP, 2 * LANES), 1) == back, 1.0, 0.0).astype(BF)
 
-    keys = LAYERS * 3 * GROUPS
-    row = iota((3 * KEYS, keys), 0)
-    tap = jnp.where(row >= KEYS, 1, 0) + jnp.where(row >= 2 * KEYS, 1, 0)
-    row = row - KEYS * tap
-    layer = jnp.where(row >= GROUPS, 1, 0) + jnp.where(row >= 2 * GROUPS, 1, 0)
-    key = 2 * GROUPS * layer + GROUPS * tap + row
-    chosen = jnp.where((iota((3 * KEYS, keys), 1) == key) & (row < 3 * GROUPS), 1.0, 0.0).astype(BF)
     copies[1].wait()
-    guide_t = dot_t(chosen, guide_in[...]).astype(BF)
-    guide_out[...] = jnp.concatenate([guide_t, guide_t], axis=1)
+    guide_out[...] = spread_guide(guide_in[...])
     copies[2].wait()
     masks[...] = valid_in[...].astype(F32)
     copies[0].wait()
@@ -220,13 +234,7 @@
         logits = dot_t(guide[...], gate_rows[at : at + 2 * LANES, :])
         for i in range(2):
             t = 2 * two + i
-            z = logits[:, i * LANES : (i + 1) * LANES]
-            z = (0.55 + 0.45 * jnp.tanh(0.5 * z)).astype(BF).astype(F32)
-            taps = [z[k * KEYS : (k + 1) * KEYS] for k in range(3)]
-            scale = 1.0 / (taps[0] + taps[1] + taps[2])
-            wts[t, 0:KEYS, :] = jnp.where(room_left >= t, taps[0] * scale, 0.0)
-            wts[t, KEYS : 2 * KEYS, :] = taps[1] * scale
-            wts[t, 2 * KEYS : 3 * KEYS, :] = jnp.where(room_right < t, taps[2] * scale, 0.0)
+            normalise(logits[:, i * LANES : (i + 1) * LANES], wts, t, room_left, room_right)
 
 
 def late_kernel(
@@ -329,7 +337,7 @@
     return jnp.transpose(joined, (1, 0, 2)).reshape(1, sub, n * BLOCK)
 
 
-def on_device(features, valid_cols, offsets, guide_weight):
+def halo_plan(features, valid_cols, offsets, guide_weight):
     own = features[0]
     n = lax.axis_size("cols")
     right = [(c, c + 1) for c in range(n - 1)]
@@ -362,8 +370,233 @@
         [skew, pltpu.VMEM(quad_rows, BF), pltpu.VMEM((RUN, DISP, LANES), F32), square, square],
         1, (offsets, second, left_second, lhs, early_rows, wts, flip), 1_000_000_000,
     )
-    pieces = lax.all_gather(result, ("cols", "view"), axis=0)
+    copies = jnp.broadcast_to(result[None], (2 * n, LINES, WIDE))
+    pieces = lax.all_to_all(copies, ("cols", "view"), split_axis=0, concat_axis=0, tiled=True)
     return join(pieces, own.shape[0] // n, n)
+
+
+LINE_RUN = 8
+MASK_ROWS = 16
+
+
+def constants_kernel(guide, order, flip, guide_out, spread):
+    row = iota((LANES, LANES), 0)
+    from_lane = LANES - 1 - LINE_RUN * (row & (PARTS - 1)) - (row >> 4)
+    order[...] = jnp.where(iota((LANES, LANES), 1) == from_lane, 1.0, 0.0).astype(BF)
+    back = 2 * LANES - 1 - iota((DISP, 2 * LANES), 0)
+    flip[...] = jnp.where(iota((DISP, 2 * LANES), 1) == back, 1.0, 0.0).astype(BF)
+    guide_out[...] = spread_guide(guide[...])
+    block_of = spread.shape[1] // LINE_RUN - 1 - (iota(spread.shape, 1) >> 3)
+    spread[...] = jnp.where(iota(spread.shape, 0) == block_of, 1.0, 0.0).astype(BF)
+
+
+def pack_kernel(first, own, valid, out, own_in, valid_in, sems):
+    targets = out.shape[0]
+    start = 0 if first else 1
+    copies = [
+        pltpu.make_async_copy(own.at[2 * i + start], own_in.at[i], sems.at[i]) for i in range(targets)
+    ]
+    copies.append(pltpu.make_async_copy(valid, valid_in, sems.at[targets]))
+    for copy in copies:
+        copy.start()
+    copies[-1].wait()
+    masks = valid_in[...].astype(F32)
+    factor = jnp.where(lax.axis_index("view") == 1, masks[1:2, :], 1.0).astype(BF)
+    ref_mask = jnp.broadcast_to(masks[0:1, :], (MASK_ROWS, BLOCK)).astype(BF)
+    for i in range(targets):
+        copies[i].wait()
+        out[i, :CHANNELS, :] = own_in[i] * factor
+        if first:
+            out[i, CHANNELS:, :] = ref_mask
+
+
+def line_kernel(
+    which, offsets, blocks, masks, order, flip, guide, spread, *rest
+):
+    if which:
+        earlier, out, gate_rows, cost_rows, vol, done, wts = rest
+    else:
+        out, gate_rows, cost_rows, vol, done, wts = rest
+    tiles = blocks.shape[0]
+    width = tiles * LANES
+    at = lax.axis_index("cols") * (2 * offsets.shape[0] // tiles) + 2 * lax.axis_index("view") + which
+    off = offsets[at]
+
+    def tile_of(view, w):
+        lo = (w % 2) * LANES
+        return blocks[2 * (w // 2) + view, :CHANNELS, lo : lo + LANES]
+
+    ch_lane = iota((CHANNELS, LANES), 1)
+    rolled = [pltpu.roll(tile_of(1, w).astype(F32), off, 1) for w in range(tiles)]
+    empty = jnp.zeros((CHANNELS, LANES), F32)
+    shifted = [empty.astype(BF)] * 2
+    for w in range(tiles):
+        shifted.append(jnp.where(ch_lane < off, rolled[w - 1] if w else empty, rolled[w]).astype(BF))
+    shifted = [jnp.concatenate([tile, tile], axis=0) for tile in shifted]
+
+    diagonal = iota((8, LANES), 1) - LINE_RUN * iota((8, LANES), 0)
+    low_half = iota((LANES, LANES), 1) < CHANNELS
+    scale = 1.0 / math.sqrt(CHANNELS)
+    for quad in range(tiles // 4):
+        refs, masked = [], []
+        for w in range(4 * quad, 4 * quad + 4):
+            tile = tile_of(0, w)
+            lo = (w % 2) * LANES
+            mask = masks[2 * (w // 2), CHANNELS : CHANNELS + 1, lo : lo + LANES].astype(F32) * scale
+            refs.append(tile)
+            masked.append(tile * mask.astype(BF))
+        cols = dot_t(order[...], jnp.concatenate(refs, axis=0))
+        masked = dot_t(order[...], jnp.concatenate(masked, axis=0))
+        for q in range(4):
+            w = 4 * quad + q
+            place = (tiles - 1 - w) * PARTS
+            keep = low_half if q % 2 == 0 else ~low_half
+            lo = (q // 2) * LANES
+            gates = jnp.where(keep, cols[:, lo : lo + LANES], 0.0).astype(BF)
+            lhs = jnp.where(keep, masked[:, lo : lo + LANES], 0.0).astype(BF)
+            rhs = jnp.concatenate(shifted[w : w + 3], axis=1)
+            products = jnp.dot(lhs, rhs, preferred_element_type=F32)
+            for t in range(LINE_RUN):
+                row = t * LANES + place
+                gate_rows[row : row + PARTS, :] = gates[t * PARTS : (t + 1) * PARTS]
+                halves = []
+                for half in range(2):
+                    base = half * LANES // 2 + t
+                    r = t * PARTS + 8 * half
+                    turned = [
+                        pltpu.roll(
+                            products[r : r + 8, i * LANES : (i + 1) * LANES],
+                            base, 1, stride=LINE_RUN, stride_axis=0,
+                        )
+                        for i in range(3)
+                    ]
+                    beyond = diagonal >= base
+                    halves.append(
+                        jnp.concatenate(
+                            [jnp.where(beyond, turned[1], turned[0]), jnp.where(beyond, turned[2], turned[1])],
+                            axis=1,
+                        )
+                    )
+                cost_rows[row : row + PARTS, :] = jnp.concatenate(halves, axis=0).astype(BF)
+
+    x_base = width - 1 - LINE_RUN * iota((KEYS, LANES), 1)
+    row = iota((KEYS, LANES), 0)
+    reach = jnp.where(row >= 2 * GROUPS, 9, jnp.where(row >= GROUPS, 3, 1))
+    room_left = x_base - reach
+    room_right = x_base + reach - width
+    for two in range(LINE_RUN // 2):
+        lo = 2 * two * LANES
+        costs = dot_t(flip[...], cost_rows[lo : lo + 2 * LANES, :])
+        logits = dot_t(guide[...], gate_rows[lo : lo + 2 * LANES, :])
+        for i in range(2):
+            t = 2 * two + i
+            vol[t] = costs[:, i * LANES : (i + 1) * LANES]
+            normalise(logits[:, i * LANES : (i + 1) * LANES], wts, t, room_left, room_right)
+
+    def aggregate(group, top):
+        at = pl.multiple_of(group * DGROUP, DGROUP)
+        v = [[vol[t, pl.ds(at + 8 * h, 8), :] for t in range(LINE_RUN)] for h in range(2)]
+        for layer in range(LAYERS):
+            s = 3**layer
+            fresh = [[], []]
+            for t in range(LINE_RUN):
+                w = [wts[t, pl.ds(k * KEYS + layer * GROUPS + group, 1), :] for k in range(3)]
+                w = [jnp.broadcast_to(a, (8, LANES)) for a in w]
+                for h in range(2):
+                    blk, r = divmod(t + s, LINE_RUN)
+                    before = pltpu.roll(v[h][r], LANES - blk, 1) if blk else v[h][r]
+                    blk, r = divmod(t - s, LINE_RUN)
+                    after = pltpu.roll(v[h][r], -blk, 1) if blk else v[h][r]
+                    fresh[h].append(w[0] * before + w[1] * v[h][t] + w[2] * after)
+            v = fresh
+        for h in range(2):
+            for t in range(LINE_RUN):
+                done[t, pl.ds(at + 8 * h, 8), :] = v[h][t]
+        return tuple(jnp.maximum(top[t], jnp.maximum(v[0][t], v[1][t])) for t in range(LINE_RUN))
+
+    top = lax.fori_loop(0, GROUPS, aggregate, (jnp.full((8, LANES), -jnp.inf, F32),) * LINE_RUN)
+    top = [jnp.max(a, axis=0, keepdims=True) for a in top]
+    sub = iota((8, LANES), 0)
+    totals = jnp.zeros((8, LANES), F32)
+    moments = totals
+    for t in range(LINE_RUN):
+        total = jnp.zeros((8, LANES), F32)
+        moment = total
+        for i in range(DISP // 8):
+            e = jnp.exp(SHARPNESS * (done[t, 8 * i : 8 * i + 8, :] - top[t]))
+            total = total + e
+            if i:
+                moment = moment + float(8 * i) * e
+        moment = moment + sub.astype(F32) * total
+        here = sub == LINE_RUN - 1 - t
+        totals = jnp.where(here, jnp.sum(total, axis=0, keepdims=True), totals)
+        moments = jnp.where(here, jnp.sum(moment, axis=0, keepdims=True), moments)
+    vals = (moments / totals + off.astype(F32)) * (1.0 / DISP)
+    high = vals.astype(BF)
+    rest_of = vals - high.astype(F32)
+    middle = rest_of.astype(BF)
+    low = (rest_of - middle.astype(F32)).astype(BF)
+    zero = jnp.zeros((8, LANES), BF)
+    pieces = jnp.dot(
+        jnp.concatenate([high, middle, low, zero], axis=0), spread[...], preferred_element_type=F32
+    )
+    pieces = pieces[0:8] + pieces[8:16] + pieces[16:24]
+    wanted = iota((8, width), 0) == (iota((8, width), 1) & (LINE_RUN - 1))
+    line = jnp.sum(jnp.where(wanted, pieces, 0.0), axis=0, keepdims=True)
+    if which:
+        out[0:1, :] = earlier[...]
+        out[1:2, :] = line
+    else:
+        out[...] = line
+
+
+def lines_plan(features, valid_cols, offsets, guide_weight):
+    own = features[0]
+    n = lax.axis_size("cols")
+    devices = 2 * n
+    width = n * BLOCK
+    got = []
+    for first in (True, False):
+        rows = CHANNELS + (MASK_ROWS if first else 0)
+        (packed,) = call(
+            functools.partial(pack_kernel, first),
+            [((devices, rows, BLOCK), BF)],
+            [
+                pltpu.VMEM((devices, CHANNELS, BLOCK), BF),
+                pltpu.VMEM(valid_cols.shape, jnp.int32),
+                pltpu.SemaphoreType.DMA((devices + 1,)),
+            ],
+            0, (own, valid_cols), 1_000_000, pl.ANY,
+        )
+        got.append(lax.all_to_all(packed, ("cols", "view"), split_axis=0, concat_axis=0, tiled=True))
+    consts = call(
+        constants_kernel,
+        [((LANES, LANES), BF), ((DISP, 2 * LANES), BF), ((3 * KEYS, LANES), BF), ((LANES, width), BF)],
+        [], 0, (guide_weight,), 1_000_000,
+    )
+    line = ()
+    for which in range(2):
+        line = call(
+            functools.partial(line_kernel, which),
+            [((1 + which, width), F32)],
+            [
+                pltpu.VMEM((LINE_RUN * LANES, LANES), BF),
+                pltpu.VMEM((LINE_RUN * LANES, 2 * LANES), BF),
+                pltpu.VMEM((LINE_RUN, DISP, LANES), F32),
+                pltpu.VMEM((LINE_RUN, DISP, LANES), F32),
+                pltpu.VMEM((LINE_RUN, 3 * KEYS, LANES), F32),
+            ],
+            1, (offsets, got[which], got[0], *consts, *line), 1_000_000_000,
+        )
+    return lax.all_gather(line[0], "view", axis=0, tiled=True)[None]
+
+
+def on_device(features, valid_cols, offsets, guide_weight):
+    n = lax.axis_size("cols")
+    lines = features.shape[1]
+    if lines == 4 * n and n * BLOCK == LINE_RUN * LANES:
+        return lines_plan(features, valid_cols, offsets, guide_weight)
+    return halo_plan(features, valid_cols, offsets, guide_weight)
 
 
 def solution(mesh):

time: 36.8 us -> 41.2 us (1.12)
  blocking collectives: 15.1 us -> 1.81 us
  waiting for transfers between devices: 1.32 us -> 13.9 us
  Pallas kernels: 8.46 us -> 12.1 us
  starting transfers between devices: 8.43 us -> 9.88 us
  other arithmetic: 0.69 us -> 0 us
  local copies, waits for them, and re-layouts: 2.46 us -> 3.03 us
    all_to_all x0 -> x2, waiting for transfers between devices: none -> 13.9 us  [lines_plan(): lax.all_to_all(packed, ('cols', 'view'), split_axis=0, concat_axis=0, til...]
    all_gather x1, blocking collectives: 15.1 us -> 1.81 us  [lines_plan(): return lax.all_gather(line[0], 'view', axis=0, tiled=True)[None]]
    all_to_all x0 -> x2, starting transfers between devices: none -> 9.88 us  [lines_plan(): lax.all_to_all(packed, ('cols', 'view'), split_axis=0, concat_axis=0, til...]
    ppermute x3 -> x0, starting transfers between devices: 8.43 us -> none  [the longest x1 4.5 us: on_device(): left_first = lax.ppermute(first, 'cols', right)]
    pallas_call x4 -> x5, Pallas kernels: 8.46 us -> 12.1 us  [call(): pl.pallas_call(kernel, out_shape=[jax.ShapeDtypeStruct(shape, dtype) for...]
    ppermute x3 -> x0, waiting for transfers between devices: 1.32 us -> none  [the longest x1 1.12 us: on_device(): left_first = lax.ppermute(first, 'cols', right)]
    select_n x1 -> x0, other arithmetic: 0.68 us -> none  [join(): joined = jnp.where(keep, main, tail)]
    broadcast_in_dim x0 -> x1, local copies, waits for them, and re-layouts: none -> 0.63 us  [lines_plan(): return lax.all_gather(line[0], 'view', axis=0, tiled=True)[None]]
  transfers between devices with their start and end apart: 3 -> 2, of which waited for: 2 -> 2; matrix products, arithmetic and copies ran while one was open for 0% -> 0% of each run, Pallas kernels for 7% -> 15%
where the time goes in v4:
time: 41.2 us; the launch traced here: 40.8 us
  waiting for transfers between devices  13.9 us (34%)
  Pallas kernels  12.1 us (29%)
  starting transfers between devices  9.88 us (24%)
  local copies, waits for them, and re-layouts  3.03 us (7%)
  blocking collectives  1.81 us (4%)
    all_to_all x2, waiting for transfers between devices, lines_plan(): lax.all_to_all(packed, ('cols', 'view'), split_axis=0, concat_axis=0, til...  13.9 us
    pallas_call x5, Pallas kernels, call(): pl.pallas_call(kernel, out_shape=[jax.ShapeDtypeStruct(shape, dtype) for...  12.1 us
    all_to_all x2, starting transfers between devices, lines_plan(): lax.all_to_all(packed, ('cols', 'view'), split_axis=0, concat_axis=0, til...  9.88 us
    unnamed x12, local copies, waits for them, and re-layouts  2.4 us
    all_gather x1, blocking collectives, lines_plan(): return lax.all_gather(line[0], 'view', axis=0, tiled=True)[None]  1.81 us
  transfers between devices with their start and end apart: 2, of which 2 were waited for; matrix products, arithmetic and copies ran while one was open for 0% of the time, Pallas kernels for 15%

profile of v4, /device:TPU:0, one launch (start us, length us, event | category | flops | bytes accessed | tf_op | source)
XLA Modules:
  0.0 40.8 jit_solution(16603783949851105427)
XLA Ops:
  0.0 0.0 copy-start
  0.0 1.0 %copy-done = bf16[1,16,64,256]{3,2,1,0:T(8,128)(2,1)S(1)} copy-done((bf16[1,16,64,256]{3,2,1,0:T(8,128)(2,1)S(1)}, bf16[1,16,64,256]{3,2,1,0:T(8,128)(2,1)}, u32[]{:S(2)}) %copy-start) | copy-done | bytes 524312
  1.0 0.0 copy-start.3
  1.0 0.7 %copy-done.3 = s32[2,256]{1,0:T(2,128)S(1)} copy-done((s32[2,256]{1,0:T(2,128)S(1)}, s32[2,256]{1,0:T(2,128)}, u32[]{:S(2)}) %copy-start.3) | copy-done | bytes 2072
  1.7 1.2 %shard_map.47 = bf16[8,80,256]{2,1,0:T(8,128)(2,1)} custom-call(bf16[16,64,256]{2,1,0:T(8,128)(2,1)S(1)} %bitcast.2, s32[2,256]{1,0:T(2,128)S(1)} %copy-done.3), custom_call_target="tpu_custom_call" | custom-call | flops 1000000 | bytes 1000000 | tf_op jit(solution)/shard_map/pallas_call | solution.py:50
  2.9 0.0 copy-start.1
  2.9 0.0 copy-start.4
  2.9 6.5 %all-to-all-start.1 = ((bf16[8,80,256]{2,1,0:T(8,128)(2,1)}), bf16[8,80,256]{2,1,0:T(8,128)(2,1)S(1)}, u32[]{:S(2)}, u32[]{:S(2)}) async-start(bf16[8,80,256]{2,1,0:T(8,128)(2,1)} %shard_map.47), calls=%async_computation.1 | async-start | bytes 655360 | tf_op jit(solution)/shard_map/all_to_all | solution.py:571
  9.4 0.0 copy-done.1
  9.4 0.0 copy-done.4
  9.4 1.2 %shard_map.46 = bf16[8,64,256]{2,1,0:T(8,128)(2,1)} custom-call(bf16[16,64,256]{2,1,0:T(8,128)(2,1)S(1)} %bitcast.3, s32[2,256]{1,0:T(2,128)S(1)} %copy-done.4), custom_call_target="tpu_custom_call" | custom-call | flops 1000000 | bytes 1000000 | tf_op jit(solution)/shard_map/pallas_call | solution.py:50
  10.6 0.0 copy-start.2
  10.6 9.9 %all-to-all-done.1.blocks.masks = bf16[8,80,256]{2,1,0:T(8,128)(2,1)S(1)} async-done(((bf16[8,80,256]{2,1,0:T(8,128)(2,1)}), bf16[8,80,256]{2,1,0:T(8,128)(2,1)S(1)}, u32[]{:S(2)}, u32[]{:S(2)}) %all-to-all-start.1) | async-done | bytes 327712 | tf_op jit(solution)/shard_map/all_to_all | solution.py:571
  20.5 3.4 %all-to-all-start = ((bf16[8,64,256]{2,1,0:T(8,128)(2,1)}), bf16[8,64,256]{2,1,0:T(8,128)(2,1)S(1)}, u32[]{:S(2)}, u32[]{:S(2)}) async-start(bf16[8,64,256]{2,1,0:T(8,128)(2,1)} %shard_map.46), calls=%async_computation | async-start | bytes 524288 | tf_op jit(solution)/shard_map/all_to_all | solution.py:571
  24.0 0.0 copy-done.2
  24.0 0.3 shard_map.48
  24.3 0.0 copy-start.5
  24.3 0.7 %copy-done.5 = s32[16]{0:T(128)S(1)} copy-done((s32[16]{0:T(128)S(1)}, s32[16]{0:T(128)}, u32[]{:S(2)}) %copy-start.5) | copy-done | bytes 88
  24.9 4.7 %shard_map.49.rest_0_ = f32[1,1024]{1,0:T(1,128)S(1)} custom-call(s32[16]{0:T(128)S(1)} %copy-done.5, bf16[8,80,256]{2,1,0:T(8,128)(2,1)S(1)} %all-to-all-done.1.blocks.masks, bf16[8,80,256]{2,1,0:T(8,128)(2,1)S(1)} %all-to-all-done.1.blocks.masks, bf16[128,128]{1,0:T(8,128)(2,1)S(1)} %get-tuple-element.9.order, ...), custom_call_target="tpu_custom_call" | custom-call | flops 1000000000 | bytes 1000000 | tf_op jit(solution)/shard_map/pallas_call | solution.py:50
  29.7 4.0 %all-to-all-done.blocks = bf16[8,64,256]{2,1,0:T(8,128)(2,1)S(1)} async-done(((bf16[8,64,256]{2,1,0:T(8,128)(2,1)}), bf16[8,64,256]{2,1,0:T(8,128)(2,1)S(1)}, u32[]{:S(2)}, u32[]{:S(2)}) %all-to-all-start) | async-done | bytes 262176 | tf_op jit(solution)/shard_map/all_to_all | solution.py:571
  33.6 4.7 %shard_map.50 = f32[2,1024]{1,0:T(2,128)S(1)} custom-call(s32[16]{0:T(128)S(1)} %copy-done.5, bf16[8,64,256]{2,1,0:T(8,128)(2,1)S(1)} %all-to-all-done.blocks, bf16[8,80,256]{2,1,0:T(8,128)(2,1)S(1)} %all-to-all-done.1.blocks.masks, bf16[128,128]{1,0:T(8,128)(2,1)S(1)} %get-tuple-element.9.order, bf16[192,256]{1,0:T(8,128)(2,1)S(1)} %get-tuple-element.10.flip, ...), custom_call_target="tpu_custom_call" | custom-call | flops 1000000000 | bytes 1000000 | tf_op jit(solution)/shard_map/pallas_call | solution.py:50
  38.4 1.8 %all-gather = f32[2,2,1024]{2,1,0:T(2,128)S(1)} all-gather(f32[1,2,1024]{2,1,0:T(2,128)S(1)} %bitcast.4), channel_id=1, replica_groups=mesh['tiles'=2,'cols'=4,'lines'=2,'view'=2] {'view'}, dimensions={0}, use_global_device_ids=true | all-gather | bytes 24576 | tf_op jit(solution)/shard_map/all_gather | solution.py:591
  40.2 0.6 %broadcast_in_dim.3 = f32[1,4,1024]{2,1,0:T(4,128)} reshape(f32[2,2,1024]{2,1,0:T(2,128)S(1)} %all-gather) | data formatting | bytes 32768 | tf_op jit(solution)/shard_map/broadcast_in_dim | solution.py:591
Async XLA Ops:
  0.0 1.0 %copy-start = (bf16[1,16,64,256]{3,2,1,0:T(8,128)(2,1)S(1)}, bf16[1,16,64,256]{3,2,1,0:T(8,128)(2,1)}, u32[]{:S(2)}) copy-start(bf16[1,16,64,256]{3,2,1,0:T(8,128)(2,1)} %param.4) | copy-start | bytes 1572868
  1.0 0.7 %copy-start.3 = (s32[2,256]{1,0:T(2,128)S(1)}, s32[2,256]{1,0:T(2,128)}, u32[]{:S(2)}) copy-start(s32[2,256]{1,0:T(2,128)} %valid.3) | copy-start | bytes 6148
  2.9 6.5 %copy-start.1 = (bf16[1,16,64,256]{3,2,1,0:T(8,128)(2,1)S(1)}, bf16[1,16,64,256]{3,2,1,0:T(8,128)(2,1)}, u32[]{:S(2)}) copy-start(bf16[1,16,64,256]{3,2,1,0:T(8,128)(2,1)} %param.4) | copy-start | bytes 1572868
  2.9 6.5 %copy-start.4 = (s32[2,256]{1,0:T(2,128)S(1)}, s32[2,256]{1,0:T(2,128)}, u32[]{:S(2)}) copy-start(s32[2,256]{1,0:T(2,128)} %valid.3) | copy-start | bytes 6148
  2.9 17.6 %all-to-all-start.1 = ((bf16[8,80,256]{2,1,0:T(8,128)(2,1)}), bf16[8,80,256]{2,1,0:T(8,128)(2,1)S(1)}, u32[]{:S(2)}, u32[]{:S(2)}) async-start(bf16[8,80,256]{2,1,0:T(8,128)(2,1)} %shard_map.47), calls=%async_computation.1 | async-start | bytes 655360 | tf_op jit(solution)/shard_map/all_to_all | solution.py:571
  10.6 13.4 %copy-start.2 = (bf16[64,108]{1,0:T(8,128)(2,1)S(1)}, bf16[64,108]{1,0:T(8,128)(2,1)}, u32[]{:S(2)}) copy-start(bf16[64,108]{1,0:T(8,128)(2,1)} %guide.1) | copy-start | bytes 41476
  20.5 13.1 %all-to-all-start = ((bf16[8,64,256]{2,1,0:T(8,128)(2,1)}), bf16[8,64,256]{2,1,0:T(8,128)(2,1)S(1)}, u32[]{:S(2)}, u32[]{:S(2)}) async-start(bf16[8,64,256]{2,1,0:T(8,128)(2,1)} %shard_map.46), calls=%async_computation | async-start | bytes 524288 | tf_op jit(solution)/shard_map/all_to_all | solution.py:571
  24.3 0.7 %copy-start.5 = (s32[16]{0:T(128)S(1)}, s32[16]{0:T(128)}, u32[]{:S(2)}) copy-start(s32[16]{0:T(128)} %offsets.3) | copy-start | bytes 196

commit v5 on v3

--- a/solution.py
+++ b/solution.py
@@ -1,3 +1,4 @@
+import functools
 import math
 
 import jax
@@ -57,6 +58,27 @@
     )(*args)
 
 
+def spread_guide(guide):
+    keys = LAYERS * 3 * GROUPS
+    row = iota((3 * KEYS, keys), 0)
+    tap = jnp.where(row >= KEYS, 1, 0) + jnp.where(row >= 2 * KEYS, 1, 0)
+    row = row - KEYS * tap
+    layer = jnp.where(row >= GROUPS, 1, 0) + jnp.where(row >= 2 * GROUPS, 1, 0)
+    key = 2 * GROUPS * layer + GROUPS * tap + row
+    chosen = jnp.where((iota((3 * KEYS, keys), 1) == key) & (row < 3 * GROUPS), 1.0, 0.0).astype(BF)
+    guide_t = dot_t(chosen, guide).astype(BF)
+    return jnp.concatenate([guide_t, guide_t], axis=1)
+
+
+def normalise(z, wts, t, room_left, room_right):
+    z = (0.55 + 0.45 * jnp.tanh(0.5 * z)).astype(BF).astype(F32)
+    taps = [z[k * KEYS : (k + 1) * KEYS] for k in range(3)]
+    scale = 1.0 / (taps[0] + taps[1] + taps[2])
+    wts[t, 0:KEYS, :] = jnp.where(room_left >= t, taps[0] * scale, 0.0)
+    wts[t, KEYS : 2 * KEYS, :] = taps[1] * scale
+    wts[t, 2 * KEYS : 3 * KEYS, :] = jnp.where(room_right < t, taps[2] * scale, 0.0)
+
+
 def prefetch_kernel(own, valid, guide, own_out, masks, perm, flip, guide_out, valid_in, guide_in, sems):
     copies = [
         pltpu.make_async_copy(src, dst, sems.at[i])
@@ -70,16 +92,8 @@
     back = 2 * LANES - 1 - iota((DISP, 2 * LANES), 0)
     flip[...] = jnp.where(iota((DISP, 2 * LANES), 1) == back, 1.0, 0.0).astype(BF)
 
-    keys = LAYERS * 3 * GROUPS
-    row = iota((3 * KEYS, keys), 0)
-    tap = jnp.where(row >= KEYS, 1, 0) + jnp.where(row >= 2 * KEYS, 1, 0)
-    row = row - KEYS * tap
-    layer = jnp.where(row >= GROUPS, 1, 0) + jnp.where(row >= 2 * GROUPS, 1, 0)
-    key = 2 * GROUPS * layer + GROUPS * tap + row
-    chosen = jnp.where((iota((3 * KEYS, keys), 1) == key) & (row < 3 * GROUPS), 1.0, 0.0).astype(BF)
     copies[1].wait()
-    guide_t = dot_t(chosen, guide_in[...]).astype(BF)
-    guide_out[...] = jnp.concatenate([guide_t, guide_t], axis=1)
+    guide_out[...] = spread_guide(guide_in[...])
     copies[2].wait()
     masks[...] = valid_in[...].astype(F32)
     copies[0].wait()
@@ -220,13 +234,7 @@
         logits = dot_t(guide[...], gate_rows[at : at + 2 * LANES, :])
         for i in range(2):
             t = 2 * two + i
-            z = logits[:, i * LANES : (i + 1) * LANES]
-            z = (0.55 + 0.45 * jnp.tanh(0.5 * z)).astype(BF).astype(F32)
-            taps = [z[k * KEYS : (k + 1) * KEYS] for k in range(3)]
-            scale = 1.0 / (taps[0] + taps[1] + taps[2])
-            wts[t, 0:KEYS, :] = jnp.where(room_left >= t, taps[0] * scale, 0.0)
-            wts[t, KEYS : 2 * KEYS, :] = taps[1] * scale
-            wts[t, 2 * KEYS : 3 * KEYS, :] = jnp.where(room_right < t, taps[2] * scale, 0.0)
+            normalise(logits[:, i * LANES : (i + 1) * LANES], wts, t, room_left, room_right)
 
 
 def late_kernel(
@@ -329,7 +337,7 @@
     return jnp.transpose(joined, (1, 0, 2)).reshape(1, sub, n * BLOCK)
 
 
-def on_device(features, valid_cols, offsets, guide_weight):
+def halo_plan(features, valid_cols, offsets, guide_weight):
     own = features[0]
     n = lax.axis_size("cols")
     right = [(c, c + 1) for c in range(n - 1)]
@@ -362,8 +370,207 @@
         [skew, pltpu.VMEM(quad_rows, BF), pltpu.VMEM((RUN, DISP, LANES), F32), square, square],
         1, (offsets, second, left_second, lhs, early_rows, wts, flip), 1_000_000_000,
     )
-    pieces = lax.all_gather(result, ("cols", "view"), axis=0)
+    copies = jnp.broadcast_to(result[None], (2 * n, LINES, WIDE))
+    pieces = lax.all_to_all(copies, ("cols", "view"), split_axis=0, concat_axis=0, tiled=True)
     return join(pieces, own.shape[0] // n, n)
+
+
+LINE_RUN = 16
+PAIR = 2
+LINE_PARTS = LANES // PAIR
+
+
+def constants_kernel(guide, order, flip, guide_out, spread):
+    row = iota((LANES, LANES), 0)
+    from_lane = LANES - 1 - LINE_RUN * (row & 7) - (row >> 3)
+    order[...] = jnp.where(iota((LANES, LANES), 1) == from_lane, 1.0, 0.0).astype(BF)
+    back = 2 * LANES - 1 - iota((DISP, 2 * LANES), 0)
+    flip[...] = jnp.where(iota((DISP, 2 * LANES), 1) == back, 1.0, 0.0).astype(BF)
+    guide_out[...] = spread_guide(guide[...])
+    block_of = LINE_PARTS - 1 - (iota(spread.shape, 1) >> 4)
+    here = (iota(spread.shape, 0) & (LINE_PARTS - 1)) == block_of
+    spread[...] = jnp.where(here, 1.0, 0.0).astype(BF)
+
+
+def lines_kernel(
+    offsets, blocks, valid, order, flip, guide, spread, out, gate_rows, cost_rows, vol, done, wts
+):
+    tiles = blocks.shape[0]
+    width = tiles * LANES
+    at = lax.axis_index("cols") * (PAIR * offsets.shape[0] // tiles) + PAIR * lax.axis_index("view")
+    offs = [offsets[at + i] for i in range(PAIR)]
+    ch_lane = iota((CHANNELS, LANES), 1)
+    diagonal = iota((8, LANES), 1) - LINE_RUN * iota((8, LANES), 0)
+    low_half = iota((LANES, LANES), 1) < CHANNELS
+    scale = 1.0 / math.sqrt(CHANNELS)
+    empty = jnp.zeros((CHANNELS, LANES), F32)
+
+    def mask_of(view, w):
+        lo = (w % 2) * LANES
+        return valid[w // 2, view : view + 1, lo : lo + LANES].astype(F32)
+
+    for i in range(PAIR):
+
+        def tile_of(view, w):
+            lo = (w % 2) * LANES
+            return blocks[2 * (w // 2) + view, i, :, lo : lo + LANES]
+
+        off = offs[i]
+        rolled = [pltpu.roll(tile_of(1, w).astype(F32) * mask_of(1, w), off, 1) for w in range(tiles)]
+        shifted = [empty.astype(BF)] * 2
+        for w in range(tiles):
+            shifted.append(jnp.where(ch_lane < off, rolled[w - 1] if w else empty, rolled[w]).astype(BF))
+        shifted = [jnp.concatenate([tile, tile], axis=0) for tile in shifted]
+        for quad in range(tiles // 4):
+            refs = [tile_of(0, 4 * quad + q) for q in range(4)]
+            masked = [refs[q] * (mask_of(0, 4 * quad + q) * scale).astype(BF) for q in range(4)]
+            cols = dot_t(order[...], jnp.concatenate(refs, axis=0))
+            masked = dot_t(order[...], jnp.concatenate(masked, axis=0))
+            for two in range(2):
+                lo = two * LANES
+                gates, products = [], []
+                for side in range(2):
+                    w = 4 * quad + 2 * two + side
+                    keep = low_half if side == 0 else ~low_half
+                    gates.append(jnp.where(keep, cols[:, lo : lo + LANES], 0.0))
+                    lhs = jnp.where(keep, masked[:, lo : lo + LANES], 0.0).astype(BF)
+                    rhs = jnp.concatenate(shifted[w : w + 3], axis=1)
+                    products.append(jnp.dot(lhs, rhs, preferred_element_type=F32))
+                place = i * LINE_PARTS + 8 * (tiles - 2 - 4 * quad - 2 * two)
+                for t in range(LINE_RUN):
+                    row = t * LANES + place
+                    r = 8 * t
+                    gate_rows[row : row + 16, :] = jnp.concatenate(
+                        [gates[1][r : r + 8], gates[0][r : r + 8]], axis=0
+                    ).astype(BF)
+                    beyond = diagonal >= t
+                    both = []
+                    for side in (1, 0):
+                        turned = [
+                            pltpu.roll(
+                                products[side][r : r + 8, m * LANES : (m + 1) * LANES],
+                                t, 1, stride=LINE_RUN, stride_axis=0,
+                            )
+                            for m in range(3)
+                        ]
+                        both.append(
+                            jnp.concatenate(
+                                [jnp.where(beyond, turned[1], turned[0]), jnp.where(beyond, turned[2], turned[1])],
+                                axis=1,
+                            )
+                        )
+                    cost_rows[row : row + 16, :] = jnp.concatenate(both, axis=0).astype(BF)
+
+    x_base = width - 1 - LINE_RUN * (iota((KEYS, LANES), 1) & (LINE_PARTS - 1))
+    row = iota((KEYS, LANES), 0)
+    reach = jnp.where(row >= 2 * GROUPS, 9, jnp.where(row >= GROUPS, 3, 1))
+    room_left = x_base - reach
+    room_right = x_base + reach - width
+    for two in range(LINE_RUN // 2):
+        lo = 2 * two * LANES
+        costs = dot_t(flip[...], cost_rows[lo : lo + 2 * LANES, :])
+        logits = dot_t(guide[...], gate_rows[lo : lo + 2 * LANES, :])
+        for i in range(2):
+            t = 2 * two + i
+            vol[t] = costs[:, i * LANES : (i + 1) * LANES]
+            normalise(logits[:, i * LANES : (i + 1) * LANES], wts, t, room_left, room_right)
+
+    for group in range(GROUPS):
+        for at in (group * DGROUP, group * DGROUP + 8):
+            v = [vol[t, at : at + 8, :] for t in range(LINE_RUN)]
+            for layer in range(LAYERS):
+                s = 3**layer
+                fresh = []
+                for t in range(LINE_RUN):
+                    rows = [k * KEYS + layer * GROUPS + group for k in range(3)]
+                    w = [wts[t, r : r + 1, :] for r in rows]
+                    blk, r = divmod(t + s, LINE_RUN)
+                    before = pltpu.roll(v[r], LANES - blk, 1) if blk else v[r]
+                    blk, r = divmod(t - s, LINE_RUN)
+                    after = pltpu.roll(v[r], -blk, 1) if blk else v[r]
+                    fresh.append(w[0] * before + w[1] * v[t] + w[2] * after)
+                v = fresh
+            for t in range(LINE_RUN):
+                done[t, at : at + 8, :] = v[t]
+
+    sub = iota((8, LANES), 0)
+    results = []
+    for block in range(LINE_RUN // 8):
+        totals = jnp.zeros((8, LANES), F32)
+        moments = totals
+        for s in range(8):
+            t = LINE_RUN - 1 - (8 * block + s)
+            v = [done[t, 8 * i : 8 * i + 8, :] for i in range(DISP // 8)]
+            top = v
+            while len(top) > 1:
+                top = [jnp.maximum(a, b) for a, b in zip(top[::2], top[1::2])] + top[len(top) & ~1 :]
+            top = jnp.max(top[0], axis=0, keepdims=True)
+            total = jnp.zeros((8, LANES), F32)
+            moment = total
+            for i in range(DISP // 8):
+                e = jnp.exp(SHARPNESS * (v[i] - top))
+                total = total + e
+                if i:
+                    moment = moment + float(8 * i) * e
+            moment = moment + sub.astype(F32) * total
+            totals = jnp.where(sub == s, jnp.sum(total, axis=0, keepdims=True), totals)
+            moments = jnp.where(sub == s, jnp.sum(moment, axis=0, keepdims=True), moments)
+        lane_line = iota((8, LANES), 1) >> 6
+        shift = jnp.zeros((8, LANES), F32)
+        for i in range(PAIR):
+            shift = jnp.where(lane_line == i, offs[i].astype(F32), shift)
+        results.append((moments / totals + shift) * (1.0 / DISP))
+    vals = jnp.concatenate(results, axis=0)
+    lane_line = iota((LINE_RUN, LANES), 1) >> 6
+    both = jnp.concatenate([jnp.where(lane_line == i, vals, 0.0) for i in range(PAIR)], axis=0)
+    high = both.astype(BF)
+    rest = both - high.astype(F32)
+    middle = rest.astype(BF)
+    low = (rest - middle.astype(F32)).astype(BF)
+    pieces = jnp.dot(
+        jnp.concatenate([high, middle, low], axis=0), spread[...], preferred_element_type=F32
+    )
+    size = PAIR * LINE_RUN
+    pieces = pieces[:size] + pieces[size : 2 * size] + pieces[2 * size :]
+    wanted = iota((LINE_RUN, width), 0) == (iota((LINE_RUN, width), 1) & (LINE_RUN - 1))
+    for i in range(PAIR):
+        piece = jnp.where(wanted, pieces[i * LINE_RUN : (i + 1) * LINE_RUN], 0.0)
+        out[i : i + 1, :] = jnp.sum(piece, axis=0, keepdims=True)
+
+
+def lines_plan(features, valid_cols, offsets, guide_weight):
+    n = lax.axis_size("cols")
+    devices = 2 * n
+    width = n * BLOCK
+    own = features.reshape(devices, PAIR, CHANNELS, BLOCK)
+    blocks = lax.all_to_all(own, ("cols", "view"), split_axis=0, concat_axis=0, tiled=True)
+    valid = lax.all_gather(valid_cols, "cols", axis=0)
+    consts = call(
+        constants_kernel,
+        [((LANES, LANES), BF), ((DISP, 2 * LANES), BF), ((3 * KEYS, LANES), BF), ((LANES, width), BF)],
+        [], 0, (guide_weight,), 1_000_000,
+    )
+    (rows,) = call(
+        lines_kernel,
+        [((PAIR, width), F32)],
+        [
+            pltpu.VMEM((LINE_RUN * LANES, LANES), BF),
+            pltpu.VMEM((LINE_RUN * LANES, 2 * LANES), BF),
+            pltpu.VMEM((LINE_RUN, DISP, LANES), F32),
+            pltpu.VMEM((LINE_RUN, DISP, LANES), F32),
+            pltpu.VMEM((LINE_RUN, 3 * KEYS, LANES), F32),
+        ],
+        1, (offsets, blocks, valid, *consts), 1_000_000_000,
+    )
+    return lax.all_gather(rows, "view", axis=0, tiled=True)[None]
+
+
+def on_device(features, valid_cols, offsets, guide_weight):
+    n = lax.axis_size("cols")
+    lines = features.shape[1]
+    if lines == 2 * PAIR * n and n * BLOCK == LINE_RUN * LINE_PARTS:
+        return lines_plan(features, valid_cols, offsets, guide_weight)
+    return halo_plan(features, valid_cols, offsets, guide_weight)
 
 
 def solution(mesh):

time: 36.8 us -> 34.4 us (0.935)
  blocking collectives: 15.1 us -> 21.6 us
  Pallas kernels: 8.46 us -> 4.29 us
  starting transfers between devices: 8.43 us -> 6.46 us
  waiting for transfers between devices: 1.32 us -> 0.01 us
  local copies, waits for them, and re-layouts: 2.46 us -> 1.69 us
  other arithmetic: 0.69 us -> 0 us
    ppermute x3 -> x0, starting transfers between devices: 8.43 us -> none  [the longest x1 4.5 us: on_device(): left_first = lax.ppermute(first, 'cols', right)]
    all_gather x1 -> x2, blocking collectives: 15.1 us -> 21.6 us  [the longest x1 19.8 us: lines_plan(): valid = lax.all_gather(valid_cols, 'cols', axis=0)]
    all_to_all x0 -> x1, starting transfers between devices: none -> 6.46 us  [lines_plan(): lax.all_to_all(own, ('cols', 'view'), split_axis=0, concat_axis=0, tiled=...]
    pallas_call x4 -> x2, Pallas kernels: 8.46 us -> 4.29 us  [call(): pl.pallas_call(kernel, out_shape=[jax.ShapeDtypeStruct(shape, dtype) for...]
    unnamed x8 -> x6, local copies, waits for them, and re-layouts: 2.44 us -> 1.07 us
    ppermute x3 -> x0, waiting for transfers between devices: 1.32 us -> none  [the longest x1 1.12 us: on_device(): left_first = lax.ppermute(first, 'cols', right)]
    select_n x1 -> x0, other arithmetic: 0.68 us -> none  [join(): joined = jnp.where(keep, main, tail)]
    broadcast_in_dim x0 -> x1, local copies, waits for them, and re-layouts: none -> 0.63 us  [lines_plan(): return lax.all_gather(rows, 'view', axis=0, tiled=True)[None]]
  transfers between devices with their start and end apart: 3 -> 1, of which waited for: 2 -> 0; matrix products, arithmetic and copies ran while one was open for 0% -> 0% of each run, Pallas kernels for 7% -> 1%
where the time goes in v5:
time: 34.4 us; the launch traced here: 34.1 us
  blocking collectives  21.6 us (63%)
  starting transfers between devices  6.46 us (19%)
  Pallas kernels  4.29 us (12%)
  local copies, waits for them, and re-layouts  1.69 us (5%)
    all_gather x1, blocking collectives, lines_plan(): valid = lax.all_gather(valid_cols, 'cols', axis=0)  19.8 us
    all_to_all x1, starting transfers between devices, lines_plan(): lax.all_to_all(own, ('cols', 'view'), split_axis=0, concat_axis=0, tiled=...  6.46 us
    pallas_call x2, Pallas kernels, call(): pl.pallas_call(kernel, out_shape=[jax.ShapeDtypeStruct(shape, dtype) for...  4.29 us
    all_gather x1, blocking collectives, lines_plan(): return lax.all_gather(rows, 'view', axis=0, tiled=True)[None]  1.81 us
    unnamed x6, local copies, waits for them, and re-layouts  1.07 us
  transfers between devices with their start and end apart: 1, of which 0 were waited for; matrix products, arithmetic and copies ran while one was open for 0% of the time, Pallas kernels for 1%

profile of v5, /device:TPU:0, one launch (start us, length us, event | category | flops | bytes accessed | tf_op | source)
XLA Modules:
  0.0 34.1 jit_solution(1713905830526866306)
XLA Ops:
  0.0 0.0 copy-start
  0.0 6.5 %all-to-all-start = ((bf16[8,2,64,256]{3,2,1,0:T(8,128)(2,1)}), bf16[8,2,64,256]{3,2,1,0:T(8,128)(2,1)S(1)}, u32[]{:S(2)}, u32[]{:S(2)}) async-start(bf16[8,2,64,256]{3,2,1,0:T(8,128)(2,1)} %bitcast.4), calls=%async_computation | async-start | bytes 1048576 | tf_op jit(solution)/shard_map/all_to_all | solution.py:546
  6.5 0.0 copy-done
  6.5 0.0 copy-start.2
  6.5 0.3 shard_map.46
  6.7 0.4 %copy-done.2 = s32[2,256]{1,0:T(2,128)S(1)} copy-done((s32[2,256]{1,0:T(2,128)S(1)}, s32[2,256]{1,0:T(2,128)}, u32[]{:S(2)}) %copy-start.2) | copy-done | bytes 2072
  7.2 19.8 %all-gather.1.valid = s32[4,2,256]{2,1,0:T(2,128)S(1)} all-gather(s32[1,2,256]{2,1,0:T(2,128)S(1)} %bitcast.5), channel_id=2, replica_groups=mesh['tiles'=2,'cols'=4,'lines'=2,'view'=2] {'cols'}, dimensions={0}, use_global_device_ids=true | all-gather | bytes 10240 | tf_op jit(solution)/shard_map/all_gather | solution.py:547
  26.9 0.0 all-to-all-done.blocks
  27.0 0.0 copy-start.1
  27.0 0.7 %copy-done.1 = s32[16]{0:T(128)S(1)} copy-done((s32[16]{0:T(128)S(1)}, s32[16]{0:T(128)}, u32[]{:S(2)}) %copy-start.1) | copy-done | bytes 88
  27.6 4.0 %shard_map.47 = f32[2,1024]{1,0:T(2,128)S(1)} custom-call(s32[16]{0:T(128)S(1)} %copy-done.1, bf16[8,2,64,256]{3,2,1,0:T(8,128)(2,1)S(1)} %all-to-all-done.blocks, s32[4,2,256]{2,1,0:T(2,128)S(1)} %all-gather.1.valid, bf16[128,128]{1,0:T(8,128)(2,1)S(1)} %get-tuple-element.9.order, bf16[192,256]{1,0:T(8,128)(2,1)S(1)} %get-tuple-element.10.flip, ...), custom_call_target="tpu_custom_call" | custom-call | flops 1000000000 | bytes 1000000 | tf_op jit(solution)/shard_map/pallas_call | solution.py:50
  31.6 1.8 %all-gather.2 = f32[2,2,1024]{2,1,0:T(2,128)S(1)} all-gather(f32[1,2,1024]{2,1,0:T(2,128)S(1)} %bitcast.3), channel_id=1, replica_groups=mesh['tiles'=2,'cols'=4,'lines'=2,'view'=2] {'view'}, dimensions={0}, use_global_device_ids=true | all-gather | bytes 24576 | tf_op jit(solution)/shard_map/all_gather | solution.py:565
  33.5 0.6 %broadcast_in_dim.3 = f32[1,4,1024]{2,1,0:T(4,128)} reshape(f32[2,2,1024]{2,1,0:T(2,128)S(1)} %all-gather.2) | data formatting | bytes 32768 | tf_op jit(solution)/shard_map/broadcast_in_dim | solution.py:565
Async XLA Ops:
  0.0 6.5 %copy-start = (bf16[64,108]{1,0:T(8,128)(2,1)S(1)}, bf16[64,108]{1,0:T(8,128)(2,1)}, u32[]{:S(2)}) copy-start(bf16[64,108]{1,0:T(8,128)(2,1)} %guide.1) | copy-start | bytes 41476
  0.0 26.9 %all-to-all-start = ((bf16[8,2,64,256]{3,2,1,0:T(8,128)(2,1)}), bf16[8,2,64,256]{3,2,1,0:T(8,128)(2,1)S(1)}, u32[]{:S(2)}, u32[]{:S(2)}) async-start(bf16[8,2,64,256]{3,2,1,0:T(8,128)(2,1)} %bitcast.4), calls=%async_computation | async-start | bytes 1048576 | tf_op jit(solution)/shard_map/all_to_all | solution.py:546
  6.5 0.7 %copy-start.2 = (s32[2,256]{1,0:T(2,128)S(1)}, s32[2,256]{1,0:T(2,128)}, u32[]{:S(2)}) copy-start(s32[2,256]{1,0:T(2,128)} %param.5) | copy-start | bytes 6148
  27.0 0.7 %copy-start.1 = (s32[16]{0:T(128)S(1)}, s32[16]{0:T(128)}, u32[]{:S(2)}) copy-start(s32[16]{0:T(128)} %offsets.1) | copy-start | bytes 196

commit v6 on v5

--- a/solution.py
+++ b/solution.py
@@ -393,10 +393,13 @@
 
 
 def lines_kernel(
-    offsets, blocks, valid, order, flip, guide, spread, out, gate_rows, cost_rows, vol, done, wts
+    offsets, blocks, order, flip, guide, spread, *rest
 ):
+    near, (out, valid, gate_rows, cost_rows, vol, done, wts) = rest[:-7], rest[-7:]
     tiles = blocks.shape[0]
     width = tiles * LANES
+    for k, masks in enumerate(near):
+        valid[lax.axis_index("cols") ^ k] = masks[...].astype(F32)
     at = lax.axis_index("cols") * (PAIR * offsets.shape[0] // tiles) + PAIR * lax.axis_index("view")
     offs = [offsets[at + i] for i in range(PAIR)]
     ch_lane = iota((CHANNELS, LANES), 1)
@@ -407,7 +410,7 @@
 
     def mask_of(view, w):
         lo = (w % 2) * LANES
-        return valid[w // 2, view : view + 1, lo : lo + LANES].astype(F32)
+        return valid[w // 2, view : view + 1, lo : lo + LANES]
 
     for i in range(PAIR):
 
@@ -544,7 +547,9 @@
     width = n * BLOCK
     own = features.reshape(devices, PAIR, CHANNELS, BLOCK)
     blocks = lax.all_to_all(own, ("cols", "view"), split_axis=0, concat_axis=0, tiled=True)
-    valid = lax.all_gather(valid_cols, "cols", axis=0)
+    near = [valid_cols]
+    for k in range(1, n):
+        near.append(lax.ppermute(valid_cols, "cols", [(c, c ^ k) for c in range(n)]))
     consts = call(
         constants_kernel,
         [((LANES, LANES), BF), ((DISP, 2 * LANES), BF), ((3 * KEYS, LANES), BF), ((LANES, width), BF)],
@@ -554,13 +559,14 @@
         lines_kernel,
         [((PAIR, width), F32)],
         [
+            pltpu.VMEM((n,) + valid_cols.shape, F32),
             pltpu.VMEM((LINE_RUN * LANES, LANES), BF),
             pltpu.VMEM((LINE_RUN * LANES, 2 * LANES), BF),
             pltpu.VMEM((LINE_RUN, DISP, LANES), F32),
             pltpu.VMEM((LINE_RUN, DISP, LANES), F32),
             pltpu.VMEM((LINE_RUN, 3 * KEYS, LANES), F32),
         ],
-        1, (offsets, blocks, valid, *consts), 1_000_000_000,
+        1, (offsets, blocks, *consts, *near), 1_000_000_000,
     )
     return lax.all_gather(rows, "view", axis=0, tiled=True)[None]
 

time: 34.4 us -> 29.4 us (0.85)
  blocking collectives: 21.6 us -> 1.81 us
  waiting for transfers between devices: 0.01 us -> 10.8 us
  starting transfers between devices: 6.46 us -> 10.9 us
  local copies, waits for them, and re-layouts: 1.69 us -> 1.28 us
    all_gather x1 -> x0, blocking collectives: 19.8 us -> none  [lines_plan(): valid = lax.all_gather(valid_cols, 'cols', axis=0)]
    ppermute x0 -> x3, waiting for transfers between devices: none -> 10.8 us  [lines_plan(): lax.ppermute(valid_cols, 'cols', [(c, c ^ k) for c in range(n)])]
    ppermute x0 -> x3, starting transfers between devices: none -> 4.45 us  [lines_plan(): lax.ppermute(valid_cols, 'cols', [(c, c ^ k) for c in range(n)])]
    unnamed x6, local copies, waits for them, and re-layouts: 1.07 us -> 0.66 us
  transfers between devices with their start and end apart: 1 -> 4, of which waited for: 0 -> 1; matrix products, arithmetic and copies ran while one was open for 0% -> 0% of each run, Pallas kernels for 1% -> 1%
where the time goes in v6:
time: 29.4 us; the launch traced here: 29.2 us
  starting transfers between devices  10.9 us (37%)
  waiting for transfers between devices  10.8 us (37%)
  Pallas kernels  4.33 us (15%)
  blocking collectives  1.81 us (6%)
  local copies, waits for them, and re-layouts  1.28 us (4%)
    ppermute x3, waiting for transfers between devices, lines_plan(): lax.ppermute(valid_cols, 'cols', [(c, c ^ k) for c in range(n)])  10.8 us
    all_to_all x1, starting transfers between devices, lines_plan(): lax.all_to_all(own, ('cols', 'view'), split_axis=0, concat_axis=0, tiled=...  6.46 us
    ppermute x3, starting transfers between devices, lines_plan(): lax.ppermute(valid_cols, 'cols', [(c, c ^ k) for c in range(n)])  4.45 us
    pallas_call x2, Pallas kernels, call(): pl.pallas_call(kernel, out_shape=[jax.ShapeDtypeStruct(shape, dtype) for...  4.33 us
    all_gather x1, blocking collectives, lines_plan(): return lax.all_gather(rows, 'view', axis=0, tiled=True)[None]  1.81 us
    unnamed x6, local copies, waits for them, and re-layouts  0.66 us
    broadcast_in_dim x1, local copies, waits for them, and re-layouts, lines_plan(): return lax.all_gather(rows, 'view', axis=0, tiled=True)[None]  0.63 us
  transfers between devices with their start and end apart: 4, of which 1 were waited for; matrix products, arithmetic and copies ran while one was open for 0% of the time, Pallas kernels for 1%

profile of v6, /device:TPU:0, one launch (start us, length us, event | category | flops | bytes accessed | tf_op | source)
XLA Modules:
  0.0 29.2 jit_solution(4397204722436088086)
XLA Ops:
  0.0 0.0 copy-start.1
  0.0 0.0 copy-start
  0.0 6.5 %all-to-all-start = ((bf16[8,2,64,256]{3,2,1,0:T(8,128)(2,1)}), bf16[8,2,64,256]{3,2,1,0:T(8,128)(2,1)S(1)}, u32[]{:S(2)}, u32[]{:S(2)}) async-start(bf16[8,2,64,256]{3,2,1,0:T(8,128)(2,1)} %bitcast.3), calls=%async_computation | async-start | bytes 1048576 | tf_op jit(solution)/shard_map/all_to_all | solution.py:549
  6.5 0.0 copy-done.1
  6.5 2.9 %collective-permute-start.1 = (s32[2,256]{1,0:T(2,128)S(1)}, s32[2,256]{1,0:T(2,128)S(1)}, u32[]{:S(2)}, u32[]{:S(2)}) collective-permute-start(s32[2,256]{1,0:T(2,128)S(1)} %copy-done.1), channel_id=1, source_target_pairs={{0,8},{4,12},{8,0},{12,4},{1,9},{5,13},{9,1},{13,5},{2,10},{6,14},... | collective-permute-start | bytes 6152 | tf_op jit(solution)/shard_map/ppermute | solution.py:552
  9.4 1.5 %collective-permute-start = (s32[2,256]{1,0:T(2,128)S(1)}, s32[2,256]{1,0:T(2,128)S(1)}, u32[]{:S(2)}, u32[]{:S(2)}) collective-permute-start(s32[2,256]{1,0:T(2,128)S(1)} %copy-done.1), channel_id=1, source_target_pairs={{0,4},{4,0},{8,12},{12,8},{1,5},{5,1},{9,13},{13,9},{2,6},{6,2},{1... | collective-permute-start | bytes 6152 | tf_op jit(solution)/shard_map/ppermute | solution.py:552
  10.9 0.1 collective-permute-start.2
  10.9 0.0 copy-done
  10.9 0.3 shard_map.46
  11.2 10.8 %collective-permute-done.1.rest_2_ = s32[2,256]{1,0:T(2,128)S(1)} collective-permute-done((s32[2,256]{1,0:T(2,128)S(1)}, s32[2,256]{1,0:T(2,128)S(1)}, u32[]{:S(2)}, u32[]{:S(2)}) %collective-permute-start.1) | collective-permute-done | bytes 2080 | tf_op jit(solution)/shard_map/ppermute | solution.py:552
  22.0 0.0 collective-permute-done.rest_1_
  22.0 0.0 collective-permute-done.2.rest_3_
  22.0 0.0 all-to-all-done.blocks
  22.0 0.0 copy-start.2
  22.0 0.6 %copy-done.2 = s32[16]{0:T(128)S(1)} copy-done((s32[16]{0:T(128)S(1)}, s32[16]{0:T(128)}, u32[]{:S(2)}) %copy-start.2) | copy-done | bytes 88
  22.6 4.1 %shard_map.47 = f32[2,1024]{1,0:T(2,128)S(1)} custom-call(s32[16]{0:T(128)S(1)} %copy-done.2, bf16[8,2,64,256]{3,2,1,0:T(8,128)(2,1)S(1)} %all-to-all-done.blocks, bf16[128,128]{1,0:T(8,128)(2,1)S(1)} %get-tuple-element.9.order, bf16[192,256]{1,0:T(8,128)(2,1)S(1)} %get-tuple-element.10.flip, bf16[120,128]{1,0:T(8,128)(2,1)S(1)} %get-tuple-element.11.guide, ...), custom_call_target="tpu_custom_call" | custom-call | flops 1000000000 | bytes 1000000 | tf_op jit(solution)/shard_map/pallas_call | solution.py:50
  26.7 1.8 %all-gather = f32[2,2,1024]{2,1,0:T(2,128)S(1)} all-gather(f32[1,2,1024]{2,1,0:T(2,128)S(1)} %bitcast.2), channel_id=1, replica_groups=mesh['tiles'=2,'cols'=4,'lines'=2,'view'=2] {'view'}, dimensions={0}, use_global_device_ids=true | all-gather | bytes 24576 | tf_op jit(solution)/shard_map/all_gather | solution.py:571
  28.5 0.6 %broadcast_in_dim.3 = f32[1,4,1024]{2,1,0:T(4,128)} reshape(f32[2,2,1024]{2,1,0:T(2,128)S(1)} %all-gather) | data formatting | bytes 32768 | tf_op jit(solution)/shard_map/broadcast_in_dim | solution.py:571
Async XLA Ops:
  0.0 6.5 %copy-start.1 = (s32[2,256]{1,0:T(2,128)S(1)}, s32[2,256]{1,0:T(2,128)}, u32[]{:S(2)}) copy-start(s32[2,256]{1,0:T(2,128)} %rest_0_.1) | copy-start | bytes 6148
  0.0 10.9 %copy-start = (bf16[64,108]{1,0:T(8,128)(2,1)S(1)}, bf16[64,108]{1,0:T(8,128)(2,1)}, u32[]{:S(2)}) copy-start(bf16[64,108]{1,0:T(8,128)(2,1)} %guide.1) | copy-start | bytes 41476
  0.0 22.0 %all-to-all-start = ((bf16[8,2,64,256]{3,2,1,0:T(8,128)(2,1)}), bf16[8,2,64,256]{3,2,1,0:T(8,128)(2,1)S(1)}, u32[]{:S(2)}, u32[]{:S(2)}) async-start(bf16[8,2,64,256]{3,2,1,0:T(8,128)(2,1)} %bitcast.3), calls=%async_computation | async-start | bytes 1048576 | tf_op jit(solution)/shard_map/all_to_all | solution.py:549
  6.5 15.5 %collective-permute-start.1 = (s32[2,256]{1,0:T(2,128)S(1)}, s32[2,256]{1,0:T(2,128)S(1)}, u32[]{:S(2)}, u32[]{:S(2)}) collective-permute-start(s32[2,256]{1,0:T(2,128)S(1)} %copy-done.1), channel_id=1, source_target_pairs={{0,8},{4,12},{8,0},{12,4},{1,9},{5,13},{9,1},{13,5},{2,10},{6,14},... | collective-permute-start | bytes 6152 | tf_op jit(solution)/shard_map/ppermute | solution.py:552
  9.4 12.6 %collective-permute-start = (s32[2,256]{1,0:T(2,128)S(1)}, s32[2,256]{1,0:T(2,128)S(1)}, u32[]{:S(2)}, u32[]{:S(2)}) collective-permute-start(s32[2,256]{1,0:T(2,128)S(1)} %copy-done.1), channel_id=1, source_target_pairs={{0,4},{4,0},{8,12},{12,8},{1,5},{5,1},{9,13},{13,9},{2,6},{6,2},{1... | collective-permute-start | bytes 6152 | tf_op jit(solution)/shard_map/ppermute | solution.py:552
  10.9 11.1 %collective-permute-start.2 = (s32[2,256]{1,0:T(2,128)S(1)}, s32[2,256]{1,0:T(2,128)S(1)}, u32[]{:S(2)}, u32[]{:S(2)}) collective-permute-start(s32[2,256]{1,0:T(2,128)S(1)} %copy-done.1), channel_id=1, source_target_pairs={{0,12},{4,8},{8,4},{12,0},{1,13},{5,9},{9,5},{13,1},{2,14},{6,10},... | collective-permute-start | bytes 6152 | tf_op jit(solution)/shard_map/ppermute | solution.py:552
  22.0 0.7 %copy-start.2 = (s32[16]{0:T(128)S(1)}, s32[16]{0:T(128)}, u32[]{:S(2)}) copy-start(s32[16]{0:T(128)} %offsets.1) | copy-start | bytes 196

commit v7 on v5

--- a/solution.py
+++ b/solution.py
@@ -44,16 +44,16 @@
     return lax.dot_general(a, b, (((1,), (1,)), ((), ())), preferred_element_type=F32)
 
 
-def call(kernel, outs, scratch, smem, args, flops=0, space=pltpu.VMEM):
+def call(kernel, outs, scratch, smem, args, flops=0, space=pltpu.VMEM, limit=24, to=None):
     specs = [pl.BlockSpec(memory_space=pltpu.SMEM)] * smem
     specs += [pl.BlockSpec(memory_space=space)] * (len(args) - smem)
     return pl.pallas_call(
         kernel,
         out_shape=[jax.ShapeDtypeStruct(shape, dtype) for shape, dtype in outs],
         in_specs=specs,
-        out_specs=[pl.BlockSpec(memory_space=pltpu.VMEM)] * len(outs),
+        out_specs=[pl.BlockSpec(memory_space=to or space)] * len(outs),
         scratch_shapes=scratch,
-        compiler_params=pltpu.CompilerParams(vmem_limit_bytes=24 * 1024 * 1024),
+        compiler_params=pltpu.CompilerParams(vmem_limit_bytes=limit * 1024 * 1024),
         cost_estimate=pl.CostEstimate(flops=flops, bytes_accessed=1_000_000, transcendentals=0),
     )(*args)
 
@@ -346,7 +346,7 @@
         prefetch_kernel,
         [(own.shape, BF), (valid_cols.shape, F32), ((SPAN, WIDE), BF), ((DISP, 2 * LANES), BF), ((3 * KEYS, LANES), BF)],
         [pltpu.VMEM(valid_cols.shape, jnp.int32), pltpu.VMEM(guide_weight.shape, BF), pltpu.SemaphoreType.DMA((3,))],
-        0, (own, valid_cols, guide_weight), 100_000_000, pl.ANY,
+        0, (own, valid_cols, guide_weight), 100_000_000, pl.ANY, 24, pltpu.VMEM,
     )
     first, second, ref_own = call(
         payload_kernel,
@@ -380,7 +380,39 @@
 LINE_PARTS = LANES // PAIR
 
 
-def constants_kernel(guide, order, flip, guide_out, spread):
+MASKS = 8
+
+
+def pack_kernel(keys, own, valid, *rest):
+    outs, (valid_in, masks_in, sems) = rest[-3 - len(keys) : -3], rest[-3:]
+    me = 2 * lax.axis_index("cols") + lax.axis_index("view")
+    rows = PAIR * CHANNELS
+    masked = [out for out in outs if out.shape[0] > rows]
+    copies = []
+    if masked:
+        masks = pltpu.make_async_copy(valid, valid_in, sems.at[len(keys)])
+        masks.start()
+    for i, (key, out) in enumerate(zip(keys, outs)):
+        dest = out if out.shape[0] == rows else out.at[pl.ds(0, rows)]
+        copies.append(pltpu.make_async_copy(own.at[me ^ key], dest, sems.at[i]))
+        copies[-1].start()
+    if masked:
+        masks.wait()
+        masks = valid_in[...].astype(F32)
+        masks_in[...] = jnp.where(
+            iota((MASKS, BLOCK), 0) < MASKS // 2, masks[0:1, :], masks[1:2, :]
+        ).astype(BF)
+        for i, out in enumerate(masked):
+            sem = sems.at[len(keys) + 1 + i]
+            copies.append(pltpu.make_async_copy(masks_in, out.at[pl.ds(rows, MASKS)], sem))
+            copies[-1].start()
+    for copy in copies:
+        copy.wait()
+
+
+def constants_kernel(offsets, guide, own, valid, order, flip, guide_out, spread, own_out, masks):
+    own_out[...] = own[...]
+    masks[...] = valid[...].astype(F32)
     row = iota((LANES, LANES), 0)
     from_lane = LANES - 1 - LINE_RUN * (row & 7) - (row >> 3)
     order[...] = jnp.where(iota((LANES, LANES), 1) == from_lane, 1.0, 0.0).astype(BF)
@@ -393,11 +425,21 @@
 
 
 def lines_kernel(
-    offsets, blocks, valid, order, flip, guide, spread, out, gate_rows, cost_rows, vol, done, wts
+    offsets, order, flip, guide, spread, *rest
 ):
-    tiles = blocks.shape[0]
+    pieces, (out, blocks, valid, gate_rows, cost_rows, vol, done, wts) = rest[:-8], rest[-8:]
+    near, pieces = pieces[1], (pieces[0],) + pieces[2:]
+    tiles = len(pieces)
     width = tiles * LANES
-    at = lax.axis_index("cols") * (PAIR * offsets.shape[0] // tiles) + PAIR * lax.axis_index("view")
+    me = 2 * lax.axis_index("cols") + lax.axis_index("view")
+    rows = PAIR * CHANNELS
+    for key, piece in enumerate(pieces):
+        blocks[me ^ key] = piece[:rows, :]
+        if piece.shape[0] > rows:
+            masks = piece[rows:, :].astype(F32)
+            valid[(me ^ key) // 2] = jnp.concatenate([masks[0:1], masks[MASKS // 2 : MASKS // 2 + 1]], axis=0)
+    valid[me // 2] = near[...]
+    at = PAIR * me
     offs = [offsets[at + i] for i in range(PAIR)]
     ch_lane = iota((CHANNELS, LANES), 1)
     diagonal = iota((8, LANES), 1) - LINE_RUN * iota((8, LANES), 0)
@@ -407,13 +449,13 @@
 
     def mask_of(view, w):
         lo = (w % 2) * LANES
-        return valid[w // 2, view : view + 1, lo : lo + LANES].astype(F32)
+        return valid[w // 2, view : view + 1, lo : lo + LANES]
 
     for i in range(PAIR):
 
         def tile_of(view, w):
             lo = (w % 2) * LANES
-            return blocks[2 * (w // 2) + view, i, :, lo : lo + LANES]
+            return blocks[2 * (w // 2) + view, i * CHANNELS : (i + 1) * CHANNELS, lo : lo + LANES]
 
         off = offs[i]
         rolled = [pltpu.roll(tile_of(1, w).astype(F32) * mask_of(1, w), off, 1) for w in range(tiles)]
@@ -542,25 +584,46 @@
     n = lax.axis_size("cols")
     devices = 2 * n
     width = n * BLOCK
-    own = features.reshape(devices, PAIR, CHANNELS, BLOCK)
-    blocks = lax.all_to_all(own, ("cols", "view"), split_axis=0, concat_axis=0, tiled=True)
-    valid = lax.all_gather(valid_cols, "cols", axis=0)
+    rows = PAIR * CHANNELS
+    own = features.reshape(devices, rows, BLOCK)
+    pieces = [None] * devices
+    gone = ()
+    same = tuple(range(n, devices, 2))
+    for keys in (same, tuple(key for key in reversed(range(devices)) if key not in same)):
+        gone = call(
+            functools.partial(pack_kernel, keys),
+            [((rows + (MASKS if key % 2 and key > 1 else 0), BLOCK), BF) for key in keys],
+            [
+                pltpu.VMEM(valid_cols.shape, jnp.int32),
+                pltpu.VMEM((MASKS, BLOCK), BF),
+                pltpu.SemaphoreType.DMA((2 * devices,)),
+            ],
+            0, (own, valid_cols, *gone[:1]), 1_000_000, pl.ANY, 60,
+        )
+        for key, piece in zip(keys, gone):
+            moves = [(i, i ^ key) for i in range(devices)]
+            pieces[key] = lax.ppermute(piece, ("cols", "view"), moves) if key else piece
     consts = call(
         constants_kernel,
-        [((LANES, LANES), BF), ((DISP, 2 * LANES), BF), ((3 * KEYS, LANES), BF), ((LANES, width), BF)],
-        [], 0, (guide_weight,), 1_000_000,
+        [
+            ((LANES, LANES), BF), ((DISP, 2 * LANES), BF), ((3 * KEYS, LANES), BF), ((LANES, width), BF),
+            ((rows, BLOCK), BF), (valid_cols.shape, F32),
+        ],
+        [], 1, (offsets, guide_weight, pieces[0], valid_cols), 1_000_000,
     )
     (rows,) = call(
         lines_kernel,
         [((PAIR, width), F32)],
         [
+            pltpu.VMEM((devices, rows, BLOCK), BF),
+            pltpu.VMEM((n,) + valid_cols.shape, F32),
             pltpu.VMEM((LINE_RUN * LANES, LANES), BF),
             pltpu.VMEM((LINE_RUN * LANES, 2 * LANES), BF),
             pltpu.VMEM((LINE_RUN, DISP, LANES), F32),
             pltpu.VMEM((LINE_RUN, DISP, LANES), F32),
             pltpu.VMEM((LINE_RUN, 3 * KEYS, LANES), F32),
         ],
-        1, (offsets, blocks, valid, *consts), 1_000_000_000,
+        1, (offsets, *consts, *pieces[1:]), 1_000_000_000,
     )
     return lax.all_gather(rows, "view", axis=0, tiled=True)[None]
 

time: 34.4 us -> 40.7 us (1.18)
  blocking collectives: 21.6 us -> 1.81 us
  Pallas kernels: 4.29 us -> 23.3 us
  waiting for transfers between devices: 0.01 us -> 3.77 us
  starting transfers between devices: 6.46 us -> 10 us
    all_gather x1 -> x0, blocking collectives: 19.8 us -> none  [lines_plan(): valid = lax.all_gather(valid_cols, 'cols', axis=0)]
    pallas_call x2 -> x4, Pallas kernels: 4.29 us -> 23.3 us  [call(): pl.pallas_call(kernel, out_shape=[jax.ShapeDtypeStruct(shape, dtype) for...]
    ppermute x0 -> x7, starting transfers between devices: none -> 10 us  [lines_plan(): pieces[key] = lax.ppermute(piece, ('cols', 'view'), moves) if key else piece]
    all_to_all x1 -> x0, starting transfers between devices: 6.46 us -> none  [lines_plan(): lax.all_to_all(own, ('cols', 'view'), split_axis=0, concat_axis=0, tiled=...]
    ppermute x0 -> x7, waiting for transfers between devices: none -> 3.77 us  [lines_plan(): pieces[key] = lax.ppermute(piece, ('cols', 'view'), moves) if key else piece]
    unnamed x6 -> x8, local copies, waits for them, and re-layouts: 1.07 us -> 0.92 us
  transfers between devices with their start and end apart: 1 -> 7, of which waited for: 0 -> 1; matrix products, arithmetic and copies ran while one was open for 0% -> 0% of each run, Pallas kernels for 1% -> 34%
where the time goes in v7:
time: 40.7 us; the launch traced here: 40.5 us
  Pallas kernels  23.3 us (57%)
  starting transfers between devices  10 us (25%)
  waiting for transfers between devices  3.77 us (9%)
  blocking collectives  1.81 us (4%)
  local copies, waits for them, and re-layouts  1.54 us (4%)
    pallas_call x4, Pallas kernels, call(): pl.pallas_call(kernel, out_shape=[jax.ShapeDtypeStruct(shape, dtype) for...  23.3 us
    ppermute x7, starting transfers between devices, lines_plan(): pieces[key] = lax.ppermute(piece, ('cols', 'view'), moves) if key else piece  10 us
    ppermute x7, waiting for transfers between devices, lines_plan(): pieces[key] = lax.ppermute(piece, ('cols', 'view'), moves) if key else piece  3.77 us
    all_gather x1, blocking collectives, lines_plan(): return lax.all_gather(rows, 'view', axis=0, tiled=True)[None]  1.81 us
    unnamed x8, local copies, waits for them, and re-layouts  0.92 us
  transfers between devices with their start and end apart: 7, of which 1 were waited for; matrix products, arithmetic and copies ran while one was open for 0% of the time, Pallas kernels for 34%

profile of v7, /device:TPU:0, one launch (start us, length us, event | category | flops | bytes accessed | tf_op | source)
XLA Modules:
  0.0 40.5 jit_solution(13794257104862115377)
XLA Ops:
  0.0 5.2 %shard_map.46 = (bf16[128,256]{1,0:T(8,128)(2,1)}, bf16[128,256]{1,0:T(8,128)(2,1)}) custom-call(bf16[8,128,256]{2,1,0:T(8,128)(2,1)} %bitcast.3, s32[2,256]{1,0:T(2,128)} %valid.5), custom_call_target="tpu_custom_call" | custom-call | flops 1000000 | bytes 1000000 | tf_op jit(solution)/shard_map/pallas_call | solution.py:50
  5.2 5.1 %collective-permute-start.5 = (bf16[128,256]{1,0:T(8,128)(2,1)}, bf16[128,256]{1,0:T(8,128)(2,1)S(1)}, u32[]{:S(2)}, u32[]{:S(2)}) collective-permute-start(bf16[128,256]{1,0:T(8,128)(2,1)} %get-tuple-element.31), channel_id=1, source_target_pairs={{0,12},{1,13},{4,8},{5,9},{8,4},{9,5},{12,0},{13,1},{2,14},{3,15},... | collective-permute-start | bytes 196616 | tf_op jit(solution)/shard_map/ppermute | solution.py:605
  10.3 0.0 collective-permute-start.3
  10.3 13.2 %shard_map.47 = (bf16[136,256]{1,0:T(8,128)(2,1)}, bf16[136,256]{1,0:T(8,128)(2,1)}, bf16[136,256]{1,0:T(8,128)(2,1)}, bf16[128,256]{1,0:T(8,128)(2,1)}, bf16[12...) custom-call(bf16[8,128,256]{2,1,0:T(8,128)(2,1)} %bitcast.4, s32[2,256]{1,0:T(2,128)} %valid.5, ...), custom_call_target="tpu_custom_call" | custom-call | flops 1000000 | bytes 1000000 | tf_op jit(solution)/shard_map/pallas_call | solution.py:50
  23.5 0.1 collective-permute-start.2
  23.6 2.2 %collective-permute-start.4 = (bf16[136,256]{1,0:T(8,128)(2,1)}, bf16[136,256]{1,0:T(8,128)(2,1)S(1)}, u32[]{:S(2)}, u32[]{:S(2)}) collective-permute-start(bf16[136,256]{1,0:T(8,128)(2,1)} %get-tuple-element.30), channel_id=1, source_target_pairs={{0,9},{1,8},{4,13},{5,12},{8,1},{9,0},{12,5},{13,4},{2,11},{3,10},... | collective-permute-start | bytes 208904 | tf_op jit(solution)/shard_map/ppermute | solution.py:605
  25.8 1.9 %collective-permute-start.6 = (bf16[136,256]{1,0:T(8,128)(2,1)}, bf16[136,256]{1,0:T(8,128)(2,1)S(1)}, u32[]{:S(2)}, u32[]{:S(2)}) collective-permute-start(bf16[136,256]{1,0:T(8,128)(2,1)} %get-tuple-element.32), channel_id=1, source_target_pairs={{0,13},{1,12},{4,9},{5,8},{8,5},{9,4},{12,1},{13,0},{2,15},{3,14},... | collective-permute-start | bytes 208904 | tf_op jit(solution)/shard_map/ppermute | solution.py:605
  27.7 0.0 collective-permute-done.5.rest_7_
  27.7 0.1 collective-permute-start
  27.8 0.0 collective-permute-done.3.rest_5_
  27.8 0.6 %collective-permute-start.1 = (bf16[128,256]{1,0:T(8,128)(2,1)}, bf16[128,256]{1,0:T(8,128)(2,1)S(1)}, u32[]{:S(2)}, u32[]{:S(2)}) collective-permute-start(bf16[128,256]{1,0:T(8,128)(2,1)} %get-tuple-element.28), channel_id=1, source_target_pairs={{0,4},{1,5},{4,0},{5,1},{8,12},{9,13},{12,8},{13,9},{2,6},{3,7},{6... | collective-permute-start | bytes 196616 | tf_op jit(solution)/shard_map/ppermute | solution.py:605
  28.4 0.0 copy-done.2
  28.4 0.0 copy-done.1
  28.4 0.1 copy-done.3
  28.5 0.8 %copy-done = bf16[128,256]{1,0:T(8,128)(2,1)S(1)} copy-done((bf16[128,256]{1,0:T(8,128)(2,1)S(1)}, bf16[128,256]{1,0:T(8,128)(2,1)}, u32[]{:S(2)}) %copy-start) | copy-done | bytes 65560
  29.3 0.8 %shard_map.48 = (bf16[128,128]{1,0:T(8,128)(2,1)S(1)}, bf16[192,256]{1,0:T(8,128)(2,1)S(1)}, bf16[120,128]{1,0:T(8,128)(2,1)S(1)}, bf16[128,1024]{1,0:T(8,128)(2...) custom-call(s32[16]{0:T(128)S(1)} %copy-done.3, bf16[64,108]{1,0:T(8,128)(2,1)S(1)} %copy-done.2, ...), custom_call_target="tpu_custom_call" | custom-call | flops 1000000 | bytes 1000000 | tf_op jit(solution)/shard_map/pallas_call | solution.py:50
  30.1 0.0 collective-permute-done.rest_2_
  30.1 3.8 %collective-permute-done.1.rest_3_ = bf16[128,256]{1,0:T(8,128)(2,1)S(1)} collective-permute-done((bf16[128,256]{1,0:T(8,128)(2,1)}, bf16[128,256]{1,0:T(8,128)(2,1)S(1)}, u32[]{:S(2)}, u32[]{:S(2)}) %collective-permute-start.1) | collective-permute-done | bytes 65568 | tf_op jit(solution)/shard_map/ppermute | solution.py:605
  33.9 0.0 collective-permute-done.2.rest_4_
  33.9 0.0 collective-permute-done.4.rest_6_
  33.9 0.0 collective-permute-done.6.rest_8_
  33.9 4.1 %shard_map.49 = f32[2,1024]{1,0:T(2,128)S(1)} custom-call(s32[16]{0:T(128)S(1)} %copy-done.3, bf16[128,128]{1,0:T(8,128)(2,1)S(1)} %get-tuple-element.21.order, bf16[192,256]{1,0:T(8,128)(2,1)S(1)} %get-tuple-element.22.flip, bf16[120,128]{1,0:T(8,128)(2,1)S(1)} %get-tuple-element.23.guide, bf16[128,1024]{1,0:T(8,128)(2,1)S(1)} %get-tuple-element.24.spread, ...), custom_call_target="tpu_custom_call" | custom-call | flops 1000000000 | bytes 1000000 | tf_op jit(solution)/shard_map/pallas_call | solution.py:50
  38.0 1.8 %all-gather = f32[2,2,1024]{2,1,0:T(2,128)S(1)} all-gather(f32[1,2,1024]{2,1,0:T(2,128)S(1)} %bitcast.2), channel_id=1, replica_groups=mesh['tiles'=2,'cols'=4,'lines'=2,'view'=2] {'view'}, dimensions={0}, use_global_device_ids=true | all-gather | bytes 24576 | tf_op jit(solution)/shard_map/all_gather | solution.py:628
  39.9 0.6 %broadcast_in_dim.3 = f32[1,4,1024]{2,1,0:T(4,128)} reshape(f32[2,2,1024]{2,1,0:T(2,128)S(1)} %all-gather) | data formatting | bytes 32768 | tf_op jit(solution)/shard_map/broadcast_in_dim | solution.py:628
  (4 shorter events, 0.0 us)
Async XLA Ops:
  5.2 22.5 %collective-permute-start.5 = (bf16[128,256]{1,0:T(8,128)(2,1)}, bf16[128,256]{1,0:T(8,128)(2,1)S(1)}, u32[]{:S(2)}, u32[]{:S(2)}) collective-permute-start(bf16[128,256]{1,0:T(8,128)(2,1)} %get-tuple-element.31), channel_id=1, source_target_pairs={{0,12},{1,13},{4,8},{5,9},{8,4},{9,5},{12,0},{13,1},{2,14},{3,15},... | collective-permute-start | bytes 196616 | tf_op jit(solution)/shard_map/ppermute | solution.py:605
  10.3 17.5 %collective-permute-start.3 = (bf16[128,256]{1,0:T(8,128)(2,1)}, bf16[128,256]{1,0:T(8,128)(2,1)S(1)}, u32[]{:S(2)}, u32[]{:S(2)}) collective-permute-start(bf16[128,256]{1,0:T(8,128)(2,1)} %get-tuple-element.19.rest_0_), channel_id=1, source_target_pairs={{0,8},{1,9},{4,12},{5,13},{8,0},{9,1},{12,4},{13,5},{2,10},{3,11},... | collective-permute-start | bytes 196616 | tf_op jit(solution)/shard_map/ppermute | solution.py:605
  10.3 18.1 %copy-start.2 = (bf16[64,108]{1,0:T(8,128)(2,1)S(1)}, bf16[64,108]{1,0:T(8,128)(2,1)}, u32[]{:S(2)}) copy-start(bf16[64,108]{1,0:T(8,128)(2,1)} %guide.1) | copy-start | bytes 41476
  23.5 10.4 %collective-permute-start.2 = (bf16[136,256]{1,0:T(8,128)(2,1)}, bf16[136,256]{1,0:T(8,128)(2,1)S(1)}, u32[]{:S(2)}, u32[]{:S(2)}) collective-permute-start(bf16[136,256]{1,0:T(8,128)(2,1)} %get-tuple-element.29), channel_id=1, source_target_pairs={{0,5},{1,4},{4,1},{5,0},{8,13},{9,12},{12,9},{13,8},{2,7},{3,6},{6... | collective-permute-start | bytes 208904 | tf_op jit(solution)/shard_map/ppermute | solution.py:605
  23.6 10.3 %collective-permute-start.4 = (bf16[136,256]{1,0:T(8,128)(2,1)}, bf16[136,256]{1,0:T(8,128)(2,1)S(1)}, u32[]{:S(2)}, u32[]{:S(2)}) collective-permute-start(bf16[136,256]{1,0:T(8,128)(2,1)} %get-tuple-element.30), channel_id=1, source_target_pairs={{0,9},{1,8},{4,13},{5,12},{8,1},{9,0},{12,5},{13,4},{2,11},{3,10},... | collective-permute-start | bytes 208904 | tf_op jit(solution)/shard_map/ppermute | solution.py:605
  25.8 8.1 %collective-permute-start.6 = (bf16[136,256]{1,0:T(8,128)(2,1)}, bf16[136,256]{1,0:T(8,128)(2,1)S(1)}, u32[]{:S(2)}, u32[]{:S(2)}) collective-permute-start(bf16[136,256]{1,0:T(8,128)(2,1)} %get-tuple-element.32), channel_id=1, source_target_pairs={{0,13},{1,12},{4,9},{5,8},{8,5},{9,4},{12,1},{13,0},{2,15},{3,14},... | collective-permute-start | bytes 208904 | tf_op jit(solution)/shard_map/ppermute | solution.py:605
  27.7 0.7 %copy-start.1 = (s32[2,256]{1,0:T(2,128)S(1)}, s32[2,256]{1,0:T(2,128)}, u32[]{:S(2)}) copy-start(s32[2,256]{1,0:T(2,128)} %valid.5) | copy-start | bytes 6148
  27.7 2.5 %collective-permute-start = (bf16[128,256]{1,0:T(8,128)(2,1)}, bf16[128,256]{1,0:T(8,128)(2,1)S(1)}, u32[]{:S(2)}, u32[]{:S(2)}) collective-permute-start(bf16[128,256]{1,0:T(8,128)(2,1)} %get-tuple-element.27), channel_id=1, source_target_pairs={{0,1},{1,0},{4,5},{5,4},{8,9},{9,8},{12,13},{13,12},{2,3},{3,2},{6... | collective-permute-start | bytes 196616 | tf_op jit(solution)/shard_map/ppermute | solution.py:605
  27.8 0.7 %copy-start.3 = (s32[16]{0:T(128)S(1)}, s32[16]{0:T(128)}, u32[]{:S(2)}) copy-start(s32[16]{0:T(128)} %offsets.3) | copy-start | bytes 196
  27.8 6.1 %collective-permute-start.1 = (bf16[128,256]{1,0:T(8,128)(2,1)}, bf16[128,256]{1,0:T(8,128)(2,1)S(1)}, u32[]{:S(2)}, u32[]{:S(2)}) collective-permute-start(bf16[128,256]{1,0:T(8,128)(2,1)} %get-tuple-element.28), channel_id=1, source_target_pairs={{0,4},{1,5},{4,0},{5,1},{8,12},{9,13},{12,8},{13,9},{2,6},{3,7},{6... | collective-permute-start | bytes 196616 | tf_op jit(solution)/shard_map/ppermute | solution.py:605
  28.5 0.8 %copy-start = (bf16[128,256]{1,0:T(8,128)(2,1)S(1)}, bf16[128,256]{1,0:T(8,128)(2,1)}, u32[]{:S(2)}) copy-start(bf16[128,256]{1,0:T(8,128)(2,1)} %get-tuple-element.20.own) | copy-start | bytes 196612

commit v8 on v7

--- a/solution.py
+++ b/solution.py
@@ -384,34 +384,19 @@
 
 
 def pack_kernel(keys, own, valid, *rest):
-    outs, (valid_in, masks_in, sems) = rest[-3 - len(keys) : -3], rest[-3:]
+    outs = rest[-len(keys) :]
     me = 2 * lax.axis_index("cols") + lax.axis_index("view")
     rows = PAIR * CHANNELS
-    masked = [out for out in outs if out.shape[0] > rows]
-    copies = []
-    if masked:
-        masks = pltpu.make_async_copy(valid, valid_in, sems.at[len(keys)])
-        masks.start()
-    for i, (key, out) in enumerate(zip(keys, outs)):
-        dest = out if out.shape[0] == rows else out.at[pl.ds(0, rows)]
-        copies.append(pltpu.make_async_copy(own.at[me ^ key], dest, sems.at[i]))
-        copies[-1].start()
-    if masked:
-        masks.wait()
-        masks = valid_in[...].astype(F32)
-        masks_in[...] = jnp.where(
-            iota((MASKS, BLOCK), 0) < MASKS // 2, masks[0:1, :], masks[1:2, :]
-        ).astype(BF)
-        for i, out in enumerate(masked):
-            sem = sems.at[len(keys) + 1 + i]
-            copies.append(pltpu.make_async_copy(masks_in, out.at[pl.ds(rows, MASKS)], sem))
-            copies[-1].start()
-    for copy in copies:
-        copy.wait()
-
-
-def constants_kernel(offsets, guide, own, valid, order, flip, guide_out, spread, own_out, masks):
-    own_out[...] = own[...]
+    for key, out in zip(keys, outs):
+        out[:rows, :] = own[me ^ key]
+        if out.shape[0] > rows:
+            masks = valid[...].astype(F32)
+            out[rows:, :] = jnp.where(
+                iota((MASKS, BLOCK), 0) < MASKS // 2, masks[0:1, :], masks[1:2, :]
+            ).astype(BF)
+
+
+def constants_kernel(offsets, guide, valid, order, flip, guide_out, spread, masks):
     masks[...] = valid[...].astype(F32)
     row = iota((LANES, LANES), 0)
     from_lane = LANES - 1 - LINE_RUN * (row & 7) - (row >> 3)
@@ -428,7 +413,7 @@
     offsets, order, flip, guide, spread, *rest
 ):
     pieces, (out, blocks, valid, gate_rows, cost_rows, vol, done, wts) = rest[:-8], rest[-8:]
-    near, pieces = pieces[1], (pieces[0],) + pieces[2:]
+    near, pieces = pieces[0], pieces[1:]
     tiles = len(pieces)
     width = tiles * LANES
     me = 2 * lax.axis_index("cols") + lax.axis_index("view")
@@ -588,17 +573,17 @@
     own = features.reshape(devices, rows, BLOCK)
     pieces = [None] * devices
     gone = ()
-    same = tuple(range(n, devices, 2))
-    for keys in (same, tuple(key for key in reversed(range(devices)) if key not in same)):
+    far = range(n, devices)
+    batches = (
+        tuple(key for key in far if key % 2 == 0),
+        tuple(key for key in far if key % 2),
+        tuple(reversed(range(n))),
+    )
+    for keys in batches:
         gone = call(
             functools.partial(pack_kernel, keys),
             [((rows + (MASKS if key % 2 and key > 1 else 0), BLOCK), BF) for key in keys],
-            [
-                pltpu.VMEM(valid_cols.shape, jnp.int32),
-                pltpu.VMEM((MASKS, BLOCK), BF),
-                pltpu.SemaphoreType.DMA((2 * devices,)),
-            ],
-            0, (own, valid_cols, *gone[:1]), 1_000_000, pl.ANY, 60,
+            [], 0, (own, valid_cols, *gone[:1]), 1_000_000,
         )
         for key, piece in zip(keys, gone):
             moves = [(i, i ^ key) for i in range(devices)]
@@ -607,9 +592,9 @@
         constants_kernel,
         [
             ((LANES, LANES), BF), ((DISP, 2 * LANES), BF), ((3 * KEYS, LANES), BF), ((LANES, width), BF),
-            ((rows, BLOCK), BF), (valid_cols.shape, F32),
+            (valid_cols.shape, F32),
         ],
-        [], 1, (offsets, guide_weight, pieces[0], valid_cols), 1_000_000,
+        [], 1, (offsets, guide_weight, valid_cols), 1_000_000,
     )
     (rows,) = call(
         lines_kernel,
@@ -623,7 +608,7 @@
             pltpu.VMEM((LINE_RUN, DISP, LANES), F32),
             pltpu.VMEM((LINE_RUN, 3 * KEYS, LANES), F32),
         ],
-        1, (offsets, *consts, *pieces[1:]), 1_000_000_000,
+        1, (offsets, *consts, *pieces), 1_000_000_000,
     )
     return lax.all_gather(rows, "view", axis=0, tiled=True)[None]
 

time: 40.7 us -> 26.9 us (0.66)
  Pallas kernels: 23.3 us -> 4.98 us
  waiting for transfers between devices: 3.77 us -> 7.86 us
  local copies, waits for them, and re-layouts: 1.54 us -> 2.36 us
    pallas_call x4 -> x5, Pallas kernels: 23.3 us -> 4.98 us  [call(): pl.pallas_call(kernel, out_shape=[jax.ShapeDtypeStruct(shape, dtype) for...]
    ppermute x7, waiting for transfers between devices: 3.77 us -> 7.86 us  [lines_plan(): pieces[key] = lax.ppermute(piece, ('cols', 'view'), moves) if key else piece]
    unnamed x8 -> x10, local copies, waits for them, and re-layouts: 0.92 us -> 1.74 us
  transfers between devices with their start and end apart: 7 -> 7, of which waited for: 1 -> 2; matrix products, arithmetic and copies ran while one was open for 0% -> 0% of each run, Pallas kernels for 34% -> 3%
where the time goes in v8:
time: 26.9 us; the launch traced here: 26.7 us
  starting transfers between devices  9.67 us (36%)
  waiting for transfers between devices  7.86 us (29%)
  Pallas kernels  4.98 us (19%)
  local copies, waits for them, and re-layouts  2.36 us (9%)
  blocking collectives  1.81 us (7%)
    ppermute x7, starting transfers between devices, lines_plan(): pieces[key] = lax.ppermute(piece, ('cols', 'view'), moves) if key else piece  9.67 us
    ppermute x7, waiting for transfers between devices, lines_plan(): pieces[key] = lax.ppermute(piece, ('cols', 'view'), moves) if key else piece  7.86 us
    pallas_call x5, Pallas kernels, call(): pl.pallas_call(kernel, out_shape=[jax.ShapeDtypeStruct(shape, dtype) for...  4.98 us
    all_gather x1, blocking collectives, lines_plan(): return lax.all_gather(rows, 'view', axis=0, tiled=True)[None]  1.81 us
    unnamed x10, local copies, waits for them, and re-layouts  1.74 us
    broadcast_in_dim x1, local copies, waits for them, and re-layouts, lines_plan(): return lax.all_gather(rows, 'view', axis=0, tiled=True)[None]  0.63 us
  transfers between devices with their start and end apart: 7, of which 2 were waited for; matrix products, arithmetic and copies ran while one was open for 0% of the time, Pallas kernels for 3%

profile of v8, /device:TPU:0, one launch (start us, length us, event | category | flops | bytes accessed | tf_op | source)
XLA Modules:
  0.0 26.7 jit_solution(17710441908758974872)
XLA Ops:
  0.0 1.0 %copy-done = bf16[1,16,64,256]{3,2,1,0:T(8,128)(2,1)S(1)} copy-done((bf16[1,16,64,256]{3,2,1,0:T(8,128)(2,1)S(1)}, bf16[1,16,64,256]{3,2,1,0:T(8,128)(2,1)}, u32[]{:S(2)}) %copy-start) | copy-done | bytes 524312
  1.0 0.7 %copy-done.1 = s32[2,256]{1,0:T(2,128)S(1)} copy-done((s32[2,256]{1,0:T(2,128)S(1)}, s32[2,256]{1,0:T(2,128)}, u32[]{:S(2)}) %copy-start.1) | copy-done | bytes 2072
  1.7 5.1 %collective-permute-start.5 = (bf16[128,256]{1,0:T(8,128)(2,1)S(1)}, bf16[128,256]{1,0:T(8,128)(2,1)S(1)}, u32[]{:S(2)}, u32[]{:S(2)}) collective-permute-start(bf16[128,256]{1,0:T(8,128)(2,1)S(1)} %get-tuple-element.29), channel_id=1, source_target_pairs={{0,12},{1,13},{4,8},{5,9},{8,4},{9,5},{12,0},{13,1},{2,14},{3,15},... | collective-permute-start | bytes 196616 | tf_op jit(solution)/shard_map/ppermute | solution.py:590
  6.9 0.0 collective-permute-start.3
  6.9 0.8 %collective-permute-start.6 = (bf16[136,256]{1,0:T(8,128)(2,1)S(1)}, bf16[136,256]{1,0:T(8,128)(2,1)S(1)}, u32[]{:S(2)}, u32[]{:S(2)}) collective-permute-start(bf16[136,256]{1,0:T(8,128)(2,1)S(1)} %get-tuple-element.30), channel_id=1, source_target_pairs={{0,13},{1,12},{4,9},{5,8},{8,5},{9,4},{12,1},{13,0},{2,15},{3,14},... | collective-permute-start | bytes 208904 | tf_op jit(solution)/shard_map/ppermute | solution.py:590
  7.7 1.1 %collective-permute-start.4 = (bf16[136,256]{1,0:T(8,128)(2,1)S(1)}, bf16[136,256]{1,0:T(8,128)(2,1)S(1)}, u32[]{:S(2)}, u32[]{:S(2)}) collective-permute-start(bf16[136,256]{1,0:T(8,128)(2,1)S(1)} %get-tuple-element.24.rest_0_), channel_id=1, source_target_pairs={{0,9},{1,8},{4,13},{5,12},{8,1},{9,0},{12,5},{13,4},{2,11},{3,10},... | collective-permute-start | bytes 208904 | tf_op jit(solution)/shard_map/ppermute | solution.py:590
  8.9 0.0 copy-start.2
  8.9 1.5 %collective-permute-start.2 = (bf16[136,256]{1,0:T(8,128)(2,1)S(1)}, bf16[136,256]{1,0:T(8,128)(2,1)S(1)}, u32[]{:S(2)}, u32[]{:S(2)}) collective-permute-start(bf16[136,256]{1,0:T(8,128)(2,1)S(1)} %get-tuple-element.28), channel_id=1, source_target_pairs={{0,5},{1,4},{4,1},{5,0},{8,13},{9,12},{12,9},{13,8},{2,7},{3,6},{6... | collective-permute-start | bytes 208904 | tf_op jit(solution)/shard_map/ppermute | solution.py:590
  10.3 0.0 collective-permute-done.5.rest_7_
  10.3 1.0 %collective-permute-start = (bf16[128,256]{1,0:T(8,128)(2,1)S(1)}, bf16[128,256]{1,0:T(8,128)(2,1)S(1)}, u32[]{:S(2)}, u32[]{:S(2)}) collective-permute-start(bf16[128,256]{1,0:T(8,128)(2,1)S(1)} %get-tuple-element.26), channel_id=1, source_target_pairs={{0,1},{1,0},{4,5},{5,4},{8,9},{9,8},{12,13},{13,12},{2,3},{3,2},{6... | collective-permute-start | bytes 196616 | tf_op jit(solution)/shard_map/ppermute | solution.py:590
  11.3 4.6 %collective-permute-done.3.rest_5_ = bf16[128,256]{1,0:T(8,128)(2,1)S(1)} collective-permute-done((bf16[128,256]{1,0:T(8,128)(2,1)S(1)}, bf16[128,256]{1,0:T(8,128)(2,1)S(1)}, u32[]{:S(2)}, u32[]{:S(2)}) %collective-permute-start.3) | collective-permute-done | bytes 65568 | tf_op jit(solution)/shard_map/ppermute | solution.py:590
  15.9 0.2 collective-permute-start.1
  16.1 0.0 copy-done.3
  16.1 0.0 copy-done.2
  16.1 0.0 copy-done.4
  16.1 0.8 %shard_map.46 = (bf16[128,128]{1,0:T(8,128)(2,1)S(1)}, bf16[192,256]{1,0:T(8,128)(2,1)S(1)}, bf16[120,128]{1,0:T(8,128)(2,1)S(1)}, bf16[128,1024]{1,0:T(8,128)(2,1)S(1)}, f32[2,256]{1,0:T(2,128)S(1)}) custom-call(s32[16]{0:T(128)S(1)} %copy-done.4, bf16[64,108]{1,0:T(8,128)(2,1)S(1)} %copy-done.3, s32[2,256]{1,0:T(2,128)S(1)} %copy-done.2), custom_call_target="tpu_custom_call" | custom-call | flops 1000000 | bytes 1000000 | tf_op jit(solution)/shard_map/pallas_call | solution.py:50
  16.9 0.0 collective-permute-done.rest_2_
  16.9 3.2 %collective-permute-done.1.rest_3_ = bf16[128,256]{1,0:T(8,128)(2,1)S(1)} collective-permute-done((bf16[128,256]{1,0:T(8,128)(2,1)S(1)}, bf16[128,256]{1,0:T(8,128)(2,1)S(1)}, u32[]{:S(2)}, u32[]{:S(2)}) %collective-permute-start.1) | collective-permute-done | bytes 65568 | tf_op jit(solution)/shard_map/ppermute | solution.py:590
  20.2 0.0 collective-permute-done.6.rest_8_
  20.2 0.0 collective-permute-done.4.rest_6_
  20.2 0.0 collective-permute-done.2.rest_4_
  20.2 4.1 %shard_map.50 = f32[2,1024]{1,0:T(2,128)S(1)} custom-call(s32[16]{0:T(128)S(1)} %copy-done.4, bf16[128,128]{1,0:T(8,128)(2,1)S(1)} %get-tuple-element.18.order, bf16[192,256]{1,0:T(8,128)(2,1)S(1)} %get-tuple-element.19.flip, bf16[120,128]{1,0:T(8,128)(2,1)S(1)} %get-tuple-element.20.guide, bf16[128,1024]{1,0:T(8,128)(2,1)S(1)} %get-tuple-element.21.spread, ...), custom_call_target="tpu_custom_call" | custom-call | flops 1000000000 | bytes 1000000 | tf_op jit(solution)/shard_map/pallas_call | solution.py:50
  24.3 1.8 %all-gather = f32[2,2,1024]{2,1,0:T(2,128)S(1)} all-gather(f32[1,2,1024]{2,1,0:T(2,128)S(1)} %bitcast.5), channel_id=1, replica_groups=mesh['tiles'=2,'cols'=4,'lines'=2,'view'=2] {'view'}, dimensions={0}, use_global_device_ids=true | all-gather | bytes 24576 | tf_op jit(solution)/shard_map/all_gather | solution.py:613
  26.1 0.6 %broadcast_in_dim.3 = f32[1,4,1024]{2,1,0:T(4,128)} reshape(f32[2,2,1024]{2,1,0:T(2,128)S(1)} %all-gather) | data formatting | bytes 32768 | tf_op jit(solution)/shard_map/broadcast_in_dim | solution.py:613
  (7 shorter events, 0.1 us)
Async XLA Ops:
  0.0 1.0 %copy-start = (bf16[1,16,64,256]{3,2,1,0:T(8,128)(2,1)S(1)}, bf16[1,16,64,256]{3,2,1,0:T(8,128)(2,1)}, u32[]{:S(2)}) copy-start(bf16[1,16,64,256]{3,2,1,0:T(8,128)(2,1)} %param.4) | copy-start | bytes 1572868
  1.0 0.7 %copy-start.1 = (s32[2,256]{1,0:T(2,128)S(1)}, s32[2,256]{1,0:T(2,128)}, u32[]{:S(2)}) copy-start(s32[2,256]{1,0:T(2,128)} %valid.7) | copy-start | bytes 6148
  1.7 8.6 %collective-permute-start.5 = (bf16[128,256]{1,0:T(8,128)(2,1)S(1)}, bf16[128,256]{1,0:T(8,128)(2,1)S(1)}, u32[]{:S(2)}, u32[]{:S(2)}) collective-permute-start(bf16[128,256]{1,0:T(8,128)(2,1)S(1)} %get-tuple-element.29), channel_id=1, source_target_pairs={{0,12},{1,13},{4,8},{5,9},{8,4},{9,5},{12,0},{13,1},{2,14},{3,15},... | collective-permute-start | bytes 196616 | tf_op jit(solution)/shard_map/ppermute | solution.py:590
  6.9 9.0 %collective-permute-start.3 = (bf16[128,256]{1,0:T(8,128)(2,1)S(1)}, bf16[128,256]{1,0:T(8,128)(2,1)S(1)}, u32[]{:S(2)}, u32[]{:S(2)}) collective-permute-start(bf16[128,256]{1,0:T(8,128)(2,1)S(1)} %get-tuple-element.23.rest_0_), channel_id=1, source_target_pairs={{0,8},{1,9},{4,12},{5,13},{8,0},{9,1},{12,4},{13,5},{2,10},{3,11},... | collective-permute-start | bytes 196616 | tf_op jit(solution)/shard_map/ppermute | solution.py:590
  6.9 13.3 %collective-permute-start.6 = (bf16[136,256]{1,0:T(8,128)(2,1)S(1)}, bf16[136,256]{1,0:T(8,128)(2,1)S(1)}, u32[]{:S(2)}, u32[]{:S(2)}) collective-permute-start(bf16[136,256]{1,0:T(8,128)(2,1)S(1)} %get-tuple-element.30), channel_id=1, source_target_pairs={{0,13},{1,12},{4,9},{5,8},{8,5},{9,4},{12,1},{13,0},{2,15},{3,14},... | collective-permute-start | bytes 208904 | tf_op jit(solution)/shard_map/ppermute | solution.py:590
  7.7 12.4 %collective-permute-start.4 = (bf16[136,256]{1,0:T(8,128)(2,1)S(1)}, bf16[136,256]{1,0:T(8,128)(2,1)S(1)}, u32[]{:S(2)}, u32[]{:S(2)}) collective-permute-start(bf16[136,256]{1,0:T(8,128)(2,1)S(1)} %get-tuple-element.24.rest_0_), channel_id=1, source_target_pairs={{0,9},{1,8},{4,13},{5,12},{8,1},{9,0},{12,5},{13,4},{2,11},{3,10},... | collective-permute-start | bytes 208904 | tf_op jit(solution)/shard_map/ppermute | solution.py:590
  8.8 7.3 %copy-start.3 = (bf16[64,108]{1,0:T(8,128)(2,1)S(1)}, bf16[64,108]{1,0:T(8,128)(2,1)}, u32[]{:S(2)}) copy-start(bf16[64,108]{1,0:T(8,128)(2,1)} %guide.1) | copy-start | bytes 41476
  8.9 7.2 %copy-start.2 = (s32[2,256]{1,0:T(2,128)S(1)}, s32[2,256]{1,0:T(2,128)}, u32[]{:S(2)}) copy-start(s32[2,256]{1,0:T(2,128)} %valid.7) | copy-start | bytes 6148
  8.9 11.3 %collective-permute-start.2 = (bf16[136,256]{1,0:T(8,128)(2,1)S(1)}, bf16[136,256]{1,0:T(8,128)(2,1)S(1)}, u32[]{:S(2)}, u32[]{:S(2)}) collective-permute-start(bf16[136,256]{1,0:T(8,128)(2,1)S(1)} %get-tuple-element.28), channel_id=1, source_target_pairs={{0,5},{1,4},{4,1},{5,0},{8,13},{9,12},{12,9},{13,8},{2,7},{3,6},{6... | collective-permute-start | bytes 208904 | tf_op jit(solution)/shard_map/ppermute | solution.py:590
  10.3 5.8 %copy-start.4 = (s32[16]{0:T(128)S(1)}, s32[16]{0:T(128)}, u32[]{:S(2)}) copy-start(s32[16]{0:T(128)} %offsets.3) | copy-start | bytes 196
  10.3 6.6 %collective-permute-start = (bf16[128,256]{1,0:T(8,128)(2,1)S(1)}, bf16[128,256]{1,0:T(8,128)(2,1)S(1)}, u32[]{:S(2)}, u32[]{:S(2)}) collective-permute-start(bf16[128,256]{1,0:T(8,128)(2,1)S(1)} %get-tuple-element.26), channel_id=1, source_target_pairs={{0,1},{1,0},{4,5},{5,4},{8,9},{9,8},{12,13},{13,12},{2,3},{3,2},{6... | collective-permute-start | bytes 196616 | tf_op jit(solution)/shard_map/ppermute | solution.py:590
  15.9 4.3 %collective-permute-start.1 = (bf16[128,256]{1,0:T(8,128)(2,1)S(1)}, bf16[128,256]{1,0:T(8,128)(2,1)S(1)}, u32[]{:S(2)}, u32[]{:S(2)}) collective-permute-start(bf16[128,256]{1,0:T(8,128)(2,1)S(1)} %get-tuple-element.27), channel_id=1, source_target_pairs={{0,4},{1,5},{4,0},{5,1},{8,12},{9,13},{12,8},{13,9},{2,6},{3,7},{6... | collective-permute-start | bytes 196616 | tf_op jit(solution)/shard_map/ppermute | solution.py:590

commit v9 on v8

--- a/solution.py
+++ b/solution.py
@@ -383,17 +383,16 @@
 MASKS = 8
 
 
-def pack_kernel(keys, own, valid, *rest):
-    outs = rest[-len(keys) :]
+def pack_kernel(key, own, *rest):
+    out = rest[-1]
     me = 2 * lax.axis_index("cols") + lax.axis_index("view")
     rows = PAIR * CHANNELS
-    for key, out in zip(keys, outs):
-        out[:rows, :] = own[me ^ key]
-        if out.shape[0] > rows:
-            masks = valid[...].astype(F32)
-            out[rows:, :] = jnp.where(
-                iota((MASKS, BLOCK), 0) < MASKS // 2, masks[0:1, :], masks[1:2, :]
-            ).astype(BF)
+    out[:rows, :] = own[me ^ key]
+    if out.shape[0] > rows:
+        masks = rest[0][...].astype(F32)
+        out[rows:, :] = jnp.where(
+            iota((MASKS, BLOCK), 0) < MASKS // 2, masks[0:1, :], masks[1:2, :]
+        ).astype(BF)
 
 
 def constants_kernel(offsets, guide, valid, order, flip, guide_out, spread, masks):
@@ -573,21 +572,18 @@
     own = features.reshape(devices, rows, BLOCK)
     pieces = [None] * devices
     gone = ()
-    far = range(n, devices)
-    batches = (
-        tuple(key for key in far if key % 2 == 0),
-        tuple(key for key in far if key % 2),
-        tuple(reversed(range(n))),
-    )
-    for keys in batches:
-        gone = call(
-            functools.partial(pack_kernel, keys),
-            [((rows + (MASKS if key % 2 and key > 1 else 0), BLOCK), BF) for key in keys],
-            [], 0, (own, valid_cols, *gone[:1]), 1_000_000,
+    for key, after in ((6, None), (4, None), (1, None), (2, None), (7, None), (5, 1), (3, 2), (0, None)):
+        masked = key % 2 and key > 1
+        (piece,) = call(
+            functools.partial(pack_kernel, key),
+            [((rows + (MASKS if masked else 0), BLOCK), BF)],
+            [], 0,
+            (own,) + ((valid_cols,) if masked else ()) + gone + (() if after is None else (pieces[after],)),
+            1_000_000,
         )
-        for key, piece in zip(keys, gone):
-            moves = [(i, i ^ key) for i in range(devices)]
-            pieces[key] = lax.ppermute(piece, ("cols", "view"), moves) if key else piece
+        gone = (piece,)
+        moves = [(i, i ^ key) for i in range(devices)]
+        pieces[key] = lax.ppermute(piece, ("cols", "view"), moves) if key else piece
     consts = call(
         constants_kernel,
         [

time: 26.9 us -> 26.3 us (0.978)
  starting transfers between devices: 9.67 us -> 12.5 us
  waiting for transfers between devices: 7.86 us -> 5.04 us
  local copies, waits for them, and re-layouts: 2.36 us -> 1.69 us
    ppermute x7, waiting for transfers between devices: 7.86 us -> 5.04 us  [lines_plan(): pieces[key] = lax.ppermute(piece, ('cols', 'view'), moves) if key else piece]
    ppermute x7, starting transfers between devices: 9.67 us -> 12.5 us  [lines_plan(): pieces[key] = lax.ppermute(piece, ('cols', 'view'), moves) if key else piece]
    unnamed x10, local copies, waits for them, and re-layouts: 1.74 us -> 1.07 us
    pallas_call x5 -> x10, Pallas kernels: 4.98 us -> 5.01 us  [call(): pl.pallas_call(kernel, out_shape=[jax.ShapeDtypeStruct(shape, dtype) for...]
where the time goes in v9:
time: 26.3 us; the launch traced here: 26.1 us
  starting transfers between devices  12.5 us (48%)
  waiting for transfers between devices  5.04 us (19%)
  Pallas kernels  5.01 us (19%)
  blocking collectives  1.81 us (7%)
  local copies, waits for them, and re-layouts  1.69 us (6%)
    ppermute x7, starting transfers between devices, lines_plan(): pieces[key] = lax.ppermute(piece, ('cols', 'view'), moves) if key else piece  12.5 us
    ppermute x7, waiting for transfers between devices, lines_plan(): pieces[key] = lax.ppermute(piece, ('cols', 'view'), moves) if key else piece  5.04 us
    pallas_call x10, Pallas kernels, call(): pl.pallas_call(kernel, out_shape=[jax.ShapeDtypeStruct(shape, dtype) for...  5.01 us
    all_gather x1, blocking collectives, lines_plan(): return lax.all_gather(rows, 'view', axis=0, tiled=True)[None]  1.81 us
    unnamed x10, local copies, waits for them, and re-layouts  1.07 us
    broadcast_in_dim x1, local copies, waits for them, and re-layouts, lines_plan(): return lax.all_gather(rows, 'view', axis=0, tiled=True)[None]  0.63 us
  transfers between devices with their start and end apart: 7, of which 2 were waited for; matrix products, arithmetic and copies ran while one was open for 0% of the time, Pallas kernels for 3%

profile of v9, /device:TPU:0, one launch (start us, length us, event | category | flops | bytes accessed | tf_op | source)
XLA Modules:
  0.0 26.1 jit_solution(4324389194026515024)
XLA Ops:
  0.0 1.0 %copy-done = bf16[1,16,64,256]{3,2,1,0:T(8,128)(2,1)S(1)} copy-done((bf16[1,16,64,256]{3,2,1,0:T(8,128)(2,1)S(1)}, bf16[1,16,64,256]{3,2,1,0:T(8,128)(2,1)}, u32[]{:S(2)}) %copy-start) | copy-done | bytes 524312
  1.1 0.0 copy-start.1
  1.1 0.0 copy-start.2
  1.1 0.5 %collective-permute-start = (bf16[128,256]{1,0:T(8,128)(2,1)S(1)}, bf16[128,256]{1,0:T(8,128)(2,1)S(1)}, u32[]{:S(2)}, u32[]{:S(2)}) collective-permute-start(bf16[128,256]{1,0:T(8,128)(2,1)S(1)} %shard_map.49.rest_0_), channel_id=1, source_target_pairs={{0,1},{1,0},{4,5},{5,4},{8,9},{9,8},{12,13},{13,12},{2,3},{3,2},{6... | collective-permute-start | bytes 196616 | tf_op jit(solution)/shard_map/ppermute | solution.py:586
  1.6 2.7 %collective-permute-start.1 = (bf16[128,256]{1,0:T(8,128)(2,1)S(1)}, bf16[128,256]{1,0:T(8,128)(2,1)S(1)}, u32[]{:S(2)}, u32[]{:S(2)}) collective-permute-start(bf16[128,256]{1,0:T(8,128)(2,1)S(1)} %shard_map.50.rest_1_), channel_id=1, source_target_pairs={{0,4},{1,5},{4,0},{5,1},{8,12},{9,13},{12,8},{13,9},{2,6},{3,7},{6... | collective-permute-start | bytes 196616 | tf_op jit(solution)/shard_map/ppermute | solution.py:586
  4.3 0.0 copy-done.1
  4.3 2.3 %collective-permute-start.6 = (bf16[136,256]{1,0:T(8,128)(2,1)S(1)}, bf16[136,256]{1,0:T(8,128)(2,1)S(1)}, u32[]{:S(2)}, u32[]{:S(2)}) collective-permute-start(bf16[136,256]{1,0:T(8,128)(2,1)S(1)} %shard_map.51.rest_1_), channel_id=1, source_target_pairs={{0,13},{1,12},{4,9},{5,8},{8,5},{9,4},{12,1},{13,0},{2,15},{3,14},... | collective-permute-start | bytes 208904 | tf_op jit(solution)/shard_map/ppermute | solution.py:586
  6.7 0.0 collective-permute-done.rest_2_
  6.7 0.0 copy-start.3
  6.7 0.0 copy-start.4
  6.7 0.2 collective-permute-done.1.rest_2_.rest_3_
  7.0 1.1 %collective-permute-start.2 = (bf16[136,256]{1,0:T(8,128)(2,1)S(1)}, bf16[136,256]{1,0:T(8,128)(2,1)S(1)}, u32[]{:S(2)}, u32[]{:S(2)}) collective-permute-start(bf16[136,256]{1,0:T(8,128)(2,1)S(1)} %shard_map.53.rest_0_), channel_id=1, source_target_pairs={{0,5},{1,4},{4,1},{5,0},{8,13},{9,12},{12,9},{13,8},{2,7},{3,6},{6... | collective-permute-start | bytes 208904 | tf_op jit(solution)/shard_map/ppermute | solution.py:586
  8.1 3.1 %collective-permute-start.4 = (bf16[136,256]{1,0:T(8,128)(2,1)S(1)}, bf16[136,256]{1,0:T(8,128)(2,1)S(1)}, u32[]{:S(2)}, u32[]{:S(2)}) collective-permute-start(bf16[136,256]{1,0:T(8,128)(2,1)S(1)} %shard_map.52.rest_1_), channel_id=1, source_target_pairs={{0,9},{1,8},{4,13},{5,12},{8,1},{9,0},{12,5},{13,4},{2,11},{3,10},... | collective-permute-start | bytes 208904 | tf_op jit(solution)/shard_map/ppermute | solution.py:586
  11.1 0.3 %collective-permute-start.3 = (bf16[128,256]{1,0:T(8,128)(2,1)S(1)}, bf16[128,256]{1,0:T(8,128)(2,1)S(1)}, u32[]{:S(2)}, u32[]{:S(2)}) collective-permute-start(bf16[128,256]{1,0:T(8,128)(2,1)S(1)} %shard_map.48.rest_0_), channel_id=1, source_target_pairs={{0,8},{1,9},{4,12},{5,13},{8,0},{9,1},{12,4},{13,5},{2,10},{3,11},... | collective-permute-start | bytes 196616 | tf_op jit(solution)/shard_map/ppermute | solution.py:586
  11.5 2.5 %collective-permute-start.5 = (bf16[128,256]{1,0:T(8,128)(2,1)S(1)}, bf16[128,256]{1,0:T(8,128)(2,1)S(1)}, u32[]{:S(2)}, u32[]{:S(2)}) collective-permute-start(bf16[128,256]{1,0:T(8,128)(2,1)S(1)} %shard_map.47.rest_0_), channel_id=1, source_target_pairs={{0,12},{1,13},{4,8},{5,9},{8,4},{9,5},{12,0},{13,1},{2,14},{3,15},... | collective-permute-start | bytes 196616 | tf_op jit(solution)/shard_map/ppermute | solution.py:586
  13.9 0.8 %shard_map.46 = (bf16[128,128]{1,0:T(8,128)(2,1)S(1)}, bf16[192,256]{1,0:T(8,128)(2,1)S(1)}, bf16[120,128]{1,0:T(8,128)(2,1)S(1)}, bf16[128,1024]{1,0:T(8,128)(2,1)S(1)}, f32[2,256]{1,0:T(2,128)S(1)}) custom-call(s32[16]{0:T(128)S(1)} %copy-done.4, bf16[64,108]{1,0:T(8,128)(2,1)S(1)} %copy-done.3, s32[2,256]{1,0:T(2,128)S(1)} %copy-done.2), custom_call_target="tpu_custom_call" | custom-call | flops 1000000 | bytes 1000000 | tf_op jit(solution)/shard_map/pallas_call | solution.py:50
  14.8 4.8 %collective-permute-done.3.rest_5_ = bf16[128,256]{1,0:T(8,128)(2,1)S(1)} collective-permute-done((bf16[128,256]{1,0:T(8,128)(2,1)S(1)}, bf16[128,256]{1,0:T(8,128)(2,1)S(1)}, u32[]{:S(2)}, u32[]{:S(2)}) %collective-permute-start.3) | collective-permute-done | bytes 65568 | tf_op jit(solution)/shard_map/ppermute | solution.py:586
  19.5 0.0 collective-permute-done.5.rest_7_
  19.5 0.0 collective-permute-done.6.rest_8_
  19.6 0.0 collective-permute-done.2.rest_4_
  19.6 0.0 collective-permute-done.4.rest_6_
  19.6 4.1 %shard_map.55 = f32[2,1024]{1,0:T(2,128)S(1)} custom-call(s32[16]{0:T(128)S(1)} %copy-done.4, bf16[128,128]{1,0:T(8,128)(2,1)S(1)} %get-tuple-element.10.order, bf16[192,256]{1,0:T(8,128)(2,1)S(1)} %get-tuple-element.11.flip, bf16[120,128]{1,0:T(8,128)(2,1)S(1)} %get-tuple-element.12.guide, bf16[128,1024]{1,0:T(8,128)(2,1)S(1)} %get-tuple-element.13.spread, ...), custom_call_target="tpu_custom_call" | custom-call | flops 1000000000 | bytes 1000000 | tf_op jit(solution)/shard_map/pallas_call | solution.py:50
  23.7 1.8 %all-gather = f32[2,2,1024]{2,1,0:T(2,128)S(1)} all-gather(f32[1,2,1024]{2,1,0:T(2,128)S(1)} %bitcast.10), channel_id=1, replica_groups=mesh['tiles'=2,'cols'=4,'lines'=2,'view'=2] {'view'}, dimensions={0}, use_global_device_ids=true | all-gather | bytes 24576 | tf_op jit(solution)/shard_map/all_gather | solution.py:609
  25.5 0.6 %broadcast_in_dim.3 = f32[1,4,1024]{2,1,0:T(4,128)} reshape(f32[2,2,1024]{2,1,0:T(2,128)S(1)} %all-gather) | data formatting | bytes 32768 | tf_op jit(solution)/shard_map/broadcast_in_dim | solution.py:609
  (12 shorter events, 0.1 us)
Async XLA Ops:
  0.0 1.0 %copy-start = (bf16[1,16,64,256]{3,2,1,0:T(8,128)(2,1)S(1)}, bf16[1,16,64,256]{3,2,1,0:T(8,128)(2,1)}, u32[]{:S(2)}) copy-start(bf16[1,16,64,256]{3,2,1,0:T(8,128)(2,1)} %param.4) | copy-start | bytes 1572868
  1.1 3.2 %copy-start.1 = (bf16[1,16,64,256]{3,2,1,0:T(8,128)(2,1)S(1)}, bf16[1,16,64,256]{3,2,1,0:T(8,128)(2,1)}, u32[]{:S(2)}) copy-start(bf16[1,16,64,256]{3,2,1,0:T(8,128)(2,1)} %param.4) | copy-start | bytes 1572868
  1.1 3.2 %copy-start.2 = (s32[2,256]{1,0:T(2,128)S(1)}, s32[2,256]{1,0:T(2,128)}, u32[]{:S(2)}) copy-start(s32[2,256]{1,0:T(2,128)} %rest_0_.5) | copy-start | bytes 6148
  1.1 5.6 %collective-permute-start = (bf16[128,256]{1,0:T(8,128)(2,1)S(1)}, bf16[128,256]{1,0:T(8,128)(2,1)S(1)}, u32[]{:S(2)}, u32[]{:S(2)}) collective-permute-start(bf16[128,256]{1,0:T(8,128)(2,1)S(1)} %shard_map.49.rest_0_), channel_id=1, source_target_pairs={{0,1},{1,0},{4,5},{5,4},{8,9},{9,8},{12,13},{13,12},{2,3},{3,2},{6... | collective-permute-start | bytes 196616 | tf_op jit(solution)/shard_map/ppermute | solution.py:586
  1.6 5.3 %collective-permute-start.1 = (bf16[128,256]{1,0:T(8,128)(2,1)S(1)}, bf16[128,256]{1,0:T(8,128)(2,1)S(1)}, u32[]{:S(2)}, u32[]{:S(2)}) collective-permute-start(bf16[128,256]{1,0:T(8,128)(2,1)S(1)} %shard_map.50.rest_1_), channel_id=1, source_target_pairs={{0,4},{1,5},{4,0},{5,1},{8,12},{9,13},{12,8},{13,9},{2,6},{3,7},{6... | collective-permute-start | bytes 196616 | tf_op jit(solution)/shard_map/ppermute | solution.py:586
  4.3 15.2 %collective-permute-start.6 = (bf16[136,256]{1,0:T(8,128)(2,1)S(1)}, bf16[136,256]{1,0:T(8,128)(2,1)S(1)}, u32[]{:S(2)}, u32[]{:S(2)}) collective-permute-start(bf16[136,256]{1,0:T(8,128)(2,1)S(1)} %shard_map.51.rest_1_), channel_id=1, source_target_pairs={{0,13},{1,12},{4,9},{5,8},{8,5},{9,4},{12,1},{13,0},{2,15},{3,14},... | collective-permute-start | bytes 208904 | tf_op jit(solution)/shard_map/ppermute | solution.py:586
  6.7 7.2 %copy-start.3 = (bf16[64,108]{1,0:T(8,128)(2,1)S(1)}, bf16[64,108]{1,0:T(8,128)(2,1)}, u32[]{:S(2)}) copy-start(bf16[64,108]{1,0:T(8,128)(2,1)} %guide.1) | copy-start | bytes 41476
  6.7 7.2 %copy-start.4 = (s32[16]{0:T(128)S(1)}, s32[16]{0:T(128)}, u32[]{:S(2)}) copy-start(s32[16]{0:T(128)} %offsets.3) | copy-start | bytes 196
  7.0 12.6 %collective-permute-start.2 = (bf16[136,256]{1,0:T(8,128)(2,1)S(1)}, bf16[136,256]{1,0:T(8,128)(2,1)S(1)}, u32[]{:S(2)}, u32[]{:S(2)}) collective-permute-start(bf16[136,256]{1,0:T(8,128)(2,1)S(1)} %shard_map.53.rest_0_), channel_id=1, source_target_pairs={{0,5},{1,4},{4,1},{5,0},{8,13},{9,12},{12,9},{13,8},{2,7},{3,6},{6... | collective-permute-start | bytes 208904 | tf_op jit(solution)/shard_map/ppermute | solution.py:586
  8.1 11.5 %collective-permute-start.4 = (bf16[136,256]{1,0:T(8,128)(2,1)S(1)}, bf16[136,256]{1,0:T(8,128)(2,1)S(1)}, u32[]{:S(2)}, u32[]{:S(2)}) collective-permute-start(bf16[136,256]{1,0:T(8,128)(2,1)S(1)} %shard_map.52.rest_1_), channel_id=1, source_target_pairs={{0,9},{1,8},{4,13},{5,12},{8,1},{9,0},{12,5},{13,4},{2,11},{3,10},... | collective-permute-start | bytes 208904 | tf_op jit(solution)/shard_map/ppermute | solution.py:586
  11.1 8.4 %collective-permute-start.3 = (bf16[128,256]{1,0:T(8,128)(2,1)S(1)}, bf16[128,256]{1,0:T(8,128)(2,1)S(1)}, u32[]{:S(2)}, u32[]{:S(2)}) collective-permute-start(bf16[128,256]{1,0:T(8,128)(2,1)S(1)} %shard_map.48.rest_0_), channel_id=1, source_target_pairs={{0,8},{1,9},{4,12},{5,13},{8,0},{9,1},{12,4},{13,5},{2,10},{3,11},... | collective-permute-start | bytes 196616 | tf_op jit(solution)/shard_map/ppermute | solution.py:586
  11.5 8.1 %collective-permute-start.5 = (bf16[128,256]{1,0:T(8,128)(2,1)S(1)}, bf16[128,256]{1,0:T(8,128)(2,1)S(1)}, u32[]{:S(2)}, u32[]{:S(2)}) collective-permute-start(bf16[128,256]{1,0:T(8,128)(2,1)S(1)} %shard_map.47.rest_0_), channel_id=1, source_target_pairs={{0,12},{1,13},{4,8},{5,9},{8,4},{9,5},{12,0},{13,1},{2,14},{3,15},... | collective-permute-start | bytes 196616 | tf_op jit(solution)/shard_map/ppermute | solution.py:586

commit v10 on v9

--- a/solution.py
+++ b/solution.py
@@ -572,13 +572,13 @@
     own = features.reshape(devices, rows, BLOCK)
     pieces = [None] * devices
     gone = ()
-    for key, after in ((6, None), (4, None), (1, None), (2, None), (7, None), (5, 1), (3, 2), (0, None)):
+    for key in (1, 2, 6, 4, 7, 5, 3, 0):
         masked = key % 2 and key > 1
         (piece,) = call(
             functools.partial(pack_kernel, key),
             [((rows + (MASKS if masked else 0), BLOCK), BF)],
             [], 0,
-            (own,) + ((valid_cols,) if masked else ()) + gone + (() if after is None else (pieces[after],)),
+            (own,) + ((valid_cols,) if masked else ()) + gone,
             1_000_000,
         )
         gone = (piece,)

time: 26.3 us -> 22.9 us (0.87)
  starting transfers between devices: 12.5 us -> 10.1 us
  waiting for transfers between devices: 5.04 us -> 3.82 us
    ppermute x7, starting transfers between devices: 12.5 us -> 10.1 us  [lines_plan(): pieces[key] = lax.ppermute(piece, ('cols', 'view'), moves) if key else piece]
    ppermute x7, waiting for transfers between devices: 5.04 us -> 3.82 us  [lines_plan(): pieces[key] = lax.ppermute(piece, ('cols', 'view'), moves) if key else piece]
  transfers between devices with their start and end apart: 7 -> 7, of which waited for: 2 -> 2; matrix products, arithmetic and copies ran while one was open for 0% -> 0% of each run, Pallas kernels for 3% -> 4%
where the time goes in v10:
time: 22.9 us; the launch traced here: 22.6 us
  starting transfers between devices  10.1 us (44%)
  Pallas kernels  5.02 us (22%)
  waiting for transfers between devices  3.82 us (17%)
  blocking collectives  1.81 us (8%)
  local copies, waits for them, and re-layouts  1.69 us (7%)
    ppermute x7, starting transfers between devices, lines_plan(): pieces[key] = lax.ppermute(piece, ('cols', 'view'), moves) if key else piece  10.1 us
    pallas_call x10, Pallas kernels, call(): pl.pallas_call(kernel, out_shape=[jax.ShapeDtypeStruct(shape, dtype) for...  5.02 us
    ppermute x7, waiting for transfers between devices, lines_plan(): pieces[key] = lax.ppermute(piece, ('cols', 'view'), moves) if key else piece  3.82 us
    all_gather x1, blocking collectives, lines_plan(): return lax.all_gather(rows, 'view', axis=0, tiled=True)[None]  1.81 us
    unnamed x10, local copies, waits for them, and re-layouts  1.07 us
    broadcast_in_dim x1, local copies, waits for them, and re-layouts, lines_plan(): return lax.all_gather(rows, 'view', axis=0, tiled=True)[None]  0.63 us
  transfers between devices with their start and end apart: 7, of which 2 were waited for; matrix products, arithmetic and copies ran while one was open for 0% of the time, Pallas kernels for 4%

profile of v10, /device:TPU:0, one launch (start us, length us, event | category | flops | bytes accessed | tf_op | source)
XLA Modules:
  0.0 22.6 jit_solution(11487524145419242199)
XLA Ops:
  0.0 1.0 %copy-done = bf16[1,16,64,256]{3,2,1,0:T(8,128)(2,1)S(1)} copy-done((bf16[1,16,64,256]{3,2,1,0:T(8,128)(2,1)S(1)}, bf16[1,16,64,256]{3,2,1,0:T(8,128)(2,1)}, u32[]{:S(2)}) %copy-start) | copy-done | bytes 524312
  1.1 0.0 copy-start.1
  1.1 0.0 copy-start.2
  1.1 4.1 %collective-permute-start.3 = (bf16[128,256]{1,0:T(8,128)(2,1)S(1)}, bf16[128,256]{1,0:T(8,128)(2,1)S(1)}, u32[]{:S(2)}, u32[]{:S(2)}) collective-permute-start(bf16[128,256]{1,0:T(8,128)(2,1)S(1)} %shard_map.50.rest_1_), channel_id=1, source_target_pairs={{0,8},{1,9},{4,12},{5,13},{8,0},{9,1},{12,4},{13,5},{2,10},{3,11},... | collective-permute-start | bytes 196616 | tf_op jit(solution)/shard_map/ppermute | solution.py:586
  5.2 1.3 %collective-permute-start.5 = (bf16[128,256]{1,0:T(8,128)(2,1)S(1)}, bf16[128,256]{1,0:T(8,128)(2,1)S(1)}, u32[]{:S(2)}, u32[]{:S(2)}) collective-permute-start(bf16[128,256]{1,0:T(8,128)(2,1)S(1)} %shard_map.49.rest_0_), channel_id=1, source_target_pairs={{0,12},{1,13},{4,8},{5,9},{8,4},{9,5},{12,0},{13,1},{2,14},{3,15},... | collective-permute-start | bytes 196616 | tf_op jit(solution)/shard_map/ppermute | solution.py:586
  6.6 0.0 copy-done.2
  6.7 0.0 copy-start.3
  6.7 0.0 copy-start.4
  6.7 0.1 collective-permute-start.2
  6.8 2.7 %collective-permute-start.4 = (bf16[136,256]{1,0:T(8,128)(2,1)S(1)}, bf16[136,256]{1,0:T(8,128)(2,1)S(1)}, u32[]{:S(2)}, u32[]{:S(2)}) collective-permute-start(bf16[136,256]{1,0:T(8,128)(2,1)S(1)} %shard_map.52.rest_1_), channel_id=1, source_target_pairs={{0,9},{1,8},{4,13},{5,12},{8,1},{9,0},{12,5},{13,4},{2,11},{3,10},... | collective-permute-start | bytes 208904 | tf_op jit(solution)/shard_map/ppermute | solution.py:586
  9.5 0.2 %collective-permute-start.6 = (bf16[136,256]{1,0:T(8,128)(2,1)S(1)}, bf16[136,256]{1,0:T(8,128)(2,1)S(1)}, u32[]{:S(2)}, u32[]{:S(2)}) collective-permute-start(bf16[136,256]{1,0:T(8,128)(2,1)S(1)} %shard_map.51.rest_1_), channel_id=1, source_target_pairs={{0,13},{1,12},{4,9},{5,8},{8,5},{9,4},{12,1},{13,0},{2,15},{3,14},... | collective-permute-start | bytes 208904 | tf_op jit(solution)/shard_map/ppermute | solution.py:586
  9.8 0.0 collective-permute-done.3.rest_5_
  9.8 1.6 %collective-permute-start.1 = (bf16[128,256]{1,0:T(8,128)(2,1)S(1)}, bf16[128,256]{1,0:T(8,128)(2,1)S(1)}, u32[]{:S(2)}, u32[]{:S(2)}) collective-permute-start(bf16[128,256]{1,0:T(8,128)(2,1)S(1)} %shard_map.48.rest_0_), channel_id=1, source_target_pairs={{0,4},{1,5},{4,0},{5,1},{8,12},{9,13},{12,8},{13,9},{2,6},{3,7},{6... | collective-permute-start | bytes 196616 | tf_op jit(solution)/shard_map/ppermute | solution.py:586
  11.4 0.3 %collective-permute-done.5.rest_7_ = bf16[128,256]{1,0:T(8,128)(2,1)S(1)} collective-permute-done((bf16[128,256]{1,0:T(8,128)(2,1)S(1)}, bf16[128,256]{1,0:T(8,128)(2,1)S(1)}, u32[]{:S(2)}, u32[]{:S(2)}) %collective-permute-start.5) | collective-permute-done | bytes 65568 | tf_op jit(solution)/shard_map/ppermute | solution.py:586
  11.7 0.0 collective-permute-start
  11.8 0.8 %shard_map.46 = (bf16[128,128]{1,0:T(8,128)(2,1)S(1)}, bf16[192,256]{1,0:T(8,128)(2,1)S(1)}, bf16[120,128]{1,0:T(8,128)(2,1)S(1)}, bf16[128,1024]{1,0:T(8,128)(2,1)S(1)}, f32[2,256]{1,0:T(2,128)S(1)}) custom-call(s32[16]{0:T(128)S(1)} %copy-done.4, bf16[64,108]{1,0:T(8,128)(2,1)S(1)} %copy-done.3, s32[2,256]{1,0:T(2,128)S(1)} %copy-done.2), custom_call_target="tpu_custom_call" | custom-call | flops 1000000 | bytes 1000000 | tf_op jit(solution)/shard_map/pallas_call | solution.py:50
  12.6 3.5 %collective-permute-done.1.rest_3_ = bf16[128,256]{1,0:T(8,128)(2,1)S(1)} collective-permute-done((bf16[128,256]{1,0:T(8,128)(2,1)S(1)}, bf16[128,256]{1,0:T(8,128)(2,1)S(1)}, u32[]{:S(2)}, u32[]{:S(2)}) %collective-permute-start.1) | collective-permute-done | bytes 65568 | tf_op jit(solution)/shard_map/ppermute | solution.py:586
  16.0 0.0 collective-permute-done.rest_2_
  16.0 0.0 collective-permute-done.2.rest_4_
  16.1 0.0 collective-permute-done.4.rest_6_
  16.1 0.0 collective-permute-done.6.rest_8_
  16.1 4.1 %shard_map.55 = f32[2,1024]{1,0:T(2,128)S(1)} custom-call(s32[16]{0:T(128)S(1)} %copy-done.4, bf16[128,128]{1,0:T(8,128)(2,1)S(1)} %get-tuple-element.10.order, bf16[192,256]{1,0:T(8,128)(2,1)S(1)} %get-tuple-element.11.flip, bf16[120,128]{1,0:T(8,128)(2,1)S(1)} %get-tuple-element.12.guide, bf16[128,1024]{1,0:T(8,128)(2,1)S(1)} %get-tuple-element.13.spread, ...), custom_call_target="tpu_custom_call" | custom-call | flops 1000000000 | bytes 1000000 | tf_op jit(solution)/shard_map/pallas_call | solution.py:50
  20.2 1.8 %all-gather = f32[2,2,1024]{2,1,0:T(2,128)S(1)} all-gather(f32[1,2,1024]{2,1,0:T(2,128)S(1)} %bitcast.10), channel_id=1, replica_groups=mesh['tiles'=2,'cols'=4,'lines'=2,'view'=2] {'view'}, dimensions={0}, use_global_device_ids=true | all-gather | bytes 24576 | tf_op jit(solution)/shard_map/all_gather | solution.py:609
  22.0 0.6 %broadcast_in_dim.3 = f32[1,4,1024]{2,1,0:T(4,128)} reshape(f32[2,2,1024]{2,1,0:T(2,128)S(1)} %all-gather) | data formatting | bytes 32768 | tf_op jit(solution)/shard_map/broadcast_in_dim | solution.py:609
  (12 shorter events, 0.1 us)
Async XLA Ops:
  0.0 1.0 %copy-start = (bf16[1,16,64,256]{3,2,1,0:T(8,128)(2,1)S(1)}, bf16[1,16,64,256]{3,2,1,0:T(8,128)(2,1)}, u32[]{:S(2)}) copy-start(bf16[1,16,64,256]{3,2,1,0:T(8,128)(2,1)} %param.4) | copy-start | bytes 1572868
  1.1 5.5 %copy-start.1 = (bf16[1,16,64,256]{3,2,1,0:T(8,128)(2,1)S(1)}, bf16[1,16,64,256]{3,2,1,0:T(8,128)(2,1)}, u32[]{:S(2)}) copy-start(bf16[1,16,64,256]{3,2,1,0:T(8,128)(2,1)} %param.4) | copy-start | bytes 1572868
  1.1 5.5 %copy-start.2 = (s32[2,256]{1,0:T(2,128)S(1)}, s32[2,256]{1,0:T(2,128)}, u32[]{:S(2)}) copy-start(s32[2,256]{1,0:T(2,128)} %rest_0_.5) | copy-start | bytes 6148
  1.1 8.6 %collective-permute-start.3 = (bf16[128,256]{1,0:T(8,128)(2,1)S(1)}, bf16[128,256]{1,0:T(8,128)(2,1)S(1)}, u32[]{:S(2)}, u32[]{:S(2)}) collective-permute-start(bf16[128,256]{1,0:T(8,128)(2,1)S(1)} %shard_map.50.rest_1_), channel_id=1, source_target_pairs={{0,8},{1,9},{4,12},{5,13},{8,0},{9,1},{12,4},{13,5},{2,10},{3,11},... | collective-permute-start | bytes 196616 | tf_op jit(solution)/shard_map/ppermute | solution.py:586
  5.2 6.5 %collective-permute-start.5 = (bf16[128,256]{1,0:T(8,128)(2,1)S(1)}, bf16[128,256]{1,0:T(8,128)(2,1)S(1)}, u32[]{:S(2)}, u32[]{:S(2)}) collective-permute-start(bf16[128,256]{1,0:T(8,128)(2,1)S(1)} %shard_map.49.rest_0_), channel_id=1, source_target_pairs={{0,12},{1,13},{4,8},{5,9},{8,4},{9,5},{12,0},{13,1},{2,14},{3,15},... | collective-permute-start | bytes 196616 | tf_op jit(solution)/shard_map/ppermute | solution.py:586
  6.7 5.1 %copy-start.3 = (bf16[64,108]{1,0:T(8,128)(2,1)S(1)}, bf16[64,108]{1,0:T(8,128)(2,1)}, u32[]{:S(2)}) copy-start(bf16[64,108]{1,0:T(8,128)(2,1)} %guide.1) | copy-start | bytes 41476
  6.7 5.1 %copy-start.4 = (s32[16]{0:T(128)S(1)}, s32[16]{0:T(128)}, u32[]{:S(2)}) copy-start(s32[16]{0:T(128)} %offsets.3) | copy-start | bytes 196
  6.7 9.4 %collective-permute-start.2 = (bf16[136,256]{1,0:T(8,128)(2,1)S(1)}, bf16[136,256]{1,0:T(8,128)(2,1)S(1)}, u32[]{:S(2)}, u32[]{:S(2)}) collective-permute-start(bf16[136,256]{1,0:T(8,128)(2,1)S(1)} %shard_map.53.rest_0_), channel_id=1, source_target_pairs={{0,5},{1,4},{4,1},{5,0},{8,13},{9,12},{12,9},{13,8},{2,7},{3,6},{6... | collective-permute-start | bytes 208904 | tf_op jit(solution)/shard_map/ppermute | solution.py:586
  6.8 9.3 %collective-permute-start.4 = (bf16[136,256]{1,0:T(8,128)(2,1)S(1)}, bf16[136,256]{1,0:T(8,128)(2,1)S(1)}, u32[]{:S(2)}, u32[]{:S(2)}) collective-permute-start(bf16[136,256]{1,0:T(8,128)(2,1)S(1)} %shard_map.52.rest_1_), channel_id=1, source_target_pairs={{0,9},{1,8},{4,13},{5,12},{8,1},{9,0},{12,5},{13,4},{2,11},{3,10},... | collective-permute-start | bytes 208904 | tf_op jit(solution)/shard_map/ppermute | solution.py:586
  9.5 6.5 %collective-permute-start.6 = (bf16[136,256]{1,0:T(8,128)(2,1)S(1)}, bf16[136,256]{1,0:T(8,128)(2,1)S(1)}, u32[]{:S(2)}, u32[]{:S(2)}) collective-permute-start(bf16[136,256]{1,0:T(8,128)(2,1)S(1)} %shard_map.51.rest_1_), channel_id=1, source_target_pairs={{0,13},{1,12},{4,9},{5,8},{8,5},{9,4},{12,1},{13,0},{2,15},{3,14},... | collective-permute-start | bytes 208904 | tf_op jit(solution)/shard_map/ppermute | solution.py:586
  9.8 6.3 %collective-permute-start.1 = (bf16[128,256]{1,0:T(8,128)(2,1)S(1)}, bf16[128,256]{1,0:T(8,128)(2,1)S(1)}, u32[]{:S(2)}, u32[]{:S(2)}) collective-permute-start(bf16[128,256]{1,0:T(8,128)(2,1)S(1)} %shard_map.48.rest_0_), channel_id=1, source_target_pairs={{0,4},{1,5},{4,0},{5,1},{8,12},{9,13},{12,8},{13,9},{2,6},{3,7},{6... | collective-permute-start | bytes 196616 | tf_op jit(solution)/shard_map/ppermute | solution.py:586
  11.7 4.3 %collective-permute-start = (bf16[128,256]{1,0:T(8,128)(2,1)S(1)}, bf16[128,256]{1,0:T(8,128)(2,1)S(1)}, u32[]{:S(2)}, u32[]{:S(2)}) collective-permute-start(bf16[128,256]{1,0:T(8,128)(2,1)S(1)} %shard_map.47.rest_0_), channel_id=1, source_target_pairs={{0,1},{1,0},{4,5},{5,4},{8,9},{9,8},{12,13},{13,12},{2,3},{3,2},{6... | collective-permute-start | bytes 196616 | tf_op jit(solution)/shard_map/ppermute | solution.py:586

commit v11 on v10

--- a/solution.py
+++ b/solution.py
@@ -381,6 +381,7 @@
 
 
 MASKS = 8
+GATE_FLOOR = 11.0 / 9.0
 
 
 def pack_kernel(key, own, *rest):
@@ -402,7 +403,7 @@
     order[...] = jnp.where(iota((LANES, LANES), 1) == from_lane, 1.0, 0.0).astype(BF)
     back = 2 * LANES - 1 - iota((DISP, 2 * LANES), 0)
     flip[...] = jnp.where(iota((DISP, 2 * LANES), 1) == back, 1.0, 0.0).astype(BF)
-    guide_out[...] = spread_guide(guide[...])
+    guide_out[...] = spread_guide(guide[...]) * 0.5
     block_of = LINE_PARTS - 1 - (iota(spread.shape, 1) >> 4)
     here = (iota(spread.shape, 0) & (LINE_PARTS - 1)) == block_of
     spread[...] = jnp.where(here, 1.0, 0.0).astype(BF)
@@ -446,7 +447,6 @@
         shifted = [empty.astype(BF)] * 2
         for w in range(tiles):
             shifted.append(jnp.where(ch_lane < off, rolled[w - 1] if w else empty, rolled[w]).astype(BF))
-        shifted = [jnp.concatenate([tile, tile], axis=0) for tile in shifted]
         for quad in range(tiles // 4):
             refs = [tile_of(0, 4 * quad + q) for q in range(4)]
             masked = [refs[q] * (mask_of(0, 4 * quad + q) * scale).astype(BF) for q in range(4)]
@@ -455,12 +455,15 @@
             for two in range(2):
                 lo = two * LANES
                 gates, products = [], []
+                lhs = masked[:, lo : lo + LANES].astype(BF)
                 for side in range(2):
                     w = 4 * quad + 2 * two + side
                     keep = low_half if side == 0 else ~low_half
                     gates.append(jnp.where(keep, cols[:, lo : lo + LANES], 0.0))
-                    lhs = jnp.where(keep, masked[:, lo : lo + LANES], 0.0).astype(BF)
-                    rhs = jnp.concatenate(shifted[w : w + 3], axis=1)
+                    window = jnp.concatenate(shifted[w : w + 3], axis=1)
+                    rhs = [jnp.zeros_like(window)] * 2
+                    rhs[side] = window
+                    rhs = jnp.concatenate(rhs, axis=0)
                     products.append(jnp.dot(lhs, rhs, preferred_element_type=F32))
                 place = i * LINE_PARTS + 8 * (tiles - 2 - 4 * quad - 2 * two)
                 for t in range(LINE_RUN):
@@ -492,6 +495,7 @@
     reach = jnp.where(row >= 2 * GROUPS, 9, jnp.where(row >= GROUPS, 3, 1))
     room_left = x_base - reach
     room_right = x_base + reach - width
+    unit = jnp.where(row >= 2 * GROUPS, SHARPNESS / math.log(2.0), 1.0)
     for two in range(LINE_RUN // 2):
         lo = 2 * two * LANES
         costs = dot_t(flip[...], cost_rows[lo : lo + 2 * LANES, :])
@@ -499,7 +503,16 @@
         for i in range(2):
             t = 2 * two + i
             vol[t] = costs[:, i * LANES : (i + 1) * LANES]
-            normalise(logits[:, i * LANES : (i + 1) * LANES], wts, t, room_left, room_right)
+            z = jnp.tanh(logits[:, i * LANES : (i + 1) * LANES]) + GATE_FLOOR
+            taps = [z[m * KEYS : (m + 1) * KEYS] for m in range(3)]
+            factor = unit / (taps[0] + taps[1] + taps[2])
+            taps = [tap * factor for tap in taps]
+            if t >= LINE_RUN - 9:
+                taps[0] = jnp.where(room_left >= t, taps[0], 0.0)
+            if t < 9:
+                taps[2] = jnp.where(room_right < t, taps[2], 0.0)
+            for m in range(3):
+                wts[t, m * KEYS : (m + 1) * KEYS, :] = taps[m]
 
     for group in range(GROUPS):
         for at in (group * DGROUP, group * DGROUP + 8):
@@ -531,14 +544,13 @@
             while len(top) > 1:
                 top = [jnp.maximum(a, b) for a, b in zip(top[::2], top[1::2])] + top[len(top) & ~1 :]
             top = jnp.max(top[0], axis=0, keepdims=True)
-            total = jnp.zeros((8, LANES), F32)
+            total = jnp.exp2(v[-1] - top)
             moment = total
-            for i in range(DISP // 8):
-                e = jnp.exp(SHARPNESS * (v[i] - top))
-                total = total + e
+            for i in range(DISP // 8 - 2, -1, -1):
+                total = total + jnp.exp2(v[i] - top)
                 if i:
-                    moment = moment + float(8 * i) * e
-            moment = moment + sub.astype(F32) * total
+                    moment = moment + total
+            moment = 8.0 * moment + sub.astype(F32) * total
             totals = jnp.where(sub == s, jnp.sum(total, axis=0, keepdims=True), totals)
             moments = jnp.where(sub == s, jnp.sum(moment, axis=0, keepdims=True), moments)
         lane_line = iota((8, LANES), 1) >> 6
@@ -606,7 +618,9 @@
         ],
         1, (offsets, *consts, *pieces), 1_000_000_000,
     )
-    return lax.all_gather(rows, "view", axis=0, tiled=True)[None]
+    others = lax.ppermute(rows, "view", [(0, 1), (1, 0)])
+    first = lax.axis_index("view") == 0
+    return jnp.where(first, jnp.concatenate([rows, others]), jnp.concatenate([others, rows]))[None]
 
 
 def on_device(features, valid_cols, offsets, guide_weight):

time: 22.9 us -> 22.1 us (0.965)
  blocking collectives: 1.81 us -> 0 us
  waiting for transfers between devices: 3.82 us -> 4.67 us
  other arithmetic: 0 us -> 0.62 us
  local copies, waits for them, and re-layouts: 1.69 us -> 1.07 us
  starting transfers between devices: 10.1 us -> 10.5 us
    all_gather x1 -> x0, blocking collectives: 1.81 us -> none  [lines_plan(): return lax.all_gather(rows, 'view', axis=0, tiled=True)[None]]
    ppermute x0 -> x1, waiting for transfers between devices: none -> 0.86 us  [lines_plan(): others = lax.ppermute(rows, 'view', [(0, 1), (1, 0)])]
    broadcast_in_dim x1 -> x0, local copies, waits for them, and re-layouts: 0.63 us -> none  [lines_plan(): return lax.all_gather(rows, 'view', axis=0, tiled=True)[None]]
    select_n x0 -> x1, other arithmetic: none -> 0.62 us  [lines_plan(): jnp.where(first, jnp.concatenate([rows, others]), jnp.concatenate([others...]
    ppermute x0 -> x1, starting transfers between devices: none -> 0.38 us  [lines_plan(): others = lax.ppermute(rows, 'view', [(0, 1), (1, 0)])]
  transfers between devices with their start and end apart: 7 -> 8, of which waited for: 2 -> 3; matrix products, arithmetic and copies ran while one was open for 0% -> 0% of each run, Pallas kernels for 4% -> 4%
where the time goes in v11:
time: 22.1 us; the launch traced here: 21.8 us
  starting transfers between devices  10.5 us (48%)
  Pallas kernels  4.81 us (22%)
  waiting for transfers between devices  4.67 us (21%)
  local copies, waits for them, and re-layouts  1.07 us (5%)
  other arithmetic  0.62 us (3%)
    ppermute x7, starting transfers between devices, lines_plan(): pieces[key] = lax.ppermute(piece, ('cols', 'view'), moves) if key else piece  10.1 us
    pallas_call x10, Pallas kernels, call(): pl.pallas_call(kernel, out_shape=[jax.ShapeDtypeStruct(shape, dtype) for...  4.81 us
    ppermute x7, waiting for transfers between devices, lines_plan(): pieces[key] = lax.ppermute(piece, ('cols', 'view'), moves) if key else piece  3.82 us
    unnamed x10, local copies, waits for them, and re-layouts  1.07 us
    ppermute x1, waiting for transfers between devices, lines_plan(): others = lax.ppermute(rows, 'view', [(0, 1), (1, 0)])  0.86 us
    select_n x1, other arithmetic, lines_plan(): jnp.where(first, jnp.concatenate([rows, others]), jnp.concatenate([others...  0.62 us
  transfers between devices with their start and end apart: 8, of which 3 were waited for; matrix products, arithmetic and copies ran while one was open for 0% of the time, Pallas kernels for 4%

profile of v11, /device:TPU:0, one launch (start us, length us, event | category | flops | bytes accessed | tf_op | source)
XLA Modules:
  0.0 21.8 jit_solution(3846712025864337392)
XLA Ops:
  0.0 1.0 %copy-done = bf16[1,16,64,256]{3,2,1,0:T(8,128)(2,1)S(1)} copy-done((bf16[1,16,64,256]{3,2,1,0:T(8,128)(2,1)S(1)}, bf16[1,16,64,256]{3,2,1,0:T(8,128)(2,1)}, u32[]{:S(2)}) %copy-start) | copy-done | bytes 524312
  1.1 0.0 copy-start.1
  1.1 0.0 copy-start.2
  1.1 4.1 %collective-permute-start.3 = (bf16[128,256]{1,0:T(8,128)(2,1)S(1)}, bf16[128,256]{1,0:T(8,128)(2,1)S(1)}, u32[]{:S(2)}, u32[]{:S(2)}) collective-permute-start(bf16[128,256]{1,0:T(8,128)(2,1)S(1)} %shard_map.50.rest_1_), channel_id=1, source_target_pairs={{0,8},{1,9},{4,12},{5,13},{8,0},{9,1},{12,4},{13,5},{2,10},{3,11},... | collective-permute-start | bytes 196616 | tf_op jit(solution)/shard_map/ppermute | solution.py:598
  5.2 1.3 %collective-permute-start.5 = (bf16[128,256]{1,0:T(8,128)(2,1)S(1)}, bf16[128,256]{1,0:T(8,128)(2,1)S(1)}, u32[]{:S(2)}, u32[]{:S(2)}) collective-permute-start(bf16[128,256]{1,0:T(8,128)(2,1)S(1)} %shard_map.49.rest_0_), channel_id=1, source_target_pairs={{0,12},{1,13},{4,8},{5,9},{8,4},{9,5},{12,0},{13,1},{2,14},{3,15},... | collective-permute-start | bytes 196616 | tf_op jit(solution)/shard_map/ppermute | solution.py:598
  6.7 0.0 copy-start.3
  6.7 0.0 copy-start.4
  6.7 0.1 collective-permute-start.2
  6.8 2.7 %collective-permute-start.4 = (bf16[136,256]{1,0:T(8,128)(2,1)S(1)}, bf16[136,256]{1,0:T(8,128)(2,1)S(1)}, u32[]{:S(2)}, u32[]{:S(2)}) collective-permute-start(bf16[136,256]{1,0:T(8,128)(2,1)S(1)} %shard_map.52.rest_1_), channel_id=1, source_target_pairs={{0,9},{1,8},{4,13},{5,12},{8,1},{9,0},{12,5},{13,4},{2,11},{3,10},... | collective-permute-start | bytes 208904 | tf_op jit(solution)/shard_map/ppermute | solution.py:598
  9.5 0.2 %collective-permute-start.6 = (bf16[136,256]{1,0:T(8,128)(2,1)S(1)}, bf16[136,256]{1,0:T(8,128)(2,1)S(1)}, u32[]{:S(2)}, u32[]{:S(2)}) collective-permute-start(bf16[136,256]{1,0:T(8,128)(2,1)S(1)} %shard_map.51.rest_1_), channel_id=1, source_target_pairs={{0,13},{1,12},{4,9},{5,8},{8,5},{9,4},{12,1},{13,0},{2,15},{3,14},... | collective-permute-start | bytes 208904 | tf_op jit(solution)/shard_map/ppermute | solution.py:598
  9.8 0.0 collective-permute-done.3.rest_5_
  9.8 1.6 %collective-permute-start.1 = (bf16[128,256]{1,0:T(8,128)(2,1)S(1)}, bf16[128,256]{1,0:T(8,128)(2,1)S(1)}, u32[]{:S(2)}, u32[]{:S(2)}) collective-permute-start(bf16[128,256]{1,0:T(8,128)(2,1)S(1)} %shard_map.48.rest_0_), channel_id=1, source_target_pairs={{0,4},{1,5},{4,0},{5,1},{8,12},{9,13},{12,8},{13,9},{2,6},{3,7},{6... | collective-permute-start | bytes 196616 | tf_op jit(solution)/shard_map/ppermute | solution.py:598
  11.4 0.3 %collective-permute-done.5.rest_7_ = bf16[128,256]{1,0:T(8,128)(2,1)S(1)} collective-permute-done((bf16[128,256]{1,0:T(8,128)(2,1)S(1)}, bf16[128,256]{1,0:T(8,128)(2,1)S(1)}, u32[]{:S(2)}, u32[]{:S(2)}) %collective-permute-start.5) | collective-permute-done | bytes 65568 | tf_op jit(solution)/shard_map/ppermute | solution.py:598
  11.7 0.0 collective-permute-start
  11.8 0.8 %shard_map.46 = (bf16[128,128]{1,0:T(8,128)(2,1)S(1)}, bf16[192,256]{1,0:T(8,128)(2,1)S(1)}, bf16[120,128]{1,0:T(8,128)(2,1)S(1)}, bf16[128,1024]{1,0:T(8,128)(2,1)S(1)}, f32[2,256]{1,0:T(2,128)S(1)}) custom-call(s32[16]{0:T(128)S(1)} %copy-done.4, bf16[64,108]{1,0:T(8,128)(2,1)S(1)} %copy-done.3, s32[2,256]{1,0:T(2,128)S(1)} %copy-done.2), custom_call_target="tpu_custom_call" | custom-call | flops 1000000 | bytes 1000000 | tf_op jit(solution)/shard_map/pallas_call | solution.py:50
  12.6 3.5 %collective-permute-done.1.rest_3_ = bf16[128,256]{1,0:T(8,128)(2,1)S(1)} collective-permute-done((bf16[128,256]{1,0:T(8,128)(2,1)S(1)}, bf16[128,256]{1,0:T(8,128)(2,1)S(1)}, u32[]{:S(2)}, u32[]{:S(2)}) %collective-permute-start.1) | collective-permute-done | bytes 65568 | tf_op jit(solution)/shard_map/ppermute | solution.py:598
  16.0 0.0 collective-permute-done.rest_2_
  16.0 0.0 collective-permute-done.2.rest_4_
  16.1 0.0 collective-permute-done.4.rest_6_
  16.1 0.0 collective-permute-done.6.rest_8_
  16.1 3.9 %shard_map.55 = f32[2,1024]{1,0:T(2,128)S(1)} custom-call(s32[16]{0:T(128)S(1)} %copy-done.4, bf16[128,128]{1,0:T(8,128)(2,1)S(1)} %get-tuple-element.10.order, bf16[192,256]{1,0:T(8,128)(2,1)S(1)} %get-tuple-element.11.flip, bf16[120,128]{1,0:T(8,128)(2,1)S(1)} %get-tuple-element.12.guide, bf16[128,1024]{1,0:T(8,128)(2,1)S(1)} %get-tuple-element.13.spread, ...), custom_call_target="tpu_custom_call" | custom-call | flops 1000000000 | bytes 1000000 | tf_op jit(solution)/shard_map/pallas_call | solution.py:50
  20.0 0.4 %collective-permute-start.7 = (f32[2,1024]{1,0:T(2,128)S(1)}, f32[2,1024]{1,0:T(2,128)S(1)}, u32[]{:S(2)}, u32[]{:S(2)}) collective-permute-start(f32[2,1024]{1,0:T(2,128)S(1)} %shard_map.55), channel_id=1, source_target_pairs={{0,1},{1,0},{2,3},{3,2},{4,5},{5,4},{6,7},{7,6},{8,9},{9,8},{10,11... | collective-permute-start | bytes 24584 | tf_op jit(solution)/shard_map/ppermute | solution.py:621
  20.4 0.9 %collective-permute-done.7 = f32[2,1024]{1,0:T(2,128)S(1)} collective-permute-done((f32[2,1024]{1,0:T(2,128)S(1)}, f32[2,1024]{1,0:T(2,128)S(1)}, u32[]{:S(2)}, u32[]{:S(2)}) %collective-permute-start.7) | collective-permute-done | bytes 8224 | tf_op jit(solution)/shard_map/ppermute | solution.py:621
  21.2 0.6 %maximum_select_fusion = f32[1,4,1024]{2,1,0:T(4,128)} fusion(f32[1,2,1024]{2,1,0:T(2,128)S(1)} %bitcast.12, f32[1,2,1024]{2,1,0:T(2,128)S(1)} %bitcast.11, pred[]{:T(512)S(6)} %eq.3), kind=kLoop, calls=%fused_computation | loop fusion | flops 12288 | bytes 32769 | tf_op jit(solution)/shard_map/jit(_where)/select_n | solution.py:623
  (13 shorter events, 0.1 us)
Async XLA Ops:
  0.0 1.0 %copy-start = (bf16[1,16,64,256]{3,2,1,0:T(8,128)(2,1)S(1)}, bf16[1,16,64,256]{3,2,1,0:T(8,128)(2,1)}, u32[]{:S(2)}) copy-start(bf16[1,16,64,256]{3,2,1,0:T(8,128)(2,1)} %param.4) | copy-start | bytes 1572868
  1.1 5.5 %copy-start.1 = (bf16[1,16,64,256]{3,2,1,0:T(8,128)(2,1)S(1)}, bf16[1,16,64,256]{3,2,1,0:T(8,128)(2,1)}, u32[]{:S(2)}) copy-start(bf16[1,16,64,256]{3,2,1,0:T(8,128)(2,1)} %param.4) | copy-start | bytes 1572868
  1.1 5.5 %copy-start.2 = (s32[2,256]{1,0:T(2,128)S(1)}, s32[2,256]{1,0:T(2,128)}, u32[]{:S(2)}) copy-start(s32[2,256]{1,0:T(2,128)} %rest_0_.5) | copy-start | bytes 6148
  1.1 8.6 %collective-permute-start.3 = (bf16[128,256]{1,0:T(8,128)(2,1)S(1)}, bf16[128,256]{1,0:T(8,128)(2,1)S(1)}, u32[]{:S(2)}, u32[]{:S(2)}) collective-permute-start(bf16[128,256]{1,0:T(8,128)(2,1)S(1)} %shard_map.50.rest_1_), channel_id=1, source_target_pairs={{0,8},{1,9},{4,12},{5,13},{8,0},{9,1},{12,4},{13,5},{2,10},{3,11},... | collective-permute-start | bytes 196616 | tf_op jit(solution)/shard_map/ppermute | solution.py:598
  5.2 6.5 %collective-permute-start.5 = (bf16[128,256]{1,0:T(8,128)(2,1)S(1)}, bf16[128,256]{1,0:T(8,128)(2,1)S(1)}, u32[]{:S(2)}, u32[]{:S(2)}) collective-permute-start(bf16[128,256]{1,0:T(8,128)(2,1)S(1)} %shard_map.49.rest_0_), channel_id=1, source_target_pairs={{0,12},{1,13},{4,8},{5,9},{8,4},{9,5},{12,0},{13,1},{2,14},{3,15},... | collective-permute-start | bytes 196616 | tf_op jit(solution)/shard_map/ppermute | solution.py:598
  6.7 5.1 %copy-start.3 = (bf16[64,108]{1,0:T(8,128)(2,1)S(1)}, bf16[64,108]{1,0:T(8,128)(2,1)}, u32[]{:S(2)}) copy-start(bf16[64,108]{1,0:T(8,128)(2,1)} %guide.1) | copy-start | bytes 41476
  6.7 5.1 %copy-start.4 = (s32[16]{0:T(128)S(1)}, s32[16]{0:T(128)}, u32[]{:S(2)}) copy-start(s32[16]{0:T(128)} %offsets.3) | copy-start | bytes 196
  6.7 9.4 %collective-permute-start.2 = (bf16[136,256]{1,0:T(8,128)(2,1)S(1)}, bf16[136,256]{1,0:T(8,128)(2,1)S(1)}, u32[]{:S(2)}, u32[]{:S(2)}) collective-permute-start(bf16[136,256]{1,0:T(8,128)(2,1)S(1)} %shard_map.53.rest_0_), channel_id=1, source_target_pairs={{0,5},{1,4},{4,1},{5,0},{8,13},{9,12},{12,9},{13,8},{2,7},{3,6},{6... | collective-permute-start | bytes 208904 | tf_op jit(solution)/shard_map/ppermute | solution.py:598
  6.8 9.3 %collective-permute-start.4 = (bf16[136,256]{1,0:T(8,128)(2,1)S(1)}, bf16[136,256]{1,0:T(8,128)(2,1)S(1)}, u32[]{:S(2)}, u32[]{:S(2)}) collective-permute-start(bf16[136,256]{1,0:T(8,128)(2,1)S(1)} %shard_map.52.rest_1_), channel_id=1, source_target_pairs={{0,9},{1,8},{4,13},{5,12},{8,1},{9,0},{12,5},{13,4},{2,11},{3,10},... | collective-permute-start | bytes 208904 | tf_op jit(solution)/shard_map/ppermute | solution.py:598
  9.5 6.5 %collective-permute-start.6 = (bf16[136,256]{1,0:T(8,128)(2,1)S(1)}, bf16[136,256]{1,0:T(8,128)(2,1)S(1)}, u32[]{:S(2)}, u32[]{:S(2)}) collective-permute-start(bf16[136,256]{1,0:T(8,128)(2,1)S(1)} %shard_map.51.rest_1_), channel_id=1, source_target_pairs={{0,13},{1,12},{4,9},{5,8},{8,5},{9,4},{12,1},{13,0},{2,15},{3,14},... | collective-permute-start | bytes 208904 | tf_op jit(solution)/shard_map/ppermute | solution.py:598
  9.8 6.3 %collective-permute-start.1 = (bf16[128,256]{1,0:T(8,128)(2,1)S(1)}, bf16[128,256]{1,0:T(8,128)(2,1)S(1)}, u32[]{:S(2)}, u32[]{:S(2)}) collective-permute-start(bf16[128,256]{1,0:T(8,128)(2,1)S(1)} %shard_map.48.rest_0_), channel_id=1, source_target_pairs={{0,4},{1,5},{4,0},{5,1},{8,12},{9,13},{12,8},{13,9},{2,6},{3,7},{6... | collective-permute-start | bytes 196616 | tf_op jit(solution)/shard_map/ppermute | solution.py:598
  11.7 4.3 %collective-permute-start = (bf16[128,256]{1,0:T(8,128)(2,1)S(1)}, bf16[128,256]{1,0:T(8,128)(2,1)S(1)}, u32[]{:S(2)}, u32[]{:S(2)}) collective-permute-start(bf16[128,256]{1,0:T(8,128)(2,1)S(1)} %shard_map.47.rest_0_), channel_id=1, source_target_pairs={{0,1},{1,0},{4,5},{5,4},{8,9},{9,8},{12,13},{13,12},{2,3},{3,2},{6... | collective-permute-start | bytes 196616 | tf_op jit(solution)/shard_map/ppermute | solution.py:598
  20.0 1.2 %collective-permute-start.7 = (f32[2,1024]{1,0:T(2,128)S(1)}, f32[2,1024]{1,0:T(2,128)S(1)}, u32[]{:S(2)}, u32[]{:S(2)}) collective-permute-start(f32[2,1024]{1,0:T(2,128)S(1)} %shard_map.55), channel_id=1, source_target_pairs={{0,1},{1,0},{2,3},{3,2},{4,5},{5,4},{6,7},{7,6},{8,9},{9,8},{10,11... | collective-permute-start | bytes 24584 | tf_op jit(solution)/shard_map/ppermute | solution.py:621

commit v12 on v3

--- a/solution.py
+++ b/solution.py
@@ -1,3 +1,4 @@
+import functools
 import math
 
 import jax
@@ -43,18 +44,39 @@
     return lax.dot_general(a, b, (((1,), (1,)), ((), ())), preferred_element_type=F32)
 
 
-def call(kernel, outs, scratch, smem, args, flops=0, space=pltpu.VMEM):
+def call(kernel, outs, scratch, smem, args, flops=0, space=pltpu.VMEM, limit=24, to=None):
     specs = [pl.BlockSpec(memory_space=pltpu.SMEM)] * smem
     specs += [pl.BlockSpec(memory_space=space)] * (len(args) - smem)
     return pl.pallas_call(
         kernel,
         out_shape=[jax.ShapeDtypeStruct(shape, dtype) for shape, dtype in outs],
         in_specs=specs,
-        out_specs=[pl.BlockSpec(memory_space=pltpu.VMEM)] * len(outs),
+        out_specs=[pl.BlockSpec(memory_space=to or space)] * len(outs),
         scratch_shapes=scratch,
-        compiler_params=pltpu.CompilerParams(vmem_limit_bytes=24 * 1024 * 1024),
+        compiler_params=pltpu.CompilerParams(vmem_limit_bytes=limit * 1024 * 1024),
         cost_estimate=pl.CostEstimate(flops=flops, bytes_accessed=1_000_000, transcendentals=0),
     )(*args)
+
+
+def spread_guide(guide):
+    keys = LAYERS * 3 * GROUPS
+    row = iota((3 * KEYS, keys), 0)
+    tap = jnp.where(row >= KEYS, 1, 0) + jnp.where(row >= 2 * KEYS, 1, 0)
+    row = row - KEYS * tap
+    layer = jnp.where(row >= GROUPS, 1, 0) + jnp.where(row >= 2 * GROUPS, 1, 0)
+    key = 2 * GROUPS * layer + GROUPS * tap + row
+    chosen = jnp.where((iota((3 * KEYS, keys), 1) == key) & (row < 3 * GROUPS), 1.0, 0.0).astype(BF)
+    guide_t = dot_t(chosen, guide).astype(BF)
+    return jnp.concatenate([guide_t, guide_t], axis=1)
+
+
+def normalise(z, wts, t, room_left, room_right):
+    z = (0.55 + 0.45 * jnp.tanh(0.5 * z)).astype(BF).astype(F32)
+    taps = [z[k * KEYS : (k + 1) * KEYS] for k in range(3)]
+    scale = 1.0 / (taps[0] + taps[1] + taps[2])
+    wts[t, 0:KEYS, :] = jnp.where(room_left >= t, taps[0] * scale, 0.0)
+    wts[t, KEYS : 2 * KEYS, :] = taps[1] * scale
+    wts[t, 2 * KEYS : 3 * KEYS, :] = jnp.where(room_right < t, taps[2] * scale, 0.0)
 
 
 def prefetch_kernel(own, valid, guide, own_out, masks, perm, flip, guide_out, valid_in, guide_in, sems):
@@ -70,16 +92,8 @@
     back = 2 * LANES - 1 - iota((DISP, 2 * LANES), 0)
     flip[...] = jnp.where(iota((DISP, 2 * LANES), 1) == back, 1.0, 0.0).astype(BF)
 
-    keys = LAYERS * 3 * GROUPS
-    row = iota((3 * KEYS, keys), 0)
-    tap = jnp.where(row >= KEYS, 1, 0) + jnp.where(row >= 2 * KEYS, 1, 0)
-    row = row - KEYS * tap
-    layer = jnp.where(row >= GROUPS, 1, 0) + jnp.where(row >= 2 * GROUPS, 1, 0)
-    key = 2 * GROUPS * layer + GROUPS * tap + row
-    chosen = jnp.where((iota((3 * KEYS, keys), 1) == key) & (row < 3 * GROUPS), 1.0, 0.0).astype(BF)
     copies[1].wait()
-    guide_t = dot_t(chosen, guide_in[...]).astype(BF)
-    guide_out[...] = jnp.concatenate([guide_t, guide_t], axis=1)
+    guide_out[...] = spread_guide(guide_in[...])
     copies[2].wait()
     masks[...] = valid_in[...].astype(F32)
     copies[0].wait()
@@ -220,13 +234,7 @@
         logits = dot_t(guide[...], gate_rows[at : at + 2 * LANES, :])
         for i in range(2):
             t = 2 * two + i
-            z = logits[:, i * LANES : (i + 1) * LANES]
-            z = (0.55 + 0.45 * jnp.tanh(0.5 * z)).astype(BF).astype(F32)
-            taps = [z[k * KEYS : (k + 1) * KEYS] for k in range(3)]
-            scale = 1.0 / (taps[0] + taps[1] + taps[2])
-            wts[t, 0:KEYS, :] = jnp.where(room_left >= t, taps[0] * scale, 0.0)
-            wts[t, KEYS : 2 * KEYS, :] = taps[1] * scale
-            wts[t, 2 * KEYS : 3 * KEYS, :] = jnp.where(room_right < t, taps[2] * scale, 0.0)
+            normalise(logits[:, i * LANES : (i + 1) * LANES], wts, t, room_left, room_right)
 
 
 def late_kernel(
@@ -329,7 +337,7 @@
     return jnp.transpose(joined, (1, 0, 2)).reshape(1, sub, n * BLOCK)
 
 
-def on_device(features, valid_cols, offsets, guide_weight):
+def halo_plan(features, valid_cols, offsets, guide_weight):
     own = features[0]
     n = lax.axis_size("cols")
     right = [(c, c + 1) for c in range(n - 1)]
@@ -338,7 +346,7 @@
         prefetch_kernel,
         [(own.shape, BF), (valid_cols.shape, F32), ((SPAN, WIDE), BF), ((DISP, 2 * LANES), BF), ((3 * KEYS, LANES), BF)],
         [pltpu.VMEM(valid_cols.shape, jnp.int32), pltpu.VMEM(guide_weight.shape, BF), pltpu.SemaphoreType.DMA((3,))],
-        0, (own, valid_cols, guide_weight), 100_000_000, pl.ANY,
+        0, (own, valid_cols, guide_weight), 100_000_000, pl.ANY, 24, pltpu.VMEM,
     )
     first, second, ref_own = call(
         payload_kernel,
@@ -362,8 +370,270 @@
         [skew, pltpu.VMEM(quad_rows, BF), pltpu.VMEM((RUN, DISP, LANES), F32), square, square],
         1, (offsets, second, left_second, lhs, early_rows, wts, flip), 1_000_000_000,
     )
-    pieces = lax.all_gather(result, ("cols", "view"), axis=0)
+    copies = jnp.broadcast_to(result[None], (2 * n, LINES, WIDE))
+    pieces = lax.all_to_all(copies, ("cols", "view"), split_axis=0, concat_axis=0, tiled=True)
     return join(pieces, own.shape[0] // n, n)
+
+
+LINE_RUN = 8
+PAIR = 2
+MASKS = 8
+GATE_FLOOR = 11.0 / 9.0
+
+
+def pack_kernel(hop, line, own, *rest):
+    out = rest[-1]
+    view = lax.axis_index("view")
+    target = (2 * lax.axis_index("cols") + view) ^ (2 * hop)
+    if line is None:
+        out[...] = own[target]
+        return
+    lo = line * CHANNELS
+    other = rest[0][target, lo : lo + CHANNELS, :]
+    rows = CHANNELS
+    if hop == 2:
+        out[:rows, :] = other
+    else:
+        rows = 2 * CHANNELS
+        mine = own[target, lo : lo + CHANNELS, :]
+        out[:CHANNELS, :] = jnp.where(view == 0, mine, other)
+        out[CHANNELS:rows, :] = jnp.where(view == 0, other, mine)
+    if out.shape[0] > rows:
+        masks = rest[1][...].astype(F32)
+        out[rows:, :] = jnp.where(
+            iota((MASKS, BLOCK), 0) < MASKS // 2, masks[0:1, :], masks[1:2, :]
+        ).astype(BF)
+
+
+def constants_kernel(offsets, guide, order, flip, guide_out, spread):
+    row = iota((LANES, LANES), 0)
+    from_lane = LANES - 1 - LINE_RUN * (row & (PARTS - 1)) - (row >> 4)
+    order[...] = jnp.where(iota((LANES, LANES), 1) == from_lane, 1.0, 0.0).astype(BF)
+    back = 2 * LANES - 1 - iota((DISP, 2 * LANES), 0)
+    flip[...] = jnp.where(iota((DISP, 2 * LANES), 1) == back, 1.0, 0.0).astype(BF)
+    guide_out[...] = spread_guide(guide[...]) * 0.5
+    block_of = LANES - 1 - (iota(spread.shape, 1) >> 3)
+    spread[...] = jnp.where(iota(spread.shape, 0) == block_of, 1.0, 0.0).astype(BF)
+
+
+def line_kernel(line, offsets, order, flip, guide, spread, zero, one, two, two_more, three, masks, *rest):
+    if line:
+        earlier, *rest = rest
+        out, refs, secs, gate_rows, cost_rows, vol, done, wts = rest
+        valid = masks
+    else:
+        out, valid, refs, secs, gate_rows, cost_rows, vol, done, wts = rest
+    block = lax.axis_index("cols")
+    view = lax.axis_index("view")
+    n = refs.shape[0]
+    tiles = 2 * n
+    width = tiles * LANES
+    off = offsets[PAIR * (2 * block + view) + line]
+
+    for hop, piece in ((0, zero), (1, one), (3, three)):
+        refs[block ^ hop] = piece[:CHANNELS, :]
+        secs[block ^ hop] = piece[CHANNELS : 2 * CHANNELS, :]
+    lo = line * CHANNELS
+    near = two[lo : lo + CHANNELS, :]
+    refs[block ^ 2] = jnp.where(view == 0, near, two_more[:CHANNELS, :])
+    secs[block ^ 2] = jnp.where(view == 0, two_more[:CHANNELS, :], near)
+    if not line:
+        valid[block] = masks[...].astype(F32)
+        for hop, piece, lo in ((1, one, 2 * CHANNELS), (2, two_more, CHANNELS), (3, three, 2 * CHANNELS)):
+            got = piece[lo : lo + MASKS, :].astype(F32)
+            valid[block ^ hop] = jnp.concatenate([got[0:1], got[MASKS // 2 : MASKS // 2 + 1]], axis=0)
+
+    def tile_of(source, w):
+        lo = (w % 2) * LANES
+        return source[w // 2, :, lo : lo + LANES]
+
+    def mask_of(view, w):
+        lo = (w % 2) * LANES
+        return valid[w // 2, view : view + 1, lo : lo + LANES]
+
+    ch_lane = iota((CHANNELS, LANES), 1)
+    rolled = [pltpu.roll(tile_of(secs, w).astype(F32) * mask_of(1, w), off, 1) for w in range(tiles)]
+    empty = jnp.zeros((CHANNELS, LANES), F32)
+    shifted = [empty.astype(BF)] * 2
+    for w in range(tiles):
+        shifted.append(jnp.where(ch_lane < off, rolled[w - 1] if w else empty, rolled[w]).astype(BF))
+
+    reached = iota((8, LANES), 1) + LINE_RUN * iota((8, LANES), 0)
+    low_half = iota((LANES, LANES), 1) < CHANNELS
+    scale = 1.0 / math.sqrt(CHANNELS)
+    for quad in range(tiles // 4):
+        raw = [tile_of(refs, 4 * quad + q) for q in range(4)]
+        masked = [raw[q] * (mask_of(0, 4 * quad + q) * scale).astype(BF) for q in range(4)]
+        cols = dot_t(order[...], jnp.concatenate(raw, axis=0))
+        masked = dot_t(order[...], jnp.concatenate(masked, axis=0))
+        for q in range(4):
+            w = 4 * quad + q
+            place = (tiles - 1 - w) * PARTS
+            lo = (q // 2) * LANES
+            keep = low_half if q % 2 == 0 else ~low_half
+            gates = jnp.where(keep, cols[:, lo : lo + LANES], 0.0).astype(BF)
+            window = jnp.concatenate(shifted[w : w + 3], axis=1)
+            rhs = [jnp.zeros_like(window)] * 2
+            rhs[q % 2] = window
+            products = jnp.dot(
+                masked[:, lo : lo + LANES].astype(BF), jnp.concatenate(rhs, axis=0), preferred_element_type=F32
+            )
+            for t in range(LINE_RUN):
+                row = t * LANES + place
+                gate_rows[row : row + PARTS, :] = gates[t * PARTS : (t + 1) * PARTS]
+                halves = []
+                for half in range(2):
+                    base = half * LANES // 2 + t
+                    r = t * PARTS + 8 * half
+                    part = [products[r : r + 8, m * LANES : (m + 1) * LANES] for m in range(3)]
+                    within = reached < LANES - base
+                    halves.append(
+                        jnp.concatenate(
+                            [
+                                pltpu.roll(
+                                    jnp.where(within, part[m + 1], part[m]),
+                                    base, 1, stride=LINE_RUN, stride_axis=0,
+                                )
+                                for m in range(2)
+                            ],
+                            axis=1,
+                        )
+                    )
+                cost_rows[row : row + PARTS, :] = jnp.concatenate(halves, axis=0).astype(BF)
+
+    x_base = width - 1 - LINE_RUN * iota((KEYS, LANES), 1)
+    row = iota((KEYS, LANES), 0)
+    reach = jnp.where(row >= 2 * GROUPS, 9, jnp.where(row >= GROUPS, 3, 1))
+    room_left = x_base - reach
+    room_right = x_base + reach - width
+    unit = jnp.where(row >= 2 * GROUPS, SHARPNESS / math.log(2.0), 1.0)
+    for two_t in range(LINE_RUN // 2):
+        lo = 2 * two_t * LANES
+        costs = dot_t(flip[...], cost_rows[lo : lo + 2 * LANES, :])
+        logits = dot_t(guide[...], gate_rows[lo : lo + 2 * LANES, :])
+        for i in range(2):
+            t = 2 * two_t + i
+            vol[t] = costs[:, i * LANES : (i + 1) * LANES]
+            z = jnp.tanh(logits[:, i * LANES : (i + 1) * LANES]) + GATE_FLOOR
+            taps = [z[m * KEYS : (m + 1) * KEYS] for m in range(3)]
+            factor = unit / (taps[0] + taps[1] + taps[2])
+            taps = [tap * factor for tap in taps]
+            taps[0] = jnp.where(room_left >= t, taps[0], 0.0)
+            taps[2] = jnp.where(room_right < t, taps[2], 0.0)
+            for m in range(3):
+                wts[t, m * KEYS : (m + 1) * KEYS, :] = taps[m]
+
+    for group in range(GROUPS):
+        for at in (group * DGROUP, group * DGROUP + 8):
+            v = [vol[t, at : at + 8, :] for t in range(LINE_RUN)]
+            for layer in range(LAYERS):
+                s = 3**layer
+                fresh = []
+                for t in range(LINE_RUN):
+                    w = [wts[t, r : r + 1, :] for r in [m * KEYS + layer * GROUPS + group for m in range(3)]]
+                    blk, r = divmod(t + s, LINE_RUN)
+                    before = pltpu.roll(v[r], LANES - blk, 1) if blk else v[r]
+                    blk, r = divmod(t - s, LINE_RUN)
+                    after = pltpu.roll(v[r], -blk, 1) if blk else v[r]
+                    fresh.append(w[0] * before + w[1] * v[t] + w[2] * after)
+                v = fresh
+            for t in range(LINE_RUN):
+                done[t, at : at + 8, :] = v[t]
+
+    sub = iota((8, LANES), 0)
+    totals = jnp.zeros((8, LANES), F32)
+    moments = totals
+    for t in range(LINE_RUN):
+        v = [done[t, 8 * i : 8 * i + 8, :] for i in range(DISP // 8)]
+        top = v
+        while len(top) > 1:
+            top = [jnp.maximum(a, b) for a, b in zip(top[::2], top[1::2])] + top[len(top) & ~1 :]
+        top = jnp.max(top[0], axis=0, keepdims=True)
+        total = jnp.exp2(v[-1] - top)
+        moment = total
+        for i in range(DISP // 8 - 2, -1, -1):
+            total = total + jnp.exp2(v[i] - top)
+            if i:
+                moment = moment + total
+        moment = 8.0 * moment + sub.astype(F32) * total
+        here = sub == LINE_RUN - 1 - t
+        totals = jnp.where(here, jnp.sum(total, axis=0, keepdims=True), totals)
+        moments = jnp.where(here, jnp.sum(moment, axis=0, keepdims=True), moments)
+    vals = (moments / totals + off.astype(F32)) * (1.0 / DISP)
+    high = vals.astype(BF)
+    left = vals - high.astype(F32)
+    middle = left.astype(BF)
+    low = (left - middle.astype(F32)).astype(BF)
+    spare = jnp.zeros((8, LANES), BF)
+    parts = jnp.dot(
+        jnp.concatenate([high, middle, low, spare], axis=0), spread[...], preferred_element_type=F32
+    )
+    parts = parts[0:8] + parts[8:16] + parts[16:24]
+    wanted = iota((8, width), 0) == (iota((8, width), 1) & (LINE_RUN - 1))
+    result = jnp.sum(jnp.where(wanted, parts, 0.0), axis=0, keepdims=True)
+    if line:
+        out[0:1, :] = earlier[...]
+        out[1:2, :] = result
+    else:
+        out[...] = result
+
+
+def lines_plan(features, valid_cols, offsets, guide_weight):
+    n = lax.axis_size("cols")
+    devices = 2 * n
+    width = n * BLOCK
+    own = features.reshape(devices, PAIR * CHANNELS, BLOCK)
+    other = lax.ppermute(own, "view", [(0, 1), (1, 0)])
+    got = {}
+    gone = ()
+    for hop, line in ((2, None), (3, 0), (2, 0), (1, 0), (3, 1), (2, 1), (1, 1), (0, 0), (0, 1)):
+        masked = hop and line == 0
+        rows = CHANNELS if hop == 2 and line is not None else 2 * CHANNELS
+        (piece,) = call(
+            functools.partial(pack_kernel, hop, line),
+            [((rows + (MASKS if masked else 0), BLOCK), BF)],
+            [], 0,
+            (own,) + (() if line is None else (other,)) + ((valid_cols,) if masked else ()) + gone,
+            1_000_000,
+        )
+        gone = (piece,)
+        got[hop, line] = lax.ppermute(piece, "cols", [(c, c ^ hop) for c in range(n)]) if hop else piece
+    consts = call(
+        constants_kernel,
+        [((LANES, LANES), BF), ((DISP, 2 * LANES), BF), ((3 * KEYS, LANES), BF), ((LANES, width), BF)],
+        [], 1, (offsets, guide_weight), 1_000_000,
+    )
+    scratch = [
+        pltpu.VMEM((n, CHANNELS, BLOCK), BF),
+        pltpu.VMEM((n, CHANNELS, BLOCK), BF),
+        pltpu.VMEM((LINE_RUN * LANES, LANES), BF),
+        pltpu.VMEM((LINE_RUN * LANES, 2 * LANES), BF),
+        pltpu.VMEM((LINE_RUN, DISP, LANES), F32),
+        pltpu.VMEM((LINE_RUN, DISP, LANES), F32),
+        pltpu.VMEM((LINE_RUN, 3 * KEYS, LANES), F32),
+    ]
+    both = ((n,) + valid_cols.shape, F32)
+    masks, more = valid_cols, ()
+    for line in range(PAIR):
+        pieces = [got[0, line], got[1, line], got[2, None], got[2, line], got[3, line]]
+        rows, *kept = call(
+            functools.partial(line_kernel, line),
+            [((1 + line, width), F32)] + ([] if line else [both]),
+            scratch, 1, (offsets, *consts, *pieces, masks, *more), 1_000_000_000,
+        )
+        if kept:
+            masks, more = kept[0], (rows,)
+    others = lax.ppermute(rows, "view", [(0, 1), (1, 0)])
+    first = lax.axis_index("view") == 0
+    return jnp.where(first, jnp.concatenate([rows, others]), jnp.concatenate([others, rows]))[None]
+
+
+def on_device(features, valid_cols, offsets, guide_weight):
+    n = lax.axis_size("cols")
+    lines = features.shape[1]
+    if lines == 2 * PAIR * n and n * BLOCK == LINE_RUN * LANES:
+        return lines_plan(features, valid_cols, offsets, guide_weight)
+    return halo_plan(features, valid_cols, offsets, guide_weight)
 
 
 def solution(mesh):

time: 36.8 us -> 27 us (0.73)
  blocking collectives: 15.1 us -> 0 us
  waiting for transfers between devices: 1.32 us -> 6.33 us
  starting transfers between devices: 8.43 us -> 12.3 us
  Pallas kernels: 8.46 us -> 6.34 us
  local copies, waits for them, and re-layouts: 2.46 us -> 1.06 us
    all_gather x1 -> x0, blocking collectives: 15.1 us -> none  [on_device(): pieces = lax.all_gather(result, ('cols', 'view'), axis=0)]
    ppermute x3 -> x9, waiting for transfers between devices: 1.32 us -> 6.33 us  [the longest x7 4.48 us: lines_plan(): lax.ppermute(piece, 'cols', [(c, c ^ hop) for c in range(n)])]
    ppermute x3 -> x9, starting transfers between devices: 8.43 us -> 12.3 us  [the longest x7 11.8 us: lines_plan(): lax.ppermute(piece, 'cols', [(c, c ^ hop) for c in range(n)])]
    pallas_call x4 -> x12, Pallas kernels: 8.46 us -> 6.34 us  [call(): pl.pallas_call(kernel, out_shape=[jax.ShapeDtypeStruct(shape, dtype) for...]
    unnamed x8 -> x10, local copies, waits for them, and re-layouts: 2.44 us -> 1.06 us
  transfers between devices with their start and end apart: 3 -> 9, of which waited for: 2 -> 5; matrix products, arithmetic and copies ran while one was open for 0% -> 0% of each run, Pallas kernels for 7% -> 13%
where the time goes in v12:
time: 27 us; the launch traced here: 26.8 us
  starting transfers between devices  12.3 us (46%)
  Pallas kernels  6.34 us (23%)
  waiting for transfers between devices  6.33 us (23%)
  local copies, waits for them, and re-layouts  1.06 us (4%)
  other arithmetic  0.62 us (2%)
    ppermute x7, starting transfers between devices, lines_plan(): lax.ppermute(piece, 'cols', [(c, c ^ hop) for c in range(n)])  11.8 us
    pallas_call x12, Pallas kernels, call(): pl.pallas_call(kernel, out_shape=[jax.ShapeDtypeStruct(shape, dtype) for...  6.34 us
    ppermute x7, waiting for transfers between devices, lines_plan(): lax.ppermute(piece, 'cols', [(c, c ^ hop) for c in range(n)])  4.48 us
    ppermute x1, waiting for transfers between devices, lines_plan(): others = lax.ppermute(rows, 'view', [(0, 1), (1, 0)])  1.15 us
    unnamed x10, local copies, waits for them, and re-layouts  1.06 us
    ppermute x1, waiting for transfers between devices, lines_plan(): other = lax.ppermute(own, 'view', [(0, 1), (1, 0)])  0.7 us
    select_n x1, other arithmetic, lines_plan(): jnp.where(first, jnp.concatenate([rows, others]), jnp.concatenate([others...  0.62 us
  transfers between devices with their start and end apart: 9, of which 5 were waited for; matrix products, arithmetic and copies ran while one was open for 0% of the time, Pallas kernels for 13%

profile of v12, /device:TPU:0, one launch (start us, length us, event | category | flops | bytes accessed | tf_op | source)
XLA Modules:
  0.0 26.8 jit_solution(2175682848890496490)
XLA Ops:
  0.0 0.5 %collective-permute-start = (bf16[8,128,256]{2,1,0:T(8,128)(2,1)}, bf16[8,128,256]{2,1,0:T(8,128)(2,1)S(1)}, u32[]{:S(2)}, u32[]{:S(2)}) collective-permute-start(bf16[8,128,256]{2,1,0:T(8,128)(2,1)} %bitcast.3), channel_id=1, source_target_pairs={{0,1},{1,0},{2,3},{3,2},{4,5},{5,4},{6,7},{7,6},{8,9},{9,8},{10,11... | collective-permute-start | bytes 1572872 | tf_op jit(solution)/shard_map/ppermute | solution.py:586
  0.5 1.0 %copy-done = bf16[1,16,64,256]{3,2,1,0:T(8,128)(2,1)S(1)} copy-done((bf16[1,16,64,256]{3,2,1,0:T(8,128)(2,1)S(1)}, bf16[1,16,64,256]{3,2,1,0:T(8,128)(2,1)}, u32[]{:S(2)}) %copy-start) | copy-done | bytes 524312
  1.5 0.7 %collective-permute-done.rest_0_ = bf16[8,128,256]{2,1,0:T(8,128)(2,1)S(1)} collective-permute-done((bf16[8,128,256]{2,1,0:T(8,128)(2,1)}, bf16[8,128,256]{2,1,0:T(8,128)(2,1)S(1)}, u32[]{:S(2)}, u32[]{:S(2)}) %collective-permute-start) | collective-permute-done | bytes 524320 | tf_op jit(solution)/shard_map/ppermute | solution.py:586
  2.2 0.0 copy-start.3
  2.3 0.0 copy-start.4
  2.3 0.0 copy-start.1
  2.3 3.0 %collective-permute-start.5 = (bf16[136,256]{1,0:T(8,128)(2,1)S(1)}, bf16[136,256]{1,0:T(8,128)(2,1)S(1)}, u32[]{:S(2)}, u32[]{:S(2)}) collective-permute-start(bf16[136,256]{1,0:T(8,128)(2,1)S(1)} %shard_map.50.rest_1_), channel_id=1, source_target_pairs={{0,4},{4,0},{8,12},{12,8},{1,5},{5,1},{9,13},{13,9},{2,6},{6,2},{1... | collective-permute-start | bytes 208904 | tf_op jit(solution)/shard_map/ppermute | solution.py:600
  5.3 2.5 %collective-permute-start.7 = (bf16[136,256]{1,0:T(8,128)(2,1)S(1)}, bf16[136,256]{1,0:T(8,128)(2,1)S(1)}, u32[]{:S(2)}, u32[]{:S(2)}) collective-permute-start(bf16[136,256]{1,0:T(8,128)(2,1)S(1)} %shard_map.48.rest_2_), channel_id=1, source_target_pairs={{0,12},{4,8},{8,4},{12,0},{1,13},{5,9},{9,5},{13,1},{2,14},{6,10},... | collective-permute-start | bytes 208904 | tf_op jit(solution)/shard_map/ppermute | solution.py:600
  7.8 0.1 collective-permute-start.2
  7.9 2.8 %collective-permute-start.6 = (bf16[72,256]{1,0:T(8,128)(2,1)S(1)}, bf16[72,256]{1,0:T(8,128)(2,1)S(1)}, u32[]{:S(2)}, u32[]{:S(2)}) collective-permute-start(bf16[72,256]{1,0:T(8,128)(2,1)S(1)} %shard_map.49.rest_2_), channel_id=1, source_target_pairs={{0,8},{4,12},{8,0},{12,4},{1,9},{5,13},{9,1},{13,5},{2,10},{6,14},... | collective-permute-start | bytes 110600 | tf_op jit(solution)/shard_map/ppermute | solution.py:600
  10.7 0.8 %shard_map.46 = (bf16[128,128]{1,0:T(8,128)(2,1)S(1)}, bf16[192,256]{1,0:T(8,128)(2,1)S(1)}, bf16[120,128]{1,0:T(8,128)(2,1)S(1)}, bf16[128,1024]{1,0:T(8,128)(2,1)S(1)}) custom-call(s32[16]{0:T(128)S(1)} %copy-done.4, bf16[64,108]{1,0:T(8,128)(2,1)S(1)} %copy-done.3), custom_call_target="tpu_custom_call" | custom-call | flops 1000000 | bytes 1000000 | tf_op jit(solution)/shard_map/pallas_call | solution.py:50
  11.6 0.7 %collective-permute-start.1 = (bf16[128,256]{1,0:T(8,128)(2,1)S(1)}, bf16[128,256]{1,0:T(8,128)(2,1)S(1)}, u32[]{:S(2)}, u32[]{:S(2)}) collective-permute-start(bf16[128,256]{1,0:T(8,128)(2,1)S(1)} %shard_map.53.rest_1_), channel_id=1, source_target_pairs={{0,4},{4,0},{8,12},{12,8},{1,5},{5,1},{9,13},{13,9},{2,6},{6,2},{1... | collective-permute-start | bytes 196616 | tf_op jit(solution)/shard_map/ppermute | solution.py:600
  12.4 2.9 %collective-permute-done.2.two = bf16[128,256]{1,0:T(8,128)(2,1)S(1)} collective-permute-done((bf16[128,256]{1,0:T(8,128)(2,1)S(1)}, bf16[128,256]{1,0:T(8,128)(2,1)S(1)}, u32[]{:S(2)}, u32[]{:S(2)}) %collective-permute-start.2) | collective-permute-done | bytes 65568 | tf_op jit(solution)/shard_map/ppermute | solution.py:600
  15.3 0.0 collective-permute-start.3
  15.3 0.8 %collective-permute-done.6.two_more = bf16[72,256]{1,0:T(8,128)(2,1)S(1)} collective-permute-done((bf16[72,256]{1,0:T(8,128)(2,1)S(1)}, bf16[72,256]{1,0:T(8,128)(2,1)S(1)}, u32[]{:S(2)}, u32[]{:S(2)}) %collective-permute-start.6) | collective-permute-done | bytes 36896 | tf_op jit(solution)/shard_map/ppermute | solution.py:600
  16.1 2.6 %collective-permute-start.4 = (bf16[128,256]{1,0:T(8,128)(2,1)S(1)}, bf16[128,256]{1,0:T(8,128)(2,1)S(1)}, u32[]{:S(2)}, u32[]{:S(2)}) collective-permute-start(bf16[128,256]{1,0:T(8,128)(2,1)S(1)} %shard_map.51.rest_1_), channel_id=1, source_target_pairs={{0,12},{4,8},{8,4},{12,0},{1,13},{5,9},{9,5},{13,1},{2,14},{6,10},... | collective-permute-start | bytes 196616 | tf_op jit(solution)/shard_map/ppermute | solution.py:600
  18.8 0.0 collective-permute-done.5.one
  18.8 0.0 collective-permute-done.7.three
  18.8 2.7 %shard_map.56 = (f32[1,1024]{1,0:T(1,128)S(1)}, f32[4,2,256]{2,1,0:T(2,128)S(1)}) custom-call(s32[16]{0:T(128)S(1)} %copy-done.4, bf16[128,128]{1,0:T(8,128)(2,1)S(1)} %get-tuple-element.11.order, bf16[192,256]{1,0:T(8,128)(2,1)S(1)} %get-tuple-element.12.flip, bf16[120,128]{1,0:T(8,128)(2,1)S(1)} %get-tuple-element.13.guide, ...), custom_call_target="tpu_custom_call" | custom-call | flops 1000000000 | bytes 1000000 | tf_op jit(solution)/shard_map/pallas_call | solution.py:50
  21.5 0.7 %collective-permute-done.4.three = bf16[128,256]{1,0:T(8,128)(2,1)S(1)} collective-permute-done((bf16[128,256]{1,0:T(8,128)(2,1)S(1)}, bf16[128,256]{1,0:T(8,128)(2,1)S(1)}, u32[]{:S(2)}, u32[]{:S(2)}) %collective-permute-start.4) | collective-permute-done | bytes 65568 | tf_op jit(solution)/shard_map/ppermute | solution.py:600
  22.2 2.7 %shard_map.57 = f32[2,1024]{1,0:T(2,128)S(1)} custom-call(s32[16]{0:T(128)S(1)} %copy-done.4, bf16[128,128]{1,0:T(8,128)(2,1)S(1)} %get-tuple-element.11.order, bf16[192,256]{1,0:T(8,128)(2,1)S(1)} %get-tuple-element.12.flip, bf16[120,128]{1,0:T(8,128)(2,1)S(1)} %get-tuple-element.13.guide, bf16[128,1024]{1,0:T(8,128)(2,1)S(1)} %get-tuple-element.14.spread, ...), custom_call_target="tpu_custom_call" | custom-call | flops 1000000000 | bytes 1000000 | tf_op jit(solution)/shard_map/pallas_call | solution.py:50
  24.9 0.1 collective-permute-start.8
  25.0 1.2 %collective-permute-done.8 = f32[2,1024]{1,0:T(2,128)S(1)} collective-permute-done((f32[2,1024]{1,0:T(2,128)S(1)}, f32[2,1024]{1,0:T(2,128)S(1)}, u32[]{:S(2)}, u32[]{:S(2)}) %collective-permute-start.8) | collective-permute-done | bytes 8224 | tf_op jit(solution)/shard_map/ppermute | solution.py:626
  26.2 0.6 %maximum_select_fusion = f32[1,4,1024]{2,1,0:T(4,128)} fusion(f32[1,2,1024]{2,1,0:T(2,128)S(1)} %bitcast.14, f32[1,2,1024]{2,1,0:T(2,128)S(1)} %bitcast.13, pred[]{:T(512)S(6)} %eq.3), kind=kLoop, calls=%fused_computation | loop fusion | flops 12288 | bytes 32769 | tf_op jit(solution)/shard_map/jit(_where)/select_n | solution.py:628
  (17 shorter events, 0.2 us)
Async XLA Ops:
  0.0 2.2 %collective-permute-start = (bf16[8,128,256]{2,1,0:T(8,128)(2,1)}, bf16[8,128,256]{2,1,0:T(8,128)(2,1)S(1)}, u32[]{:S(2)}, u32[]{:S(2)}) collective-permute-start(bf16[8,128,256]{2,1,0:T(8,128)(2,1)} %bitcast.3), channel_id=1, source_target_pairs={{0,1},{1,0},{2,3},{3,2},{4,5},{5,4},{6,7},{7,6},{8,9},{9,8},{10,11... | collective-permute-start | bytes 1572872 | tf_op jit(solution)/shard_map/ppermute | solution.py:586
  0.5 1.0 %copy-start = (bf16[1,16,64,256]{3,2,1,0:T(8,128)(2,1)S(1)}, bf16[1,16,64,256]{3,2,1,0:T(8,128)(2,1)}, u32[]{:S(2)}) copy-start(bf16[1,16,64,256]{3,2,1,0:T(8,128)(2,1)} %param.4) | copy-start | bytes 1572868
  1.5 0.7 %copy-start.2 = (s32[2,256]{1,0:T(2,128)S(1)}, s32[2,256]{1,0:T(2,128)}, u32[]{:S(2)}) copy-start(s32[2,256]{1,0:T(2,128)} %masks.1) | copy-start | bytes 6148
  2.2 8.5 %copy-start.3 = (bf16[64,108]{1,0:T(8,128)(2,1)S(1)}, bf16[64,108]{1,0:T(8,128)(2,1)}, u32[]{:S(2)}) copy-start(bf16[64,108]{1,0:T(8,128)(2,1)} %guide.1) | copy-start | bytes 41476
  2.3 8.5 %copy-start.4 = (s32[16]{0:T(128)S(1)}, s32[16]{0:T(128)}, u32[]{:S(2)}) copy-start(s32[16]{0:T(128)} %offsets.5) | copy-start | bytes 196
  2.3 9.3 %copy-start.1 = (bf16[1,16,64,256]{3,2,1,0:T(8,128)(2,1)S(1)}, bf16[1,16,64,256]{3,2,1,0:T(8,128)(2,1)}, u32[]{:S(2)}) copy-start(bf16[1,16,64,256]{3,2,1,0:T(8,128)(2,1)} %param.4) | copy-start | bytes 1572868
  2.3 16.5 %collective-permute-start.5 = (bf16[136,256]{1,0:T(8,128)(2,1)S(1)}, bf16[136,256]{1,0:T(8,128)(2,1)S(1)}, u32[]{:S(2)}, u32[]{:S(2)}) collective-permute-start(bf16[136,256]{1,0:T(8,128)(2,1)S(1)} %shard_map.50.rest_1_), channel_id=1, source_target_pairs={{0,4},{4,0},{8,12},{12,8},{1,5},{5,1},{9,13},{13,9},{2,6},{6,2},{1... | collective-permute-start | bytes 208904 | tf_op jit(solution)/shard_map/ppermute | solution.py:600
  5.3 13.5 %collective-permute-start.7 = (bf16[136,256]{1,0:T(8,128)(2,1)S(1)}, bf16[136,256]{1,0:T(8,128)(2,1)S(1)}, u32[]{:S(2)}, u32[]{:S(2)}) collective-permute-start(bf16[136,256]{1,0:T(8,128)(2,1)S(1)} %shard_map.48.rest_2_), channel_id=1, source_target_pairs={{0,12},{4,8},{8,4},{12,0},{1,13},{5,9},{9,5},{13,1},{2,14},{6,10},... | collective-permute-start | bytes 208904 | tf_op jit(solution)/shard_map/ppermute | solution.py:600
  7.8 7.5 %collective-permute-start.2 = (bf16[128,256]{1,0:T(8,128)(2,1)S(1)}, bf16[128,256]{1,0:T(8,128)(2,1)S(1)}, u32[]{:S(2)}, u32[]{:S(2)}) collective-permute-start(bf16[128,256]{1,0:T(8,128)(2,1)S(1)} %shard_map.47.rest_2_), channel_id=1, source_target_pairs={{0,8},{4,12},{8,0},{12,4},{1,9},{5,13},{9,1},{13,5},{2,10},{6,14},... | collective-permute-start | bytes 196616 | tf_op jit(solution)/shard_map/ppermute | solution.py:600
  7.9 8.2 %collective-permute-start.6 = (bf16[72,256]{1,0:T(8,128)(2,1)S(1)}, bf16[72,256]{1,0:T(8,128)(2,1)S(1)}, u32[]{:S(2)}, u32[]{:S(2)}) collective-permute-start(bf16[72,256]{1,0:T(8,128)(2,1)S(1)} %shard_map.49.rest_2_), channel_id=1, source_target_pairs={{0,8},{4,12},{8,0},{12,4},{1,9},{5,13},{9,1},{13,5},{2,10},{6,14},... | collective-permute-start | bytes 110600 | tf_op jit(solution)/shard_map/ppermute | solution.py:600
  11.6 9.9 %collective-permute-start.1 = (bf16[128,256]{1,0:T(8,128)(2,1)S(1)}, bf16[128,256]{1,0:T(8,128)(2,1)S(1)}, u32[]{:S(2)}, u32[]{:S(2)}) collective-permute-start(bf16[128,256]{1,0:T(8,128)(2,1)S(1)} %shard_map.53.rest_1_), channel_id=1, source_target_pairs={{0,4},{4,0},{8,12},{12,8},{1,5},{5,1},{9,13},{13,9},{2,6},{6,2},{1... | collective-permute-start | bytes 196616 | tf_op jit(solution)/shard_map/ppermute | solution.py:600
  15.3 6.1 %collective-permute-start.3 = (bf16[64,256]{1,0:T(8,128)(2,1)S(1)}, bf16[64,256]{1,0:T(8,128)(2,1)S(1)}, u32[]{:S(2)}, u32[]{:S(2)}) collective-permute-start(bf16[64,256]{1,0:T(8,128)(2,1)S(1)} %shard_map.52.rest_1_), channel_id=1, source_target_pairs={{0,8},{4,12},{8,0},{12,4},{1,9},{5,13},{9,1},{13,5},{2,10},{6,14},... | collective-permute-start | bytes 98312 | tf_op jit(solution)/shard_map/ppermute | solution.py:600
  16.1 6.1 %collective-permute-start.4 = (bf16[128,256]{1,0:T(8,128)(2,1)S(1)}, bf16[128,256]{1,0:T(8,128)(2,1)S(1)}, u32[]{:S(2)}, u32[]{:S(2)}) collective-permute-start(bf16[128,256]{1,0:T(8,128)(2,1)S(1)} %shard_map.51.rest_1_), channel_id=1, source_target_pairs={{0,12},{4,8},{8,4},{12,0},{1,13},{5,9},{9,5},{13,1},{2,14},{6,10},... | collective-permute-start | bytes 196616 | tf_op jit(solution)/shard_map/ppermute | solution.py:600
  24.9 1.2 %collective-permute-start.8 = (f32[2,1024]{1,0:T(2,128)S(1)}, f32[2,1024]{1,0:T(2,128)S(1)}, u32[]{:S(2)}, u32[]{:S(2)}) collective-permute-start(f32[2,1024]{1,0:T(2,128)S(1)} %shard_map.57), channel_id=1, source_target_pairs={{0,1},{1,0},{2,3},{3,2},{4,5},{5,4},{6,7},{7,6},{8,9},{9,8},{10,11... | collective-permute-start | bytes 24584 | tf_op jit(solution)/shard_map/ppermute | solution.py:626

commit v13 on v11

--- a/solution.py
+++ b/solution.py
@@ -427,7 +427,7 @@
     at = PAIR * me
     offs = [offsets[at + i] for i in range(PAIR)]
     ch_lane = iota((CHANNELS, LANES), 1)
-    diagonal = iota((8, LANES), 1) - LINE_RUN * iota((8, LANES), 0)
+    reached = iota((8, LANES), 1) + LINE_RUN * iota((8, LANES), 0)
     low_half = iota((LANES, LANES), 1) < CHANNELS
     scale = 1.0 / math.sqrt(CHANNELS)
     empty = jnp.zeros((CHANNELS, LANES), F32)
@@ -472,19 +472,19 @@
                     gate_rows[row : row + 16, :] = jnp.concatenate(
                         [gates[1][r : r + 8], gates[0][r : r + 8]], axis=0
                     ).astype(BF)
-                    beyond = diagonal >= t
+                    within = reached < LANES - t
                     both = []
                     for side in (1, 0):
-                        turned = [
-                            pltpu.roll(
-                                products[side][r : r + 8, m * LANES : (m + 1) * LANES],
-                                t, 1, stride=LINE_RUN, stride_axis=0,
-                            )
-                            for m in range(3)
-                        ]
+                        part = [products[side][r : r + 8, m * LANES : (m + 1) * LANES] for m in range(3)]
                         both.append(
                             jnp.concatenate(
-                                [jnp.where(beyond, turned[1], turned[0]), jnp.where(beyond, turned[2], turned[1])],
+                                [
+                                    pltpu.roll(
+                                        jnp.where(within, part[m + 1], part[m]),
+                                        t, 1, stride=LINE_RUN, stride_axis=0,
+                                    )
+                                    for m in range(2)
+                                ],
                                 axis=1,
                             )
                         )
@@ -586,6 +586,11 @@
     gone = ()
     for key in (1, 2, 6, 4, 7, 5, 3, 0):
         masked = key % 2 and key > 1
+        if key in (4, 6):
+            me = 2 * lax.axis_index("cols") + lax.axis_index("view")
+            piece = lax.dynamic_index_in_dim(own, me ^ key, 0, False)
+            pieces[key] = lax.ppermute(piece, ("cols", "view"), [(i, i ^ key) for i in range(devices)])
+            continue
         (piece,) = call(
             functools.partial(pack_kernel, key),
             [((rows + (MASKS if masked else 0), BLOCK), BF)],

time: 22.1 us -> 25.5 us (1.15)
  waiting for transfers between devices: 4.67 us -> 8.14 us
  local copies, waits for them, and re-layouts: 1.07 us -> 1.74 us
  starting transfers between devices: 10.5 us -> 9.95 us
    ppermute x0 -> x2, waiting for transfers between devices: none -> 6.97 us  [lines_plan(): lax.ppermute(piece, ('cols', 'view'), [(i, i ^ key) for i in range(device...]
    ppermute x7 -> x5, waiting for transfers between devices: 3.82 us -> 0.01 us  [lines_plan(): pieces[key] = lax.ppermute(piece, ('cols', 'view'), moves) if key else piece]
    ppermute x7 -> x5, starting transfers between devices: 10.1 us -> 7.26 us  [lines_plan(): pieces[key] = lax.ppermute(piece, ('cols', 'view'), moves) if key else piece]
    ppermute x0 -> x2, starting transfers between devices: none -> 2.62 us  [lines_plan(): lax.ppermute(piece, ('cols', 'view'), [(i, i ^ key) for i in range(device...]
    unnamed x10, local copies, waits for them, and re-layouts: 1.07 us -> 1.73 us
    ppermute x1, starting transfers between devices: 0.38 us -> 0.07 us  [lines_plan(): others = lax.ppermute(rows, 'view', [(0, 1), (1, 0)])]
    ppermute x1, waiting for transfers between devices: 0.86 us -> 1.15 us  [lines_plan(): others = lax.ppermute(rows, 'view', [(0, 1), (1, 0)])]
    pallas_call x10 -> x8, Pallas kernels: 4.81 us -> 4.75 us  [call(): pl.pallas_call(kernel, out_shape=[jax.ShapeDtypeStruct(shape, dtype) for...]
  transfers between devices with their start and end apart: 8 -> 8, of which waited for: 3 -> 3; matrix products, arithmetic and copies ran while one was open for 0% -> 0% of each run, Pallas kernels for 4% -> 3%
where the time goes in v13:
time: 25.5 us; the launch traced here: 25.3 us
  starting transfers between devices  9.95 us (39%)
  waiting for transfers between devices  8.14 us (32%)
  Pallas kernels  4.75 us (19%)
  local copies, waits for them, and re-layouts  1.74 us (7%)
  other arithmetic  0.62 us (2%)
    ppermute x5, starting transfers between devices, lines_plan(): pieces[key] = lax.ppermute(piece, ('cols', 'view'), moves) if key else piece  7.26 us
    ppermute x2, waiting for transfers between devices, lines_plan(): lax.ppermute(piece, ('cols', 'view'), [(i, i ^ key) for i in range(device...  6.97 us
    pallas_call x8, Pallas kernels, call(): pl.pallas_call(kernel, out_shape=[jax.ShapeDtypeStruct(shape, dtype) for...  4.75 us
    ppermute x2, starting transfers between devices, lines_plan(): lax.ppermute(piece, ('cols', 'view'), [(i, i ^ key) for i in range(device...  2.62 us
    unnamed x10, local copies, waits for them, and re-layouts  1.73 us
    ppermute x1, waiting for transfers between devices, lines_plan(): others = lax.ppermute(rows, 'view', [(0, 1), (1, 0)])  1.15 us
    select_n x1, other arithmetic, lines_plan(): jnp.where(first, jnp.concatenate([rows, others]), jnp.concatenate([others...  0.62 us
  transfers between devices with their start and end apart: 8, of which 3 were waited for; matrix products, arithmetic and copies ran while one was open for 0% of the time, Pallas kernels for 3%

profile of v13, /device:TPU:0, one launch (start us, length us, event | category | flops | bytes accessed | tf_op | source)
XLA Modules:
  0.0 25.3 jit_solution(10995409602856769973)
XLA Ops:
  0.0 1.0 %copy-done = bf16[1,16,64,256]{3,2,1,0:T(8,128)(2,1)S(1)} copy-done((bf16[1,16,64,256]{3,2,1,0:T(8,128)(2,1)S(1)}, bf16[1,16,64,256]{3,2,1,0:T(8,128)(2,1)}, u32[]{:S(2)}) %copy-start) | copy-done | bytes 524312
  1.1 0.5 %collective-permute-start = (bf16[128,256]{1,0:T(8,128)(2,1)S(1)}, bf16[128,256]{1,0:T(8,128)(2,1)S(1)}, u32[]{:S(2)}, u32[]{:S(2)}) collective-permute-start(bf16[128,256]{1,0:T(8,128)(2,1)S(1)} %shard_map.47.rest_0_), channel_id=1, source_target_pairs={{0,1},{1,0},{4,5},{5,4},{8,9},{9,8},{12,13},{13,12},{2,3},{3,2},{6... | collective-permute-start | bytes 196616 | tf_op jit(solution)/shard_map/ppermute | solution.py:603
  1.6 2.7 %collective-permute-start.1 = (bf16[128,256]{1,0:T(8,128)(2,1)S(1)}, bf16[128,256]{1,0:T(8,128)(2,1)S(1)}, u32[]{:S(2)}, u32[]{:S(2)}) collective-permute-start(bf16[128,256]{1,0:T(8,128)(2,1)S(1)} %shard_map.48.rest_1_), channel_id=1, source_target_pairs={{0,4},{1,5},{4,0},{5,1},{8,12},{9,13},{12,8},{13,9},{2,6},{3,7},{6... | collective-permute-start | bytes 196616 | tf_op jit(solution)/shard_map/ppermute | solution.py:603
  4.3 0.0 copy-done.1
  4.3 0.0 copy-done.2
  4.3 2.4 %collective-permute-start.6 = (bf16[136,256]{1,0:T(8,128)(2,1)S(1)}, bf16[136,256]{1,0:T(8,128)(2,1)S(1)}, u32[]{:S(2)}, u32[]{:S(2)}) collective-permute-start(bf16[136,256]{1,0:T(8,128)(2,1)S(1)} %shard_map.49.rest_1_), channel_id=1, source_target_pairs={{0,13},{1,12},{4,9},{5,8},{8,5},{9,4},{12,1},{13,0},{2,15},{3,14},... | collective-permute-start | bytes 208904 | tf_op jit(solution)/shard_map/ppermute | solution.py:603
  6.7 0.1 collective-permute-start.4
  6.8 1.6 %collective-permute-start.2 = (bf16[136,256]{1,0:T(8,128)(2,1)S(1)}, bf16[136,256]{1,0:T(8,128)(2,1)S(1)}, u32[]{:S(2)}, u32[]{:S(2)}) collective-permute-start(bf16[136,256]{1,0:T(8,128)(2,1)S(1)} %shard_map.51.rest_0_), channel_id=1, source_target_pairs={{0,5},{1,4},{4,1},{5,0},{8,13},{9,12},{12,9},{13,8},{2,7},{3,6},{6... | collective-permute-start | bytes 208904 | tf_op jit(solution)/shard_map/ppermute | solution.py:603
  8.4 0.0 collective-permute-done.1.rest_3_
  8.4 2.6 %collective-permute-start.5 = (bf16[128,256]{1,0:T(8,128)(2,1)S(1)}, bf16[128,256]{1,0:T(8,128)(2,1)S(1)}, u32[]{:S(2)}, u32[]{:S(2)}) collective-permute-start(bf16[128,256]{1,0:T(8,128)(2,1)S(1)} %get-tuple-element.15), channel_id=1, source_target_pairs={{0,12},{1,13},{4,8},{5,9},{8,4},{9,5},{12,0},{13,1},{2,14},{3,15},... | collective-permute-start | bytes 196616 | tf_op jit(solution)/shard_map/ppermute | solution.py:592
  11.0 0.0 collective-permute-done.rest_2_
  11.0 0.0 collective-permute-start.3
  11.1 0.7 %copy-done.3 = bf16[64,108]{1,0:T(8,128)(2,1)S(1)} copy-done((bf16[64,108]{1,0:T(8,128)(2,1)S(1)}, bf16[64,108]{1,0:T(8,128)(2,1)}, u32[]{:S(2)}) %copy-start.3) | copy-done | bytes 13848
  11.7 0.0 copy-done.4
  11.7 0.8 %shard_map.46 = (bf16[128,128]{1,0:T(8,128)(2,1)S(1)}, bf16[192,256]{1,0:T(8,128)(2,1)S(1)}, bf16[120,128]{1,0:T(8,128)(2,1)S(1)}, bf16[128,1024]{1,0:T(8,128)(2,1)S(1)}, f32[2,256]{1,0:T(2,128)S(1)}) custom-call(s32[16]{0:T(128)S(1)} %copy-done.4, bf16[64,108]{1,0:T(8,128)(2,1)S(1)} %copy-done.3, s32[2,256]{1,0:T(2,128)S(1)} %copy-done.2), custom_call_target="tpu_custom_call" | custom-call | flops 1000000 | bytes 1000000 | tf_op jit(solution)/shard_map/pallas_call | solution.py:50
  12.5 2.9 %collective-permute-done.5.rest_7_ = bf16[128,256]{1,0:T(8,128)(2,1)S(1)} collective-permute-done((bf16[128,256]{1,0:T(8,128)(2,1)S(1)}, bf16[128,256]{1,0:T(8,128)(2,1)S(1)}, u32[]{:S(2)}, u32[]{:S(2)}) %collective-permute-start.5) | collective-permute-done | bytes 65568 | tf_op jit(solution)/shard_map/ppermute | solution.py:592
  15.5 4.1 %collective-permute-done.3.rest_5_ = bf16[128,256]{1,0:T(8,128)(2,1)S(1)} collective-permute-done((bf16[128,256]{1,0:T(8,128)(2,1)S(1)}, bf16[128,256]{1,0:T(8,128)(2,1)S(1)}, u32[]{:S(2)}, u32[]{:S(2)}) %collective-permute-start.3) | collective-permute-done | bytes 65568 | tf_op jit(solution)/shard_map/ppermute | solution.py:592
  19.5 0.0 collective-permute-done.2.rest_4_
  19.5 0.0 collective-permute-done.4.rest_6_
  19.5 0.0 collective-permute-done.6.rest_8_
  19.5 3.9 %shard_map.53 = f32[2,1024]{1,0:T(2,128)S(1)} custom-call(s32[16]{0:T(128)S(1)} %copy-done.4, bf16[128,128]{1,0:T(8,128)(2,1)S(1)} %get-tuple-element.10.order, bf16[192,256]{1,0:T(8,128)(2,1)S(1)} %get-tuple-element.11.flip, bf16[120,128]{1,0:T(8,128)(2,1)S(1)} %get-tuple-element.12.guide, bf16[128,1024]{1,0:T(8,128)(2,1)S(1)} %get-tuple-element.13.spread, ...), custom_call_target="tpu_custom_call" | custom-call | flops 1000000000 | bytes 1000000 | tf_op jit(solution)/shard_map/pallas_call | solution.py:50
  23.4 0.1 collective-permute-start.7
  23.5 1.2 %collective-permute-done.7 = f32[2,1024]{1,0:T(2,128)S(1)} collective-permute-done((f32[2,1024]{1,0:T(2,128)S(1)}, f32[2,1024]{1,0:T(2,128)S(1)}, u32[]{:S(2)}, u32[]{:S(2)}) %collective-permute-start.7) | collective-permute-done | bytes 8224 | tf_op jit(solution)/shard_map/ppermute | solution.py:626
  24.7 0.6 %maximum_select_fusion = f32[1,4,1024]{2,1,0:T(4,128)} fusion(f32[1,2,1024]{2,1,0:T(2,128)S(1)} %bitcast.15, f32[1,2,1024]{2,1,0:T(2,128)S(1)} %bitcast.14, pred[]{:T(512)S(6)} %eq.3), kind=kLoop, calls=%fused_computation.2 | loop fusion | flops 12288 | bytes 32769 | tf_op jit(solution)/shard_map/jit(_where)/select_n | solution.py:628
  (12 shorter events, 0.1 us)
Async XLA Ops:
  0.0 1.0 %copy-start = (bf16[1,16,64,256]{3,2,1,0:T(8,128)(2,1)S(1)}, bf16[1,16,64,256]{3,2,1,0:T(8,128)(2,1)}, u32[]{:S(2)}) copy-start(bf16[1,16,64,256]{3,2,1,0:T(8,128)(2,1)} %param.4) | copy-start | bytes 1572868
  1.0 3.2 %copy-start.1 = (bf16[1,16,64,256]{3,2,1,0:T(8,128)(2,1)S(1)}, bf16[1,16,64,256]{3,2,1,0:T(8,128)(2,1)}, u32[]{:S(2)}) copy-start(bf16[1,16,64,256]{3,2,1,0:T(8,128)(2,1)} %param.4) | copy-start | bytes 1572868
  1.1 3.2 %copy-start.2 = (s32[2,256]{1,0:T(2,128)S(1)}, s32[2,256]{1,0:T(2,128)}, u32[]{:S(2)}) copy-start(s32[2,256]{1,0:T(2,128)} %rest_0_.5) | copy-start | bytes 6148
  1.1 10.0 %collective-permute-start = (bf16[128,256]{1,0:T(8,128)(2,1)S(1)}, bf16[128,256]{1,0:T(8,128)(2,1)S(1)}, u32[]{:S(2)}, u32[]{:S(2)}) collective-permute-start(bf16[128,256]{1,0:T(8,128)(2,1)S(1)} %shard_map.47.rest_0_), channel_id=1, source_target_pairs={{0,1},{1,0},{4,5},{5,4},{8,9},{9,8},{12,13},{13,12},{2,3},{3,2},{6... | collective-permute-start | bytes 196616 | tf_op jit(solution)/shard_map/ppermute | solution.py:603
  1.6 6.8 %collective-permute-start.1 = (bf16[128,256]{1,0:T(8,128)(2,1)S(1)}, bf16[128,256]{1,0:T(8,128)(2,1)S(1)}, u32[]{:S(2)}, u32[]{:S(2)}) collective-permute-start(bf16[128,256]{1,0:T(8,128)(2,1)S(1)} %shard_map.48.rest_1_), channel_id=1, source_target_pairs={{0,4},{1,5},{4,0},{5,1},{8,12},{9,13},{12,8},{13,9},{2,6},{3,7},{6... | collective-permute-start | bytes 196616 | tf_op jit(solution)/shard_map/ppermute | solution.py:603
  4.3 15.3 %collective-permute-start.6 = (bf16[136,256]{1,0:T(8,128)(2,1)S(1)}, bf16[136,256]{1,0:T(8,128)(2,1)S(1)}, u32[]{:S(2)}, u32[]{:S(2)}) collective-permute-start(bf16[136,256]{1,0:T(8,128)(2,1)S(1)} %shard_map.49.rest_1_), channel_id=1, source_target_pairs={{0,13},{1,12},{4,9},{5,8},{8,5},{9,4},{12,1},{13,0},{2,15},{3,14},... | collective-permute-start | bytes 208904 | tf_op jit(solution)/shard_map/ppermute | solution.py:603
  6.7 12.9 %collective-permute-start.4 = (bf16[136,256]{1,0:T(8,128)(2,1)S(1)}, bf16[136,256]{1,0:T(8,128)(2,1)S(1)}, u32[]{:S(2)}, u32[]{:S(2)}) collective-permute-start(bf16[136,256]{1,0:T(8,128)(2,1)S(1)} %shard_map.50.rest_1_), channel_id=1, source_target_pairs={{0,9},{1,8},{4,13},{5,12},{8,1},{9,0},{12,5},{13,4},{2,11},{3,10},... | collective-permute-start | bytes 208904 | tf_op jit(solution)/shard_map/ppermute | solution.py:603
  6.8 12.7 %collective-permute-start.2 = (bf16[136,256]{1,0:T(8,128)(2,1)S(1)}, bf16[136,256]{1,0:T(8,128)(2,1)S(1)}, u32[]{:S(2)}, u32[]{:S(2)}) collective-permute-start(bf16[136,256]{1,0:T(8,128)(2,1)S(1)} %shard_map.51.rest_0_), channel_id=1, source_target_pairs={{0,5},{1,4},{4,1},{5,0},{8,13},{9,12},{12,9},{13,8},{2,7},{3,6},{6... | collective-permute-start | bytes 208904 | tf_op jit(solution)/shard_map/ppermute | solution.py:603
  8.4 7.1 %collective-permute-start.5 = (bf16[128,256]{1,0:T(8,128)(2,1)S(1)}, bf16[128,256]{1,0:T(8,128)(2,1)S(1)}, u32[]{:S(2)}, u32[]{:S(2)}) collective-permute-start(bf16[128,256]{1,0:T(8,128)(2,1)S(1)} %get-tuple-element.15), channel_id=1, source_target_pairs={{0,12},{1,13},{4,8},{5,9},{8,4},{9,5},{12,0},{13,1},{2,14},{3,15},... | collective-permute-start | bytes 196616 | tf_op jit(solution)/shard_map/ppermute | solution.py:592
  11.0 0.7 %copy-start.3 = (bf16[64,108]{1,0:T(8,128)(2,1)S(1)}, bf16[64,108]{1,0:T(8,128)(2,1)}, u32[]{:S(2)}) copy-start(bf16[64,108]{1,0:T(8,128)(2,1)} %guide.1) | copy-start | bytes 41476
  11.0 0.7 %copy-start.4 = (s32[16]{0:T(128)S(1)}, s32[16]{0:T(128)}, u32[]{:S(2)}) copy-start(s32[16]{0:T(128)} %offsets.3) | copy-start | bytes 196
  11.0 8.5 %collective-permute-start.3 = (bf16[128,256]{1,0:T(8,128)(2,1)S(1)}, bf16[128,256]{1,0:T(8,128)(2,1)S(1)}, u32[]{:S(2)}, u32[]{:S(2)}) collective-permute-start(bf16[128,256]{1,0:T(8,128)(2,1)S(1)} %get-tuple-element.16), channel_id=1, source_target_pairs={{0,8},{1,9},{4,12},{5,13},{8,0},{9,1},{12,4},{13,5},{2,10},{3,11},... | collective-permute-start | bytes 196616 | tf_op jit(solution)/shard_map/ppermute | solution.py:592
  23.4 1.2 %collective-permute-start.7 = (f32[2,1024]{1,0:T(2,128)S(1)}, f32[2,1024]{1,0:T(2,128)S(1)}, u32[]{:S(2)}, u32[]{:S(2)}) collective-permute-start(f32[2,1024]{1,0:T(2,128)S(1)} %shard_map.53), channel_id=1, source_target_pairs={{0,1},{1,0},{2,3},{3,2},{4,5},{5,4},{6,7},{7,6},{8,9},{9,8},{10,11... | collective-permute-start | bytes 24584 | tf_op jit(solution)/shard_map/ppermute | solution.py:626

commit v14 on v13

--- a/solution.py
+++ b/solution.py
@@ -382,6 +382,7 @@
 
 MASKS = 8
 GATE_FLOOR = 11.0 / 9.0
+TAP_ROWS = 4 * GROUPS
 
 
 def pack_kernel(key, own, *rest):
@@ -403,16 +404,22 @@
     order[...] = jnp.where(iota((LANES, LANES), 1) == from_lane, 1.0, 0.0).astype(BF)
     back = 2 * LANES - 1 - iota((DISP, 2 * LANES), 0)
     flip[...] = jnp.where(iota((DISP, 2 * LANES), 1) == back, 1.0, 0.0).astype(BF)
-    guide_out[...] = spread_guide(guide[...]) * 0.5
+    keys = LAYERS * 3 * GROUPS
+    row = iota((3 * TAP_ROWS, keys), 0)
+    tap = jnp.where(row >= TAP_ROWS, 1, 0) + jnp.where(row >= 2 * TAP_ROWS, 1, 0)
+    row = row - TAP_ROWS * tap
+    layer = row & 3
+    key = 3 * GROUPS * layer + GROUPS * tap + (row >> 2)
+    chosen = (iota((3 * TAP_ROWS, keys), 1) == key) & (layer < LAYERS)
+    guide_t = (0.5 * dot_t(jnp.where(chosen, 1.0, 0.0).astype(BF), guide[...])).astype(BF)
+    guide_out[...] = jnp.concatenate([guide_t, guide_t], axis=1)
     block_of = LINE_PARTS - 1 - (iota(spread.shape, 1) >> 4)
     here = (iota(spread.shape, 0) & (LINE_PARTS - 1)) == block_of
     spread[...] = jnp.where(here, 1.0, 0.0).astype(BF)
 
 
-def lines_kernel(
-    offsets, order, flip, guide, spread, *rest
-):
-    pieces, (out, blocks, valid, gate_rows, cost_rows, vol, done, wts) = rest[:-8], rest[-8:]
+def lines_kernel(offsets, order, flip, guide, spread, *rest):
+    pieces, (out, blocks, valid, gate_rows, cost_rows, vol, done, wts, sums) = rest[:-9], rest[-9:]
     near, pieces = pieces[0], pieces[1:]
     tiles = len(pieces)
     width = tiles * LANES
@@ -425,7 +432,6 @@
             valid[(me ^ key) // 2] = jnp.concatenate([masks[0:1], masks[MASKS // 2 : MASKS // 2 + 1]], axis=0)
     valid[me // 2] = near[...]
     at = PAIR * me
-    offs = [offsets[at + i] for i in range(PAIR)]
     ch_lane = iota((CHANNELS, LANES), 1)
     reached = iota((8, LANES), 1) + LINE_RUN * iota((8, LANES), 0)
     low_half = iota((LANES, LANES), 1) < CHANNELS
@@ -436,13 +442,13 @@
         lo = (w % 2) * LANES
         return valid[w // 2, view : view + 1, lo : lo + LANES]
 
-    for i in range(PAIR):
-
+    def correlate(i, carry):
         def tile_of(view, w):
             lo = (w % 2) * LANES
-            return blocks[2 * (w // 2) + view, i * CHANNELS : (i + 1) * CHANNELS, lo : lo + LANES]
-
-        off = offs[i]
+            channels = pl.ds(pl.multiple_of(i * CHANNELS, CHANNELS), CHANNELS)
+            return blocks[2 * (w // 2) + view, channels, lo : lo + LANES]
+
+        off = offsets[at + i]
         rolled = [pltpu.roll(tile_of(1, w).astype(F32) * mask_of(1, w), off, 1) for w in range(tiles)]
         shifted = [empty.astype(BF)] * 2
         for w in range(tiles):
@@ -465,11 +471,10 @@
                     rhs[side] = window
                     rhs = jnp.concatenate(rhs, axis=0)
                     products.append(jnp.dot(lhs, rhs, preferred_element_type=F32))
-                place = i * LINE_PARTS + 8 * (tiles - 2 - 4 * quad - 2 * two)
+                place = 8 * (tiles - 2 - 4 * quad - 2 * two)
                 for t in range(LINE_RUN):
-                    row = t * LANES + place
                     r = 8 * t
-                    gate_rows[row : row + 16, :] = jnp.concatenate(
+                    gate_rows[t, i, place : place + 16, :] = jnp.concatenate(
                         [gates[1][r : r + 8], gates[0][r : r + 8]], axis=0
                     ).astype(BF)
                     within = reached < LANES - t
@@ -488,41 +493,50 @@
                                 axis=1,
                             )
                         )
-                    cost_rows[row : row + 16, :] = jnp.concatenate(both, axis=0).astype(BF)
-
-    x_base = width - 1 - LINE_RUN * (iota((KEYS, LANES), 1) & (LINE_PARTS - 1))
-    row = iota((KEYS, LANES), 0)
-    reach = jnp.where(row >= 2 * GROUPS, 9, jnp.where(row >= GROUPS, 3, 1))
+                    cost_rows[t, i, place : place + 16, :] = jnp.concatenate(both, axis=0).astype(BF)
+        return carry
+
+    lax.fori_loop(0, PAIR, correlate, 0)
+
+    x_base = width - 1 - LINE_RUN * (iota((TAP_ROWS, LANES), 1) & (LINE_PARTS - 1))
+    layer = iota((TAP_ROWS, LANES), 0) & 3
+    reach = jnp.where(layer == 2, 9, jnp.where(layer == 1, 3, 1))
     room_left = x_base - reach
     room_right = x_base + reach - width
-    unit = jnp.where(row >= 2 * GROUPS, SHARPNESS / math.log(2.0), 1.0)
-    for two in range(LINE_RUN // 2):
-        lo = 2 * two * LANES
-        costs = dot_t(flip[...], cost_rows[lo : lo + 2 * LANES, :])
-        logits = dot_t(guide[...], gate_rows[lo : lo + 2 * LANES, :])
+    unit = jnp.where(layer == 2, SHARPNESS / math.log(2.0), 1.0)
+
+    def prepare(two, carry):
+        pair = pl.ds(2 * two, 2)
+        costs = dot_t(flip[...], cost_rows[pair].reshape(2 * LANES, 2 * LANES))
+        logits = dot_t(guide[...], gate_rows[pair].reshape(2 * LANES, LANES))
         for i in range(2):
             t = 2 * two + i
-            vol[t] = costs[:, i * LANES : (i + 1) * LANES]
+            cost = costs[:, i * LANES : (i + 1) * LANES]
+            for tile in range(DISP // 8):
+                vol[tile, t] = cost[8 * tile : 8 * tile + 8]
             z = jnp.tanh(logits[:, i * LANES : (i + 1) * LANES]) + GATE_FLOOR
-            taps = [z[m * KEYS : (m + 1) * KEYS] for m in range(3)]
+            taps = [z[m * TAP_ROWS : (m + 1) * TAP_ROWS] for m in range(3)]
             factor = unit / (taps[0] + taps[1] + taps[2])
             taps = [tap * factor for tap in taps]
-            if t >= LINE_RUN - 9:
-                taps[0] = jnp.where(room_left >= t, taps[0], 0.0)
-            if t < 9:
-                taps[2] = jnp.where(room_right < t, taps[2], 0.0)
+            taps[0] = jnp.where(room_left >= t, taps[0], 0.0)
+            taps[2] = jnp.where(room_right < t, taps[2], 0.0)
             for m in range(3):
-                wts[t, m * KEYS : (m + 1) * KEYS, :] = taps[m]
-
-    for group in range(GROUPS):
-        for at in (group * DGROUP, group * DGROUP + 8):
-            v = [vol[t, at : at + 8, :] for t in range(LINE_RUN)]
+                for pair_of in range(GROUPS // 2):
+                    wts[pair_of, t, m] = taps[m][8 * pair_of : 8 * pair_of + 8]
+        return carry
+
+    lax.fori_loop(0, LINE_RUN // 2, prepare, 0)
+
+    def aggregate(pair_of, carry):
+        for quarter in range(4):
+            tile = 4 * pair_of + quarter
+            v = [vol[tile, t] for t in range(LINE_RUN)]
             for layer in range(LAYERS):
                 s = 3**layer
+                row = 4 * (quarter // 2) + layer
                 fresh = []
                 for t in range(LINE_RUN):
-                    rows = [k * KEYS + layer * GROUPS + group for k in range(3)]
-                    w = [wts[t, r : r + 1, :] for r in rows]
+                    w = [wts[pair_of, t, m, row : row + 1, :] for m in range(3)]
                     blk, r = divmod(t + s, LINE_RUN)
                     before = pltpu.roll(v[r], LANES - blk, 1) if blk else v[r]
                     blk, r = divmod(t - s, LINE_RUN)
@@ -530,16 +544,18 @@
                     fresh.append(w[0] * before + w[1] * v[t] + w[2] * after)
                 v = fresh
             for t in range(LINE_RUN):
-                done[t, at : at + 8, :] = v[t]
-
+                done[tile, t] = v[t]
+        return carry
+
+    lax.fori_loop(0, GROUPS // 2, aggregate, 0)
     sub = iota((8, LANES), 0)
-    results = []
-    for block in range(LINE_RUN // 8):
+
+    def softmax(half, carry):
         totals = jnp.zeros((8, LANES), F32)
         moments = totals
         for s in range(8):
-            t = LINE_RUN - 1 - (8 * block + s)
-            v = [done[t, 8 * i : 8 * i + 8, :] for i in range(DISP // 8)]
+            t = LINE_RUN - 1 - 8 * half - s
+            v = [done[i, t] for i in range(DISP // 8)]
             top = v
             while len(top) > 1:
                 top = [jnp.maximum(a, b) for a, b in zip(top[::2], top[1::2])] + top[len(top) & ~1 :]
@@ -553,27 +569,29 @@
             moment = 8.0 * moment + sub.astype(F32) * total
             totals = jnp.where(sub == s, jnp.sum(total, axis=0, keepdims=True), totals)
             moments = jnp.where(sub == s, jnp.sum(moment, axis=0, keepdims=True), moments)
-        lane_line = iota((8, LANES), 1) >> 6
-        shift = jnp.zeros((8, LANES), F32)
-        for i in range(PAIR):
-            shift = jnp.where(lane_line == i, offs[i].astype(F32), shift)
-        results.append((moments / totals + shift) * (1.0 / DISP))
-    vals = jnp.concatenate(results, axis=0)
+        sums[half] = moments / totals
+        return carry
+
+    lax.fori_loop(0, LINE_RUN // 8, softmax, 0)
     lane_line = iota((LINE_RUN, LANES), 1) >> 6
+    shift = jnp.zeros((LINE_RUN, LANES), F32)
+    for i in range(PAIR):
+        shift = jnp.where(lane_line == i, offsets[at + i].astype(F32), shift)
+    vals = (sums[...].reshape(LINE_RUN, LANES) + shift) * (1.0 / DISP)
     both = jnp.concatenate([jnp.where(lane_line == i, vals, 0.0) for i in range(PAIR)], axis=0)
     high = both.astype(BF)
-    rest = both - high.astype(F32)
-    middle = rest.astype(BF)
-    low = (rest - middle.astype(F32)).astype(BF)
-    pieces = jnp.dot(
+    left = both - high.astype(F32)
+    middle = left.astype(BF)
+    low = (left - middle.astype(F32)).astype(BF)
+    parts = jnp.dot(
         jnp.concatenate([high, middle, low], axis=0), spread[...], preferred_element_type=F32
     )
     size = PAIR * LINE_RUN
-    pieces = pieces[:size] + pieces[size : 2 * size] + pieces[2 * size :]
+    parts = parts[:size] + parts[size : 2 * size] + parts[2 * size :]
     wanted = iota((LINE_RUN, width), 0) == (iota((LINE_RUN, width), 1) & (LINE_RUN - 1))
     for i in range(PAIR):
-        piece = jnp.where(wanted, pieces[i * LINE_RUN : (i + 1) * LINE_RUN], 0.0)
-        out[i : i + 1, :] = jnp.sum(piece, axis=0, keepdims=True)
+        part = jnp.where(wanted, parts[i * LINE_RUN : (i + 1) * LINE_RUN], 0.0)
+        out[i : i + 1, :] = jnp.sum(part, axis=0, keepdims=True)
 
 
 def lines_plan(features, valid_cols, offsets, guide_weight):
@@ -586,11 +604,6 @@
     gone = ()
     for key in (1, 2, 6, 4, 7, 5, 3, 0):
         masked = key % 2 and key > 1
-        if key in (4, 6):
-            me = 2 * lax.axis_index("cols") + lax.axis_index("view")
-            piece = lax.dynamic_index_in_dim(own, me ^ key, 0, False)
-            pieces[key] = lax.ppermute(piece, ("cols", "view"), [(i, i ^ key) for i in range(devices)])
-            continue
         (piece,) = call(
             functools.partial(pack_kernel, key),
             [((rows + (MASKS if masked else 0), BLOCK), BF)],
@@ -604,7 +617,7 @@
     consts = call(
         constants_kernel,
         [
-            ((LANES, LANES), BF), ((DISP, 2 * LANES), BF), ((3 * KEYS, LANES), BF), ((LANES, width), BF),
+            ((LANES, LANES), BF), ((DISP, 2 * LANES), BF), ((3 * TAP_ROWS, LANES), BF), ((LANES, width), BF),
             (valid_cols.shape, F32),
         ],
         [], 1, (offsets, guide_weight, valid_cols), 1_000_000,
@@ -615,11 +628,12 @@
         [
             pltpu.VMEM((devices, rows, BLOCK), BF),
             pltpu.VMEM((n,) + valid_cols.shape, F32),
-            pltpu.VMEM((LINE_RUN * LANES, LANES), BF),
-            pltpu.VMEM((LINE_RUN * LANES, 2 * LANES), BF),
-            pltpu.VMEM((LINE_RUN, DISP, LANES), F32),
-            pltpu.VMEM((LINE_RUN, DISP, LANES), F32),
-            pltpu.VMEM((LINE_RUN, 3 * KEYS, LANES), F32),
+            pltpu.VMEM((LINE_RUN, PAIR, LINE_PARTS, LANES), BF),
+            pltpu.VMEM((LINE_RUN, PAIR, LINE_PARTS, 2 * LANES), BF),
+            pltpu.VMEM((DISP // 8, LINE_RUN, 8, LANES), F32),
+            pltpu.VMEM((DISP // 8, LINE_RUN, 8, LANES), F32),
+            pltpu.VMEM((GROUPS // 2, LINE_RUN, 3, 8, LANES), F32),
+            pltpu.VMEM((LINE_RUN // 8, 8, LANES), F32),
         ],
         1, (offsets, *consts, *pieces), 1_000_000_000,
     )

time: 25.5 us -> 24.1 us (0.945)
  waiting for transfers between devices: 8.14 us -> 4.66 us
  Pallas kernels: 4.75 us -> 6.91 us
  local copies, waits for them, and re-layouts: 1.74 us -> 1.07 us
  starting transfers between devices: 9.95 us -> 10.5 us
    ppermute x2 -> x0, waiting for transfers between devices: 6.97 us -> none  [lines_plan(): lax.ppermute(piece, ('cols', 'view'), [(i, i ^ key) for i in range(device...]
    ppermute x5 -> x7, waiting for transfers between devices: 0.01 us -> 3.8 us  [lines_plan(): pieces[key] = lax.ppermute(piece, ('cols', 'view'), moves) if key else piece]
    ppermute x5 -> x7, starting transfers between devices: 7.26 us -> 10.1 us  [lines_plan(): pieces[key] = lax.ppermute(piece, ('cols', 'view'), moves) if key else piece]
    ppermute x2 -> x0, starting transfers between devices: 2.62 us -> none  [lines_plan(): lax.ppermute(piece, ('cols', 'view'), [(i, i ^ key) for i in range(device...]
    pallas_call x8 -> x10, Pallas kernels: 4.75 us -> 6.91 us  [call(): pl.pallas_call(kernel, out_shape=[jax.ShapeDtypeStruct(shape, dtype) for...]
    unnamed x10, local copies, waits for them, and re-layouts: 1.73 us -> 1.07 us
    ppermute x1, starting transfers between devices: 0.07 us -> 0.37 us  [lines_plan(): others = lax.ppermute(rows, 'view', [(0, 1), (1, 0)])]
    ppermute x1, waiting for transfers between devices: 1.15 us -> 0.87 us  [lines_plan(): others = lax.ppermute(rows, 'view', [(0, 1), (1, 0)])]
  transfers between devices with their start and end apart: 8 -> 8, of which waited for: 3 -> 3; matrix products, arithmetic and copies ran while one was open for 0% -> 0% of each run, Pallas kernels for 3% -> 4%
where the time goes in v14:
time: 24.1 us; the launch traced here: 23.9 us
  starting transfers between devices  10.5 us (44%)
  Pallas kernels  6.91 us (29%)
  waiting for transfers between devices  4.66 us (19%)
  local copies, waits for them, and re-layouts  1.07 us (4%)
  other arithmetic  0.62 us (3%)
    ppermute x7, starting transfers between devices, lines_plan(): pieces[key] = lax.ppermute(piece, ('cols', 'view'), moves) if key else piece  10.1 us
    pallas_call x10, Pallas kernels, call(): pl.pallas_call(kernel, out_shape=[jax.ShapeDtypeStruct(shape, dtype) for...  6.91 us
    ppermute x7, waiting for transfers between devices, lines_plan(): pieces[key] = lax.ppermute(piece, ('cols', 'view'), moves) if key else piece  3.8 us
    unnamed x10, local copies, waits for them, and re-layouts  1.07 us
    ppermute x1, waiting for transfers between devices, lines_plan(): others = lax.ppermute(rows, 'view', [(0, 1), (1, 0)])  0.87 us
    select_n x1, other arithmetic, lines_plan(): jnp.where(first, jnp.concatenate([rows, others]), jnp.concatenate([others...  0.62 us
  transfers between devices with their start and end apart: 8, of which 3 were waited for; matrix products, arithmetic and copies ran while one was open for 0% of the time, Pallas kernels for 4%

profile of v14, /device:TPU:0, one launch (start us, length us, event | category | flops | bytes accessed | tf_op | source)
XLA Modules:
  0.0 23.9 jit_solution(12809909775365965476)
XLA Ops:
  0.0 1.0 %copy-done = bf16[1,16,64,256]{3,2,1,0:T(8,128)(2,1)S(1)} copy-done((bf16[1,16,64,256]{3,2,1,0:T(8,128)(2,1)S(1)}, bf16[1,16,64,256]{3,2,1,0:T(8,128)(2,1)}, u32[]{:S(2)}) %copy-start) | copy-done | bytes 524312
  1.1 0.0 copy-start.1
  1.1 0.0 copy-start.2
  1.1 4.1 %collective-permute-start.3 = (bf16[128,256]{1,0:T(8,128)(2,1)S(1)}, bf16[128,256]{1,0:T(8,128)(2,1)S(1)}, u32[]{:S(2)}, u32[]{:S(2)}) collective-permute-start(bf16[128,256]{1,0:T(8,128)(2,1)S(1)} %shard_map.50.rest_1_), channel_id=1, source_target_pairs={{0,8},{1,9},{4,12},{5,13},{8,0},{9,1},{12,4},{13,5},{2,10},{3,11},... | collective-permute-start | bytes 196616 | tf_op jit(solution)/shard_map/ppermute | solution.py:616
  5.2 1.3 %collective-permute-start.5 = (bf16[128,256]{1,0:T(8,128)(2,1)S(1)}, bf16[128,256]{1,0:T(8,128)(2,1)S(1)}, u32[]{:S(2)}, u32[]{:S(2)}) collective-permute-start(bf16[128,256]{1,0:T(8,128)(2,1)S(1)} %shard_map.49.rest_0_), channel_id=1, source_target_pairs={{0,12},{1,13},{4,8},{5,9},{8,4},{9,5},{12,0},{13,1},{2,14},{3,15},... | collective-permute-start | bytes 196616 | tf_op jit(solution)/shard_map/ppermute | solution.py:616
  6.7 0.0 copy-start.3
  6.7 0.0 copy-start.4
  6.7 0.1 collective-permute-start.2
  6.8 2.7 %collective-permute-start.4 = (bf16[136,256]{1,0:T(8,128)(2,1)S(1)}, bf16[136,256]{1,0:T(8,128)(2,1)S(1)}, u32[]{:S(2)}, u32[]{:S(2)}) collective-permute-start(bf16[136,256]{1,0:T(8,128)(2,1)S(1)} %shard_map.52.rest_1_), channel_id=1, source_target_pairs={{0,9},{1,8},{4,13},{5,12},{8,1},{9,0},{12,5},{13,4},{2,11},{3,10},... | collective-permute-start | bytes 208904 | tf_op jit(solution)/shard_map/ppermute | solution.py:616
  9.5 0.2 %collective-permute-start.6 = (bf16[136,256]{1,0:T(8,128)(2,1)S(1)}, bf16[136,256]{1,0:T(8,128)(2,1)S(1)}, u32[]{:S(2)}, u32[]{:S(2)}) collective-permute-start(bf16[136,256]{1,0:T(8,128)(2,1)S(1)} %shard_map.51.rest_1_), channel_id=1, source_target_pairs={{0,13},{1,12},{4,9},{5,8},{8,5},{9,4},{12,1},{13,0},{2,15},{3,14},... | collective-permute-start | bytes 208904 | tf_op jit(solution)/shard_map/ppermute | solution.py:616
  9.8 0.0 collective-permute-done.3.rest_5_
  9.8 1.6 %collective-permute-start.1 = (bf16[128,256]{1,0:T(8,128)(2,1)S(1)}, bf16[128,256]{1,0:T(8,128)(2,1)S(1)}, u32[]{:S(2)}, u32[]{:S(2)}) collective-permute-start(bf16[128,256]{1,0:T(8,128)(2,1)S(1)} %shard_map.48.rest_0_), channel_id=1, source_target_pairs={{0,4},{1,5},{4,0},{5,1},{8,12},{9,13},{12,8},{13,9},{2,6},{3,7},{6... | collective-permute-start | bytes 196616 | tf_op jit(solution)/shard_map/ppermute | solution.py:616
  11.4 0.3 %collective-permute-done.5.rest_7_ = bf16[128,256]{1,0:T(8,128)(2,1)S(1)} collective-permute-done((bf16[128,256]{1,0:T(8,128)(2,1)S(1)}, bf16[128,256]{1,0:T(8,128)(2,1)S(1)}, u32[]{:S(2)}, u32[]{:S(2)}) %collective-permute-start.5) | collective-permute-done | bytes 65568 | tf_op jit(solution)/shard_map/ppermute | solution.py:616
  11.7 0.0 collective-permute-start
  11.8 0.8 %shard_map.46 = (bf16[128,128]{1,0:T(8,128)(2,1)S(1)}, bf16[192,256]{1,0:T(8,128)(2,1)S(1)}, bf16[144,128]{1,0:T(8,128)(2,1)S(1)}, bf16[128,1024]{1,0:T(8,128)(2,1)S(1)}, f32[2,256]{1,0:T(2,128)S(1)}) custom-call(s32[16]{0:T(128)S(1)} %copy-done.4, bf16[64,108]{1,0:T(8,128)(2,1)S(1)} %copy-done.3, s32[2,256]{1,0:T(2,128)S(1)} %copy-done.2), custom_call_target="tpu_custom_call" | custom-call | flops 1000000 | bytes 1000000 | tf_op jit(solution)/shard_map/pallas_call | solution.py:50
  12.6 3.4 %collective-permute-done.1.rest_3_ = bf16[128,256]{1,0:T(8,128)(2,1)S(1)} collective-permute-done((bf16[128,256]{1,0:T(8,128)(2,1)S(1)}, bf16[128,256]{1,0:T(8,128)(2,1)S(1)}, u32[]{:S(2)}, u32[]{:S(2)}) %collective-permute-start.1) | collective-permute-done | bytes 65568 | tf_op jit(solution)/shard_map/ppermute | solution.py:616
  16.0 0.0 collective-permute-done.rest_2_
  16.0 0.0 collective-permute-done.2.rest_4_
  16.1 0.0 collective-permute-done.4.rest_6_
  16.1 0.0 collective-permute-done.6.rest_8_
  16.1 6.0 %shard_map.55 = f32[2,1024]{1,0:T(2,128)S(1)} custom-call(s32[16]{0:T(128)S(1)} %copy-done.4, bf16[128,128]{1,0:T(8,128)(2,1)S(1)} %get-tuple-element.10.order, bf16[192,256]{1,0:T(8,128)(2,1)S(1)} %get-tuple-element.11.flip, bf16[144,128]{1,0:T(8,128)(2,1)S(1)} %get-tuple-element.12.guide, bf16[128,1024]{1,0:T(8,128)(2,1)S(1)} %get-tuple-element.13.spread, ...), custom_call_target="tpu_custom_call" | custom-call | flops 1000000000 | bytes 1000000 | tf_op jit(solution)/shard_map/pallas_call | solution.py:50
  22.1 0.4 %collective-permute-start.7 = (f32[2,1024]{1,0:T(2,128)S(1)}, f32[2,1024]{1,0:T(2,128)S(1)}, u32[]{:S(2)}, u32[]{:S(2)}) collective-permute-start(f32[2,1024]{1,0:T(2,128)S(1)} %shard_map.55), channel_id=1, source_target_pairs={{0,1},{1,0},{2,3},{3,2},{4,5},{5,4},{6,7},{7,6},{8,9},{9,8},{10,11... | collective-permute-start | bytes 24584 | tf_op jit(solution)/shard_map/ppermute | solution.py:640
  22.4 0.9 %collective-permute-done.7 = f32[2,1024]{1,0:T(2,128)S(1)} collective-permute-done((f32[2,1024]{1,0:T(2,128)S(1)}, f32[2,1024]{1,0:T(2,128)S(1)}, u32[]{:S(2)}, u32[]{:S(2)}) %collective-permute-start.7) | collective-permute-done | bytes 8224 | tf_op jit(solution)/shard_map/ppermute | solution.py:640
  23.3 0.6 %maximum_select_fusion = f32[1,4,1024]{2,1,0:T(4,128)} fusion(f32[1,2,1024]{2,1,0:T(2,128)S(1)} %bitcast.12, f32[1,2,1024]{2,1,0:T(2,128)S(1)} %bitcast.11, pred[]{:T(512)S(6)} %eq.3), kind=kLoop, calls=%fused_computation | loop fusion | flops 12288 | bytes 32769 | tf_op jit(solution)/shard_map/jit(_where)/select_n | solution.py:642
  (13 shorter events, 0.1 us)
Async XLA Ops:
  0.0 1.0 %copy-start = (bf16[1,16,64,256]{3,2,1,0:T(8,128)(2,1)S(1)}, bf16[1,16,64,256]{3,2,1,0:T(8,128)(2,1)}, u32[]{:S(2)}) copy-start(bf16[1,16,64,256]{3,2,1,0:T(8,128)(2,1)} %param.4) | copy-start | bytes 1572868
  1.1 5.5 %copy-start.1 = (bf16[1,16,64,256]{3,2,1,0:T(8,128)(2,1)S(1)}, bf16[1,16,64,256]{3,2,1,0:T(8,128)(2,1)}, u32[]{:S(2)}) copy-start(bf16[1,16,64,256]{3,2,1,0:T(8,128)(2,1)} %param.4) | copy-start | bytes 1572868
  1.1 5.5 %copy-start.2 = (s32[2,256]{1,0:T(2,128)S(1)}, s32[2,256]{1,0:T(2,128)}, u32[]{:S(2)}) copy-start(s32[2,256]{1,0:T(2,128)} %rest_0_.5) | copy-start | bytes 6148
  1.1 8.6 %collective-permute-start.3 = (bf16[128,256]{1,0:T(8,128)(2,1)S(1)}, bf16[128,256]{1,0:T(8,128)(2,1)S(1)}, u32[]{:S(2)}, u32[]{:S(2)}) collective-permute-start(bf16[128,256]{1,0:T(8,128)(2,1)S(1)} %shard_map.50.rest_1_), channel_id=1, source_target_pairs={{0,8},{1,9},{4,12},{5,13},{8,0},{9,1},{12,4},{13,5},{2,10},{3,11},... | collective-permute-start | bytes 196616 | tf_op jit(solution)/shard_map/ppermute | solution.py:616
  5.2 6.5 %collective-permute-start.5 = (bf16[128,256]{1,0:T(8,128)(2,1)S(1)}, bf16[128,256]{1,0:T(8,128)(2,1)S(1)}, u32[]{:S(2)}, u32[]{:S(2)}) collective-permute-start(bf16[128,256]{1,0:T(8,128)(2,1)S(1)} %shard_map.49.rest_0_), channel_id=1, source_target_pairs={{0,12},{1,13},{4,8},{5,9},{8,4},{9,5},{12,0},{13,1},{2,14},{3,15},... | collective-permute-start | bytes 196616 | tf_op jit(solution)/shard_map/ppermute | solution.py:616
  6.7 5.1 %copy-start.3 = (bf16[64,108]{1,0:T(8,128)(2,1)S(1)}, bf16[64,108]{1,0:T(8,128)(2,1)}, u32[]{:S(2)}) copy-start(bf16[64,108]{1,0:T(8,128)(2,1)} %guide.1) | copy-start | bytes 41476
  6.7 5.1 %copy-start.4 = (s32[16]{0:T(128)S(1)}, s32[16]{0:T(128)}, u32[]{:S(2)}) copy-start(s32[16]{0:T(128)} %offsets.3) | copy-start | bytes 196
  6.7 9.4 %collective-permute-start.2 = (bf16[136,256]{1,0:T(8,128)(2,1)S(1)}, bf16[136,256]{1,0:T(8,128)(2,1)S(1)}, u32[]{:S(2)}, u32[]{:S(2)}) collective-permute-start(bf16[136,256]{1,0:T(8,128)(2,1)S(1)} %shard_map.53.rest_0_), channel_id=1, source_target_pairs={{0,5},{1,4},{4,1},{5,0},{8,13},{9,12},{12,9},{13,8},{2,7},{3,6},{6... | collective-permute-start | bytes 208904 | tf_op jit(solution)/shard_map/ppermute | solution.py:616
  6.8 9.3 %collective-permute-start.4 = (bf16[136,256]{1,0:T(8,128)(2,1)S(1)}, bf16[136,256]{1,0:T(8,128)(2,1)S(1)}, u32[]{:S(2)}, u32[]{:S(2)}) collective-permute-start(bf16[136,256]{1,0:T(8,128)(2,1)S(1)} %shard_map.52.rest_1_), channel_id=1, source_target_pairs={{0,9},{1,8},{4,13},{5,12},{8,1},{9,0},{12,5},{13,4},{2,11},{3,10},... | collective-permute-start | bytes 208904 | tf_op jit(solution)/shard_map/ppermute | solution.py:616
  9.5 6.5 %collective-permute-start.6 = (bf16[136,256]{1,0:T(8,128)(2,1)S(1)}, bf16[136,256]{1,0:T(8,128)(2,1)S(1)}, u32[]{:S(2)}, u32[]{:S(2)}) collective-permute-start(bf16[136,256]{1,0:T(8,128)(2,1)S(1)} %shard_map.51.rest_1_), channel_id=1, source_target_pairs={{0,13},{1,12},{4,9},{5,8},{8,5},{9,4},{12,1},{13,0},{2,15},{3,14},... | collective-permute-start | bytes 208904 | tf_op jit(solution)/shard_map/ppermute | solution.py:616
  9.8 6.3 %collective-permute-start.1 = (bf16[128,256]{1,0:T(8,128)(2,1)S(1)}, bf16[128,256]{1,0:T(8,128)(2,1)S(1)}, u32[]{:S(2)}, u32[]{:S(2)}) collective-permute-start(bf16[128,256]{1,0:T(8,128)(2,1)S(1)} %shard_map.48.rest_0_), channel_id=1, source_target_pairs={{0,4},{1,5},{4,0},{5,1},{8,12},{9,13},{12,8},{13,9},{2,6},{3,7},{6... | collective-permute-start | bytes 196616 | tf_op jit(solution)/shard_map/ppermute | solution.py:616
  11.7 4.3 %collective-permute-start = (bf16[128,256]{1,0:T(8,128)(2,1)S(1)}, bf16[128,256]{1,0:T(8,128)(2,1)S(1)}, u32[]{:S(2)}, u32[]{:S(2)}) collective-permute-start(bf16[128,256]{1,0:T(8,128)(2,1)S(1)} %shard_map.47.rest_0_), channel_id=1, source_target_pairs={{0,1},{1,0},{4,5},{5,4},{8,9},{9,8},{12,13},{13,12},{2,3},{3,2},{6... | collective-permute-start | bytes 196616 | tf_op jit(solution)/shard_map/ppermute | solution.py:616
  22.1 1.2 %collective-permute-start.7 = (f32[2,1024]{1,0:T(2,128)S(1)}, f32[2,1024]{1,0:T(2,128)S(1)}, u32[]{:S(2)}, u32[]{:S(2)}) collective-permute-start(f32[2,1024]{1,0:T(2,128)S(1)} %shard_map.55), channel_id=1, source_target_pairs={{0,1},{1,0},{2,3},{3,2},{4,5},{5,4},{6,7},{7,6},{8,9},{9,8},{10,11... | collective-permute-start | bytes 24584 | tf_op jit(solution)/shard_map/ppermute | solution.py:640

commit v15 on v13

--- a/solution.py
+++ b/solution.py
@@ -515,22 +515,24 @@
                 wts[t, m * KEYS : (m + 1) * KEYS, :] = taps[m]
 
     for group in range(GROUPS):
-        for at in (group * DGROUP, group * DGROUP + 8):
-            v = [vol[t, at : at + 8, :] for t in range(LINE_RUN)]
-            for layer in range(LAYERS):
-                s = 3**layer
-                fresh = []
-                for t in range(LINE_RUN):
-                    rows = [k * KEYS + layer * GROUPS + group for k in range(3)]
-                    w = [wts[t, r : r + 1, :] for r in rows]
+        starts = [group * DGROUP + 8 * half for half in range(2)]
+        v = [[vol[t, at : at + 8, :] for t in range(LINE_RUN)] for at in starts]
+        for layer in range(LAYERS):
+            s = 3**layer
+            fresh = [[], []]
+            for t in range(LINE_RUN):
+                rows = [k * KEYS + layer * GROUPS + group for k in range(3)]
+                w = [jnp.broadcast_to(wts[t, r : r + 1, :], (8, LANES)) for r in rows]
+                for half in range(2):
                     blk, r = divmod(t + s, LINE_RUN)
-                    before = pltpu.roll(v[r], LANES - blk, 1) if blk else v[r]
+                    before = pltpu.roll(v[half][r], LANES - blk, 1) if blk else v[half][r]
                     blk, r = divmod(t - s, LINE_RUN)
-                    after = pltpu.roll(v[r], -blk, 1) if blk else v[r]
-                    fresh.append(w[0] * before + w[1] * v[t] + w[2] * after)
-                v = fresh
+                    after = pltpu.roll(v[half][r], -blk, 1) if blk else v[half][r]
+                    fresh[half].append(w[0] * before + w[1] * v[half][t] + w[2] * after)
+            v = fresh
+        for half, at in enumerate(starts):
             for t in range(LINE_RUN):
-                done[t, at : at + 8, :] = v[t]
+                done[t, at : at + 8, :] = v[half][t]
 
     sub = iota((8, LANES), 0)
     results = []
@@ -586,11 +588,6 @@
     gone = ()
     for key in (1, 2, 6, 4, 7, 5, 3, 0):
         masked = key % 2 and key > 1
-        if key in (4, 6):
-            me = 2 * lax.axis_index("cols") + lax.axis_index("view")
-            piece = lax.dynamic_index_in_dim(own, me ^ key, 0, False)
-            pieces[key] = lax.ppermute(piece, ("cols", "view"), [(i, i ^ key) for i in range(devices)])
-            continue
         (piece,) = call(
             functools.partial(pack_kernel, key),
             [((rows + (MASKS if masked else 0), BLOCK), BF)],

time: 25.5 us -> 22 us (0.86)
  waiting for transfers between devices: 8.14 us -> 4.67 us
  local copies, waits for them, and re-layouts: 1.74 us -> 1.07 us
  starting transfers between devices: 9.95 us -> 10.5 us
    ppermute x2 -> x0, waiting for transfers between devices: 6.97 us -> none  [lines_plan(): lax.ppermute(piece, ('cols', 'view'), [(i, i ^ key) for i in range(device...]
    ppermute x5 -> x7, waiting for transfers between devices: 0.01 us -> 3.82 us  [lines_plan(): pieces[key] = lax.ppermute(piece, ('cols', 'view'), moves) if key else piece]
    ppermute x5 -> x7, starting transfers between devices: 7.26 us -> 10.1 us  [lines_plan(): pieces[key] = lax.ppermute(piece, ('cols', 'view'), moves) if key else piece]
    ppermute x2 -> x0, starting transfers between devices: 2.62 us -> none  [lines_plan(): lax.ppermute(piece, ('cols', 'view'), [(i, i ^ key) for i in range(device...]
    unnamed x10, local copies, waits for them, and re-layouts: 1.73 us -> 1.07 us
    ppermute x1, starting transfers between devices: 0.07 us -> 0.38 us  [lines_plan(): others = lax.ppermute(rows, 'view', [(0, 1), (1, 0)])]
    ppermute x1, waiting for transfers between devices: 1.15 us -> 0.86 us  [lines_plan(): others = lax.ppermute(rows, 'view', [(0, 1), (1, 0)])]
    pallas_call x8 -> x10, Pallas kernels: 4.75 us -> 4.74 us  [call(): pl.pallas_call(kernel, out_shape=[jax.ShapeDtypeStruct(shape, dtype) for...]
  transfers between devices with their start and end apart: 8 -> 8, of which waited for: 3 -> 3; matrix products, arithmetic and copies ran while one was open for 0% -> 0% of each run, Pallas kernels for 3% -> 4%
where the time goes in v15:
time: 22 us; the launch traced here: 21.8 us
  starting transfers between devices  10.5 us (48%)
  Pallas kernels  4.74 us (22%)
  waiting for transfers between devices  4.67 us (21%)
  local copies, waits for them, and re-layouts  1.07 us (5%)
  other arithmetic  0.62 us (3%)
    ppermute x7, starting transfers between devices, lines_plan(): pieces[key] = lax.ppermute(piece, ('cols', 'view'), moves) if key else piece  10.1 us
    pallas_call x10, Pallas kernels, call(): pl.pallas_call(kernel, out_shape=[jax.ShapeDtypeStruct(shape, dtype) for...  4.74 us
    ppermute x7, waiting for transfers between devices, lines_plan(): pieces[key] = lax.ppermute(piece, ('cols', 'view'), moves) if key else piece  3.82 us
    unnamed x10, local copies, waits for them, and re-layouts  1.07 us
    ppermute x1, waiting for transfers between devices, lines_plan(): others = lax.ppermute(rows, 'view', [(0, 1), (1, 0)])  0.86 us
    select_n x1, other arithmetic, lines_plan(): jnp.where(first, jnp.concatenate([rows, others]), jnp.concatenate([others...  0.62 us
  transfers between devices with their start and end apart: 8, of which 3 were waited for; matrix products, arithmetic and copies ran while one was open for 0% of the time, Pallas kernels for 4%

profile of v15, /device:TPU:0, one launch (start us, length us, event | category | flops | bytes accessed | tf_op | source)
XLA Modules:
  0.0 21.8 jit_solution(10869418959956551037)
XLA Ops:
  0.0 1.0 %copy-done = bf16[1,16,64,256]{3,2,1,0:T(8,128)(2,1)S(1)} copy-done((bf16[1,16,64,256]{3,2,1,0:T(8,128)(2,1)S(1)}, bf16[1,16,64,256]{3,2,1,0:T(8,128)(2,1)}, u32[]{:S(2)}) %copy-start) | copy-done | bytes 524312
  1.1 0.0 copy-start.1
  1.1 0.0 copy-start.2
  1.1 4.1 %collective-permute-start.3 = (bf16[128,256]{1,0:T(8,128)(2,1)S(1)}, bf16[128,256]{1,0:T(8,128)(2,1)S(1)}, u32[]{:S(2)}, u32[]{:S(2)}) collective-permute-start(bf16[128,256]{1,0:T(8,128)(2,1)S(1)} %shard_map.50.rest_1_), channel_id=1, source_target_pairs={{0,8},{1,9},{4,12},{5,13},{8,0},{9,1},{12,4},{13,5},{2,10},{3,11},... | collective-permute-start | bytes 196616 | tf_op jit(solution)/shard_map/ppermute | solution.py:600
  5.2 1.3 %collective-permute-start.5 = (bf16[128,256]{1,0:T(8,128)(2,1)S(1)}, bf16[128,256]{1,0:T(8,128)(2,1)S(1)}, u32[]{:S(2)}, u32[]{:S(2)}) collective-permute-start(bf16[128,256]{1,0:T(8,128)(2,1)S(1)} %shard_map.49.rest_0_), channel_id=1, source_target_pairs={{0,12},{1,13},{4,8},{5,9},{8,4},{9,5},{12,0},{13,1},{2,14},{3,15},... | collective-permute-start | bytes 196616 | tf_op jit(solution)/shard_map/ppermute | solution.py:600
  6.7 0.0 copy-start.3
  6.7 0.0 copy-start.4
  6.7 0.1 collective-permute-start.2
  6.8 2.7 %collective-permute-start.4 = (bf16[136,256]{1,0:T(8,128)(2,1)S(1)}, bf16[136,256]{1,0:T(8,128)(2,1)S(1)}, u32[]{:S(2)}, u32[]{:S(2)}) collective-permute-start(bf16[136,256]{1,0:T(8,128)(2,1)S(1)} %shard_map.52.rest_1_), channel_id=1, source_target_pairs={{0,9},{1,8},{4,13},{5,12},{8,1},{9,0},{12,5},{13,4},{2,11},{3,10},... | collective-permute-start | bytes 208904 | tf_op jit(solution)/shard_map/ppermute | solution.py:600
  9.5 0.2 %collective-permute-start.6 = (bf16[136,256]{1,0:T(8,128)(2,1)S(1)}, bf16[136,256]{1,0:T(8,128)(2,1)S(1)}, u32[]{:S(2)}, u32[]{:S(2)}) collective-permute-start(bf16[136,256]{1,0:T(8,128)(2,1)S(1)} %shard_map.51.rest_1_), channel_id=1, source_target_pairs={{0,13},{1,12},{4,9},{5,8},{8,5},{9,4},{12,1},{13,0},{2,15},{3,14},... | collective-permute-start | bytes 208904 | tf_op jit(solution)/shard_map/ppermute | solution.py:600
  9.8 0.0 collective-permute-done.3.rest_5_
  9.8 1.6 %collective-permute-start.1 = (bf16[128,256]{1,0:T(8,128)(2,1)S(1)}, bf16[128,256]{1,0:T(8,128)(2,1)S(1)}, u32[]{:S(2)}, u32[]{:S(2)}) collective-permute-start(bf16[128,256]{1,0:T(8,128)(2,1)S(1)} %shard_map.48.rest_0_), channel_id=1, source_target_pairs={{0,4},{1,5},{4,0},{5,1},{8,12},{9,13},{12,8},{13,9},{2,6},{3,7},{6... | collective-permute-start | bytes 196616 | tf_op jit(solution)/shard_map/ppermute | solution.py:600
  11.4 0.3 %collective-permute-done.5.rest_7_ = bf16[128,256]{1,0:T(8,128)(2,1)S(1)} collective-permute-done((bf16[128,256]{1,0:T(8,128)(2,1)S(1)}, bf16[128,256]{1,0:T(8,128)(2,1)S(1)}, u32[]{:S(2)}, u32[]{:S(2)}) %collective-permute-start.5) | collective-permute-done | bytes 65568 | tf_op jit(solution)/shard_map/ppermute | solution.py:600
  11.7 0.0 collective-permute-start
  11.8 0.8 %shard_map.46 = (bf16[128,128]{1,0:T(8,128)(2,1)S(1)}, bf16[192,256]{1,0:T(8,128)(2,1)S(1)}, bf16[120,128]{1,0:T(8,128)(2,1)S(1)}, bf16[128,1024]{1,0:T(8,128)(2,1)S(1)}, f32[2,256]{1,0:T(2,128)S(1)}) custom-call(s32[16]{0:T(128)S(1)} %copy-done.4, bf16[64,108]{1,0:T(8,128)(2,1)S(1)} %copy-done.3, s32[2,256]{1,0:T(2,128)S(1)} %copy-done.2), custom_call_target="tpu_custom_call" | custom-call | flops 1000000 | bytes 1000000 | tf_op jit(solution)/shard_map/pallas_call | solution.py:50
  12.6 3.5 %collective-permute-done.1.rest_3_ = bf16[128,256]{1,0:T(8,128)(2,1)S(1)} collective-permute-done((bf16[128,256]{1,0:T(8,128)(2,1)S(1)}, bf16[128,256]{1,0:T(8,128)(2,1)S(1)}, u32[]{:S(2)}, u32[]{:S(2)}) %collective-permute-start.1) | collective-permute-done | bytes 65568 | tf_op jit(solution)/shard_map/ppermute | solution.py:600
  16.0 0.0 collective-permute-done.rest_2_
  16.0 0.0 collective-permute-done.2.rest_4_
  16.1 0.0 collective-permute-done.4.rest_6_
  16.1 0.0 collective-permute-done.6.rest_8_
  16.1 3.8 %shard_map.55 = f32[2,1024]{1,0:T(2,128)S(1)} custom-call(s32[16]{0:T(128)S(1)} %copy-done.4, bf16[128,128]{1,0:T(8,128)(2,1)S(1)} %get-tuple-element.10.order, bf16[192,256]{1,0:T(8,128)(2,1)S(1)} %get-tuple-element.11.flip, bf16[120,128]{1,0:T(8,128)(2,1)S(1)} %get-tuple-element.12.guide, bf16[128,1024]{1,0:T(8,128)(2,1)S(1)} %get-tuple-element.13.spread, ...), custom_call_target="tpu_custom_call" | custom-call | flops 1000000000 | bytes 1000000 | tf_op jit(solution)/shard_map/pallas_call | solution.py:50
  19.9 0.4 %collective-permute-start.7 = (f32[2,1024]{1,0:T(2,128)S(1)}, f32[2,1024]{1,0:T(2,128)S(1)}, u32[]{:S(2)}, u32[]{:S(2)}) collective-permute-start(f32[2,1024]{1,0:T(2,128)S(1)} %shard_map.55), channel_id=1, source_target_pairs={{0,1},{1,0},{2,3},{3,2},{4,5},{5,4},{6,7},{7,6},{8,9},{9,8},{10,11... | collective-permute-start | bytes 24584 | tf_op jit(solution)/shard_map/ppermute | solution.py:623
  20.3 0.9 %collective-permute-done.7 = f32[2,1024]{1,0:T(2,128)S(1)} collective-permute-done((f32[2,1024]{1,0:T(2,128)S(1)}, f32[2,1024]{1,0:T(2,128)S(1)}, u32[]{:S(2)}, u32[]{:S(2)}) %collective-permute-start.7) | collective-permute-done | bytes 8224 | tf_op jit(solution)/shard_map/ppermute | solution.py:623
  21.1 0.6 %maximum_select_fusion = f32[1,4,1024]{2,1,0:T(4,128)} fusion(f32[1,2,1024]{2,1,0:T(2,128)S(1)} %bitcast.12, f32[1,2,1024]{2,1,0:T(2,128)S(1)} %bitcast.11, pred[]{:T(512)S(6)} %eq.3), kind=kLoop, calls=%fused_computation | loop fusion | flops 12288 | bytes 32769 | tf_op jit(solution)/shard_map/jit(_where)/select_n | solution.py:625
  (13 shorter events, 0.1 us)
Async XLA Ops:
  0.0 1.0 %copy-start = (bf16[1,16,64,256]{3,2,1,0:T(8,128)(2,1)S(1)}, bf16[1,16,64,256]{3,2,1,0:T(8,128)(2,1)}, u32[]{:S(2)}) copy-start(bf16[1,16,64,256]{3,2,1,0:T(8,128)(2,1)} %param.4) | copy-start | bytes 1572868
  1.1 5.5 %copy-start.1 = (bf16[1,16,64,256]{3,2,1,0:T(8,128)(2,1)S(1)}, bf16[1,16,64,256]{3,2,1,0:T(8,128)(2,1)}, u32[]{:S(2)}) copy-start(bf16[1,16,64,256]{3,2,1,0:T(8,128)(2,1)} %param.4) | copy-start | bytes 1572868
  1.1 5.5 %copy-start.2 = (s32[2,256]{1,0:T(2,128)S(1)}, s32[2,256]{1,0:T(2,128)}, u32[]{:S(2)}) copy-start(s32[2,256]{1,0:T(2,128)} %rest_0_.5) | copy-start | bytes 6148
  1.1 8.6 %collective-permute-start.3 = (bf16[128,256]{1,0:T(8,128)(2,1)S(1)}, bf16[128,256]{1,0:T(8,128)(2,1)S(1)}, u32[]{:S(2)}, u32[]{:S(2)}) collective-permute-start(bf16[128,256]{1,0:T(8,128)(2,1)S(1)} %shard_map.50.rest_1_), channel_id=1, source_target_pairs={{0,8},{1,9},{4,12},{5,13},{8,0},{9,1},{12,4},{13,5},{2,10},{3,11},... | collective-permute-start | bytes 196616 | tf_op jit(solution)/shard_map/ppermute | solution.py:600
  5.2 6.5 %collective-permute-start.5 = (bf16[128,256]{1,0:T(8,128)(2,1)S(1)}, bf16[128,256]{1,0:T(8,128)(2,1)S(1)}, u32[]{:S(2)}, u32[]{:S(2)}) collective-permute-start(bf16[128,256]{1,0:T(8,128)(2,1)S(1)} %shard_map.49.rest_0_), channel_id=1, source_target_pairs={{0,12},{1,13},{4,8},{5,9},{8,4},{9,5},{12,0},{13,1},{2,14},{3,15},... | collective-permute-start | bytes 196616 | tf_op jit(solution)/shard_map/ppermute | solution.py:600
  6.7 5.1 %copy-start.3 = (bf16[64,108]{1,0:T(8,128)(2,1)S(1)}, bf16[64,108]{1,0:T(8,128)(2,1)}, u32[]{:S(2)}) copy-start(bf16[64,108]{1,0:T(8,128)(2,1)} %guide.1) | copy-start | bytes 41476
  6.7 5.1 %copy-start.4 = (s32[16]{0:T(128)S(1)}, s32[16]{0:T(128)}, u32[]{:S(2)}) copy-start(s32[16]{0:T(128)} %offsets.3) | copy-start | bytes 196
  6.7 9.4 %collective-permute-start.2 = (bf16[136,256]{1,0:T(8,128)(2,1)S(1)}, bf16[136,256]{1,0:T(8,128)(2,1)S(1)}, u32[]{:S(2)}, u32[]{:S(2)}) collective-permute-start(bf16[136,256]{1,0:T(8,128)(2,1)S(1)} %shard_map.53.rest_0_), channel_id=1, source_target_pairs={{0,5},{1,4},{4,1},{5,0},{8,13},{9,12},{12,9},{13,8},{2,7},{3,6},{6... | collective-permute-start | bytes 208904 | tf_op jit(solution)/shard_map/ppermute | solution.py:600
  6.8 9.3 %collective-permute-start.4 = (bf16[136,256]{1,0:T(8,128)(2,1)S(1)}, bf16[136,256]{1,0:T(8,128)(2,1)S(1)}, u32[]{:S(2)}, u32[]{:S(2)}) collective-permute-start(bf16[136,256]{1,0:T(8,128)(2,1)S(1)} %shard_map.52.rest_1_), channel_id=1, source_target_pairs={{0,9},{1,8},{4,13},{5,12},{8,1},{9,0},{12,5},{13,4},{2,11},{3,10},... | collective-permute-start | bytes 208904 | tf_op jit(solution)/shard_map/ppermute | solution.py:600
  9.5 6.5 %collective-permute-start.6 = (bf16[136,256]{1,0:T(8,128)(2,1)S(1)}, bf16[136,256]{1,0:T(8,128)(2,1)S(1)}, u32[]{:S(2)}, u32[]{:S(2)}) collective-permute-start(bf16[136,256]{1,0:T(8,128)(2,1)S(1)} %shard_map.51.rest_1_), channel_id=1, source_target_pairs={{0,13},{1,12},{4,9},{5,8},{8,5},{9,4},{12,1},{13,0},{2,15},{3,14},... | collective-permute-start | bytes 208904 | tf_op jit(solution)/shard_map/ppermute | solution.py:600
  9.8 6.3 %collective-permute-start.1 = (bf16[128,256]{1,0:T(8,128)(2,1)S(1)}, bf16[128,256]{1,0:T(8,128)(2,1)S(1)}, u32[]{:S(2)}, u32[]{:S(2)}) collective-permute-start(bf16[128,256]{1,0:T(8,128)(2,1)S(1)} %shard_map.48.rest_0_), channel_id=1, source_target_pairs={{0,4},{1,5},{4,0},{5,1},{8,12},{9,13},{12,8},{13,9},{2,6},{3,7},{6... | collective-permute-start | bytes 196616 | tf_op jit(solution)/shard_map/ppermute | solution.py:600
  11.7 4.3 %collective-permute-start = (bf16[128,256]{1,0:T(8,128)(2,1)S(1)}, bf16[128,256]{1,0:T(8,128)(2,1)S(1)}, u32[]{:S(2)}, u32[]{:S(2)}) collective-permute-start(bf16[128,256]{1,0:T(8,128)(2,1)S(1)} %shard_map.47.rest_0_), channel_id=1, source_target_pairs={{0,1},{1,0},{4,5},{5,4},{8,9},{9,8},{12,13},{13,12},{2,3},{3,2},{6... | collective-permute-start | bytes 196616 | tf_op jit(solution)/shard_map/ppermute | solution.py:600
  19.9 1.2 %collective-permute-start.7 = (f32[2,1024]{1,0:T(2,128)S(1)}, f32[2,1024]{1,0:T(2,128)S(1)}, u32[]{:S(2)}, u32[]{:S(2)}) collective-permute-start(f32[2,1024]{1,0:T(2,128)S(1)} %shard_map.55), channel_id=1, source_target_pairs={{0,1},{1,0},{2,3},{3,2},{4,5},{5,4},{6,7},{7,6},{8,9},{9,8},{10,11... | collective-permute-start | bytes 24584 | tf_op jit(solution)/shard_map/ppermute | solution.py:623

commit v16 on v14

--- a/solution.py
+++ b/solution.py
@@ -445,7 +445,7 @@
     def correlate(i, carry):
         def tile_of(view, w):
             lo = (w % 2) * LANES
-            channels = pl.ds(pl.multiple_of(i * CHANNELS, CHANNELS), CHANNELS)
+            channels = slice(i * CHANNELS, (i + 1) * CHANNELS)
             return blocks[2 * (w // 2) + view, channels, lo : lo + LANES]
 
         off = offsets[at + i]
@@ -496,7 +496,8 @@
                     cost_rows[t, i, place : place + 16, :] = jnp.concatenate(both, axis=0).astype(BF)
         return carry
 
-    lax.fori_loop(0, PAIR, correlate, 0)
+    for step in range(PAIR):
+        correlate(step, 0)
 
     x_base = width - 1 - LINE_RUN * (iota((TAP_ROWS, LANES), 1) & (LINE_PARTS - 1))
     layer = iota((TAP_ROWS, LANES), 0) & 3
@@ -525,26 +526,29 @@
                     wts[pair_of, t, m] = taps[m][8 * pair_of : 8 * pair_of + 8]
         return carry
 
-    lax.fori_loop(0, LINE_RUN // 2, prepare, 0)
+    for step in range(LINE_RUN // 2):
+        prepare(step, 0)
 
     def aggregate(pair_of, carry):
-        for quarter in range(4):
-            tile = 4 * pair_of + quarter
-            v = [vol[tile, t] for t in range(LINE_RUN)]
+        for group in range(2):
+            tile = 4 * pair_of + 2 * group
+            v = [[vol[tile + half, t] for t in range(LINE_RUN)] for half in range(2)]
             for layer in range(LAYERS):
                 s = 3**layer
-                row = 4 * (quarter // 2) + layer
-                fresh = []
+                row = 4 * group + layer
+                fresh = [[], []]
                 for t in range(LINE_RUN):
-                    w = [wts[pair_of, t, m, row : row + 1, :] for m in range(3)]
-                    blk, r = divmod(t + s, LINE_RUN)
-                    before = pltpu.roll(v[r], LANES - blk, 1) if blk else v[r]
-                    blk, r = divmod(t - s, LINE_RUN)
-                    after = pltpu.roll(v[r], -blk, 1) if blk else v[r]
-                    fresh.append(w[0] * before + w[1] * v[t] + w[2] * after)
+                    w = [jnp.broadcast_to(wts[pair_of, t, m, row : row + 1, :], (8, LANES)) for m in range(3)]
+                    for half in range(2):
+                        blk, r = divmod(t + s, LINE_RUN)
+                        before = pltpu.roll(v[half][r], LANES - blk, 1) if blk else v[half][r]
+                        blk, r = divmod(t - s, LINE_RUN)
+                        after = pltpu.roll(v[half][r], -blk, 1) if blk else v[half][r]
+                        fresh[half].append(w[0] * before + w[1] * v[half][t] + w[2] * after)
                 v = fresh
-            for t in range(LINE_RUN):
-                done[tile, t] = v[t]
+            for half in range(2):
+                for t in range(LINE_RUN):
+                    done[tile + half, t] = v[half][t]
         return carry
 
     lax.fori_loop(0, GROUPS // 2, aggregate, 0)
@@ -572,7 +576,8 @@
         sums[half] = moments / totals
         return carry
 
-    lax.fori_loop(0, LINE_RUN // 8, softmax, 0)
+    for step in range(LINE_RUN // 8):
+        softmax(step, 0)
     lane_line = iota((LINE_RUN, LANES), 1) >> 6
     shift = jnp.zeros((LINE_RUN, LANES), F32)
     for i in range(PAIR):

time: 24.1 us -> 22.6 us (0.938)
  Pallas kernels: 6.91 us -> 5.35 us
    pallas_call x10, Pallas kernels: 6.91 us -> 5.35 us  [call(): pl.pallas_call(kernel, out_shape=[jax.ShapeDtypeStruct(shape, dtype) for...]
where the time goes in v16:
time: 22.6 us; the launch traced here: 22.4 us
  starting transfers between devices  10.5 us (46%)
  Pallas kernels  5.35 us (24%)
  waiting for transfers between devices  4.65 us (21%)
  local copies, waits for them, and re-layouts  1.07 us (5%)
  other arithmetic  0.62 us (3%)
    ppermute x7, starting transfers between devices, lines_plan(): pieces[key] = lax.ppermute(piece, ('cols', 'view'), moves) if key else piece  10.1 us
    pallas_call x10, Pallas kernels, call(): pl.pallas_call(kernel, out_shape=[jax.ShapeDtypeStruct(shape, dtype) for...  5.35 us
    ppermute x7, waiting for transfers between devices, lines_plan(): pieces[key] = lax.ppermute(piece, ('cols', 'view'), moves) if key else piece  3.8 us
    unnamed x10, local copies, waits for them, and re-layouts  1.07 us
    ppermute x1, waiting for transfers between devices, lines_plan(): others = lax.ppermute(rows, 'view', [(0, 1), (1, 0)])  0.86 us
    select_n x1, other arithmetic, lines_plan(): jnp.where(first, jnp.concatenate([rows, others]), jnp.concatenate([others...  0.62 us
  transfers between devices with their start and end apart: 8, of which 3 were waited for; matrix products, arithmetic and copies ran while one was open for 0% of the time, Pallas kernels for 4%

profile of v16, /device:TPU:0, one launch (start us, length us, event | category | flops | bytes accessed | tf_op | source)
XLA Modules:
  0.0 22.4 jit_solution(8276792818849504675)
XLA Ops:
  0.0 1.0 %copy-done = bf16[1,16,64,256]{3,2,1,0:T(8,128)(2,1)S(1)} copy-done((bf16[1,16,64,256]{3,2,1,0:T(8,128)(2,1)S(1)}, bf16[1,16,64,256]{3,2,1,0:T(8,128)(2,1)}, u32[]{:S(2)}) %copy-start) | copy-done | bytes 524312
  1.1 0.0 copy-start.1
  1.1 0.0 copy-start.2
  1.1 4.1 %collective-permute-start.3 = (bf16[128,256]{1,0:T(8,128)(2,1)S(1)}, bf16[128,256]{1,0:T(8,128)(2,1)S(1)}, u32[]{:S(2)}, u32[]{:S(2)}) collective-permute-start(bf16[128,256]{1,0:T(8,128)(2,1)S(1)} %shard_map.50.rest_1_), channel_id=1, source_target_pairs={{0,8},{1,9},{4,12},{5,13},{8,0},{9,1},{12,4},{13,5},{2,10},{3,11},... | collective-permute-start | bytes 196616 | tf_op jit(solution)/shard_map/ppermute | solution.py:621
  5.2 1.3 %collective-permute-start.5 = (bf16[128,256]{1,0:T(8,128)(2,1)S(1)}, bf16[128,256]{1,0:T(8,128)(2,1)S(1)}, u32[]{:S(2)}, u32[]{:S(2)}) collective-permute-start(bf16[128,256]{1,0:T(8,128)(2,1)S(1)} %shard_map.49.rest_0_), channel_id=1, source_target_pairs={{0,12},{1,13},{4,8},{5,9},{8,4},{9,5},{12,0},{13,1},{2,14},{3,15},... | collective-permute-start | bytes 196616 | tf_op jit(solution)/shard_map/ppermute | solution.py:621
  6.7 0.0 copy-start.3
  6.7 0.0 copy-start.4
  6.7 0.1 collective-permute-start.2
  6.8 2.7 %collective-permute-start.4 = (bf16[136,256]{1,0:T(8,128)(2,1)S(1)}, bf16[136,256]{1,0:T(8,128)(2,1)S(1)}, u32[]{:S(2)}, u32[]{:S(2)}) collective-permute-start(bf16[136,256]{1,0:T(8,128)(2,1)S(1)} %shard_map.52.rest_1_), channel_id=1, source_target_pairs={{0,9},{1,8},{4,13},{5,12},{8,1},{9,0},{12,5},{13,4},{2,11},{3,10},... | collective-permute-start | bytes 208904 | tf_op jit(solution)/shard_map/ppermute | solution.py:621
  9.5 0.2 %collective-permute-start.6 = (bf16[136,256]{1,0:T(8,128)(2,1)S(1)}, bf16[136,256]{1,0:T(8,128)(2,1)S(1)}, u32[]{:S(2)}, u32[]{:S(2)}) collective-permute-start(bf16[136,256]{1,0:T(8,128)(2,1)S(1)} %shard_map.51.rest_1_), channel_id=1, source_target_pairs={{0,13},{1,12},{4,9},{5,8},{8,5},{9,4},{12,1},{13,0},{2,15},{3,14},... | collective-permute-start | bytes 208904 | tf_op jit(solution)/shard_map/ppermute | solution.py:621
  9.8 0.0 collective-permute-done.3.rest_5_
  9.8 1.6 %collective-permute-start.1 = (bf16[128,256]{1,0:T(8,128)(2,1)S(1)}, bf16[128,256]{1,0:T(8,128)(2,1)S(1)}, u32[]{:S(2)}, u32[]{:S(2)}) collective-permute-start(bf16[128,256]{1,0:T(8,128)(2,1)S(1)} %shard_map.48.rest_0_), channel_id=1, source_target_pairs={{0,4},{1,5},{4,0},{5,1},{8,12},{9,13},{12,8},{13,9},{2,6},{3,7},{6... | collective-permute-start | bytes 196616 | tf_op jit(solution)/shard_map/ppermute | solution.py:621
  11.4 0.3 %collective-permute-done.5.rest_7_ = bf16[128,256]{1,0:T(8,128)(2,1)S(1)} collective-permute-done((bf16[128,256]{1,0:T(8,128)(2,1)S(1)}, bf16[128,256]{1,0:T(8,128)(2,1)S(1)}, u32[]{:S(2)}, u32[]{:S(2)}) %collective-permute-start.5) | collective-permute-done | bytes 65568 | tf_op jit(solution)/shard_map/ppermute | solution.py:621
  11.7 0.0 collective-permute-start
  11.8 0.8 %shard_map.46 = (bf16[128,128]{1,0:T(8,128)(2,1)S(1)}, bf16[192,256]{1,0:T(8,128)(2,1)S(1)}, bf16[144,128]{1,0:T(8,128)(2,1)S(1)}, bf16[128,1024]{1,0:T(8,128)(2,1)S(1)}, f32[2,256]{1,0:T(2,128)S(1)}) custom-call(s32[16]{0:T(128)S(1)} %copy-done.4, bf16[64,108]{1,0:T(8,128)(2,1)S(1)} %copy-done.3, s32[2,256]{1,0:T(2,128)S(1)} %copy-done.2), custom_call_target="tpu_custom_call" | custom-call | flops 1000000 | bytes 1000000 | tf_op jit(solution)/shard_map/pallas_call | solution.py:50
  12.6 3.4 %collective-permute-done.1.rest_3_ = bf16[128,256]{1,0:T(8,128)(2,1)S(1)} collective-permute-done((bf16[128,256]{1,0:T(8,128)(2,1)S(1)}, bf16[128,256]{1,0:T(8,128)(2,1)S(1)}, u32[]{:S(2)}, u32[]{:S(2)}) %collective-permute-start.1) | collective-permute-done | bytes 65568 | tf_op jit(solution)/shard_map/ppermute | solution.py:621
  16.0 0.0 collective-permute-done.rest_2_
  16.0 0.0 collective-permute-done.2.rest_4_
  16.1 0.0 collective-permute-done.4.rest_6_
  16.1 0.0 collective-permute-done.6.rest_8_
  16.1 4.4 %shard_map.55 = f32[2,1024]{1,0:T(2,128)S(1)} custom-call(s32[16]{0:T(128)S(1)} %copy-done.4, bf16[128,128]{1,0:T(8,128)(2,1)S(1)} %get-tuple-element.10.order, bf16[192,256]{1,0:T(8,128)(2,1)S(1)} %get-tuple-element.11.flip, bf16[144,128]{1,0:T(8,128)(2,1)S(1)} %get-tuple-element.12.guide, bf16[128,1024]{1,0:T(8,128)(2,1)S(1)} %get-tuple-element.13.spread, ...), custom_call_target="tpu_custom_call" | custom-call | flops 1000000000 | bytes 1000000 | tf_op jit(solution)/shard_map/pallas_call | solution.py:50
  20.5 0.4 %collective-permute-start.7 = (f32[2,1024]{1,0:T(2,128)S(1)}, f32[2,1024]{1,0:T(2,128)S(1)}, u32[]{:S(2)}, u32[]{:S(2)}) collective-permute-start(f32[2,1024]{1,0:T(2,128)S(1)} %shard_map.55), channel_id=1, source_target_pairs={{0,1},{1,0},{2,3},{3,2},{4,5},{5,4},{6,7},{7,6},{8,9},{9,8},{10,11... | collective-permute-start | bytes 24584 | tf_op jit(solution)/shard_map/ppermute | solution.py:645
  20.9 0.9 %collective-permute-done.7 = f32[2,1024]{1,0:T(2,128)S(1)} collective-permute-done((f32[2,1024]{1,0:T(2,128)S(1)}, f32[2,1024]{1,0:T(2,128)S(1)}, u32[]{:S(2)}, u32[]{:S(2)}) %collective-permute-start.7) | collective-permute-done | bytes 8224 | tf_op jit(solution)/shard_map/ppermute | solution.py:645
  21.7 0.6 %maximum_select_fusion = f32[1,4,1024]{2,1,0:T(4,128)} fusion(f32[1,2,1024]{2,1,0:T(2,128)S(1)} %bitcast.12, f32[1,2,1024]{2,1,0:T(2,128)S(1)} %bitcast.11, pred[]{:T(512)S(6)} %eq.3), kind=kLoop, calls=%fused_computation | loop fusion | flops 12288 | bytes 32769 | tf_op jit(solution)/shard_map/jit(_where)/select_n | solution.py:647
  (13 shorter events, 0.1 us)
Async XLA Ops:
  0.0 1.0 %copy-start = (bf16[1,16,64,256]{3,2,1,0:T(8,128)(2,1)S(1)}, bf16[1,16,64,256]{3,2,1,0:T(8,128)(2,1)}, u32[]{:S(2)}) copy-start(bf16[1,16,64,256]{3,2,1,0:T(8,128)(2,1)} %param.4) | copy-start | bytes 1572868
  1.1 5.5 %copy-start.1 = (bf16[1,16,64,256]{3,2,1,0:T(8,128)(2,1)S(1)}, bf16[1,16,64,256]{3,2,1,0:T(8,128)(2,1)}, u32[]{:S(2)}) copy-start(bf16[1,16,64,256]{3,2,1,0:T(8,128)(2,1)} %param.4) | copy-start | bytes 1572868
  1.1 5.5 %copy-start.2 = (s32[2,256]{1,0:T(2,128)S(1)}, s32[2,256]{1,0:T(2,128)}, u32[]{:S(2)}) copy-start(s32[2,256]{1,0:T(2,128)} %rest_0_.5) | copy-start | bytes 6148
  1.1 8.6 %collective-permute-start.3 = (bf16[128,256]{1,0:T(8,128)(2,1)S(1)}, bf16[128,256]{1,0:T(8,128)(2,1)S(1)}, u32[]{:S(2)}, u32[]{:S(2)}) collective-permute-start(bf16[128,256]{1,0:T(8,128)(2,1)S(1)} %shard_map.50.rest_1_), channel_id=1, source_target_pairs={{0,8},{1,9},{4,12},{5,13},{8,0},{9,1},{12,4},{13,5},{2,10},{3,11},... | collective-permute-start | bytes 196616 | tf_op jit(solution)/shard_map/ppermute | solution.py:621
  5.2 6.5 %collective-permute-start.5 = (bf16[128,256]{1,0:T(8,128)(2,1)S(1)}, bf16[128,256]{1,0:T(8,128)(2,1)S(1)}, u32[]{:S(2)}, u32[]{:S(2)}) collective-permute-start(bf16[128,256]{1,0:T(8,128)(2,1)S(1)} %shard_map.49.rest_0_), channel_id=1, source_target_pairs={{0,12},{1,13},{4,8},{5,9},{8,4},{9,5},{12,0},{13,1},{2,14},{3,15},... | collective-permute-start | bytes 196616 | tf_op jit(solution)/shard_map/ppermute | solution.py:621
  6.7 5.1 %copy-start.3 = (bf16[64,108]{1,0:T(8,128)(2,1)S(1)}, bf16[64,108]{1,0:T(8,128)(2,1)}, u32[]{:S(2)}) copy-start(bf16[64,108]{1,0:T(8,128)(2,1)} %guide.1) | copy-start | bytes 41476
  6.7 5.1 %copy-start.4 = (s32[16]{0:T(128)S(1)}, s32[16]{0:T(128)}, u32[]{:S(2)}) copy-start(s32[16]{0:T(128)} %offsets.3) | copy-start | bytes 196
  6.7 9.4 %collective-permute-start.2 = (bf16[136,256]{1,0:T(8,128)(2,1)S(1)}, bf16[136,256]{1,0:T(8,128)(2,1)S(1)}, u32[]{:S(2)}, u32[]{:S(2)}) collective-permute-start(bf16[136,256]{1,0:T(8,128)(2,1)S(1)} %shard_map.53.rest_0_), channel_id=1, source_target_pairs={{0,5},{1,4},{4,1},{5,0},{8,13},{9,12},{12,9},{13,8},{2,7},{3,6},{6... | collective-permute-start | bytes 208904 | tf_op jit(solution)/shard_map/ppermute | solution.py:621
  6.8 9.3 %collective-permute-start.4 = (bf16[136,256]{1,0:T(8,128)(2,1)S(1)}, bf16[136,256]{1,0:T(8,128)(2,1)S(1)}, u32[]{:S(2)}, u32[]{:S(2)}) collective-permute-start(bf16[136,256]{1,0:T(8,128)(2,1)S(1)} %shard_map.52.rest_1_), channel_id=1, source_target_pairs={{0,9},{1,8},{4,13},{5,12},{8,1},{9,0},{12,5},{13,4},{2,11},{3,10},... | collective-permute-start | bytes 208904 | tf_op jit(solution)/shard_map/ppermute | solution.py:621
  9.5 6.5 %collective-permute-start.6 = (bf16[136,256]{1,0:T(8,128)(2,1)S(1)}, bf16[136,256]{1,0:T(8,128)(2,1)S(1)}, u32[]{:S(2)}, u32[]{:S(2)}) collective-permute-start(bf16[136,256]{1,0:T(8,128)(2,1)S(1)} %shard_map.51.rest_1_), channel_id=1, source_target_pairs={{0,13},{1,12},{4,9},{5,8},{8,5},{9,4},{12,1},{13,0},{2,15},{3,14},... | collective-permute-start | bytes 208904 | tf_op jit(solution)/shard_map/ppermute | solution.py:621
  9.8 6.3 %collective-permute-start.1 = (bf16[128,256]{1,0:T(8,128)(2,1)S(1)}, bf16[128,256]{1,0:T(8,128)(2,1)S(1)}, u32[]{:S(2)}, u32[]{:S(2)}) collective-permute-start(bf16[128,256]{1,0:T(8,128)(2,1)S(1)} %shard_map.48.rest_0_), channel_id=1, source_target_pairs={{0,4},{1,5},{4,0},{5,1},{8,12},{9,13},{12,8},{13,9},{2,6},{3,7},{6... | collective-permute-start | bytes 196616 | tf_op jit(solution)/shard_map/ppermute | solution.py:621
  11.7 4.3 %collective-permute-start = (bf16[128,256]{1,0:T(8,128)(2,1)S(1)}, bf16[128,256]{1,0:T(8,128)(2,1)S(1)}, u32[]{:S(2)}, u32[]{:S(2)}) collective-permute-start(bf16[128,256]{1,0:T(8,128)(2,1)S(1)} %shard_map.47.rest_0_), channel_id=1, source_target_pairs={{0,1},{1,0},{4,5},{5,4},{8,9},{9,8},{12,13},{13,12},{2,3},{3,2},{6... | collective-permute-start | bytes 196616 | tf_op jit(solution)/shard_map/ppermute | solution.py:621
  20.5 1.2 %collective-permute-start.7 = (f32[2,1024]{1,0:T(2,128)S(1)}, f32[2,1024]{1,0:T(2,128)S(1)}, u32[]{:S(2)}, u32[]{:S(2)}) collective-permute-start(f32[2,1024]{1,0:T(2,128)S(1)} %shard_map.55), channel_id=1, source_target_pairs={{0,1},{1,0},{2,3},{3,2},{4,5},{5,4},{6,7},{7,6},{8,9},{9,8},{10,11... | collective-permute-start | bytes 24584 | tf_op jit(solution)/shard_map/ppermute | solution.py:645

commit v17 on v15

--- a/solution.py
+++ b/solution.py
@@ -436,59 +436,27 @@
         lo = (w % 2) * LANES
         return valid[w // 2, view : view + 1, lo : lo + LANES]
 
-    for i in range(PAIR):
-
-        def tile_of(view, w):
-            lo = (w % 2) * LANES
-            return blocks[2 * (w // 2) + view, i * CHANNELS : (i + 1) * CHANNELS, lo : lo + LANES]
-
-        off = offs[i]
-        rolled = [pltpu.roll(tile_of(1, w).astype(F32) * mask_of(1, w), off, 1) for w in range(tiles)]
-        shifted = [empty.astype(BF)] * 2
-        for w in range(tiles):
-            shifted.append(jnp.where(ch_lane < off, rolled[w - 1] if w else empty, rolled[w]).astype(BF))
-        for quad in range(tiles // 4):
-            refs = [tile_of(0, 4 * quad + q) for q in range(4)]
-            masked = [refs[q] * (mask_of(0, 4 * quad + q) * scale).astype(BF) for q in range(4)]
-            cols = dot_t(order[...], jnp.concatenate(refs, axis=0))
-            masked = dot_t(order[...], jnp.concatenate(masked, axis=0))
-            for two in range(2):
-                lo = two * LANES
-                gates, products = [], []
-                lhs = masked[:, lo : lo + LANES].astype(BF)
-                for side in range(2):
-                    w = 4 * quad + 2 * two + side
-                    keep = low_half if side == 0 else ~low_half
-                    gates.append(jnp.where(keep, cols[:, lo : lo + LANES], 0.0))
-                    window = jnp.concatenate(shifted[w : w + 3], axis=1)
-                    rhs = [jnp.zeros_like(window)] * 2
-                    rhs[side] = window
-                    rhs = jnp.concatenate(rhs, axis=0)
-                    products.append(jnp.dot(lhs, rhs, preferred_element_type=F32))
-                place = i * LINE_PARTS + 8 * (tiles - 2 - 4 * quad - 2 * two)
-                for t in range(LINE_RUN):
-                    row = t * LANES + place
-                    r = 8 * t
-                    gate_rows[row : row + 16, :] = jnp.concatenate(
-                        [gates[1][r : r + 8], gates[0][r : r + 8]], axis=0
-                    ).astype(BF)
-                    within = reached < LANES - t
-                    both = []
-                    for side in (1, 0):
-                        part = [products[side][r : r + 8, m * LANES : (m + 1) * LANES] for m in range(3)]
-                        both.append(
-                            jnp.concatenate(
-                                [
-                                    pltpu.roll(
-                                        jnp.where(within, part[m + 1], part[m]),
-                                        t, 1, stride=LINE_RUN, stride_axis=0,
-                                    )
-                                    for m in range(2)
-                                ],
-                                axis=1,
-                            )
-                        )
-                    cost_rows[row : row + 16, :] = jnp.concatenate(both, axis=0).astype(BF)
+    def tile_of(view, i, w):
+        lo = (w % 2) * LANES
+        return blocks[2 * (w // 2) + view, i * CHANNELS : (i + 1) * CHANNELS, lo : lo + LANES]
+
+    def place_of(i, quad, two):
+        return i * LINE_PARTS + 8 * (tiles - 2 - 4 * quad - 2 * two)
+
+    quads = [(i, quad) for i in range(PAIR) for quad in range(tiles // 4)]
+    for i, quad in quads:
+        refs = [tile_of(0, i, 4 * quad + q) for q in range(4)]
+        cols = dot_t(order[...], jnp.concatenate(refs, axis=0))
+        for two in range(2):
+            pair = cols[:, two * LANES : (two + 1) * LANES]
+            gates = [jnp.where(low_half, pair, 0.0), jnp.where(low_half, 0.0, pair)]
+            place = place_of(i, quad, two)
+            for t in range(LINE_RUN):
+                row = t * LANES + place
+                r = 8 * t
+                gate_rows[row : row + 16, :] = jnp.concatenate(
+                    [gates[1][r : r + 8], gates[0][r : r + 8]], axis=0
+                ).astype(BF)
 
     x_base = width - 1 - LINE_RUN * (iota((KEYS, LANES), 1) & (LINE_PARTS - 1))
     row = iota((KEYS, LANES), 0)
@@ -496,13 +464,12 @@
     room_left = x_base - reach
     room_right = x_base + reach - width
     unit = jnp.where(row >= 2 * GROUPS, SHARPNESS / math.log(2.0), 1.0)
-    for two in range(LINE_RUN // 2):
+
+    def weigh(two):
         lo = 2 * two * LANES
-        costs = dot_t(flip[...], cost_rows[lo : lo + 2 * LANES, :])
         logits = dot_t(guide[...], gate_rows[lo : lo + 2 * LANES, :])
         for i in range(2):
             t = 2 * two + i
-            vol[t] = costs[:, i * LANES : (i + 1) * LANES]
             z = jnp.tanh(logits[:, i * LANES : (i + 1) * LANES]) + GATE_FLOOR
             taps = [z[m * KEYS : (m + 1) * KEYS] for m in range(3)]
             factor = unit / (taps[0] + taps[1] + taps[2])
@@ -513,6 +480,61 @@
                 taps[2] = jnp.where(room_right < t, taps[2], 0.0)
             for m in range(3):
                 wts[t, m * KEYS : (m + 1) * KEYS, :] = taps[m]
+
+    shifted = []
+    for i in range(PAIR):
+        off = offs[i]
+        rolled = [pltpu.roll(tile_of(1, i, w).astype(F32) * mask_of(1, w), off, 1) for w in range(tiles)]
+        line = [empty.astype(BF)] * 2
+        for w in range(tiles):
+            line.append(jnp.where(ch_lane < off, rolled[w - 1] if w else empty, rolled[w]).astype(BF))
+        shifted.append(line)
+
+    step = 0
+    for i, quad in quads:
+        masked = [
+            tile_of(0, i, 4 * quad + q) * (mask_of(0, 4 * quad + q) * scale).astype(BF) for q in range(4)
+        ]
+        masked = dot_t(order[...], jnp.concatenate(masked, axis=0))
+        for two in range(2):
+            products = []
+            lhs = masked[:, two * LANES : (two + 1) * LANES].astype(BF)
+            for side in range(2):
+                w = 4 * quad + 2 * two + side
+                window = jnp.concatenate(shifted[i][w : w + 3], axis=1)
+                rhs = [jnp.zeros_like(window)] * 2
+                rhs[side] = window
+                rhs = jnp.concatenate(rhs, axis=0)
+                products.append(jnp.dot(lhs, rhs, preferred_element_type=F32))
+            place = place_of(i, quad, two)
+            for t in range(LINE_RUN):
+                row = t * LANES + place
+                r = 8 * t
+                within = reached < LANES - t
+                both = []
+                for side in (1, 0):
+                    part = [products[side][r : r + 8, m * LANES : (m + 1) * LANES] for m in range(3)]
+                    both.append(
+                        jnp.concatenate(
+                            [
+                                pltpu.roll(
+                                    jnp.where(within, part[m + 1], part[m]),
+                                    t, 1, stride=LINE_RUN, stride_axis=0,
+                                )
+                                for m in range(2)
+                            ],
+                            axis=1,
+                        )
+                    )
+                cost_rows[row : row + 16, :] = jnp.concatenate(both, axis=0).astype(BF)
+            weigh(step)
+            step += 1
+
+    for two in range(LINE_RUN // 2):
+        lo = 2 * two * LANES
+        costs = dot_t(flip[...], cost_rows[lo : lo + 2 * LANES, :])
+        for i in range(2):
+            vol[2 * two + i] = costs[:, i * LANES : (i + 1) * LANES]
 
     for group in range(GROUPS):
         starts = [group * DGROUP + 8 * half for half in range(2)]
@@ -586,13 +608,19 @@
     own = features.reshape(devices, rows, BLOCK)
     pieces = [None] * devices
     gone = ()
+    me = 2 * lax.axis_index("cols") + lax.axis_index("view")
+    heads = [lax.dynamic_index_in_dim(own, me ^ key, 0, False) for key in (6, 4)]
     for key in (1, 2, 6, 4, 7, 5, 3, 0):
         masked = key % 2 and key > 1
+        if key in (4, 6):
+            piece = heads[0 if key == 6 else 1]
+            pieces[key] = lax.ppermute(piece, ("cols", "view"), [(i, i ^ key) for i in range(devices)])
+            continue
         (piece,) = call(
             functools.partial(pack_kernel, key),
             [((rows + (MASKS if masked else 0), BLOCK), BF)],
             [], 0,
-            (own,) + ((valid_cols,) if masked else ()) + gone,
+            (own,) + ((valid_cols,) if masked else ()) + gone + tuple(heads),
             1_000_000,
         )
         gone = (piece,)

time: 22 us -> 26.5 us (1.20)
  waiting for transfers between devices: 4.67 us -> 8.86 us
  local copies, waits for them, and re-layouts: 1.07 us -> 1.94 us
  starting transfers between devices: 10.5 us -> 9.98 us
    ppermute x0 -> x2, waiting for transfers between devices: none -> 7.7 us  [lines_plan(): lax.ppermute(piece, ('cols', 'view'), [(i, i ^ key) for i in range(device...]
    ppermute x7 -> x5, waiting for transfers between devices: 3.82 us -> 0.01 us  [lines_plan(): pieces[key] = lax.ppermute(piece, ('cols', 'view'), moves) if key else piece]
    ppermute x7 -> x5, starting transfers between devices: 10.1 us -> 7.37 us  [lines_plan(): pieces[key] = lax.ppermute(piece, ('cols', 'view'), moves) if key else piece]
    ppermute x0 -> x2, starting transfers between devices: none -> 2.55 us  [lines_plan(): lax.ppermute(piece, ('cols', 'view'), [(i, i ^ key) for i in range(device...]
    squeeze x0 -> x1, local copies, waits for them, and re-layouts: none -> 0.88 us  [lines_plan(): lax.dynamic_index_in_dim(own, me ^ key, 0, False)]
    ppermute x1, starting transfers between devices: 0.38 us -> 0.07 us  [lines_plan(): others = lax.ppermute(rows, 'view', [(0, 1), (1, 0)])]
    ppermute x1, waiting for transfers between devices: 0.86 us -> 1.15 us  [lines_plan(): others = lax.ppermute(rows, 'view', [(0, 1), (1, 0)])]
    pallas_call x10 -> x8, Pallas kernels: 4.74 us -> 4.81 us  [call(): pl.pallas_call(kernel, out_shape=[jax.ShapeDtypeStruct(shape, dtype) for...]
  transfers between devices with their start and end apart: 8 -> 8, of which waited for: 3 -> 2; matrix products, arithmetic and copies ran while one was open for 0% -> 0% of each run, Pallas kernels for 4% -> 3%
where the time goes in v17:
time: 26.5 us; the launch traced here: 26.3 us
  starting transfers between devices  9.98 us (38%)
  waiting for transfers between devices  8.86 us (33%)
  Pallas kernels  4.81 us (18%)
  local copies, waits for them, and re-layouts  1.94 us (7%)
  other arithmetic  0.62 us (2%)
    ppermute x2, waiting for transfers between devices, lines_plan(): lax.ppermute(piece, ('cols', 'view'), [(i, i ^ key) for i in range(device...  7.7 us
    ppermute x5, starting transfers between devices, lines_plan(): pieces[key] = lax.ppermute(piece, ('cols', 'view'), moves) if key else piece  7.37 us
    pallas_call x8, Pallas kernels, call(): pl.pallas_call(kernel, out_shape=[jax.ShapeDtypeStruct(shape, dtype) for...  4.81 us
    ppermute x2, starting transfers between devices, lines_plan(): lax.ppermute(piece, ('cols', 'view'), [(i, i ^ key) for i in range(device...  2.55 us
    ppermute x1, waiting for transfers between devices, lines_plan(): others = lax.ppermute(rows, 'view', [(0, 1), (1, 0)])  1.15 us
    unnamed x10, local copies, waits for them, and re-layouts  1.06 us
    squeeze x1, local copies, waits for them, and re-layouts, lines_plan(): lax.dynamic_index_in_dim(own, me ^ key, 0, False)  0.88 us
    select_n x1, other arithmetic, lines_plan(): jnp.where(first, jnp.concatenate([rows, others]), jnp.concatenate([others...  0.62 us
  transfers between devices with their start and end apart: 8, of which 2 were waited for; matrix products, arithmetic and copies ran while one was open for 0% of the time, Pallas kernels for 3%

profile of v17, /device:TPU:0, one launch (start us, length us, event | category | flops | bytes accessed | tf_op | source)
XLA Modules:
  0.0 26.3 jit_solution(2247934710982550115)
XLA Ops:
  0.0 0.9 %dynamic-slice_bitcast_fusion = (bf16[128,256]{1,0:T(8,128)(2,1)S(1)}, bf16[128,256]{1,0:T(8,128)(2,1)S(1)}) fusion(bf16[8,128,256]{2,1,0:T(8,128)(2,1)} %bitcast.7, s32[]{:T(128)S(6)} %select_n.24, s32[]{:T(128)S(6)} %select_n.23), kind=kLoop, calls=%fused_computation | loop fusion | bytes 262152 | tf_op jit(solution)/shard_map/jit(dynamic_index_in_dim)/squeeze | solution.py:612
  0.9 0.0 copy-start
  0.9 1.0 %copy-done = bf16[1,16,64,256]{3,2,1,0:T(8,128)(2,1)S(1)} copy-done((bf16[1,16,64,256]{3,2,1,0:T(8,128)(2,1)S(1)}, bf16[1,16,64,256]{3,2,1,0:T(8,128)(2,1)}, u32[]{:S(2)}) %copy-start) | copy-done | bytes 524312
  2.0 3.1 %collective-permute-start.1 = (bf16[128,256]{1,0:T(8,128)(2,1)S(1)}, bf16[128,256]{1,0:T(8,128)(2,1)S(1)}, u32[]{:S(2)}, u32[]{:S(2)}) collective-permute-start(bf16[128,256]{1,0:T(8,128)(2,1)S(1)} %shard_map.48.rest_1_), channel_id=1, source_target_pairs={{0,4},{1,5},{4,0},{5,1},{8,12},{9,13},{12,8},{13,9},{2,6},{3,7},{6... | collective-permute-start | bytes 196616 | tf_op jit(solution)/shard_map/ppermute | solution.py:628
  5.1 0.0 collective-permute-start
  5.2 0.0 copy-start.3
  5.2 0.0 copy-start.4
  5.2 0.4 %collective-permute-start.2 = (bf16[136,256]{1,0:T(8,128)(2,1)S(1)}, bf16[136,256]{1,0:T(8,128)(2,1)S(1)}, u32[]{:S(2)}, u32[]{:S(2)}) collective-permute-start(bf16[136,256]{1,0:T(8,128)(2,1)S(1)} %shard_map.51.rest_0_), channel_id=1, source_target_pairs={{0,5},{1,4},{4,1},{5,0},{8,13},{9,12},{12,9},{13,8},{2,7},{3,6},{6... | collective-permute-start | bytes 208904 | tf_op jit(solution)/shard_map/ppermute | solution.py:628
  5.6 2.9 %collective-permute-start.4 = (bf16[136,256]{1,0:T(8,128)(2,1)S(1)}, bf16[136,256]{1,0:T(8,128)(2,1)S(1)}, u32[]{:S(2)}, u32[]{:S(2)}) collective-permute-start(bf16[136,256]{1,0:T(8,128)(2,1)S(1)} %shard_map.50.rest_1_), channel_id=1, source_target_pairs={{0,9},{1,8},{4,13},{5,12},{8,1},{9,0},{12,5},{13,4},{2,11},{3,10},... | collective-permute-start | bytes 208904 | tf_op jit(solution)/shard_map/ppermute | solution.py:628
  8.5 1.0 %collective-permute-start.6 = (bf16[136,256]{1,0:T(8,128)(2,1)S(1)}, bf16[136,256]{1,0:T(8,128)(2,1)S(1)}, u32[]{:S(2)}, u32[]{:S(2)}) collective-permute-start(bf16[136,256]{1,0:T(8,128)(2,1)S(1)} %shard_map.49.rest_1_), channel_id=1, source_target_pairs={{0,13},{1,12},{4,9},{5,8},{8,5},{9,4},{12,1},{13,0},{2,15},{3,14},... | collective-permute-start | bytes 208904 | tf_op jit(solution)/shard_map/ppermute | solution.py:628
  9.5 0.0 collective-permute-done.1.rest_3_
  9.5 1.7 %collective-permute-start.3 = (bf16[128,256]{1,0:T(8,128)(2,1)S(1)}, bf16[128,256]{1,0:T(8,128)(2,1)S(1)}, u32[]{:S(2)}, u32[]{:S(2)}) collective-permute-start(bf16[128,256]{1,0:T(8,128)(2,1)S(1)} %get-tuple-element.15.rest_1_.rest_2_.rest_3_), channel_id=1, source_target_pairs={{0,8},{1,9},{4,12},{5,13},{8,0},{9,1},{12,4},{13,5},{2,10},{3,11},... | collective-permute-start | bytes 196616 | tf_op jit(solution)/shard_map/ppermute | solution.py:617
  11.1 0.0 collective-permute-done.rest_2_
  11.2 0.9 %collective-permute-start.5 = (bf16[128,256]{1,0:T(8,128)(2,1)S(1)}, bf16[128,256]{1,0:T(8,128)(2,1)S(1)}, u32[]{:S(2)}, u32[]{:S(2)}) collective-permute-start(bf16[128,256]{1,0:T(8,128)(2,1)S(1)} %get-tuple-element.16.rest_0_.rest_1_.rest_2_), channel_id=1, source_target_pairs={{0,12},{1,13},{4,8},{5,9},{8,4},{9,5},{12,0},{13,1},{2,14},{3,15},... | collective-permute-start | bytes 196616 | tf_op jit(solution)/shard_map/ppermute | solution.py:617
  12.0 0.8 %shard_map.46 = (bf16[128,128]{1,0:T(8,128)(2,1)S(1)}, bf16[192,256]{1,0:T(8,128)(2,1)S(1)}, bf16[120,128]{1,0:T(8,128)(2,1)S(1)}, bf16[128,1024]{1,0:T(8,128)(2,1)S(1)}, f32[2,256]{1,0:T(2,128)S(1)}) custom-call(s32[16]{0:T(128)S(1)} %copy-done.4, bf16[64,108]{1,0:T(8,128)(2,1)S(1)} %copy-done.3, s32[2,256]{1,0:T(2,128)S(1)} %copy-done.2), custom_call_target="tpu_custom_call" | custom-call | flops 1000000 | bytes 1000000 | tf_op jit(solution)/shard_map/pallas_call | solution.py:50
  12.8 7.7 %collective-permute-done.3.rest_5_ = bf16[128,256]{1,0:T(8,128)(2,1)S(1)} collective-permute-done((bf16[128,256]{1,0:T(8,128)(2,1)S(1)}, bf16[128,256]{1,0:T(8,128)(2,1)S(1)}, u32[]{:S(2)}, u32[]{:S(2)}) %collective-permute-start.3) | collective-permute-done | bytes 65568 | tf_op jit(solution)/shard_map/ppermute | solution.py:617
  20.5 0.0 collective-permute-done.5.rest_7_
  20.5 0.0 collective-permute-done.2.rest_4_
  20.5 0.0 collective-permute-done.4.rest_6_
  20.5 0.0 collective-permute-done.6.rest_8_
  20.6 3.9 %shard_map.53 = f32[2,1024]{1,0:T(2,128)S(1)} custom-call(s32[16]{0:T(128)S(1)} %copy-done.4, bf16[128,128]{1,0:T(8,128)(2,1)S(1)} %get-tuple-element.10.order, bf16[192,256]{1,0:T(8,128)(2,1)S(1)} %get-tuple-element.11.flip, bf16[120,128]{1,0:T(8,128)(2,1)S(1)} %get-tuple-element.12.guide, bf16[128,1024]{1,0:T(8,128)(2,1)S(1)} %get-tuple-element.13.spread, ...), custom_call_target="tpu_custom_call" | custom-call | flops 1000000000 | bytes 1000000 | tf_op jit(solution)/shard_map/pallas_call | solution.py:50
  24.5 0.1 collective-permute-start.7
  24.6 1.2 %collective-permute-done.7 = f32[2,1024]{1,0:T(2,128)S(1)} collective-permute-done((f32[2,1024]{1,0:T(2,128)S(1)}, f32[2,1024]{1,0:T(2,128)S(1)}, u32[]{:S(2)}, u32[]{:S(2)}) %collective-permute-start.7) | collective-permute-done | bytes 8224 | tf_op jit(solution)/shard_map/ppermute | solution.py:651
  25.7 0.6 %maximum_select_fusion = f32[1,4,1024]{2,1,0:T(4,128)} fusion(f32[1,2,1024]{2,1,0:T(2,128)S(1)} %bitcast.15, f32[1,2,1024]{2,1,0:T(2,128)S(1)} %bitcast.14, pred[]{:T(512)S(6)} %eq.3), kind=kLoop, calls=%fused_computation.2 | loop fusion | flops 12288 | bytes 32769 | tf_op jit(solution)/shard_map/jit(_where)/select_n | solution.py:653
  (12 shorter events, 0.1 us)
Async XLA Ops:
  0.9 1.0 %copy-start = (bf16[1,16,64,256]{3,2,1,0:T(8,128)(2,1)S(1)}, bf16[1,16,64,256]{3,2,1,0:T(8,128)(2,1)}, u32[]{:S(2)}) copy-start(bf16[1,16,64,256]{3,2,1,0:T(8,128)(2,1)} %param.4) | copy-start | bytes 1572868
  1.9 3.1 %copy-start.1 = (bf16[1,16,64,256]{3,2,1,0:T(8,128)(2,1)S(1)}, bf16[1,16,64,256]{3,2,1,0:T(8,128)(2,1)}, u32[]{:S(2)}) copy-start(bf16[1,16,64,256]{3,2,1,0:T(8,128)(2,1)} %param.4) | copy-start | bytes 1572868
  1.9 3.1 %copy-start.2 = (s32[2,256]{1,0:T(2,128)S(1)}, s32[2,256]{1,0:T(2,128)}, u32[]{:S(2)}) copy-start(s32[2,256]{1,0:T(2,128)} %rest_0_.5) | copy-start | bytes 6148
  2.0 7.5 %collective-permute-start.1 = (bf16[128,256]{1,0:T(8,128)(2,1)S(1)}, bf16[128,256]{1,0:T(8,128)(2,1)S(1)}, u32[]{:S(2)}, u32[]{:S(2)}) collective-permute-start(bf16[128,256]{1,0:T(8,128)(2,1)S(1)} %shard_map.48.rest_1_), channel_id=1, source_target_pairs={{0,4},{1,5},{4,0},{5,1},{8,12},{9,13},{12,8},{13,9},{2,6},{3,7},{6... | collective-permute-start | bytes 196616 | tf_op jit(solution)/shard_map/ppermute | solution.py:628
  5.1 6.1 %collective-permute-start = (bf16[128,256]{1,0:T(8,128)(2,1)S(1)}, bf16[128,256]{1,0:T(8,128)(2,1)S(1)}, u32[]{:S(2)}, u32[]{:S(2)}) collective-permute-start(bf16[128,256]{1,0:T(8,128)(2,1)S(1)} %shard_map.47.rest_0_), channel_id=1, source_target_pairs={{0,1},{1,0},{4,5},{5,4},{8,9},{9,8},{12,13},{13,12},{2,3},{3,2},{6... | collective-permute-start | bytes 196616 | tf_op jit(solution)/shard_map/ppermute | solution.py:628
  5.2 6.9 %copy-start.3 = (bf16[64,108]{1,0:T(8,128)(2,1)S(1)}, bf16[64,108]{1,0:T(8,128)(2,1)}, u32[]{:S(2)}) copy-start(bf16[64,108]{1,0:T(8,128)(2,1)} %guide.1) | copy-start | bytes 41476
  5.2 6.9 %copy-start.4 = (s32[16]{0:T(128)S(1)}, s32[16]{0:T(128)}, u32[]{:S(2)}) copy-start(s32[16]{0:T(128)} %offsets.3) | copy-start | bytes 196
  5.2 15.4 %collective-permute-start.2 = (bf16[136,256]{1,0:T(8,128)(2,1)S(1)}, bf16[136,256]{1,0:T(8,128)(2,1)S(1)}, u32[]{:S(2)}, u32[]{:S(2)}) collective-permute-start(bf16[136,256]{1,0:T(8,128)(2,1)S(1)} %shard_map.51.rest_0_), channel_id=1, source_target_pairs={{0,5},{1,4},{4,1},{5,0},{8,13},{9,12},{12,9},{13,8},{2,7},{3,6},{6... | collective-permute-start | bytes 208904 | tf_op jit(solution)/shard_map/ppermute | solution.py:628
  5.6 14.9 %collective-permute-start.4 = (bf16[136,256]{1,0:T(8,128)(2,1)S(1)}, bf16[136,256]{1,0:T(8,128)(2,1)S(1)}, u32[]{:S(2)}, u32[]{:S(2)}) collective-permute-start(bf16[136,256]{1,0:T(8,128)(2,1)S(1)} %shard_map.50.rest_1_), channel_id=1, source_target_pairs={{0,9},{1,8},{4,13},{5,12},{8,1},{9,0},{12,5},{13,4},{2,11},{3,10},... | collective-permute-start | bytes 208904 | tf_op jit(solution)/shard_map/ppermute | solution.py:628
  8.5 12.1 %collective-permute-start.6 = (bf16[136,256]{1,0:T(8,128)(2,1)S(1)}, bf16[136,256]{1,0:T(8,128)(2,1)S(1)}, u32[]{:S(2)}, u32[]{:S(2)}) collective-permute-start(bf16[136,256]{1,0:T(8,128)(2,1)S(1)} %shard_map.49.rest_1_), channel_id=1, source_target_pairs={{0,13},{1,12},{4,9},{5,8},{8,5},{9,4},{12,1},{13,0},{2,15},{3,14},... | collective-permute-start | bytes 208904 | tf_op jit(solution)/shard_map/ppermute | solution.py:628
  9.5 11.1 %collective-permute-start.3 = (bf16[128,256]{1,0:T(8,128)(2,1)S(1)}, bf16[128,256]{1,0:T(8,128)(2,1)S(1)}, u32[]{:S(2)}, u32[]{:S(2)}) collective-permute-start(bf16[128,256]{1,0:T(8,128)(2,1)S(1)} %get-tuple-element.15.rest_1_.rest_2_.rest_3_), channel_id=1, source_target_pairs={{0,8},{1,9},{4,12},{5,13},{8,0},{9,1},{12,4},{13,5},{2,10},{3,11},... | collective-permute-start | bytes 196616 | tf_op jit(solution)/shard_map/ppermute | solution.py:617
  11.2 9.4 %collective-permute-start.5 = (bf16[128,256]{1,0:T(8,128)(2,1)S(1)}, bf16[128,256]{1,0:T(8,128)(2,1)S(1)}, u32[]{:S(2)}, u32[]{:S(2)}) collective-permute-start(bf16[128,256]{1,0:T(8,128)(2,1)S(1)} %get-tuple-element.16.rest_0_.rest_1_.rest_2_), channel_id=1, source_target_pairs={{0,12},{1,13},{4,8},{5,9},{8,4},{9,5},{12,0},{13,1},{2,14},{3,15},... | collective-permute-start | bytes 196616 | tf_op jit(solution)/shard_map/ppermute | solution.py:617
  24.5 1.2 %collective-permute-start.7 = (f32[2,1024]{1,0:T(2,128)S(1)}, f32[2,1024]{1,0:T(2,128)S(1)}, u32[]{:S(2)}, u32[]{:S(2)}) collective-permute-start(f32[2,1024]{1,0:T(2,128)S(1)} %shard_map.53), channel_id=1, source_target_pairs={{0,1},{1,0},{2,3},{3,2},{4,5},{5,4},{6,7},{7,6},{8,9},{9,8},{10,11... | collective-permute-start | bytes 24584 | tf_op jit(solution)/shard_map/ppermute | solution.py:651

commit v18 on v17

--- a/solution.py
+++ b/solution.py
@@ -396,11 +396,13 @@
         ).astype(BF)
 
 
-def constants_kernel(offsets, guide, valid, order, flip, guide_out, spread, masks):
+def constants_kernel(offsets, guide, valid, order, order_band, flip, guide_out, spread, masks):
     masks[...] = valid[...].astype(F32)
     row = iota((LANES, LANES), 0)
     from_lane = LANES - 1 - LINE_RUN * (row & 7) - (row >> 3)
     order[...] = jnp.where(iota((LANES, LANES), 1) == from_lane, 1.0, 0.0).astype(BF)
+    from_lane = LANES - 1 - (row & 64) - 8 * (row & 7) - ((row >> 3) & 7)
+    order_band[...] = jnp.where(iota((LANES, LANES), 1) == from_lane, 1.0, 0.0).astype(BF)
     back = 2 * LANES - 1 - iota((DISP, 2 * LANES), 0)
     flip[...] = jnp.where(iota((DISP, 2 * LANES), 1) == back, 1.0, 0.0).astype(BF)
     guide_out[...] = spread_guide(guide[...]) * 0.5
@@ -410,9 +412,9 @@
 
 
 def lines_kernel(
-    offsets, order, flip, guide, spread, *rest
+    offsets, order, order_band, flip, guide, spread, *rest
 ):
-    pieces, (out, blocks, valid, gate_rows, cost_rows, vol, done, wts) = rest[:-8], rest[-8:]
+    pieces, (out, blocks, valid, gate_rows, cost_rows, vol, done, wts, band) = rest[:-9], rest[-9:]
     near, pieces = pieces[0], pieces[1:]
     tiles = len(pieces)
     width = tiles * LANES
@@ -481,52 +483,53 @@
             for m in range(3):
                 wts[t, m * KEYS : (m + 1) * KEYS, :] = taps[m]
 
-    shifted = []
+    shifted, halfway = [], []
+    low_lane = ch_lane < LANES // 2
     for i in range(PAIR):
         off = offs[i]
         rolled = [pltpu.roll(tile_of(1, i, w).astype(F32) * mask_of(1, w), off, 1) for w in range(tiles)]
-        line = [empty.astype(BF)] * 2
+        line = [empty, empty]
         for w in range(tiles):
-            line.append(jnp.where(ch_lane < off, rolled[w - 1] if w else empty, rolled[w]).astype(BF))
-        shifted.append(line)
-
+            line.append(jnp.where(ch_lane < off, rolled[w - 1] if w else empty, rolled[w]))
+        turned = [empty] + [pltpu.roll(tile, LANES // 2, 1) if w else tile for w, tile in enumerate(line[1:])]
+        shifted.append([tile.astype(BF) for tile in line])
+        halfway.append([jnp.where(low_lane, a, b).astype(BF) for a, b in zip(turned, turned[1:])])
+
+    reached = iota((8, LANES), 1) + 8 * iota((8, LANES), 0)
     step = 0
     for i, quad in quads:
         masked = [
             tile_of(0, i, 4 * quad + q) * (mask_of(0, 4 * quad + q) * scale).astype(BF) for q in range(4)
         ]
-        masked = dot_t(order[...], jnp.concatenate(masked, axis=0))
+        masked = dot_t(order_band[...], jnp.concatenate(masked, axis=0))
         for two in range(2):
-            products = []
-            lhs = masked[:, two * LANES : (two + 1) * LANES].astype(BF)
-            for side in range(2):
-                w = 4 * quad + 2 * two + side
-                window = jnp.concatenate(shifted[i][w : w + 3], axis=1)
-                rhs = [jnp.zeros_like(window)] * 2
-                rhs[side] = window
-                rhs = jnp.concatenate(rhs, axis=0)
-                products.append(jnp.dot(lhs, rhs, preferred_element_type=F32))
+            w = 4 * quad + 2 * two
+            pair = masked[:, two * LANES : (two + 1) * LANES]
+            sides = [jnp.where(low_half, pair, 0.0).astype(BF), jnp.where(low_half, 0.0, pair).astype(BF)]
+            for half, source, first in ((0, shifted[i], w + 1), (1, halfway[i], w)):
+                lo = half * LANES // 2
+                lhs = jnp.concatenate([side[lo : lo + LANES // 2] for side in sides], axis=0)
+                rhs = jnp.concatenate(
+                    [jnp.concatenate(source[first + side : first + side + 2], axis=1) for side in range(2)], axis=0
+                )
+                products = jnp.dot(lhs, rhs, preferred_element_type=F32)
+                for side in range(2):
+                    for t in range(8):
+                        r = side * LANES // 2 + 8 * t
+                        near, far = products[r : r + 8, :LANES], products[r : r + 8, LANES:]
+                        joined = jnp.where(reached < LANES - t, far, near)
+                        for v, value in enumerate((near, joined)):
+                            band[i, w + side, t, v, 8 * half : 8 * half + 8, :] = pltpu.roll(
+                                value, t, 1, stride=8, stride_axis=0
+                            )
             place = place_of(i, quad, two)
             for t in range(LINE_RUN):
                 row = t * LANES + place
-                r = 8 * t
-                within = reached < LANES - t
-                both = []
-                for side in (1, 0):
-                    part = [products[side][r : r + 8, m * LANES : (m + 1) * LANES] for m in range(3)]
-                    both.append(
-                        jnp.concatenate(
-                            [
-                                pltpu.roll(
-                                    jnp.where(within, part[m + 1], part[m]),
-                                    t, 1, stride=LINE_RUN, stride_axis=0,
-                                )
-                                for m in range(2)
-                            ],
-                            axis=1,
-                        )
-                    )
-                cost_rows[row : row + 16, :] = jnp.concatenate(both, axis=0).astype(BF)
+                for v in range(2):
+                    both = [
+                        band[i, w + side, t % 8, v, pl.ds(t // 8, 8, stride=2), :] for side in (1, 0)
+                    ]
+                    cost_rows[row : row + 16, v * LANES : (v + 1) * LANES] = jnp.concatenate(both, axis=0).astype(BF)
             weigh(step)
             step += 1
 
@@ -608,19 +611,13 @@
     own = features.reshape(devices, rows, BLOCK)
     pieces = [None] * devices
     gone = ()
-    me = 2 * lax.axis_index("cols") + lax.axis_index("view")
-    heads = [lax.dynamic_index_in_dim(own, me ^ key, 0, False) for key in (6, 4)]
     for key in (1, 2, 6, 4, 7, 5, 3, 0):
         masked = key % 2 and key > 1
-        if key in (4, 6):
-            piece = heads[0 if key == 6 else 1]
-            pieces[key] = lax.ppermute(piece, ("cols", "view"), [(i, i ^ key) for i in range(devices)])
-            continue
         (piece,) = call(
             functools.partial(pack_kernel, key),
             [((rows + (MASKS if masked else 0), BLOCK), BF)],
             [], 0,
-            (own,) + ((valid_cols,) if masked else ()) + gone + tuple(heads),
+            (own,) + ((valid_cols,) if masked else ()) + gone,
             1_000_000,
         )
         gone = (piece,)
@@ -629,8 +626,8 @@
     consts = call(
         constants_kernel,
         [
-            ((LANES, LANES), BF), ((DISP, 2 * LANES), BF), ((3 * KEYS, LANES), BF), ((LANES, width), BF),
-            (valid_cols.shape, F32),
+            ((LANES, LANES), BF), ((LANES, LANES), BF), ((DISP, 2 * LANES), BF), ((3 * KEYS, LANES), BF),
+            ((LANES, width), BF), (valid_cols.shape, F32),
         ],
         [], 1, (offsets, guide_weight, valid_cols), 1_000_000,
     )
@@ -645,6 +642,7 @@
             pltpu.VMEM((LINE_RUN, DISP, LANES), F32),
             pltpu.VMEM((LINE_RUN, DISP, LANES), F32),
             pltpu.VMEM((LINE_RUN, 3 * KEYS, LANES), F32),
+            pltpu.VMEM((PAIR, devices, 8, 2, 16, LANES), F32),
         ],
         1, (offsets, *consts, *pieces), 1_000_000_000,
     )

time: 26.5 us -> 22 us (0.83)
  waiting for transfers between devices: 8.86 us -> 4.68 us
  local copies, waits for them, and re-layouts: 1.94 us -> 1.07 us
  starting transfers between devices: 9.98 us -> 10.5 us
    ppermute x2 -> x0, waiting for transfers between devices: 7.7 us -> none  [lines_plan(): lax.ppermute(piece, ('cols', 'view'), [(i, i ^ key) for i in range(device...]
    ppermute x5 -> x7, waiting for transfers between devices: 0.01 us -> 3.8 us  [lines_plan(): pieces[key] = lax.ppermute(piece, ('cols', 'view'), moves) if key else piece]
    ppermute x5 -> x7, starting transfers between devices: 7.37 us -> 10.1 us  [lines_plan(): pieces[key] = lax.ppermute(piece, ('cols', 'view'), moves) if key else piece]
    ppermute x2 -> x0, starting transfers between devices: 2.55 us -> none  [lines_plan(): lax.ppermute(piece, ('cols', 'view'), [(i, i ^ key) for i in range(device...]
    squeeze x1 -> x0, local copies, waits for them, and re-layouts: 0.88 us -> none  [lines_plan(): lax.dynamic_index_in_dim(own, me ^ key, 0, False)]
    ppermute x1, starting transfers between devices: 0.07 us -> 0.35 us  [lines_plan(): others = lax.ppermute(rows, 'view', [(0, 1), (1, 0)])]
    ppermute x1, waiting for transfers between devices: 1.15 us -> 0.89 us  [lines_plan(): others = lax.ppermute(rows, 'view', [(0, 1), (1, 0)])]
    pallas_call x8 -> x10, Pallas kernels: 4.81 us -> 4.81 us  [call(): pl.pallas_call(kernel, out_shape=[jax.ShapeDtypeStruct(shape, dtype) for...]
  transfers between devices with their start and end apart: 8 -> 8, of which waited for: 2 -> 3; matrix products, arithmetic and copies ran while one was open for 0% -> 0% of each run, Pallas kernels for 3% -> 4%
where the time goes in v18:
time: 22 us; the launch traced here: 21.8 us
  starting transfers between devices  10.5 us (48%)
  Pallas kernels  4.81 us (22%)
  waiting for transfers between devices  4.68 us (21%)
  local copies, waits for them, and re-layouts  1.07 us (5%)
  other arithmetic  0.62 us (3%)
    ppermute x7, starting transfers between devices, lines_plan(): pieces[key] = lax.ppermute(piece, ('cols', 'view'), moves) if key else piece  10.1 us
    pallas_call x10, Pallas kernels, call(): pl.pallas_call(kernel, out_shape=[jax.ShapeDtypeStruct(shape, dtype) for...  4.81 us
    ppermute x7, waiting for transfers between devices, lines_plan(): pieces[key] = lax.ppermute(piece, ('cols', 'view'), moves) if key else piece  3.8 us
    unnamed x10, local copies, waits for them, and re-layouts  1.07 us
    ppermute x1, waiting for transfers between devices, lines_plan(): others = lax.ppermute(rows, 'view', [(0, 1), (1, 0)])  0.89 us
    select_n x1, other arithmetic, lines_plan(): jnp.where(first, jnp.concatenate([rows, others]), jnp.concatenate([others...  0.62 us
  transfers between devices with their start and end apart: 8, of which 3 were waited for; matrix products, arithmetic and copies ran while one was open for 0% of the time, Pallas kernels for 4%

profile of v18, /device:TPU:0, one launch (start us, length us, event | category | flops | bytes accessed | tf_op | source)
XLA Modules:
  0.0 21.8 jit_solution(6918328373307757779)
XLA Ops:
  0.0 1.0 %copy-done = bf16[1,16,64,256]{3,2,1,0:T(8,128)(2,1)S(1)} copy-done((bf16[1,16,64,256]{3,2,1,0:T(8,128)(2,1)S(1)}, bf16[1,16,64,256]{3,2,1,0:T(8,128)(2,1)}, u32[]{:S(2)}) %copy-start) | copy-done | bytes 524312
  1.1 0.0 copy-start.1
  1.1 0.0 copy-start.2
  1.1 4.1 %collective-permute-start.3 = (bf16[128,256]{1,0:T(8,128)(2,1)S(1)}, bf16[128,256]{1,0:T(8,128)(2,1)S(1)}, u32[]{:S(2)}, u32[]{:S(2)}) collective-permute-start(bf16[128,256]{1,0:T(8,128)(2,1)S(1)} %shard_map.50.rest_1_), channel_id=1, source_target_pairs={{0,8},{1,9},{4,12},{5,13},{8,0},{9,1},{12,4},{13,5},{2,10},{3,11},... | collective-permute-start | bytes 196616 | tf_op jit(solution)/shard_map/ppermute | solution.py:625
  5.2 1.3 %collective-permute-start.5 = (bf16[128,256]{1,0:T(8,128)(2,1)S(1)}, bf16[128,256]{1,0:T(8,128)(2,1)S(1)}, u32[]{:S(2)}, u32[]{:S(2)}) collective-permute-start(bf16[128,256]{1,0:T(8,128)(2,1)S(1)} %shard_map.49.rest_0_), channel_id=1, source_target_pairs={{0,12},{1,13},{4,8},{5,9},{8,4},{9,5},{12,0},{13,1},{2,14},{3,15},... | collective-permute-start | bytes 196616 | tf_op jit(solution)/shard_map/ppermute | solution.py:625
  6.7 0.0 copy-start.3
  6.7 0.0 copy-start.4
  6.7 0.1 collective-permute-start.2
  6.8 2.7 %collective-permute-start.4 = (bf16[136,256]{1,0:T(8,128)(2,1)S(1)}, bf16[136,256]{1,0:T(8,128)(2,1)S(1)}, u32[]{:S(2)}, u32[]{:S(2)}) collective-permute-start(bf16[136,256]{1,0:T(8,128)(2,1)S(1)} %shard_map.52.rest_1_), channel_id=1, source_target_pairs={{0,9},{1,8},{4,13},{5,12},{8,1},{9,0},{12,5},{13,4},{2,11},{3,10},... | collective-permute-start | bytes 208904 | tf_op jit(solution)/shard_map/ppermute | solution.py:625
  9.5 0.2 %collective-permute-start.6 = (bf16[136,256]{1,0:T(8,128)(2,1)S(1)}, bf16[136,256]{1,0:T(8,128)(2,1)S(1)}, u32[]{:S(2)}, u32[]{:S(2)}) collective-permute-start(bf16[136,256]{1,0:T(8,128)(2,1)S(1)} %shard_map.51.rest_1_), channel_id=1, source_target_pairs={{0,13},{1,12},{4,9},{5,8},{8,5},{9,4},{12,1},{13,0},{2,15},{3,14},... | collective-permute-start | bytes 208904 | tf_op jit(solution)/shard_map/ppermute | solution.py:625
  9.8 0.0 collective-permute-done.3.rest_5_
  9.8 1.6 %collective-permute-start.1 = (bf16[128,256]{1,0:T(8,128)(2,1)S(1)}, bf16[128,256]{1,0:T(8,128)(2,1)S(1)}, u32[]{:S(2)}, u32[]{:S(2)}) collective-permute-start(bf16[128,256]{1,0:T(8,128)(2,1)S(1)} %shard_map.48.rest_0_), channel_id=1, source_target_pairs={{0,4},{1,5},{4,0},{5,1},{8,12},{9,13},{12,8},{13,9},{2,6},{3,7},{6... | collective-permute-start | bytes 196616 | tf_op jit(solution)/shard_map/ppermute | solution.py:625
  11.4 0.3 %collective-permute-done.5.rest_7_ = bf16[128,256]{1,0:T(8,128)(2,1)S(1)} collective-permute-done((bf16[128,256]{1,0:T(8,128)(2,1)S(1)}, bf16[128,256]{1,0:T(8,128)(2,1)S(1)}, u32[]{:S(2)}, u32[]{:S(2)}) %collective-permute-start.5) | collective-permute-done | bytes 65568 | tf_op jit(solution)/shard_map/ppermute | solution.py:625
  11.7 0.0 collective-permute-start
  11.8 0.8 %shard_map.46 = (bf16[128,128]{1,0:T(8,128)(2,1)S(1)}, bf16[128,128]{1,0:T(8,128)(2,1)S(1)}, bf16[192,256]{1,0:T(8,128)(2,1)S(1)}, bf16[120,128]{1,0:T(8,128)(2,...) custom-call(s32[16]{0:T(128)S(1)} %copy-done.4, bf16[64,108]{1,0:T(8,128)(2,1)S(1)} %copy-done.3, ...), custom_call_target="tpu_custom_call" | custom-call | flops 1000000 | bytes 1000000 | tf_op jit(solution)/shard_map/pallas_call | solution.py:50
  12.6 3.4 %collective-permute-done.1.rest_3_ = bf16[128,256]{1,0:T(8,128)(2,1)S(1)} collective-permute-done((bf16[128,256]{1,0:T(8,128)(2,1)S(1)}, bf16[128,256]{1,0:T(8,128)(2,1)S(1)}, u32[]{:S(2)}, u32[]{:S(2)}) %collective-permute-start.1) | collective-permute-done | bytes 65568 | tf_op jit(solution)/shard_map/ppermute | solution.py:625
  16.0 0.0 collective-permute-done.rest_2_
  16.0 0.0 collective-permute-done.2.rest_4_
  16.1 0.0 collective-permute-done.4.rest_6_
  16.1 0.0 collective-permute-done.6.rest_8_
  16.1 3.9 %shard_map.55 = f32[2,1024]{1,0:T(2,128)S(1)} custom-call(s32[16]{0:T(128)S(1)} %copy-done.4, bf16[128,128]{1,0:T(8,128)(2,1)S(1)} %get-tuple-element.11.order, bf16[128,128]{1,0:T(8,128)(2,1)S(1)} %get-tuple-element.12.order_band, bf16[192,256]{1,0:T(8,128)(2,1)S(1)} %get-tuple-element.13.flip, bf16[120,128]{1,0:T(8,128)(2,1)S(1)} %get-tuple-element.14.guide, ...), custom_call_target="tpu_custom_call" | custom-call | flops 1000000000 | bytes 1000000 | tf_op jit(solution)/shard_map/pallas_call | solution.py:50
  19.9 0.4 %collective-permute-start.7 = (f32[2,1024]{1,0:T(2,128)S(1)}, f32[2,1024]{1,0:T(2,128)S(1)}, u32[]{:S(2)}, u32[]{:S(2)}) collective-permute-start(f32[2,1024]{1,0:T(2,128)S(1)} %shard_map.55), channel_id=1, source_target_pairs={{0,1},{1,0},{2,3},{3,2},{4,5},{5,4},{6,7},{7,6},{8,9},{9,8},{10,11... | collective-permute-start | bytes 24584 | tf_op jit(solution)/shard_map/ppermute | solution.py:649
  20.3 0.9 %collective-permute-done.7 = f32[2,1024]{1,0:T(2,128)S(1)} collective-permute-done((f32[2,1024]{1,0:T(2,128)S(1)}, f32[2,1024]{1,0:T(2,128)S(1)}, u32[]{:S(2)}, u32[]{:S(2)}) %collective-permute-start.7) | collective-permute-done | bytes 8224 | tf_op jit(solution)/shard_map/ppermute | solution.py:649
  21.2 0.6 %maximum_select_fusion = f32[1,4,1024]{2,1,0:T(4,128)} fusion(f32[1,2,1024]{2,1,0:T(2,128)S(1)} %bitcast.12, f32[1,2,1024]{2,1,0:T(2,128)S(1)} %bitcast.11, pred[]{:T(512)S(6)} %eq.3), kind=kLoop, calls=%fused_computation | loop fusion | flops 12288 | bytes 32769 | tf_op jit(solution)/shard_map/jit(_where)/select_n | solution.py:651
  (13 shorter events, 0.1 us)
Async XLA Ops:
  0.0 1.0 %copy-start = (bf16[1,16,64,256]{3,2,1,0:T(8,128)(2,1)S(1)}, bf16[1,16,64,256]{3,2,1,0:T(8,128)(2,1)}, u32[]{:S(2)}) copy-start(bf16[1,16,64,256]{3,2,1,0:T(8,128)(2,1)} %param.4) | copy-start | bytes 1572868
  1.1 5.5 %copy-start.1 = (bf16[1,16,64,256]{3,2,1,0:T(8,128)(2,1)S(1)}, bf16[1,16,64,256]{3,2,1,0:T(8,128)(2,1)}, u32[]{:S(2)}) copy-start(bf16[1,16,64,256]{3,2,1,0:T(8,128)(2,1)} %param.4) | copy-start | bytes 1572868
  1.1 5.5 %copy-start.2 = (s32[2,256]{1,0:T(2,128)S(1)}, s32[2,256]{1,0:T(2,128)}, u32[]{:S(2)}) copy-start(s32[2,256]{1,0:T(2,128)} %rest_0_.5) | copy-start | bytes 6148
  1.1 8.6 %collective-permute-start.3 = (bf16[128,256]{1,0:T(8,128)(2,1)S(1)}, bf16[128,256]{1,0:T(8,128)(2,1)S(1)}, u32[]{:S(2)}, u32[]{:S(2)}) collective-permute-start(bf16[128,256]{1,0:T(8,128)(2,1)S(1)} %shard_map.50.rest_1_), channel_id=1, source_target_pairs={{0,8},{1,9},{4,12},{5,13},{8,0},{9,1},{12,4},{13,5},{2,10},{3,11},... | collective-permute-start | bytes 196616 | tf_op jit(solution)/shard_map/ppermute | solution.py:625
  5.2 6.5 %collective-permute-start.5 = (bf16[128,256]{1,0:T(8,128)(2,1)S(1)}, bf16[128,256]{1,0:T(8,128)(2,1)S(1)}, u32[]{:S(2)}, u32[]{:S(2)}) collective-permute-start(bf16[128,256]{1,0:T(8,128)(2,1)S(1)} %shard_map.49.rest_0_), channel_id=1, source_target_pairs={{0,12},{1,13},{4,8},{5,9},{8,4},{9,5},{12,0},{13,1},{2,14},{3,15},... | collective-permute-start | bytes 196616 | tf_op jit(solution)/shard_map/ppermute | solution.py:625
  6.7 5.1 %copy-start.3 = (bf16[64,108]{1,0:T(8,128)(2,1)S(1)}, bf16[64,108]{1,0:T(8,128)(2,1)}, u32[]{:S(2)}) copy-start(bf16[64,108]{1,0:T(8,128)(2,1)} %guide.1) | copy-start | bytes 41476
  6.7 5.1 %copy-start.4 = (s32[16]{0:T(128)S(1)}, s32[16]{0:T(128)}, u32[]{:S(2)}) copy-start(s32[16]{0:T(128)} %offsets.3) | copy-start | bytes 196
  6.7 9.4 %collective-permute-start.2 = (bf16[136,256]{1,0:T(8,128)(2,1)S(1)}, bf16[136,256]{1,0:T(8,128)(2,1)S(1)}, u32[]{:S(2)}, u32[]{:S(2)}) collective-permute-start(bf16[136,256]{1,0:T(8,128)(2,1)S(1)} %shard_map.53.rest_0_), channel_id=1, source_target_pairs={{0,5},{1,4},{4,1},{5,0},{8,13},{9,12},{12,9},{13,8},{2,7},{3,6},{6... | collective-permute-start | bytes 208904 | tf_op jit(solution)/shard_map/ppermute | solution.py:625
  6.8 9.3 %collective-permute-start.4 = (bf16[136,256]{1,0:T(8,128)(2,1)S(1)}, bf16[136,256]{1,0:T(8,128)(2,1)S(1)}, u32[]{:S(2)}, u32[]{:S(2)}) collective-permute-start(bf16[136,256]{1,0:T(8,128)(2,1)S(1)} %shard_map.52.rest_1_), channel_id=1, source_target_pairs={{0,9},{1,8},{4,13},{5,12},{8,1},{9,0},{12,5},{13,4},{2,11},{3,10},... | collective-permute-start | bytes 208904 | tf_op jit(solution)/shard_map/ppermute | solution.py:625
  9.5 6.5 %collective-permute-start.6 = (bf16[136,256]{1,0:T(8,128)(2,1)S(1)}, bf16[136,256]{1,0:T(8,128)(2,1)S(1)}, u32[]{:S(2)}, u32[]{:S(2)}) collective-permute-start(bf16[136,256]{1,0:T(8,128)(2,1)S(1)} %shard_map.51.rest_1_), channel_id=1, source_target_pairs={{0,13},{1,12},{4,9},{5,8},{8,5},{9,4},{12,1},{13,0},{2,15},{3,14},... | collective-permute-start | bytes 208904 | tf_op jit(solution)/shard_map/ppermute | solution.py:625
  9.8 6.3 %collective-permute-start.1 = (bf16[128,256]{1,0:T(8,128)(2,1)S(1)}, bf16[128,256]{1,0:T(8,128)(2,1)S(1)}, u32[]{:S(2)}, u32[]{:S(2)}) collective-permute-start(bf16[128,256]{1,0:T(8,128)(2,1)S(1)} %shard_map.48.rest_0_), channel_id=1, source_target_pairs={{0,4},{1,5},{4,0},{5,1},{8,12},{9,13},{12,8},{13,9},{2,6},{3,7},{6... | collective-permute-start | bytes 196616 | tf_op jit(solution)/shard_map/ppermute | solution.py:625
  11.7 4.3 %collective-permute-start = (bf16[128,256]{1,0:T(8,128)(2,1)S(1)}, bf16[128,256]{1,0:T(8,128)(2,1)S(1)}, u32[]{:S(2)}, u32[]{:S(2)}) collective-permute-start(bf16[128,256]{1,0:T(8,128)(2,1)S(1)} %shard_map.47.rest_0_), channel_id=1, source_target_pairs={{0,1},{1,0},{4,5},{5,4},{8,9},{9,8},{12,13},{13,12},{2,3},{3,2},{6... | collective-permute-start | bytes 196616 | tf_op jit(solution)/shard_map/ppermute | solution.py:625
  19.9 1.2 %collective-permute-start.7 = (f32[2,1024]{1,0:T(2,128)S(1)}, f32[2,1024]{1,0:T(2,128)S(1)}, u32[]{:S(2)}, u32[]{:S(2)}) collective-permute-start(f32[2,1024]{1,0:T(2,128)S(1)} %shard_map.55), channel_id=1, source_target_pairs={{0,1},{1,0},{2,3},{3,2},{4,5},{5,4},{6,7},{7,6},{8,9},{9,8},{10,11... | collective-permute-start | bytes 24584 | tf_op jit(solution)/shard_map/ppermute | solution.py:649

commit v19 on v17

--- a/solution.py
+++ b/solution.py
@@ -412,7 +412,7 @@
 def lines_kernel(
     offsets, order, flip, guide, spread, *rest
 ):
-    pieces, (out, blocks, valid, gate_rows, cost_rows, vol, done, wts) = rest[:-8], rest[-8:]
+    pieces, (out, blocks, valid, wts) = rest[:-4], rest[-4:]
     near, pieces = pieces[0], pieces[1:]
     tiles = len(pieces)
     width = tiles * LANES
@@ -443,6 +443,16 @@
     def place_of(i, quad, two):
         return i * LINE_PARTS + 8 * (tiles - 2 - 4 * quad - 2 * two)
 
+    gate_parts, cost_parts = {}, {}
+
+    def joined(parts, two):
+        rows = [
+            parts[t, place]
+            for t in (2 * two, 2 * two + 1)
+            for place in range(0, LANES, 16)
+        ]
+        return jnp.concatenate(rows, axis=0)
+
     quads = [(i, quad) for i in range(PAIR) for quad in range(tiles // 4)]
     for i, quad in quads:
         refs = [tile_of(0, i, 4 * quad + q) for q in range(4)]
@@ -452,9 +462,8 @@
             gates = [jnp.where(low_half, pair, 0.0), jnp.where(low_half, 0.0, pair)]
             place = place_of(i, quad, two)
             for t in range(LINE_RUN):
-                row = t * LANES + place
                 r = 8 * t
-                gate_rows[row : row + 16, :] = jnp.concatenate(
+                gate_parts[t, place] = jnp.concatenate(
                     [gates[1][r : r + 8], gates[0][r : r + 8]], axis=0
                 ).astype(BF)
 
@@ -466,8 +475,7 @@
     unit = jnp.where(row >= 2 * GROUPS, SHARPNESS / math.log(2.0), 1.0)
 
     def weigh(two):
-        lo = 2 * two * LANES
-        logits = dot_t(guide[...], gate_rows[lo : lo + 2 * LANES, :])
+        logits = dot_t(guide[...], joined(gate_parts, two))
         for i in range(2):
             t = 2 * two + i
             z = jnp.tanh(logits[:, i * LANES : (i + 1) * LANES]) + GATE_FLOOR
@@ -508,7 +516,6 @@
                 products.append(jnp.dot(lhs, rhs, preferred_element_type=F32))
             place = place_of(i, quad, two)
             for t in range(LINE_RUN):
-                row = t * LANES + place
                 r = 8 * t
                 within = reached < LANES - t
                 both = []
@@ -526,19 +533,19 @@
                             axis=1,
                         )
                     )
-                cost_rows[row : row + 16, :] = jnp.concatenate(both, axis=0).astype(BF)
+                cost_parts[t, place] = jnp.concatenate(both, axis=0).astype(BF)
             weigh(step)
             step += 1
 
+    vol = []
     for two in range(LINE_RUN // 2):
-        lo = 2 * two * LANES
-        costs = dot_t(flip[...], cost_rows[lo : lo + 2 * LANES, :])
-        for i in range(2):
-            vol[2 * two + i] = costs[:, i * LANES : (i + 1) * LANES]
+        costs = dot_t(flip[...], joined(cost_parts, two))
+        vol += [costs[:, :LANES], costs[:, LANES:]]
+    done = {}
 
     for group in range(GROUPS):
         starts = [group * DGROUP + 8 * half for half in range(2)]
-        v = [[vol[t, at : at + 8, :] for t in range(LINE_RUN)] for at in starts]
+        v = [[vol[t][at : at + 8] for t in range(LINE_RUN)] for at in starts]
         for layer in range(LAYERS):
             s = 3**layer
             fresh = [[], []]
@@ -554,7 +561,7 @@
             v = fresh
         for half, at in enumerate(starts):
             for t in range(LINE_RUN):
-                done[t, at : at + 8, :] = v[half][t]
+                done[t, at // 8] = v[half][t]
 
     sub = iota((8, LANES), 0)
     results = []
@@ -563,7 +570,7 @@
         moments = totals
         for s in range(8):
             t = LINE_RUN - 1 - (8 * block + s)
-            v = [done[t, 8 * i : 8 * i + 8, :] for i in range(DISP // 8)]
+            v = [done[t, i] for i in range(DISP // 8)]
             top = v
             while len(top) > 1:
                 top = [jnp.maximum(a, b) for a, b in zip(top[::2], top[1::2])] + top[len(top) & ~1 :]
@@ -608,19 +615,13 @@
     own = features.reshape(devices, rows, BLOCK)
     pieces = [None] * devices
     gone = ()
-    me = 2 * lax.axis_index("cols") + lax.axis_index("view")
-    heads = [lax.dynamic_index_in_dim(own, me ^ key, 0, False) for key in (6, 4)]
     for key in (1, 2, 6, 4, 7, 5, 3, 0):
         masked = key % 2 and key > 1
-        if key in (4, 6):
-            piece = heads[0 if key == 6 else 1]
-            pieces[key] = lax.ppermute(piece, ("cols", "view"), [(i, i ^ key) for i in range(devices)])
-            continue
         (piece,) = call(
             functools.partial(pack_kernel, key),
             [((rows + (MASKS if masked else 0), BLOCK), BF)],
             [], 0,
-            (own,) + ((valid_cols,) if masked else ()) + gone + tuple(heads),
+            (own,) + ((valid_cols,) if masked else ()) + gone,
             1_000_000,
         )
         gone = (piece,)
@@ -640,10 +641,6 @@
         [
             pltpu.VMEM((devices, rows, BLOCK), BF),
             pltpu.VMEM((n,) + valid_cols.shape, F32),
-            pltpu.VMEM((LINE_RUN * LANES, LANES), BF),
-            pltpu.VMEM((LINE_RUN * LANES, 2 * LANES), BF),
-            pltpu.VMEM((LINE_RUN, DISP, LANES), F32),
-            pltpu.VMEM((LINE_RUN, DISP, LANES), F32),
             pltpu.VMEM((LINE_RUN, 3 * KEYS, LANES), F32),
         ],
         1, (offsets, *consts, *pieces), 1_000_000_000,

time: 26.5 us -> 22.1 us (0.83)
  waiting for transfers between devices: 8.86 us -> 4.69 us
  local copies, waits for them, and re-layouts: 1.94 us -> 1.07 us
  starting transfers between devices: 9.98 us -> 10.5 us
    ppermute x2 -> x0, waiting for transfers between devices: 7.7 us -> none  [lines_plan(): lax.ppermute(piece, ('cols', 'view'), [(i, i ^ key) for i in range(device...]
    ppermute x5 -> x7, waiting for transfers between devices: 0.01 us -> 3.82 us  [lines_plan(): pieces[key] = lax.ppermute(piece, ('cols', 'view'), moves) if key else piece]
    ppermute x5 -> x7, starting transfers between devices: 7.37 us -> 10.1 us  [lines_plan(): pieces[key] = lax.ppermute(piece, ('cols', 'view'), moves) if key else piece]
    ppermute x2 -> x0, starting transfers between devices: 2.55 us -> none  [lines_plan(): lax.ppermute(piece, ('cols', 'view'), [(i, i ^ key) for i in range(device...]
    squeeze x1 -> x0, local copies, waits for them, and re-layouts: 0.88 us -> none  [lines_plan(): lax.dynamic_index_in_dim(own, me ^ key, 0, False)]
    ppermute x1, starting transfers between devices: 0.07 us -> 0.36 us  [lines_plan(): others = lax.ppermute(rows, 'view', [(0, 1), (1, 0)])]
    ppermute x1, waiting for transfers between devices: 1.15 us -> 0.87 us  [lines_plan(): others = lax.ppermute(rows, 'view', [(0, 1), (1, 0)])]
    pallas_call x8 -> x10, Pallas kernels: 4.81 us -> 4.82 us  [call(): pl.pallas_call(kernel, out_shape=[jax.ShapeDtypeStruct(shape, dtype) for...]
  transfers between devices with their start and end apart: 8 -> 8, of which waited for: 2 -> 3; matrix products, arithmetic and copies ran while one was open for 0% -> 0% of each run, Pallas kernels for 3% -> 4%
where the time goes in v19:
time: 22.1 us; the launch traced here: 21.8 us
  starting transfers between devices  10.5 us (48%)
  Pallas kernels  4.82 us (22%)
  waiting for transfers between devices  4.69 us (21%)
  local copies, waits for them, and re-layouts  1.07 us (5%)
  other arithmetic  0.62 us (3%)
    ppermute x7, starting transfers between devices, lines_plan(): pieces[key] = lax.ppermute(piece, ('cols', 'view'), moves) if key else piece  10.1 us
    pallas_call x10, Pallas kernels, call(): pl.pallas_call(kernel, out_shape=[jax.ShapeDtypeStruct(shape, dtype) for...  4.82 us
    ppermute x7, waiting for transfers between devices, lines_plan(): pieces[key] = lax.ppermute(piece, ('cols', 'view'), moves) if key else piece  3.82 us
    unnamed x10, local copies, waits for them, and re-layouts  1.07 us
    ppermute x1, waiting for transfers between devices, lines_plan(): others = lax.ppermute(rows, 'view', [(0, 1), (1, 0)])  0.87 us
    select_n x1, other arithmetic, lines_plan(): jnp.where(first, jnp.concatenate([rows, others]), jnp.concatenate([others...  0.62 us
  transfers between devices with their start and end apart: 8, of which 3 were waited for; matrix products, arithmetic and copies ran while one was open for 0% of the time, Pallas kernels for 4%

profile of v19, /device:TPU:0, one launch (start us, length us, event | category | flops | bytes accessed | tf_op | source)
XLA Modules:
  0.0 21.8 jit_solution(8176223479325912417)
XLA Ops:
  0.0 1.0 %copy-done = bf16[1,16,64,256]{3,2,1,0:T(8,128)(2,1)S(1)} copy-done((bf16[1,16,64,256]{3,2,1,0:T(8,128)(2,1)S(1)}, bf16[1,16,64,256]{3,2,1,0:T(8,128)(2,1)}, u32[]{:S(2)}) %copy-start) | copy-done | bytes 524312
  1.1 0.0 copy-start.1
  1.1 0.0 copy-start.2
  1.1 4.1 %collective-permute-start.3 = (bf16[128,256]{1,0:T(8,128)(2,1)S(1)}, bf16[128,256]{1,0:T(8,128)(2,1)S(1)}, u32[]{:S(2)}, u32[]{:S(2)}) collective-permute-start(bf16[128,256]{1,0:T(8,128)(2,1)S(1)} %shard_map.50.rest_1_), channel_id=1, source_target_pairs={{0,8},{1,9},{4,12},{5,13},{8,0},{9,1},{12,4},{13,5},{2,10},{3,11},... | collective-permute-start | bytes 196616 | tf_op jit(solution)/shard_map/ppermute | solution.py:629
  5.2 1.3 %collective-permute-start.5 = (bf16[128,256]{1,0:T(8,128)(2,1)S(1)}, bf16[128,256]{1,0:T(8,128)(2,1)S(1)}, u32[]{:S(2)}, u32[]{:S(2)}) collective-permute-start(bf16[128,256]{1,0:T(8,128)(2,1)S(1)} %shard_map.49.rest_0_), channel_id=1, source_target_pairs={{0,12},{1,13},{4,8},{5,9},{8,4},{9,5},{12,0},{13,1},{2,14},{3,15},... | collective-permute-start | bytes 196616 | tf_op jit(solution)/shard_map/ppermute | solution.py:629
  6.7 0.0 copy-start.3
  6.7 0.0 copy-start.4
  6.7 0.1 collective-permute-start.2
  6.8 2.7 %collective-permute-start.4 = (bf16[136,256]{1,0:T(8,128)(2,1)S(1)}, bf16[136,256]{1,0:T(8,128)(2,1)S(1)}, u32[]{:S(2)}, u32[]{:S(2)}) collective-permute-start(bf16[136,256]{1,0:T(8,128)(2,1)S(1)} %shard_map.52.rest_1_), channel_id=1, source_target_pairs={{0,9},{1,8},{4,13},{5,12},{8,1},{9,0},{12,5},{13,4},{2,11},{3,10},... | collective-permute-start | bytes 208904 | tf_op jit(solution)/shard_map/ppermute | solution.py:629
  9.5 0.2 %collective-permute-start.6 = (bf16[136,256]{1,0:T(8,128)(2,1)S(1)}, bf16[136,256]{1,0:T(8,128)(2,1)S(1)}, u32[]{:S(2)}, u32[]{:S(2)}) collective-permute-start(bf16[136,256]{1,0:T(8,128)(2,1)S(1)} %shard_map.51.rest_1_), channel_id=1, source_target_pairs={{0,13},{1,12},{4,9},{5,8},{8,5},{9,4},{12,1},{13,0},{2,15},{3,14},... | collective-permute-start | bytes 208904 | tf_op jit(solution)/shard_map/ppermute | solution.py:629
  9.8 0.0 collective-permute-done.3.rest_5_
  9.8 1.6 %collective-permute-start.1 = (bf16[128,256]{1,0:T(8,128)(2,1)S(1)}, bf16[128,256]{1,0:T(8,128)(2,1)S(1)}, u32[]{:S(2)}, u32[]{:S(2)}) collective-permute-start(bf16[128,256]{1,0:T(8,128)(2,1)S(1)} %shard_map.48.rest_0_), channel_id=1, source_target_pairs={{0,4},{1,5},{4,0},{5,1},{8,12},{9,13},{12,8},{13,9},{2,6},{3,7},{6... | collective-permute-start | bytes 196616 | tf_op jit(solution)/shard_map/ppermute | solution.py:629
  11.4 0.3 %collective-permute-done.5.rest_7_ = bf16[128,256]{1,0:T(8,128)(2,1)S(1)} collective-permute-done((bf16[128,256]{1,0:T(8,128)(2,1)S(1)}, bf16[128,256]{1,0:T(8,128)(2,1)S(1)}, u32[]{:S(2)}, u32[]{:S(2)}) %collective-permute-start.5) | collective-permute-done | bytes 65568 | tf_op jit(solution)/shard_map/ppermute | solution.py:629
  11.7 0.0 collective-permute-start
  11.8 0.8 %shard_map.46 = (bf16[128,128]{1,0:T(8,128)(2,1)S(1)}, bf16[192,256]{1,0:T(8,128)(2,1)S(1)}, bf16[120,128]{1,0:T(8,128)(2,1)S(1)}, bf16[128,1024]{1,0:T(8,128)(2,1)S(1)}, f32[2,256]{1,0:T(2,128)S(1)}) custom-call(s32[16]{0:T(128)S(1)} %copy-done.4, bf16[64,108]{1,0:T(8,128)(2,1)S(1)} %copy-done.3, s32[2,256]{1,0:T(2,128)S(1)} %copy-done.2), custom_call_target="tpu_custom_call" | custom-call | flops 1000000 | bytes 1000000 | tf_op jit(solution)/shard_map/pallas_call | solution.py:50
  12.6 3.5 %collective-permute-done.1.rest_3_ = bf16[128,256]{1,0:T(8,128)(2,1)S(1)} collective-permute-done((bf16[128,256]{1,0:T(8,128)(2,1)S(1)}, bf16[128,256]{1,0:T(8,128)(2,1)S(1)}, u32[]{:S(2)}, u32[]{:S(2)}) %collective-permute-start.1) | collective-permute-done | bytes 65568 | tf_op jit(solution)/shard_map/ppermute | solution.py:629
  16.0 0.0 collective-permute-done.rest_2_
  16.0 0.0 collective-permute-done.2.rest_4_
  16.1 0.0 collective-permute-done.4.rest_6_
  16.1 0.0 collective-permute-done.6.rest_8_
  16.1 3.9 %shard_map.55 = f32[2,1024]{1,0:T(2,128)S(1)} custom-call(s32[16]{0:T(128)S(1)} %copy-done.4, bf16[128,128]{1,0:T(8,128)(2,1)S(1)} %get-tuple-element.10.order, bf16[192,256]{1,0:T(8,128)(2,1)S(1)} %get-tuple-element.11.flip, bf16[120,128]{1,0:T(8,128)(2,1)S(1)} %get-tuple-element.12.guide, bf16[128,1024]{1,0:T(8,128)(2,1)S(1)} %get-tuple-element.13.spread, ...), custom_call_target="tpu_custom_call" | custom-call | flops 1000000000 | bytes 1000000 | tf_op jit(solution)/shard_map/pallas_call | solution.py:50
  20.0 0.4 %collective-permute-start.7 = (f32[2,1024]{1,0:T(2,128)S(1)}, f32[2,1024]{1,0:T(2,128)S(1)}, u32[]{:S(2)}, u32[]{:S(2)}) collective-permute-start(f32[2,1024]{1,0:T(2,128)S(1)} %shard_map.55), channel_id=1, source_target_pairs={{0,1},{1,0},{2,3},{3,2},{4,5},{5,4},{6,7},{7,6},{8,9},{9,8},{10,11... | collective-permute-start | bytes 24584 | tf_op jit(solution)/shard_map/ppermute | solution.py:648
  20.4 0.9 %collective-permute-done.7 = f32[2,1024]{1,0:T(2,128)S(1)} collective-permute-done((f32[2,1024]{1,0:T(2,128)S(1)}, f32[2,1024]{1,0:T(2,128)S(1)}, u32[]{:S(2)}, u32[]{:S(2)}) %collective-permute-start.7) | collective-permute-done | bytes 8224 | tf_op jit(solution)/shard_map/ppermute | solution.py:648
  21.2 0.6 %maximum_select_fusion = f32[1,4,1024]{2,1,0:T(4,128)} fusion(f32[1,2,1024]{2,1,0:T(2,128)S(1)} %bitcast.12, f32[1,2,1024]{2,1,0:T(2,128)S(1)} %bitcast.11, pred[]{:T(512)S(6)} %eq.3), kind=kLoop, calls=%fused_computation | loop fusion | flops 12288 | bytes 32769 | tf_op jit(solution)/shard_map/jit(_where)/select_n | solution.py:650
  (13 shorter events, 0.1 us)
Async XLA Ops:
  0.0 1.0 %copy-start = (bf16[1,16,64,256]{3,2,1,0:T(8,128)(2,1)S(1)}, bf16[1,16,64,256]{3,2,1,0:T(8,128)(2,1)}, u32[]{:S(2)}) copy-start(bf16[1,16,64,256]{3,2,1,0:T(8,128)(2,1)} %param.4) | copy-start | bytes 1572868
  1.1 5.5 %copy-start.1 = (bf16[1,16,64,256]{3,2,1,0:T(8,128)(2,1)S(1)}, bf16[1,16,64,256]{3,2,1,0:T(8,128)(2,1)}, u32[]{:S(2)}) copy-start(bf16[1,16,64,256]{3,2,1,0:T(8,128)(2,1)} %param.4) | copy-start | bytes 1572868
  1.1 5.5 %copy-start.2 = (s32[2,256]{1,0:T(2,128)S(1)}, s32[2,256]{1,0:T(2,128)}, u32[]{:S(2)}) copy-start(s32[2,256]{1,0:T(2,128)} %rest_0_.5) | copy-start | bytes 6148
  1.1 8.6 %collective-permute-start.3 = (bf16[128,256]{1,0:T(8,128)(2,1)S(1)}, bf16[128,256]{1,0:T(8,128)(2,1)S(1)}, u32[]{:S(2)}, u32[]{:S(2)}) collective-permute-start(bf16[128,256]{1,0:T(8,128)(2,1)S(1)} %shard_map.50.rest_1_), channel_id=1, source_target_pairs={{0,8},{1,9},{4,12},{5,13},{8,0},{9,1},{12,4},{13,5},{2,10},{3,11},... | collective-permute-start | bytes 196616 | tf_op jit(solution)/shard_map/ppermute | solution.py:629
  5.2 6.5 %collective-permute-start.5 = (bf16[128,256]{1,0:T(8,128)(2,1)S(1)}, bf16[128,256]{1,0:T(8,128)(2,1)S(1)}, u32[]{:S(2)}, u32[]{:S(2)}) collective-permute-start(bf16[128,256]{1,0:T(8,128)(2,1)S(1)} %shard_map.49.rest_0_), channel_id=1, source_target_pairs={{0,12},{1,13},{4,8},{5,9},{8,4},{9,5},{12,0},{13,1},{2,14},{3,15},... | collective-permute-start | bytes 196616 | tf_op jit(solution)/shard_map/ppermute | solution.py:629
  6.7 5.1 %copy-start.3 = (bf16[64,108]{1,0:T(8,128)(2,1)S(1)}, bf16[64,108]{1,0:T(8,128)(2,1)}, u32[]{:S(2)}) copy-start(bf16[64,108]{1,0:T(8,128)(2,1)} %guide.1) | copy-start | bytes 41476
  6.7 5.1 %copy-start.4 = (s32[16]{0:T(128)S(1)}, s32[16]{0:T(128)}, u32[]{:S(2)}) copy-start(s32[16]{0:T(128)} %offsets.3) | copy-start | bytes 196
  6.7 9.4 %collective-permute-start.2 = (bf16[136,256]{1,0:T(8,128)(2,1)S(1)}, bf16[136,256]{1,0:T(8,128)(2,1)S(1)}, u32[]{:S(2)}, u32[]{:S(2)}) collective-permute-start(bf16[136,256]{1,0:T(8,128)(2,1)S(1)} %shard_map.53.rest_0_), channel_id=1, source_target_pairs={{0,5},{1,4},{4,1},{5,0},{8,13},{9,12},{12,9},{13,8},{2,7},{3,6},{6... | collective-permute-start | bytes 208904 | tf_op jit(solution)/shard_map/ppermute | solution.py:629
  6.8 9.3 %collective-permute-start.4 = (bf16[136,256]{1,0:T(8,128)(2,1)S(1)}, bf16[136,256]{1,0:T(8,128)(2,1)S(1)}, u32[]{:S(2)}, u32[]{:S(2)}) collective-permute-start(bf16[136,256]{1,0:T(8,128)(2,1)S(1)} %shard_map.52.rest_1_), channel_id=1, source_target_pairs={{0,9},{1,8},{4,13},{5,12},{8,1},{9,0},{12,5},{13,4},{2,11},{3,10},... | collective-permute-start | bytes 208904 | tf_op jit(solution)/shard_map/ppermute | solution.py:629
  9.5 6.5 %collective-permute-start.6 = (bf16[136,256]{1,0:T(8,128)(2,1)S(1)}, bf16[136,256]{1,0:T(8,128)(2,1)S(1)}, u32[]{:S(2)}, u32[]{:S(2)}) collective-permute-start(bf16[136,256]{1,0:T(8,128)(2,1)S(1)} %shard_map.51.rest_1_), channel_id=1, source_target_pairs={{0,13},{1,12},{4,9},{5,8},{8,5},{9,4},{12,1},{13,0},{2,15},{3,14},... | collective-permute-start | bytes 208904 | tf_op jit(solution)/shard_map/ppermute | solution.py:629
  9.8 6.3 %collective-permute-start.1 = (bf16[128,256]{1,0:T(8,128)(2,1)S(1)}, bf16[128,256]{1,0:T(8,128)(2,1)S(1)}, u32[]{:S(2)}, u32[]{:S(2)}) collective-permute-start(bf16[128,256]{1,0:T(8,128)(2,1)S(1)} %shard_map.48.rest_0_), channel_id=1, source_target_pairs={{0,4},{1,5},{4,0},{5,1},{8,12},{9,13},{12,8},{13,9},{2,6},{3,7},{6... | collective-permute-start | bytes 196616 | tf_op jit(solution)/shard_map/ppermute | solution.py:629
  11.7 4.3 %collective-permute-start = (bf16[128,256]{1,0:T(8,128)(2,1)S(1)}, bf16[128,256]{1,0:T(8,128)(2,1)S(1)}, u32[]{:S(2)}, u32[]{:S(2)}) collective-permute-start(bf16[128,256]{1,0:T(8,128)(2,1)S(1)} %shard_map.47.rest_0_), channel_id=1, source_target_pairs={{0,1},{1,0},{4,5},{5,4},{8,9},{9,8},{12,13},{13,12},{2,3},{3,2},{6... | collective-permute-start | bytes 196616 | tf_op jit(solution)/shard_map/ppermute | solution.py:629
  20.0 1.2 %collective-permute-start.7 = (f32[2,1024]{1,0:T(2,128)S(1)}, f32[2,1024]{1,0:T(2,128)S(1)}, u32[]{:S(2)}, u32[]{:S(2)}) collective-permute-start(f32[2,1024]{1,0:T(2,128)S(1)} %shard_map.55), channel_id=1, source_target_pairs={{0,1},{1,0},{2,3},{3,2},{4,5},{5,4},{6,7},{7,6},{8,9},{9,8},{10,11... | collective-permute-start | bytes 24584 | tf_op jit(solution)/shard_map/ppermute | solution.py:648

commit v20 on v11

--- a/solution.py
+++ b/solution.py
@@ -375,9 +375,9 @@
     return join(pieces, own.shape[0] // n, n)
 
 
-LINE_RUN = 16
+LINE_RUN = 8
 PAIR = 2
-LINE_PARTS = LANES // PAIR
+LINE_PARTS = LANES
 
 
 MASKS = 8
@@ -396,22 +396,21 @@
         ).astype(BF)
 
 
-def constants_kernel(offsets, guide, valid, order, flip, guide_out, spread, masks):
+def constants_kernel(offsets, guide, valid, order, order_band, flip, guide_out, spread, masks):
     masks[...] = valid[...].astype(F32)
     row = iota((LANES, LANES), 0)
-    from_lane = LANES - 1 - LINE_RUN * (row & 7) - (row >> 3)
+    from_lane = LANES - 1 - LINE_RUN * (row & (PARTS - 1)) - (row >> 4)
     order[...] = jnp.where(iota((LANES, LANES), 1) == from_lane, 1.0, 0.0).astype(BF)
+    from_lane = LANES - 1 - (row & 64) - LINE_RUN * (row & 7) - ((row >> 3) & 7)
+    order_band[...] = jnp.where(iota((LANES, LANES), 1) == from_lane, 1.0, 0.0).astype(BF)
     back = 2 * LANES - 1 - iota((DISP, 2 * LANES), 0)
     flip[...] = jnp.where(iota((DISP, 2 * LANES), 1) == back, 1.0, 0.0).astype(BF)
     guide_out[...] = spread_guide(guide[...]) * 0.5
-    block_of = LINE_PARTS - 1 - (iota(spread.shape, 1) >> 4)
-    here = (iota(spread.shape, 0) & (LINE_PARTS - 1)) == block_of
-    spread[...] = jnp.where(here, 1.0, 0.0).astype(BF)
-
-
-def lines_kernel(
-    offsets, order, flip, guide, spread, *rest
-):
+    block_of = LANES - 1 - (iota(spread.shape, 1) >> 3)
+    spread[...] = jnp.where(iota(spread.shape, 0) == block_of, 1.0, 0.0).astype(BF)
+
+
+def lines_kernel(offsets, order, order_band, flip, guide, spread, *rest):
     pieces, (out, blocks, valid, gate_rows, cost_rows, vol, done, wts) = rest[:-8], rest[-8:]
     near, pieces = pieces[0], pieces[1:]
     tiles = len(pieces)
@@ -427,8 +426,9 @@
     at = PAIR * me
     offs = [offsets[at + i] for i in range(PAIR)]
     ch_lane = iota((CHANNELS, LANES), 1)
-    diagonal = iota((8, LANES), 1) - LINE_RUN * iota((8, LANES), 0)
+    low_lane = ch_lane < LANES // 2
     low_half = iota((LANES, LANES), 1) < CHANNELS
+    reached = iota((8, LANES), 1) + LINE_RUN * iota((8, LANES), 0)
     scale = 1.0 / math.sqrt(CHANNELS)
     empty = jnp.zeros((CHANNELS, LANES), F32)
 
@@ -444,136 +444,134 @@
 
         off = offs[i]
         rolled = [pltpu.roll(tile_of(1, w).astype(F32) * mask_of(1, w), off, 1) for w in range(tiles)]
-        shifted = [empty.astype(BF)] * 2
+        line = [empty, empty]
         for w in range(tiles):
-            shifted.append(jnp.where(ch_lane < off, rolled[w - 1] if w else empty, rolled[w]).astype(BF))
+            line.append(jnp.where(ch_lane < off, rolled[w - 1] if w else empty, rolled[w]))
+        turned = [empty] + [pltpu.roll(tile, LANES // 2, 1) if w else tile for w, tile in enumerate(line[1:])]
+        shifted = [tile.astype(BF) for tile in line]
+        halfway = [jnp.where(low_lane, a, b).astype(BF) for a, b in zip(turned, turned[1:])]
+
         for quad in range(tiles // 4):
             refs = [tile_of(0, 4 * quad + q) for q in range(4)]
             masked = [refs[q] * (mask_of(0, 4 * quad + q) * scale).astype(BF) for q in range(4)]
             cols = dot_t(order[...], jnp.concatenate(refs, axis=0))
-            masked = dot_t(order[...], jnp.concatenate(masked, axis=0))
+            masked = dot_t(order_band[...], jnp.concatenate(masked, axis=0))
             for two in range(2):
-                lo = two * LANES
-                gates, products = [], []
-                lhs = masked[:, lo : lo + LANES].astype(BF)
+                w = 4 * quad + 2 * two
+                raw = cols[:, two * LANES : (two + 1) * LANES]
+                pair = masked[:, two * LANES : (two + 1) * LANES]
+                gates = [jnp.where(low_half, raw, 0.0).astype(BF), jnp.where(low_half, 0.0, raw).astype(BF)]
+                sides = [jnp.where(low_half, pair, 0.0).astype(BF), jnp.where(low_half, 0.0, pair).astype(BF)]
+                chunks = []
+                for half, source, first in ((0, shifted, w + 1), (1, halfway, w)):
+                    lo = half * LANES // 2
+                    lhs = jnp.concatenate([side[lo : lo + LANES // 2] for side in sides], axis=0)
+                    rhs = jnp.concatenate(
+                        [jnp.concatenate(source[first + side : first + side + 2], axis=1) for side in range(2)],
+                        axis=0,
+                    )
+                    chunks.append(jnp.dot(lhs, rhs, preferred_element_type=F32))
                 for side in range(2):
-                    w = 4 * quad + 2 * two + side
-                    keep = low_half if side == 0 else ~low_half
-                    gates.append(jnp.where(keep, cols[:, lo : lo + LANES], 0.0))
-                    window = jnp.concatenate(shifted[w : w + 3], axis=1)
-                    rhs = [jnp.zeros_like(window)] * 2
-                    rhs[side] = window
-                    rhs = jnp.concatenate(rhs, axis=0)
-                    products.append(jnp.dot(lhs, rhs, preferred_element_type=F32))
-                place = i * LINE_PARTS + 8 * (tiles - 2 - 4 * quad - 2 * two)
-                for t in range(LINE_RUN):
-                    row = t * LANES + place
-                    r = 8 * t
-                    gate_rows[row : row + 16, :] = jnp.concatenate(
-                        [gates[1][r : r + 8], gates[0][r : r + 8]], axis=0
-                    ).astype(BF)
-                    beyond = diagonal >= t
-                    both = []
-                    for side in (1, 0):
-                        turned = [
-                            pltpu.roll(
-                                products[side][r : r + 8, m * LANES : (m + 1) * LANES],
-                                t, 1, stride=LINE_RUN, stride_axis=0,
+                    place = (tiles - 1 - w - side) * PARTS
+                    for t in range(LINE_RUN):
+                        row = t * LANES + place
+                        gate_rows[i, row : row + PARTS, :] = gates[side][t * PARTS : (t + 1) * PARTS]
+                        r = side * LANES // 2 + 8 * t
+                        within = reached < LANES - t
+                        halves = []
+                        for products in chunks:
+                            close, far = products[r : r + 8, :LANES], products[r : r + 8, LANES:]
+                            halves.append(
+                                jnp.concatenate(
+                                    [
+                                        pltpu.roll(value, t, 1, stride=LINE_RUN, stride_axis=0)
+                                        for value in (close, jnp.where(within, far, close))
+                                    ],
+                                    axis=1,
+                                )
                             )
-                            for m in range(3)
-                        ]
-                        both.append(
-                            jnp.concatenate(
-                                [jnp.where(beyond, turned[1], turned[0]), jnp.where(beyond, turned[2], turned[1])],
-                                axis=1,
-                            )
-                        )
-                    cost_rows[row : row + 16, :] = jnp.concatenate(both, axis=0).astype(BF)
-
-    x_base = width - 1 - LINE_RUN * (iota((KEYS, LANES), 1) & (LINE_PARTS - 1))
+                        cost_rows[i, row : row + PARTS, :] = jnp.concatenate(halves, axis=0).astype(BF)
+
+    x_base = width - 1 - LINE_RUN * iota((KEYS, LANES), 1)
     row = iota((KEYS, LANES), 0)
     reach = jnp.where(row >= 2 * GROUPS, 9, jnp.where(row >= GROUPS, 3, 1))
     room_left = x_base - reach
     room_right = x_base + reach - width
     unit = jnp.where(row >= 2 * GROUPS, SHARPNESS / math.log(2.0), 1.0)
-    for two in range(LINE_RUN // 2):
-        lo = 2 * two * LANES
-        costs = dot_t(flip[...], cost_rows[lo : lo + 2 * LANES, :])
-        logits = dot_t(guide[...], gate_rows[lo : lo + 2 * LANES, :])
-        for i in range(2):
-            t = 2 * two + i
-            vol[t] = costs[:, i * LANES : (i + 1) * LANES]
-            z = jnp.tanh(logits[:, i * LANES : (i + 1) * LANES]) + GATE_FLOOR
-            taps = [z[m * KEYS : (m + 1) * KEYS] for m in range(3)]
-            factor = unit / (taps[0] + taps[1] + taps[2])
-            taps = [tap * factor for tap in taps]
-            if t >= LINE_RUN - 9:
+    for i in range(PAIR):
+        for two in range(LINE_RUN // 2):
+            lo = 2 * two * LANES
+            costs = dot_t(flip[...], cost_rows[i, lo : lo + 2 * LANES, :])
+            logits = dot_t(guide[...], gate_rows[i, lo : lo + 2 * LANES, :])
+            for side in range(2):
+                t = 2 * two + side
+                vol[i, t] = costs[:, side * LANES : (side + 1) * LANES]
+                z = jnp.tanh(logits[:, side * LANES : (side + 1) * LANES]) + GATE_FLOOR
+                taps = [z[m * KEYS : (m + 1) * KEYS] for m in range(3)]
+                factor = unit / (taps[0] + taps[1] + taps[2])
+                taps = [tap * factor for tap in taps]
                 taps[0] = jnp.where(room_left >= t, taps[0], 0.0)
-            if t < 9:
                 taps[2] = jnp.where(room_right < t, taps[2], 0.0)
-            for m in range(3):
-                wts[t, m * KEYS : (m + 1) * KEYS, :] = taps[m]
+                for m in range(3):
+                    wts[i, t, m * KEYS : (m + 1) * KEYS, :] = taps[m]
 
     for group in range(GROUPS):
-        for at in (group * DGROUP, group * DGROUP + 8):
-            v = [vol[t, at : at + 8, :] for t in range(LINE_RUN)]
+        starts = [group * DGROUP + 8 * half for half in range(2)]
+        for i in range(PAIR):
+            v = [[vol[i, t, at : at + 8, :] for t in range(LINE_RUN)] for at in starts]
             for layer in range(LAYERS):
                 s = 3**layer
-                fresh = []
+                fresh = [[], []]
                 for t in range(LINE_RUN):
                     rows = [k * KEYS + layer * GROUPS + group for k in range(3)]
-                    w = [wts[t, r : r + 1, :] for r in rows]
-                    blk, r = divmod(t + s, LINE_RUN)
-                    before = pltpu.roll(v[r], LANES - blk, 1) if blk else v[r]
-                    blk, r = divmod(t - s, LINE_RUN)
-                    after = pltpu.roll(v[r], -blk, 1) if blk else v[r]
-                    fresh.append(w[0] * before + w[1] * v[t] + w[2] * after)
+                    w = [jnp.broadcast_to(wts[i, t, r : r + 1, :], (8, LANES)) for r in rows]
+                    for half in range(2):
+                        blk, r = divmod(t + s, LINE_RUN)
+                        before = pltpu.roll(v[half][r], LANES - blk, 1) if blk else v[half][r]
+                        blk, r = divmod(t - s, LINE_RUN)
+                        after = pltpu.roll(v[half][r], -blk, 1) if blk else v[half][r]
+                        fresh[half].append(w[0] * before + w[1] * v[half][t] + w[2] * after)
                 v = fresh
-            for t in range(LINE_RUN):
-                done[t, at : at + 8, :] = v[t]
+            for half, at_row in enumerate(starts):
+                for t in range(LINE_RUN):
+                    done[i, t, at_row : at_row + 8, :] = v[half][t]
 
     sub = iota((8, LANES), 0)
     results = []
-    for block in range(LINE_RUN // 8):
+    for i in range(PAIR):
         totals = jnp.zeros((8, LANES), F32)
         moments = totals
-        for s in range(8):
-            t = LINE_RUN - 1 - (8 * block + s)
-            v = [done[t, 8 * i : 8 * i + 8, :] for i in range(DISP // 8)]
+        for s in range(LINE_RUN):
+            t = LINE_RUN - 1 - s
+            v = [done[i, t, 8 * j : 8 * j + 8, :] for j in range(DISP // 8)]
             top = v
             while len(top) > 1:
                 top = [jnp.maximum(a, b) for a, b in zip(top[::2], top[1::2])] + top[len(top) & ~1 :]
             top = jnp.max(top[0], axis=0, keepdims=True)
             total = jnp.exp2(v[-1] - top)
             moment = total
-            for i in range(DISP // 8 - 2, -1, -1):
-                total = total + jnp.exp2(v[i] - top)
-                if i:
+            for j in range(DISP // 8 - 2, -1, -1):
+                total = total + jnp.exp2(v[j] - top)
+                if j:
                     moment = moment + total
             moment = 8.0 * moment + sub.astype(F32) * total
             totals = jnp.where(sub == s, jnp.sum(total, axis=0, keepdims=True), totals)
             moments = jnp.where(sub == s, jnp.sum(moment, axis=0, keepdims=True), moments)
-        lane_line = iota((8, LANES), 1) >> 6
-        shift = jnp.zeros((8, LANES), F32)
-        for i in range(PAIR):
-            shift = jnp.where(lane_line == i, offs[i].astype(F32), shift)
-        results.append((moments / totals + shift) * (1.0 / DISP))
-    vals = jnp.concatenate(results, axis=0)
-    lane_line = iota((LINE_RUN, LANES), 1) >> 6
-    both = jnp.concatenate([jnp.where(lane_line == i, vals, 0.0) for i in range(PAIR)], axis=0)
+        results.append((moments / totals + offs[i].astype(F32)) * (1.0 / DISP))
+    both = jnp.concatenate(results, axis=0)
     high = both.astype(BF)
-    rest = both - high.astype(F32)
-    middle = rest.astype(BF)
-    low = (rest - middle.astype(F32)).astype(BF)
-    pieces = jnp.dot(
+    left = both - high.astype(F32)
+    middle = left.astype(BF)
+    low = (left - middle.astype(F32)).astype(BF)
+    parts = jnp.dot(
         jnp.concatenate([high, middle, low], axis=0), spread[...], preferred_element_type=F32
     )
     size = PAIR * LINE_RUN
-    pieces = pieces[:size] + pieces[size : 2 * size] + pieces[2 * size :]
+    parts = parts[:size] + parts[size : 2 * size] + parts[2 * size :]
     wanted = iota((LINE_RUN, width), 0) == (iota((LINE_RUN, width), 1) & (LINE_RUN - 1))
     for i in range(PAIR):
-        piece = jnp.where(wanted, pieces[i * LINE_RUN : (i + 1) * LINE_RUN], 0.0)
-        out[i : i + 1, :] = jnp.sum(piece, axis=0, keepdims=True)
+        part = jnp.where(wanted, parts[i * LINE_RUN : (i + 1) * LINE_RUN], 0.0)
+        out[i : i + 1, :] = jnp.sum(part, axis=0, keepdims=True)
 
 
 def lines_plan(features, valid_cols, offsets, guide_weight):
@@ -599,8 +597,8 @@
     consts = call(
         constants_kernel,
         [
-            ((LANES, LANES), BF), ((DISP, 2 * LANES), BF), ((3 * KEYS, LANES), BF), ((LANES, width), BF),
-            (valid_cols.shape, F32),
+            ((LANES, LANES), BF), ((LANES, LANES), BF), ((DISP, 2 * LANES), BF), ((3 * KEYS, LANES), BF),
+            ((LANES, width), BF), (valid_cols.shape, F32),
         ],
         [], 1, (offsets, guide_weight, valid_cols), 1_000_000,
     )
@@ -610,11 +608,11 @@
         [
             pltpu.VMEM((devices, rows, BLOCK), BF),
             pltpu.VMEM((n,) + valid_cols.shape, F32),
-            pltpu.VMEM((LINE_RUN * LANES, LANES), BF),
-            pltpu.VMEM((LINE_RUN * LANES, 2 * LANES), BF),
-            pltpu.VMEM((LINE_RUN, DISP, LANES), F32),
-            pltpu.VMEM((LINE_RUN, DISP, LANES), F32),
-            pltpu.VMEM((LINE_RUN, 3 * KEYS, LANES), F32),
+            pltpu.VMEM((PAIR, LINE_RUN * LANES, LANES), BF),
+            pltpu.VMEM((PAIR, LINE_RUN * LANES, 2 * LANES), BF),
+            pltpu.VMEM((PAIR, LINE_RUN, DISP, LANES), F32),
+            pltpu.VMEM((PAIR, LINE_RUN, DISP, LANES), F32),
+            pltpu.VMEM((PAIR, LINE_RUN, 3 * KEYS, LANES), F32),
         ],
         1, (offsets, *consts, *pieces), 1_000_000_000,
     )
@@ -626,7 +624,7 @@
 def on_device(features, valid_cols, offsets, guide_weight):
     n = lax.axis_size("cols")
     lines = features.shape[1]
-    if lines == 2 * PAIR * n and n * BLOCK == LINE_RUN * LINE_PARTS:
+    if lines == 2 * PAIR * n and n * BLOCK == LINE_RUN * LANES:
         return lines_plan(features, valid_cols, offsets, guide_weight)
     return halo_plan(features, valid_cols, offsets, guide_weight)
 

time: 22.1 us -> 21.9 us (level)
  no operation moved by 1% of the time
where the time goes in v20:
time: 21.9 us; the launch traced here: 21.7 us
  starting transfers between devices  10.5 us (48%)
  Pallas kernels  4.68 us (21%)
  waiting for transfers between devices  4.65 us (21%)
  local copies, waits for them, and re-layouts  1.07 us (5%)
  other arithmetic  0.62 us (3%)
    ppermute x7, starting transfers between devices, lines_plan(): pieces[key] = lax.ppermute(piece, ('cols', 'view'), moves) if key else piece  10.1 us
    pallas_call x10, Pallas kernels, call(): pl.pallas_call(kernel, out_shape=[jax.ShapeDtypeStruct(shape, dtype) for...  4.68 us
    ppermute x7, waiting for transfers between devices, lines_plan(): pieces[key] = lax.ppermute(piece, ('cols', 'view'), moves) if key else piece  3.79 us
    unnamed x10, local copies, waits for them, and re-layouts  1.07 us
    ppermute x1, waiting for transfers between devices, lines_plan(): others = lax.ppermute(rows, 'view', [(0, 1), (1, 0)])  0.87 us
    select_n x1, other arithmetic, lines_plan(): jnp.where(first, jnp.concatenate([rows, others]), jnp.concatenate([others...  0.62 us
  transfers between devices with their start and end apart: 8, of which 3 were waited for; matrix products, arithmetic and copies ran while one was open for 0% of the time, Pallas kernels for 4%

profile of v20, /device:TPU:0, one launch (start us, length us, event | category | flops | bytes accessed | tf_op | source)
XLA Modules:
  0.0 21.7 jit_solution(8671554577781099104)
XLA Ops:
  0.0 1.0 %copy-done = bf16[1,16,64,256]{3,2,1,0:T(8,128)(2,1)S(1)} copy-done((bf16[1,16,64,256]{3,2,1,0:T(8,128)(2,1)S(1)}, bf16[1,16,64,256]{3,2,1,0:T(8,128)(2,1)}, u32[]{:S(2)}) %copy-start) | copy-done | bytes 524312
  1.1 0.0 copy-start.1
  1.1 0.0 copy-start.2
  1.1 4.1 %collective-permute-start.3 = (bf16[128,256]{1,0:T(8,128)(2,1)S(1)}, bf16[128,256]{1,0:T(8,128)(2,1)S(1)}, u32[]{:S(2)}, u32[]{:S(2)}) collective-permute-start(bf16[128,256]{1,0:T(8,128)(2,1)S(1)} %shard_map.50.rest_1_), channel_id=1, source_target_pairs={{0,8},{1,9},{4,12},{5,13},{8,0},{9,1},{12,4},{13,5},{2,10},{3,11},... | collective-permute-start | bytes 196616 | tf_op jit(solution)/shard_map/ppermute | solution.py:596
  5.2 1.3 %collective-permute-start.5 = (bf16[128,256]{1,0:T(8,128)(2,1)S(1)}, bf16[128,256]{1,0:T(8,128)(2,1)S(1)}, u32[]{:S(2)}, u32[]{:S(2)}) collective-permute-start(bf16[128,256]{1,0:T(8,128)(2,1)S(1)} %shard_map.49.rest_0_), channel_id=1, source_target_pairs={{0,12},{1,13},{4,8},{5,9},{8,4},{9,5},{12,0},{13,1},{2,14},{3,15},... | collective-permute-start | bytes 196616 | tf_op jit(solution)/shard_map/ppermute | solution.py:596
  6.7 0.0 copy-start.3
  6.7 0.0 copy-start.4
  6.7 0.1 collective-permute-start.2
  6.8 2.7 %collective-permute-start.4 = (bf16[136,256]{1,0:T(8,128)(2,1)S(1)}, bf16[136,256]{1,0:T(8,128)(2,1)S(1)}, u32[]{:S(2)}, u32[]{:S(2)}) collective-permute-start(bf16[136,256]{1,0:T(8,128)(2,1)S(1)} %shard_map.52.rest_1_), channel_id=1, source_target_pairs={{0,9},{1,8},{4,13},{5,12},{8,1},{9,0},{12,5},{13,4},{2,11},{3,10},... | collective-permute-start | bytes 208904 | tf_op jit(solution)/shard_map/ppermute | solution.py:596
  9.5 0.2 %collective-permute-start.6 = (bf16[136,256]{1,0:T(8,128)(2,1)S(1)}, bf16[136,256]{1,0:T(8,128)(2,1)S(1)}, u32[]{:S(2)}, u32[]{:S(2)}) collective-permute-start(bf16[136,256]{1,0:T(8,128)(2,1)S(1)} %shard_map.51.rest_1_), channel_id=1, source_target_pairs={{0,13},{1,12},{4,9},{5,8},{8,5},{9,4},{12,1},{13,0},{2,15},{3,14},... | collective-permute-start | bytes 208904 | tf_op jit(solution)/shard_map/ppermute | solution.py:596
  9.8 0.0 collective-permute-done.3.rest_5_
  9.8 1.6 %collective-permute-start.1 = (bf16[128,256]{1,0:T(8,128)(2,1)S(1)}, bf16[128,256]{1,0:T(8,128)(2,1)S(1)}, u32[]{:S(2)}, u32[]{:S(2)}) collective-permute-start(bf16[128,256]{1,0:T(8,128)(2,1)S(1)} %shard_map.48.rest_0_), channel_id=1, source_target_pairs={{0,4},{1,5},{4,0},{5,1},{8,12},{9,13},{12,8},{13,9},{2,6},{3,7},{6... | collective-permute-start | bytes 196616 | tf_op jit(solution)/shard_map/ppermute | solution.py:596
  11.4 0.3 %collective-permute-done.5.rest_7_ = bf16[128,256]{1,0:T(8,128)(2,1)S(1)} collective-permute-done((bf16[128,256]{1,0:T(8,128)(2,1)S(1)}, bf16[128,256]{1,0:T(8,128)(2,1)S(1)}, u32[]{:S(2)}, u32[]{:S(2)}) %collective-permute-start.5) | collective-permute-done | bytes 65568 | tf_op jit(solution)/shard_map/ppermute | solution.py:596
  11.7 0.0 collective-permute-start
  11.8 0.8 %shard_map.46 = (bf16[128,128]{1,0:T(8,128)(2,1)S(1)}, bf16[128,128]{1,0:T(8,128)(2,1)S(1)}, bf16[192,256]{1,0:T(8,128)(2,1)S(1)}, bf16[120,128]{1,0:T(8,128)(2,...) custom-call(s32[16]{0:T(128)S(1)} %copy-done.4, bf16[64,108]{1,0:T(8,128)(2,1)S(1)} %copy-done.3, ...), custom_call_target="tpu_custom_call" | custom-call | flops 1000000 | bytes 1000000 | tf_op jit(solution)/shard_map/pallas_call | solution.py:50
  12.6 3.4 %collective-permute-done.1.rest_3_ = bf16[128,256]{1,0:T(8,128)(2,1)S(1)} collective-permute-done((bf16[128,256]{1,0:T(8,128)(2,1)S(1)}, bf16[128,256]{1,0:T(8,128)(2,1)S(1)}, u32[]{:S(2)}, u32[]{:S(2)}) %collective-permute-start.1) | collective-permute-done | bytes 65568 | tf_op jit(solution)/shard_map/ppermute | solution.py:596
  16.0 0.0 collective-permute-done.rest_2_
  16.0 0.0 collective-permute-done.2.rest_4_
  16.1 0.0 collective-permute-done.4.rest_6_
  16.1 0.0 collective-permute-done.6.rest_8_
  16.1 3.7 %shard_map.55 = f32[2,1024]{1,0:T(2,128)S(1)} custom-call(s32[16]{0:T(128)S(1)} %copy-done.4, bf16[128,128]{1,0:T(8,128)(2,1)S(1)} %get-tuple-element.11.order, bf16[128,128]{1,0:T(8,128)(2,1)S(1)} %get-tuple-element.12.order_band, bf16[192,256]{1,0:T(8,128)(2,1)S(1)} %get-tuple-element.13.flip, bf16[120,128]{1,0:T(8,128)(2,1)S(1)} %get-tuple-element.14.guide, ...), custom_call_target="tpu_custom_call" | custom-call | flops 1000000000 | bytes 1000000 | tf_op jit(solution)/shard_map/pallas_call | solution.py:50
  19.8 0.4 %collective-permute-start.7 = (f32[2,1024]{1,0:T(2,128)S(1)}, f32[2,1024]{1,0:T(2,128)S(1)}, u32[]{:S(2)}, u32[]{:S(2)}) collective-permute-start(f32[2,1024]{1,0:T(2,128)S(1)} %shard_map.55), channel_id=1, source_target_pairs={{0,1},{1,0},{2,3},{3,2},{4,5},{5,4},{6,7},{7,6},{8,9},{9,8},{10,11... | collective-permute-start | bytes 24584 | tf_op jit(solution)/shard_map/ppermute | solution.py:619
  20.2 0.9 %collective-permute-done.7 = f32[2,1024]{1,0:T(2,128)S(1)} collective-permute-done((f32[2,1024]{1,0:T(2,128)S(1)}, f32[2,1024]{1,0:T(2,128)S(1)}, u32[]{:S(2)}, u32[]{:S(2)}) %collective-permute-start.7) | collective-permute-done | bytes 8224 | tf_op jit(solution)/shard_map/ppermute | solution.py:619
  21.0 0.6 %maximum_select_fusion = f32[1,4,1024]{2,1,0:T(4,128)} fusion(f32[1,2,1024]{2,1,0:T(2,128)S(1)} %bitcast.12, f32[1,2,1024]{2,1,0:T(2,128)S(1)} %bitcast.11, pred[]{:T(512)S(6)} %eq.3), kind=kLoop, calls=%fused_computation | loop fusion | flops 12288 | bytes 32769 | tf_op jit(solution)/shard_map/jit(_where)/select_n | solution.py:621
  (13 shorter events, 0.1 us)
Async XLA Ops:
  0.0 1.0 %copy-start = (bf16[1,16,64,256]{3,2,1,0:T(8,128)(2,1)S(1)}, bf16[1,16,64,256]{3,2,1,0:T(8,128)(2,1)}, u32[]{:S(2)}) copy-start(bf16[1,16,64,256]{3,2,1,0:T(8,128)(2,1)} %param.4) | copy-start | bytes 1572868
  1.1 5.5 %copy-start.1 = (bf16[1,16,64,256]{3,2,1,0:T(8,128)(2,1)S(1)}, bf16[1,16,64,256]{3,2,1,0:T(8,128)(2,1)}, u32[]{:S(2)}) copy-start(bf16[1,16,64,256]{3,2,1,0:T(8,128)(2,1)} %param.4) | copy-start | bytes 1572868
  1.1 5.5 %copy-start.2 = (s32[2,256]{1,0:T(2,128)S(1)}, s32[2,256]{1,0:T(2,128)}, u32[]{:S(2)}) copy-start(s32[2,256]{1,0:T(2,128)} %rest_0_.5) | copy-start | bytes 6148
  1.1 8.6 %collective-permute-start.3 = (bf16[128,256]{1,0:T(8,128)(2,1)S(1)}, bf16[128,256]{1,0:T(8,128)(2,1)S(1)}, u32[]{:S(2)}, u32[]{:S(2)}) collective-permute-start(bf16[128,256]{1,0:T(8,128)(2,1)S(1)} %shard_map.50.rest_1_), channel_id=1, source_target_pairs={{0,8},{1,9},{4,12},{5,13},{8,0},{9,1},{12,4},{13,5},{2,10},{3,11},... | collective-permute-start | bytes 196616 | tf_op jit(solution)/shard_map/ppermute | solution.py:596
  5.2 6.5 %collective-permute-start.5 = (bf16[128,256]{1,0:T(8,128)(2,1)S(1)}, bf16[128,256]{1,0:T(8,128)(2,1)S(1)}, u32[]{:S(2)}, u32[]{:S(2)}) collective-permute-start(bf16[128,256]{1,0:T(8,128)(2,1)S(1)} %shard_map.49.rest_0_), channel_id=1, source_target_pairs={{0,12},{1,13},{4,8},{5,9},{8,4},{9,5},{12,0},{13,1},{2,14},{3,15},... | collective-permute-start | bytes 196616 | tf_op jit(solution)/shard_map/ppermute | solution.py:596
  6.7 5.1 %copy-start.3 = (bf16[64,108]{1,0:T(8,128)(2,1)S(1)}, bf16[64,108]{1,0:T(8,128)(2,1)}, u32[]{:S(2)}) copy-start(bf16[64,108]{1,0:T(8,128)(2,1)} %guide.1) | copy-start | bytes 41476
  6.7 5.1 %copy-start.4 = (s32[16]{0:T(128)S(1)}, s32[16]{0:T(128)}, u32[]{:S(2)}) copy-start(s32[16]{0:T(128)} %offsets.3) | copy-start | bytes 196
  6.7 9.4 %collective-permute-start.2 = (bf16[136,256]{1,0:T(8,128)(2,1)S(1)}, bf16[136,256]{1,0:T(8,128)(2,1)S(1)}, u32[]{:S(2)}, u32[]{:S(2)}) collective-permute-start(bf16[136,256]{1,0:T(8,128)(2,1)S(1)} %shard_map.53.rest_0_), channel_id=1, source_target_pairs={{0,5},{1,4},{4,1},{5,0},{8,13},{9,12},{12,9},{13,8},{2,7},{3,6},{6... | collective-permute-start | bytes 208904 | tf_op jit(solution)/shard_map/ppermute | solution.py:596
  6.8 9.3 %collective-permute-start.4 = (bf16[136,256]{1,0:T(8,128)(2,1)S(1)}, bf16[136,256]{1,0:T(8,128)(2,1)S(1)}, u32[]{:S(2)}, u32[]{:S(2)}) collective-permute-start(bf16[136,256]{1,0:T(8,128)(2,1)S(1)} %shard_map.52.rest_1_), channel_id=1, source_target_pairs={{0,9},{1,8},{4,13},{5,12},{8,1},{9,0},{12,5},{13,4},{2,11},{3,10},... | collective-permute-start | bytes 208904 | tf_op jit(solution)/shard_map/ppermute | solution.py:596
  9.5 6.5 %collective-permute-start.6 = (bf16[136,256]{1,0:T(8,128)(2,1)S(1)}, bf16[136,256]{1,0:T(8,128)(2,1)S(1)}, u32[]{:S(2)}, u32[]{:S(2)}) collective-permute-start(bf16[136,256]{1,0:T(8,128)(2,1)S(1)} %shard_map.51.rest_1_), channel_id=1, source_target_pairs={{0,13},{1,12},{4,9},{5,8},{8,5},{9,4},{12,1},{13,0},{2,15},{3,14},... | collective-permute-start | bytes 208904 | tf_op jit(solution)/shard_map/ppermute | solution.py:596
  9.8 6.3 %collective-permute-start.1 = (bf16[128,256]{1,0:T(8,128)(2,1)S(1)}, bf16[128,256]{1,0:T(8,128)(2,1)S(1)}, u32[]{:S(2)}, u32[]{:S(2)}) collective-permute-start(bf16[128,256]{1,0:T(8,128)(2,1)S(1)} %shard_map.48.rest_0_), channel_id=1, source_target_pairs={{0,4},{1,5},{4,0},{5,1},{8,12},{9,13},{12,8},{13,9},{2,6},{3,7},{6... | collective-permute-start | bytes 196616 | tf_op jit(solution)/shard_map/ppermute | solution.py:596
  11.7 4.3 %collective-permute-start = (bf16[128,256]{1,0:T(8,128)(2,1)S(1)}, bf16[128,256]{1,0:T(8,128)(2,1)S(1)}, u32[]{:S(2)}, u32[]{:S(2)}) collective-permute-start(bf16[128,256]{1,0:T(8,128)(2,1)S(1)} %shard_map.47.rest_0_), channel_id=1, source_target_pairs={{0,1},{1,0},{4,5},{5,4},{8,9},{9,8},{12,13},{13,12},{2,3},{3,2},{6... | collective-permute-start | bytes 196616 | tf_op jit(solution)/shard_map/ppermute | solution.py:596
  19.8 1.2 %collective-permute-start.7 = (f32[2,1024]{1,0:T(2,128)S(1)}, f32[2,1024]{1,0:T(2,128)S(1)}, u32[]{:S(2)}, u32[]{:S(2)}) collective-permute-start(f32[2,1024]{1,0:T(2,128)S(1)} %shard_map.55), channel_id=1, source_target_pairs={{0,1},{1,0},{2,3},{3,2},{4,5},{5,4},{6,7},{7,6},{8,9},{9,8},{10,11... | collective-permute-start | bytes 24584 | tf_op jit(solution)/shard_map/ppermute | solution.py:619

commit v21 on v20

--- a/solution.py
+++ b/solution.py
@@ -582,7 +582,7 @@
     own = features.reshape(devices, rows, BLOCK)
     pieces = [None] * devices
     gone = ()
-    for key in (1, 2, 6, 4, 7, 5, 3, 0):
+    for key in (1, 2, 6, 4, 3, 5, 7, 0):
         masked = key % 2 and key > 1
         (piece,) = call(
             functools.partial(pack_kernel, key),

time: 21.9 us -> 23 us (1.050)
  starting transfers between devices: 10.5 us -> 12.9 us
  waiting for transfers between devices: 4.65 us -> 3.5 us
    ppermute x7, starting transfers between devices: 10.1 us -> 12.6 us  [lines_plan(): pieces[key] = lax.ppermute(piece, ('cols', 'view'), moves) if key else piece]
    ppermute x7, waiting for transfers between devices: 3.79 us -> 2.56 us  [lines_plan(): pieces[key] = lax.ppermute(piece, ('cols', 'view'), moves) if key else piece]
where the time goes in v21:
time: 23 us; the launch traced here: 22.9 us
  starting transfers between devices  12.9 us (56%)
  Pallas kernels  4.68 us (20%)
  waiting for transfers between devices  3.5 us (15%)
  local copies, waits for them, and re-layouts  1.07 us (5%)
  other arithmetic  0.62 us (3%)
    ppermute x7, starting transfers between devices, lines_plan(): pieces[key] = lax.ppermute(piece, ('cols', 'view'), moves) if key else piece  12.6 us
    pallas_call x10, Pallas kernels, call(): pl.pallas_call(kernel, out_shape=[jax.ShapeDtypeStruct(shape, dtype) for...  4.68 us
    ppermute x7, waiting for transfers between devices, lines_plan(): pieces[key] = lax.ppermute(piece, ('cols', 'view'), moves) if key else piece  2.56 us
    unnamed x10, local copies, waits for them, and re-layouts  1.07 us
    ppermute x1, waiting for transfers between devices, lines_plan(): others = lax.ppermute(rows, 'view', [(0, 1), (1, 0)])  0.94 us
    select_n x1, other arithmetic, lines_plan(): jnp.where(first, jnp.concatenate([rows, others]), jnp.concatenate([others...  0.62 us
  transfers between devices with their start and end apart: 8, of which 3 were waited for; matrix products, arithmetic and copies ran while one was open for 0% of the time, Pallas kernels for 4%

profile of v21, /device:TPU:0, one launch (start us, length us, event | category | flops | bytes accessed | tf_op | source)
XLA Modules:
  0.0 22.9 jit_solution(15026260790429869486)
XLA Ops:
  0.0 1.0 %copy-done = bf16[1,16,64,256]{3,2,1,0:T(8,128)(2,1)S(1)} copy-done((bf16[1,16,64,256]{3,2,1,0:T(8,128)(2,1)S(1)}, bf16[1,16,64,256]{3,2,1,0:T(8,128)(2,1)}, u32[]{:S(2)}) %copy-start) | copy-done | bytes 524312
  1.1 0.0 copy-start.1
  1.1 0.0 copy-start.2
  1.1 4.1 %collective-permute-start.3 = (bf16[128,256]{1,0:T(8,128)(2,1)S(1)}, bf16[128,256]{1,0:T(8,128)(2,1)S(1)}, u32[]{:S(2)}, u32[]{:S(2)}) collective-permute-start(bf16[128,256]{1,0:T(8,128)(2,1)S(1)} %shard_map.50.rest_1_), channel_id=1, source_target_pairs={{0,8},{1,9},{4,12},{5,13},{8,0},{9,1},{12,4},{13,5},{2,10},{3,11},... | collective-permute-start | bytes 196616 | tf_op jit(solution)/shard_map/ppermute | solution.py:596
  5.2 1.3 %collective-permute-start.5 = (bf16[128,256]{1,0:T(8,128)(2,1)S(1)}, bf16[128,256]{1,0:T(8,128)(2,1)S(1)}, u32[]{:S(2)}, u32[]{:S(2)}) collective-permute-start(bf16[128,256]{1,0:T(8,128)(2,1)S(1)} %shard_map.49.rest_0_), channel_id=1, source_target_pairs={{0,12},{1,13},{4,8},{5,9},{8,4},{9,5},{12,0},{13,1},{2,14},{3,15},... | collective-permute-start | bytes 196616 | tf_op jit(solution)/shard_map/ppermute | solution.py:596
  6.7 0.0 copy-start.3
  6.7 0.0 copy-start.4
  6.7 1.4 %collective-permute-start.6 = (bf16[136,256]{1,0:T(8,128)(2,1)S(1)}, bf16[136,256]{1,0:T(8,128)(2,1)S(1)}, u32[]{:S(2)}, u32[]{:S(2)}) collective-permute-start(bf16[136,256]{1,0:T(8,128)(2,1)S(1)} %shard_map.53.rest_0_), channel_id=1, source_target_pairs={{0,13},{1,12},{4,9},{5,8},{8,5},{9,4},{12,1},{13,0},{2,15},{3,14},... | collective-permute-start | bytes 208904 | tf_op jit(solution)/shard_map/ppermute | solution.py:596
  8.1 0.1 collective-permute-start.4
  8.2 1.6 %collective-permute-start.2 = (bf16[136,256]{1,0:T(8,128)(2,1)S(1)}, bf16[136,256]{1,0:T(8,128)(2,1)S(1)}, u32[]{:S(2)}, u32[]{:S(2)}) collective-permute-start(bf16[136,256]{1,0:T(8,128)(2,1)S(1)} %shard_map.51.rest_1_), channel_id=1, source_target_pairs={{0,5},{1,4},{4,1},{5,0},{8,13},{9,12},{12,9},{13,8},{2,7},{3,6},{6... | collective-permute-start | bytes 208904 | tf_op jit(solution)/shard_map/ppermute | solution.py:596
  9.8 0.0 collective-permute-done.3.rest_5_
  9.8 4.1 %collective-permute-start.1 = (bf16[128,256]{1,0:T(8,128)(2,1)S(1)}, bf16[128,256]{1,0:T(8,128)(2,1)S(1)}, u32[]{:S(2)}, u32[]{:S(2)}) collective-permute-start(bf16[128,256]{1,0:T(8,128)(2,1)S(1)} %shard_map.48.rest_0_), channel_id=1, source_target_pairs={{0,4},{1,5},{4,0},{5,1},{8,12},{9,13},{12,8},{13,9},{2,6},{3,7},{6... | collective-permute-start | bytes 196616 | tf_op jit(solution)/shard_map/ppermute | solution.py:596
  13.8 0.0 collective-permute-done.5.rest_7_
  13.8 0.0 collective-permute-start
  13.9 0.8 %shard_map.46 = (bf16[128,128]{1,0:T(8,128)(2,1)S(1)}, bf16[128,128]{1,0:T(8,128)(2,1)S(1)}, bf16[192,256]{1,0:T(8,128)(2,1)S(1)}, bf16[120,128]{1,0:T(8,128)(2,...) custom-call(s32[16]{0:T(128)S(1)} %copy-done.4, bf16[64,108]{1,0:T(8,128)(2,1)S(1)} %copy-done.3, ...), custom_call_target="tpu_custom_call" | custom-call | flops 1000000 | bytes 1000000 | tf_op jit(solution)/shard_map/pallas_call | solution.py:50
  14.7 1.7 %collective-permute-done.1.rest_3_ = bf16[128,256]{1,0:T(8,128)(2,1)S(1)} collective-permute-done((bf16[128,256]{1,0:T(8,128)(2,1)S(1)}, bf16[128,256]{1,0:T(8,128)(2,1)S(1)}, u32[]{:S(2)}, u32[]{:S(2)}) %collective-permute-start.1) | collective-permute-done | bytes 65568 | tf_op jit(solution)/shard_map/ppermute | solution.py:596
  16.4 0.0 collective-permute-done.rest_2_
  16.4 0.0 collective-permute-done.6.rest_8_
  16.4 0.9 %collective-permute-done.4.rest_6_ = bf16[136,256]{1,0:T(8,128)(2,1)S(1)} collective-permute-done((bf16[136,256]{1,0:T(8,128)(2,1)S(1)}, bf16[136,256]{1,0:T(8,128)(2,1)S(1)}, u32[]{:S(2)}, u32[]{:S(2)}) %collective-permute-start.4) | collective-permute-done | bytes 69664 | tf_op jit(solution)/shard_map/ppermute | solution.py:596
  17.3 0.0 collective-permute-done.2.rest_4_
  17.3 3.7 %shard_map.55 = f32[2,1024]{1,0:T(2,128)S(1)} custom-call(s32[16]{0:T(128)S(1)} %copy-done.4, bf16[128,128]{1,0:T(8,128)(2,1)S(1)} %get-tuple-element.11.order, bf16[128,128]{1,0:T(8,128)(2,1)S(1)} %get-tuple-element.12.order_band, bf16[192,256]{1,0:T(8,128)(2,1)S(1)} %get-tuple-element.13.flip, bf16[120,128]{1,0:T(8,128)(2,1)S(1)} %get-tuple-element.14.guide, ...), custom_call_target="tpu_custom_call" | custom-call | flops 1000000000 | bytes 1000000 | tf_op jit(solution)/shard_map/pallas_call | solution.py:50
  21.0 0.3 %collective-permute-start.7 = (f32[2,1024]{1,0:T(2,128)S(1)}, f32[2,1024]{1,0:T(2,128)S(1)}, u32[]{:S(2)}, u32[]{:S(2)}) collective-permute-start(f32[2,1024]{1,0:T(2,128)S(1)} %shard_map.55), channel_id=1, source_target_pairs={{0,1},{1,0},{2,3},{3,2},{4,5},{5,4},{6,7},{7,6},{8,9},{9,8},{10,11... | collective-permute-start | bytes 24584 | tf_op jit(solution)/shard_map/ppermute | solution.py:619
  21.3 0.9 %collective-permute-done.7 = f32[2,1024]{1,0:T(2,128)S(1)} collective-permute-done((f32[2,1024]{1,0:T(2,128)S(1)}, f32[2,1024]{1,0:T(2,128)S(1)}, u32[]{:S(2)}, u32[]{:S(2)}) %collective-permute-start.7) | collective-permute-done | bytes 8224 | tf_op jit(solution)/shard_map/ppermute | solution.py:619
  22.2 0.6 %maximum_select_fusion = f32[1,4,1024]{2,1,0:T(4,128)} fusion(f32[1,2,1024]{2,1,0:T(2,128)S(1)} %bitcast.12, f32[1,2,1024]{2,1,0:T(2,128)S(1)} %bitcast.11, pred[]{:T(512)S(6)} %eq.3), kind=kLoop, calls=%fused_computation | loop fusion | flops 12288 | bytes 32769 | tf_op jit(solution)/shard_map/jit(_where)/select_n | solution.py:621
  (13 shorter events, 0.1 us)
Async XLA Ops:
  0.0 1.0 %copy-start = (bf16[1,16,64,256]{3,2,1,0:T(8,128)(2,1)S(1)}, bf16[1,16,64,256]{3,2,1,0:T(8,128)(2,1)}, u32[]{:S(2)}) copy-start(bf16[1,16,64,256]{3,2,1,0:T(8,128)(2,1)} %param.4) | copy-start | bytes 1572868
  1.1 5.5 %copy-start.1 = (bf16[1,16,64,256]{3,2,1,0:T(8,128)(2,1)S(1)}, bf16[1,16,64,256]{3,2,1,0:T(8,128)(2,1)}, u32[]{:S(2)}) copy-start(bf16[1,16,64,256]{3,2,1,0:T(8,128)(2,1)} %param.4) | copy-start | bytes 1572868
  1.1 5.5 %copy-start.2 = (s32[2,256]{1,0:T(2,128)S(1)}, s32[2,256]{1,0:T(2,128)}, u32[]{:S(2)}) copy-start(s32[2,256]{1,0:T(2,128)} %rest_0_.5) | copy-start | bytes 6148
  1.1 8.6 %collective-permute-start.3 = (bf16[128,256]{1,0:T(8,128)(2,1)S(1)}, bf16[128,256]{1,0:T(8,128)(2,1)S(1)}, u32[]{:S(2)}, u32[]{:S(2)}) collective-permute-start(bf16[128,256]{1,0:T(8,128)(2,1)S(1)} %shard_map.50.rest_1_), channel_id=1, source_target_pairs={{0,8},{1,9},{4,12},{5,13},{8,0},{9,1},{12,4},{13,5},{2,10},{3,11},... | collective-permute-start | bytes 196616 | tf_op jit(solution)/shard_map/ppermute | solution.py:596
  5.2 8.6 %collective-permute-start.5 = (bf16[128,256]{1,0:T(8,128)(2,1)S(1)}, bf16[128,256]{1,0:T(8,128)(2,1)S(1)}, u32[]{:S(2)}, u32[]{:S(2)}) collective-permute-start(bf16[128,256]{1,0:T(8,128)(2,1)S(1)} %shard_map.49.rest_0_), channel_id=1, source_target_pairs={{0,12},{1,13},{4,8},{5,9},{8,4},{9,5},{12,0},{13,1},{2,14},{3,15},... | collective-permute-start | bytes 196616 | tf_op jit(solution)/shard_map/ppermute | solution.py:596
  6.7 7.2 %copy-start.3 = (bf16[64,108]{1,0:T(8,128)(2,1)S(1)}, bf16[64,108]{1,0:T(8,128)(2,1)}, u32[]{:S(2)}) copy-start(bf16[64,108]{1,0:T(8,128)(2,1)} %guide.1) | copy-start | bytes 41476
  6.7 7.2 %copy-start.4 = (s32[16]{0:T(128)S(1)}, s32[16]{0:T(128)}, u32[]{:S(2)}) copy-start(s32[16]{0:T(128)} %offsets.3) | copy-start | bytes 196
  6.7 9.7 %collective-permute-start.6 = (bf16[136,256]{1,0:T(8,128)(2,1)S(1)}, bf16[136,256]{1,0:T(8,128)(2,1)S(1)}, u32[]{:S(2)}, u32[]{:S(2)}) collective-permute-start(bf16[136,256]{1,0:T(8,128)(2,1)S(1)} %shard_map.53.rest_0_), channel_id=1, source_target_pairs={{0,13},{1,12},{4,9},{5,8},{8,5},{9,4},{12,1},{13,0},{2,15},{3,14},... | collective-permute-start | bytes 208904 | tf_op jit(solution)/shard_map/ppermute | solution.py:596
  8.1 9.1 %collective-permute-start.4 = (bf16[136,256]{1,0:T(8,128)(2,1)S(1)}, bf16[136,256]{1,0:T(8,128)(2,1)S(1)}, u32[]{:S(2)}, u32[]{:S(2)}) collective-permute-start(bf16[136,256]{1,0:T(8,128)(2,1)S(1)} %shard_map.52.rest_1_), channel_id=1, source_target_pairs={{0,9},{1,8},{4,13},{5,12},{8,1},{9,0},{12,5},{13,4},{2,11},{3,10},... | collective-permute-start | bytes 208904 | tf_op jit(solution)/shard_map/ppermute | solution.py:596
  8.2 9.1 %collective-permute-start.2 = (bf16[136,256]{1,0:T(8,128)(2,1)S(1)}, bf16[136,256]{1,0:T(8,128)(2,1)S(1)}, u32[]{:S(2)}, u32[]{:S(2)}) collective-permute-start(bf16[136,256]{1,0:T(8,128)(2,1)S(1)} %shard_map.51.rest_1_), channel_id=1, source_target_pairs={{0,5},{1,4},{4,1},{5,0},{8,13},{9,12},{12,9},{13,8},{2,7},{3,6},{6... | collective-permute-start | bytes 208904 | tf_op jit(solution)/shard_map/ppermute | solution.py:596
  9.8 6.6 %collective-permute-start.1 = (bf16[128,256]{1,0:T(8,128)(2,1)S(1)}, bf16[128,256]{1,0:T(8,128)(2,1)S(1)}, u32[]{:S(2)}, u32[]{:S(2)}) collective-permute-start(bf16[128,256]{1,0:T(8,128)(2,1)S(1)} %shard_map.48.rest_0_), channel_id=1, source_target_pairs={{0,4},{1,5},{4,0},{5,1},{8,12},{9,13},{12,8},{13,9},{2,6},{3,7},{6... | collective-permute-start | bytes 196616 | tf_op jit(solution)/shard_map/ppermute | solution.py:596
  13.8 2.5 %collective-permute-start = (bf16[128,256]{1,0:T(8,128)(2,1)S(1)}, bf16[128,256]{1,0:T(8,128)(2,1)S(1)}, u32[]{:S(2)}, u32[]{:S(2)}) collective-permute-start(bf16[128,256]{1,0:T(8,128)(2,1)S(1)} %shard_map.47.rest_0_), channel_id=1, source_target_pairs={{0,1},{1,0},{4,5},{5,4},{8,9},{9,8},{12,13},{13,12},{2,3},{3,2},{6... | collective-permute-start | bytes 196616 | tf_op jit(solution)/shard_map/ppermute | solution.py:596
  21.0 1.2 %collective-permute-start.7 = (f32[2,1024]{1,0:T(2,128)S(1)}, f32[2,1024]{1,0:T(2,128)S(1)}, u32[]{:S(2)}, u32[]{:S(2)}) collective-permute-start(f32[2,1024]{1,0:T(2,128)S(1)} %shard_map.55), channel_id=1, source_target_pairs={{0,1},{1,0},{2,3},{3,2},{4,5},{5,4},{6,7},{7,6},{8,9},{9,8},{10,11... | collective-permute-start | bytes 24584 | tf_op jit(solution)/shard_map/ppermute | solution.py:619

commit v22 on v21

--- a/solution.py
+++ b/solution.py
@@ -581,17 +581,19 @@
     rows = PAIR * CHANNELS
     own = features.reshape(devices, rows, BLOCK)
     pieces = [None] * devices
-    gone = ()
-    for key in (1, 2, 6, 4, 3, 5, 7, 0):
+    plain, gone = (), ()
+    for key in (1, 7, 6, 4, 2, 5, 3, 0):
         masked = key % 2 and key > 1
         (piece,) = call(
             functools.partial(pack_kernel, key),
             [((rows + (MASKS if masked else 0), BLOCK), BF)],
             [], 0,
-            (own,) + ((valid_cols,) if masked else ()) + gone,
+            (own,) + ((valid_cols,) + gone if masked else plain),
             1_000_000,
         )
         gone = (piece,)
+        if not masked:
+            plain = gone
         moves = [(i, i ^ key) for i in range(devices)]
         pieces[key] = lax.ppermute(piece, ("cols", "view"), moves) if key else piece
     consts = call(

time: 23 us -> 22.8 us (level)
  the two profiles are of different devices: /device:TPU:0 before, /device:TPU:23 now
where the time goes in v22:
time: 22.8 us; the launch traced here: 22.7 us
  starting transfers between devices  9.58 us (42%)
  waiting for transfers between devices  6.61 us (29%)
  Pallas kernels  4.68 us (21%)
  local copies, waits for them, and re-layouts  1.07 us (5%)
  other arithmetic  0.62 us (3%)
    ppermute x7, starting transfers between devices, lines_plan(): pieces[key] = lax.ppermute(piece, ('cols', 'view'), moves) if key else piece  8.12 us
    ppermute x7, waiting for transfers between devices, lines_plan(): pieces[key] = lax.ppermute(piece, ('cols', 'view'), moves) if key else piece  5.78 us
    pallas_call x10, Pallas kernels, call(): pl.pallas_call(kernel, out_shape=[jax.ShapeDtypeStruct(shape, dtype) for...  4.68 us
    ppermute x1, starting transfers between devices, lines_plan(): others = lax.ppermute(rows, 'view', [(0, 1), (1, 0)])  1.46 us
    unnamed x10, local copies, waits for them, and re-layouts  1.07 us
    ppermute x1, waiting for transfers between devices, lines_plan(): others = lax.ppermute(rows, 'view', [(0, 1), (1, 0)])  0.83 us
    select_n x1, other arithmetic, lines_plan(): jnp.where(first, jnp.concatenate([rows, others]), jnp.concatenate([others...  0.62 us
  transfers between devices with their start and end apart: 8, of which 2 were waited for; matrix products, arithmetic and copies ran while one was open for 0% of the time, Pallas kernels for 4%

profile of v22, /device:TPU:23, one launch (start us, length us, event | category | flops | bytes accessed | tf_op | source)
XLA Modules:
  0.0 22.7 jit_solution(12244155516625948641)
XLA Ops:
  0.0 1.0 %copy-done = bf16[1,16,64,256]{3,2,1,0:T(8,128)(2,1)S(1)} copy-done((bf16[1,16,64,256]{3,2,1,0:T(8,128)(2,1)S(1)}, bf16[1,16,64,256]{3,2,1,0:T(8,128)(2,1)}, u32[]{:S(2)}) %copy-start) | copy-done | bytes 524312
  1.1 0.0 copy-start.1
  1.1 0.0 copy-start.2
  1.1 1.4 %collective-permute-start.1 = (bf16[128,256]{1,0:T(8,128)(2,1)S(1)}, bf16[128,256]{1,0:T(8,128)(2,1)S(1)}, u32[]{:S(2)}, u32[]{:S(2)}) collective-permute-start(bf16[128,256]{1,0:T(8,128)(2,1)S(1)} %shard_map.50.rest_0_.rest_1_), channel_id=1, source_target_pairs={{0,4},{1,5},{4,0},{5,1},{8,12},{9,13},{12,8},{13,9},{2,6},{3,7},{6... | collective-permute-start | bytes 196616 | tf_op jit(solution)/shard_map/ppermute | solution.py:598
  2.5 0.1 collective-permute-start.3
  2.6 3.5 %collective-permute-start.4 = (bf16[136,256]{1,0:T(8,128)(2,1)S(1)}, bf16[136,256]{1,0:T(8,128)(2,1)S(1)}, u32[]{:S(2)}, u32[]{:S(2)}) collective-permute-start(bf16[136,256]{1,0:T(8,128)(2,1)S(1)} %shard_map.52.rest_1_), channel_id=1, source_target_pairs={{0,9},{1,8},{4,13},{5,12},{8,1},{9,0},{12,5},{13,4},{2,11},{3,10},... | collective-permute-start | bytes 208904 | tf_op jit(solution)/shard_map/ppermute | solution.py:598
  6.1 0.1 collective-permute-start.2
  6.2 0.0 copy-start.3
  6.2 0.0 copy-start.4
  6.2 0.7 %collective-permute-start.6 = (bf16[136,256]{1,0:T(8,128)(2,1)S(1)}, bf16[136,256]{1,0:T(8,128)(2,1)S(1)}, u32[]{:S(2)}, u32[]{:S(2)}) collective-permute-start(bf16[136,256]{1,0:T(8,128)(2,1)S(1)} %shard_map.54), channel_id=1, source_target_pairs={{0,13},{1,12},{4,9},{5,8},{8,5},{9,4},{12,1},{13,0},{2,15},{3,14},... | collective-permute-start | bytes 208904 | tf_op jit(solution)/shard_map/ppermute | solution.py:598
  6.9 0.0 collective-permute-done.1.rest_3_
  6.9 1.3 %collective-permute-start.5 = (bf16[128,256]{1,0:T(8,128)(2,1)S(1)}, bf16[128,256]{1,0:T(8,128)(2,1)S(1)}, u32[]{:S(2)}, u32[]{:S(2)}) collective-permute-start(bf16[128,256]{1,0:T(8,128)(2,1)S(1)} %shard_map.48.rest_0_), channel_id=1, source_target_pairs={{0,12},{1,13},{4,8},{5,9},{8,4},{9,5},{12,0},{13,1},{2,14},{3,15},... | collective-permute-start | bytes 196616 | tf_op jit(solution)/shard_map/ppermute | solution.py:598
  8.2 0.0 collective-permute-done.3.rest_5_
  8.2 1.2 %collective-permute-start = (bf16[128,256]{1,0:T(8,128)(2,1)S(1)}, bf16[128,256]{1,0:T(8,128)(2,1)S(1)}, u32[]{:S(2)}, u32[]{:S(2)}) collective-permute-start(bf16[128,256]{1,0:T(8,128)(2,1)S(1)} %shard_map.47.rest_0_.rest_1_), channel_id=1, source_target_pairs={{0,1},{1,0},{4,5},{5,4},{8,9},{9,8},{12,13},{13,12},{2,3},{3,2},{6... | collective-permute-start | bytes 196616 | tf_op jit(solution)/shard_map/ppermute | solution.py:598
  9.4 0.8 %shard_map.46 = (bf16[128,128]{1,0:T(8,128)(2,1)S(1)}, bf16[128,128]{1,0:T(8,128)(2,1)S(1)}, bf16[192,256]{1,0:T(8,128)(2,1)S(1)}, bf16[120,128]{1,0:T(8,128)(2,...) custom-call(s32[16]{0:T(128)S(1)} %copy-done.4, bf16[64,108]{1,0:T(8,128)(2,1)S(1)} %copy-done.3, ...), custom_call_target="tpu_custom_call" | custom-call | flops 1000000 | bytes 1000000 | tf_op jit(solution)/shard_map/pallas_call | solution.py:50
  10.2 5.8 %collective-permute-done.5.rest_7_ = bf16[128,256]{1,0:T(8,128)(2,1)S(1)} collective-permute-done((bf16[128,256]{1,0:T(8,128)(2,1)S(1)}, bf16[128,256]{1,0:T(8,128)(2,1)S(1)}, u32[]{:S(2)}, u32[]{:S(2)}) %collective-permute-start.5) | collective-permute-done | bytes 65568 | tf_op jit(solution)/shard_map/ppermute | solution.py:598
  16.0 0.0 collective-permute-done.rest_2_
  16.0 0.0 collective-permute-done.2.rest_4_
  16.0 0.0 collective-permute-done.4.rest_6_
  16.0 0.0 collective-permute-done.6.rest_8_
  16.0 3.7 %shard_map.55 = f32[2,1024]{1,0:T(2,128)S(1)} custom-call(s32[16]{0:T(128)S(1)} %copy-done.4, bf16[128,128]{1,0:T(8,128)(2,1)S(1)} %get-tuple-element.11.order, bf16[128,128]{1,0:T(8,128)(2,1)S(1)} %get-tuple-element.12.order_band, bf16[192,256]{1,0:T(8,128)(2,1)S(1)} %get-tuple-element.13.flip, bf16[120,128]{1,0:T(8,128)(2,1)S(1)} %get-tuple-element.14.guide, ...), custom_call_target="tpu_custom_call" | custom-call | flops 1000000000 | bytes 1000000 | tf_op jit(solution)/shard_map/pallas_call | solution.py:50
  19.8 1.5 %collective-permute-start.7 = (f32[2,1024]{1,0:T(2,128)S(1)}, f32[2,1024]{1,0:T(2,128)S(1)}, u32[]{:S(2)}, u32[]{:S(2)}) collective-permute-start(f32[2,1024]{1,0:T(2,128)S(1)} %shard_map.55), channel_id=1, source_target_pairs={{0,1},{1,0},{2,3},{3,2},{4,5},{5,4},{6,7},{7,6},{8,9},{9,8},{10,11... | collective-permute-start | bytes 24584 | tf_op jit(solution)/shard_map/ppermute | solution.py:621
  21.2 0.8 %collective-permute-done.7 = f32[2,1024]{1,0:T(2,128)S(1)} collective-permute-done((f32[2,1024]{1,0:T(2,128)S(1)}, f32[2,1024]{1,0:T(2,128)S(1)}, u32[]{:S(2)}, u32[]{:S(2)}) %collective-permute-start.7) | collective-permute-done | bytes 8224 | tf_op jit(solution)/shard_map/ppermute | solution.py:621
  22.0 0.6 %maximum_select_fusion = f32[1,4,1024]{2,1,0:T(4,128)} fusion(f32[1,2,1024]{2,1,0:T(2,128)S(1)} %bitcast.12, f32[1,2,1024]{2,1,0:T(2,128)S(1)} %bitcast.11, pred[]{:T(512)S(6)} %eq.3), kind=kLoop, calls=%fused_computation | loop fusion | flops 12288 | bytes 32769 | tf_op jit(solution)/shard_map/jit(_where)/select_n | solution.py:623
  (13 shorter events, 0.1 us)
Async XLA Ops:
  0.0 1.0 %copy-start = (bf16[1,16,64,256]{3,2,1,0:T(8,128)(2,1)S(1)}, bf16[1,16,64,256]{3,2,1,0:T(8,128)(2,1)}, u32[]{:S(2)}) copy-start(bf16[1,16,64,256]{3,2,1,0:T(8,128)(2,1)} %param.4) | copy-start | bytes 1572868
  1.1 1.5 %copy-start.1 = (bf16[1,16,64,256]{3,2,1,0:T(8,128)(2,1)S(1)}, bf16[1,16,64,256]{3,2,1,0:T(8,128)(2,1)}, u32[]{:S(2)}) copy-start(bf16[1,16,64,256]{3,2,1,0:T(8,128)(2,1)} %param.4) | copy-start | bytes 1572868
  1.1 1.5 %copy-start.2 = (s32[2,256]{1,0:T(2,128)S(1)}, s32[2,256]{1,0:T(2,128)}, u32[]{:S(2)}) copy-start(s32[2,256]{1,0:T(2,128)} %rest_0_.5) | copy-start | bytes 6148
  1.1 5.8 %collective-permute-start.1 = (bf16[128,256]{1,0:T(8,128)(2,1)S(1)}, bf16[128,256]{1,0:T(8,128)(2,1)S(1)}, u32[]{:S(2)}, u32[]{:S(2)}) collective-permute-start(bf16[128,256]{1,0:T(8,128)(2,1)S(1)} %shard_map.50.rest_0_.rest_1_), channel_id=1, source_target_pairs={{0,4},{1,5},{4,0},{5,1},{8,12},{9,13},{12,8},{13,9},{2,6},{3,7},{6... | collective-permute-start | bytes 196616 | tf_op jit(solution)/shard_map/ppermute | solution.py:598
  2.5 5.7 %collective-permute-start.3 = (bf16[128,256]{1,0:T(8,128)(2,1)S(1)}, bf16[128,256]{1,0:T(8,128)(2,1)S(1)}, u32[]{:S(2)}, u32[]{:S(2)}) collective-permute-start(bf16[128,256]{1,0:T(8,128)(2,1)S(1)} %shard_map.49.rest_0_), channel_id=1, source_target_pairs={{0,8},{1,9},{4,12},{5,13},{8,0},{9,1},{12,4},{13,5},{2,10},{3,11},... | collective-permute-start | bytes 196616 | tf_op jit(solution)/shard_map/ppermute | solution.py:598
  2.6 13.4 %collective-permute-start.4 = (bf16[136,256]{1,0:T(8,128)(2,1)S(1)}, bf16[136,256]{1,0:T(8,128)(2,1)S(1)}, u32[]{:S(2)}, u32[]{:S(2)}) collective-permute-start(bf16[136,256]{1,0:T(8,128)(2,1)S(1)} %shard_map.52.rest_1_), channel_id=1, source_target_pairs={{0,9},{1,8},{4,13},{5,12},{8,1},{9,0},{12,5},{13,4},{2,11},{3,10},... | collective-permute-start | bytes 208904 | tf_op jit(solution)/shard_map/ppermute | solution.py:598
  6.1 9.9 %collective-permute-start.2 = (bf16[136,256]{1,0:T(8,128)(2,1)S(1)}, bf16[136,256]{1,0:T(8,128)(2,1)S(1)}, u32[]{:S(2)}, u32[]{:S(2)}) collective-permute-start(bf16[136,256]{1,0:T(8,128)(2,1)S(1)} %shard_map.53), channel_id=1, source_target_pairs={{0,5},{1,4},{4,1},{5,0},{8,13},{9,12},{12,9},{13,8},{2,7},{3,6},{6... | collective-permute-start | bytes 208904 | tf_op jit(solution)/shard_map/ppermute | solution.py:598
  6.2 3.2 %copy-start.3 = (bf16[64,108]{1,0:T(8,128)(2,1)S(1)}, bf16[64,108]{1,0:T(8,128)(2,1)}, u32[]{:S(2)}) copy-start(bf16[64,108]{1,0:T(8,128)(2,1)} %guide.1) | copy-start | bytes 41476
  6.2 3.2 %copy-start.4 = (s32[16]{0:T(128)S(1)}, s32[16]{0:T(128)}, u32[]{:S(2)}) copy-start(s32[16]{0:T(128)} %offsets.3) | copy-start | bytes 196
  6.2 9.8 %collective-permute-start.6 = (bf16[136,256]{1,0:T(8,128)(2,1)S(1)}, bf16[136,256]{1,0:T(8,128)(2,1)S(1)}, u32[]{:S(2)}, u32[]{:S(2)}) collective-permute-start(bf16[136,256]{1,0:T(8,128)(2,1)S(1)} %shard_map.54), channel_id=1, source_target_pairs={{0,13},{1,12},{4,9},{5,8},{8,5},{9,4},{12,1},{13,0},{2,15},{3,14},... | collective-permute-start | bytes 208904 | tf_op jit(solution)/shard_map/ppermute | solution.py:598
  6.9 9.1 %collective-permute-start.5 = (bf16[128,256]{1,0:T(8,128)(2,1)S(1)}, bf16[128,256]{1,0:T(8,128)(2,1)S(1)}, u32[]{:S(2)}, u32[]{:S(2)}) collective-permute-start(bf16[128,256]{1,0:T(8,128)(2,1)S(1)} %shard_map.48.rest_0_), channel_id=1, source_target_pairs={{0,12},{1,13},{4,8},{5,9},{8,4},{9,5},{12,0},{13,1},{2,14},{3,15},... | collective-permute-start | bytes 196616 | tf_op jit(solution)/shard_map/ppermute | solution.py:598
  8.2 7.8 %collective-permute-start = (bf16[128,256]{1,0:T(8,128)(2,1)S(1)}, bf16[128,256]{1,0:T(8,128)(2,1)S(1)}, u32[]{:S(2)}, u32[]{:S(2)}) collective-permute-start(bf16[128,256]{1,0:T(8,128)(2,1)S(1)} %shard_map.47.rest_0_.rest_1_), channel_id=1, source_target_pairs={{0,1},{1,0},{4,5},{5,4},{8,9},{9,8},{12,13},{13,12},{2,3},{3,2},{6... | collective-permute-start | bytes 196616 | tf_op jit(solution)/shard_map/ppermute | solution.py:598
  19.8 2.3 %collective-permute-start.7 = (f32[2,1024]{1,0:T(2,128)S(1)}, f32[2,1024]{1,0:T(2,128)S(1)}, u32[]{:S(2)}, u32[]{:S(2)}) collective-permute-start(f32[2,1024]{1,0:T(2,128)S(1)} %shard_map.55), channel_id=1, source_target_pairs={{0,1},{1,0},{2,3},{3,2},{4,5},{5,4},{6,7},{7,6},{8,9},{9,8},{10,11... | collective-permute-start | bytes 24584 | tf_op jit(solution)/shard_map/ppermute | solution.py:621

commit v23 on v20

--- a/solution.py
+++ b/solution.py
@@ -436,8 +436,7 @@
         lo = (w % 2) * LANES
         return valid[w // 2, view : view + 1, lo : lo + LANES]
 
-    for i in range(PAIR):
-
+    def correlate(i):
         def tile_of(view, w):
             lo = (w % 2) * LANES
             return blocks[2 * (w // 2) + view, i * CHANNELS : (i + 1) * CHANNELS, lo : lo + LANES]
@@ -491,6 +490,7 @@
                                 )
                             )
                         cost_rows[i, row : row + PARTS, :] = jnp.concatenate(halves, axis=0).astype(BF)
+                yield
 
     x_base = width - 1 - LINE_RUN * iota((KEYS, LANES), 1)
     row = iota((KEYS, LANES), 0)
@@ -498,7 +498,7 @@
     room_left = x_base - reach
     room_right = x_base + reach - width
     unit = jnp.where(row >= 2 * GROUPS, SHARPNESS / math.log(2.0), 1.0)
-    for i in range(PAIR):
+    def prepare(i):
         for two in range(LINE_RUN // 2):
             lo = 2 * two * LANES
             costs = dot_t(flip[...], cost_rows[i, lo : lo + 2 * LANES, :])
@@ -514,10 +514,11 @@
                 taps[2] = jnp.where(room_right < t, taps[2], 0.0)
                 for m in range(3):
                     wts[i, t, m * KEYS : (m + 1) * KEYS, :] = taps[m]
-
-    for group in range(GROUPS):
-        starts = [group * DGROUP + 8 * half for half in range(2)]
-        for i in range(PAIR):
+            yield
+
+    def aggregate(i):
+        for group in range(GROUPS):
+            starts = [group * DGROUP + 8 * half for half in range(2)]
             v = [[vol[i, t, at : at + 8, :] for t in range(LINE_RUN)] for at in starts]
             for layer in range(LAYERS):
                 s = 3**layer
@@ -535,10 +536,12 @@
             for half, at_row in enumerate(starts):
                 for t in range(LINE_RUN):
                     done[i, t, at_row : at_row + 8, :] = v[half][t]
+            yield
 
     sub = iota((8, LANES), 0)
     results = []
-    for i in range(PAIR):
+
+    def softmax(i):
         totals = jnp.zeros((8, LANES), F32)
         moments = totals
         for s in range(LINE_RUN):
@@ -557,7 +560,21 @@
             moment = 8.0 * moment + sub.astype(F32) * total
             totals = jnp.where(sub == s, jnp.sum(total, axis=0, keepdims=True), totals)
             moments = jnp.where(sub == s, jnp.sum(moment, axis=0, keepdims=True), moments)
+            yield
         results.append((moments / totals + offs[i].astype(F32)) * (1.0 / DISP))
+    def beside(first, second, count):
+        for _ in first:
+            for _ in range(count):
+                next(second, None)
+        for _ in second:
+            pass
+
+    beside(correlate(0), iter(()), 0)
+    beside(prepare(0), iter(()), 0)
+    beside(correlate(1), aggregate(0), 3)
+    beside(prepare(1), softmax(0), 2)
+    beside(aggregate(1), iter(()), 0)
+    beside(softmax(1), iter(()), 0)
     both = jnp.concatenate(results, axis=0)
     high = both.astype(BF)
     left = both - high.astype(F32)

time: 21.9 us -> 22.1 us (level)
  Pallas kernels: 4.68 us -> 4.92 us
    pallas_call x10, Pallas kernels: 4.68 us -> 4.92 us  [call(): pl.pallas_call(kernel, out_shape=[jax.ShapeDtypeStruct(shape, dtype) for...]
where the time goes in v23:
time: 22.1 us; the launch traced here: 21.9 us
  starting transfers between devices  10.5 us (48%)
  Pallas kernels  4.92 us (22%)
  waiting for transfers between devices  4.65 us (21%)
  local copies, waits for them, and re-layouts  1.07 us (5%)
  other arithmetic  0.62 us (3%)
    ppermute x7, starting transfers between devices, lines_plan(): pieces[key] = lax.ppermute(piece, ('cols', 'view'), moves) if key else piece  10.1 us
    pallas_call x10, Pallas kernels, call(): pl.pallas_call(kernel, out_shape=[jax.ShapeDtypeStruct(shape, dtype) for...  4.92 us
    ppermute x7, waiting for transfers between devices, lines_plan(): pieces[key] = lax.ppermute(piece, ('cols', 'view'), moves) if key else piece  3.79 us
    unnamed x10, local copies, waits for them, and re-layouts  1.07 us
    ppermute x1, waiting for transfers between devices, lines_plan(): others = lax.ppermute(rows, 'view', [(0, 1), (1, 0)])  0.86 us
    select_n x1, other arithmetic, lines_plan(): jnp.where(first, jnp.concatenate([rows, others]), jnp.concatenate([others...  0.62 us
  transfers between devices with their start and end apart: 8, of which 3 were waited for; matrix products, arithmetic and copies ran while one was open for 0% of the time, Pallas kernels for 4%

profile of v23, /device:TPU:0, one launch (start us, length us, event | category | flops | bytes accessed | tf_op | source)
XLA Modules:
  0.0 21.9 jit_solution(10898243714428201136)
XLA Ops:
  0.0 1.0 %copy-done = bf16[1,16,64,256]{3,2,1,0:T(8,128)(2,1)S(1)} copy-done((bf16[1,16,64,256]{3,2,1,0:T(8,128)(2,1)S(1)}, bf16[1,16,64,256]{3,2,1,0:T(8,128)(2,1)}, u32[]{:S(2)}) %copy-start) | copy-done | bytes 524312
  1.1 0.0 copy-start.1
  1.1 0.0 copy-start.2
  1.1 4.1 %collective-permute-start.3 = (bf16[128,256]{1,0:T(8,128)(2,1)S(1)}, bf16[128,256]{1,0:T(8,128)(2,1)S(1)}, u32[]{:S(2)}, u32[]{:S(2)}) collective-permute-start(bf16[128,256]{1,0:T(8,128)(2,1)S(1)} %shard_map.50.rest_1_), channel_id=1, source_target_pairs={{0,8},{1,9},{4,12},{5,13},{8,0},{9,1},{12,4},{13,5},{2,10},{3,11},... | collective-permute-start | bytes 196616 | tf_op jit(solution)/shard_map/ppermute | solution.py:613
  5.2 1.3 %collective-permute-start.5 = (bf16[128,256]{1,0:T(8,128)(2,1)S(1)}, bf16[128,256]{1,0:T(8,128)(2,1)S(1)}, u32[]{:S(2)}, u32[]{:S(2)}) collective-permute-start(bf16[128,256]{1,0:T(8,128)(2,1)S(1)} %shard_map.49.rest_0_), channel_id=1, source_target_pairs={{0,12},{1,13},{4,8},{5,9},{8,4},{9,5},{12,0},{13,1},{2,14},{3,15},... | collective-permute-start | bytes 196616 | tf_op jit(solution)/shard_map/ppermute | solution.py:613
  6.7 0.0 copy-start.3
  6.7 0.0 copy-start.4
  6.7 0.1 collective-permute-start.2
  6.8 2.7 %collective-permute-start.4 = (bf16[136,256]{1,0:T(8,128)(2,1)S(1)}, bf16[136,256]{1,0:T(8,128)(2,1)S(1)}, u32[]{:S(2)}, u32[]{:S(2)}) collective-permute-start(bf16[136,256]{1,0:T(8,128)(2,1)S(1)} %shard_map.52.rest_1_), channel_id=1, source_target_pairs={{0,9},{1,8},{4,13},{5,12},{8,1},{9,0},{12,5},{13,4},{2,11},{3,10},... | collective-permute-start | bytes 208904 | tf_op jit(solution)/shard_map/ppermute | solution.py:613
  9.5 0.2 %collective-permute-start.6 = (bf16[136,256]{1,0:T(8,128)(2,1)S(1)}, bf16[136,256]{1,0:T(8,128)(2,1)S(1)}, u32[]{:S(2)}, u32[]{:S(2)}) collective-permute-start(bf16[136,256]{1,0:T(8,128)(2,1)S(1)} %shard_map.51.rest_1_), channel_id=1, source_target_pairs={{0,13},{1,12},{4,9},{5,8},{8,5},{9,4},{12,1},{13,0},{2,15},{3,14},... | collective-permute-start | bytes 208904 | tf_op jit(solution)/shard_map/ppermute | solution.py:613
  9.8 0.0 collective-permute-done.3.rest_5_
  9.8 1.6 %collective-permute-start.1 = (bf16[128,256]{1,0:T(8,128)(2,1)S(1)}, bf16[128,256]{1,0:T(8,128)(2,1)S(1)}, u32[]{:S(2)}, u32[]{:S(2)}) collective-permute-start(bf16[128,256]{1,0:T(8,128)(2,1)S(1)} %shard_map.48.rest_0_), channel_id=1, source_target_pairs={{0,4},{1,5},{4,0},{5,1},{8,12},{9,13},{12,8},{13,9},{2,6},{3,7},{6... | collective-permute-start | bytes 196616 | tf_op jit(solution)/shard_map/ppermute | solution.py:613
  11.4 0.3 %collective-permute-done.5.rest_7_ = bf16[128,256]{1,0:T(8,128)(2,1)S(1)} collective-permute-done((bf16[128,256]{1,0:T(8,128)(2,1)S(1)}, bf16[128,256]{1,0:T(8,128)(2,1)S(1)}, u32[]{:S(2)}, u32[]{:S(2)}) %collective-permute-start.5) | collective-permute-done | bytes 65568 | tf_op jit(solution)/shard_map/ppermute | solution.py:613
  11.7 0.0 collective-permute-start
  11.8 0.8 %shard_map.46 = (bf16[128,128]{1,0:T(8,128)(2,1)S(1)}, bf16[128,128]{1,0:T(8,128)(2,1)S(1)}, bf16[192,256]{1,0:T(8,128)(2,1)S(1)}, bf16[120,128]{1,0:T(8,128)(2,...) custom-call(s32[16]{0:T(128)S(1)} %copy-done.4, bf16[64,108]{1,0:T(8,128)(2,1)S(1)} %copy-done.3, ...), custom_call_target="tpu_custom_call" | custom-call | flops 1000000 | bytes 1000000 | tf_op jit(solution)/shard_map/pallas_call | solution.py:50
  12.6 3.4 %collective-permute-done.1.rest_3_ = bf16[128,256]{1,0:T(8,128)(2,1)S(1)} collective-permute-done((bf16[128,256]{1,0:T(8,128)(2,1)S(1)}, bf16[128,256]{1,0:T(8,128)(2,1)S(1)}, u32[]{:S(2)}, u32[]{:S(2)}) %collective-permute-start.1) | collective-permute-done | bytes 65568 | tf_op jit(solution)/shard_map/ppermute | solution.py:613
  16.0 0.0 collective-permute-done.rest_2_
  16.0 0.0 collective-permute-done.2.rest_4_
  16.1 0.0 collective-permute-done.4.rest_6_
  16.1 0.0 collective-permute-done.6.rest_8_
  16.1 4.0 %shard_map.55 = f32[2,1024]{1,0:T(2,128)S(1)} custom-call(s32[16]{0:T(128)S(1)} %copy-done.4, bf16[128,128]{1,0:T(8,128)(2,1)S(1)} %get-tuple-element.11.order, bf16[128,128]{1,0:T(8,128)(2,1)S(1)} %get-tuple-element.12.order_band, bf16[192,256]{1,0:T(8,128)(2,1)S(1)} %get-tuple-element.13.flip, bf16[120,128]{1,0:T(8,128)(2,1)S(1)} %get-tuple-element.14.guide, ...), custom_call_target="tpu_custom_call" | custom-call | flops 1000000000 | bytes 1000000 | tf_op jit(solution)/shard_map/pallas_call | solution.py:50
  20.0 0.4 %collective-permute-start.7 = (f32[2,1024]{1,0:T(2,128)S(1)}, f32[2,1024]{1,0:T(2,128)S(1)}, u32[]{:S(2)}, u32[]{:S(2)}) collective-permute-start(f32[2,1024]{1,0:T(2,128)S(1)} %shard_map.55), channel_id=1, source_target_pairs={{0,1},{1,0},{2,3},{3,2},{4,5},{5,4},{6,7},{7,6},{8,9},{9,8},{10,11... | collective-permute-start | bytes 24584 | tf_op jit(solution)/shard_map/ppermute | solution.py:636
  20.4 0.9 %collective-permute-done.7 = f32[2,1024]{1,0:T(2,128)S(1)} collective-permute-done((f32[2,1024]{1,0:T(2,128)S(1)}, f32[2,1024]{1,0:T(2,128)S(1)}, u32[]{:S(2)}, u32[]{:S(2)}) %collective-permute-start.7) | collective-permute-done | bytes 8224 | tf_op jit(solution)/shard_map/ppermute | solution.py:636
  21.3 0.6 %maximum_select_fusion = f32[1,4,1024]{2,1,0:T(4,128)} fusion(f32[1,2,1024]{2,1,0:T(2,128)S(1)} %bitcast.12, f32[1,2,1024]{2,1,0:T(2,128)S(1)} %bitcast.11, pred[]{:T(512)S(6)} %eq.3), kind=kLoop, calls=%fused_computation | loop fusion | flops 12288 | bytes 32769 | tf_op jit(solution)/shard_map/jit(_where)/select_n | solution.py:638
  (13 shorter events, 0.1 us)
Async XLA Ops:
  0.0 1.0 %copy-start = (bf16[1,16,64,256]{3,2,1,0:T(8,128)(2,1)S(1)}, bf16[1,16,64,256]{3,2,1,0:T(8,128)(2,1)}, u32[]{:S(2)}) copy-start(bf16[1,16,64,256]{3,2,1,0:T(8,128)(2,1)} %param.4) | copy-start | bytes 1572868
  1.1 5.5 %copy-start.1 = (bf16[1,16,64,256]{3,2,1,0:T(8,128)(2,1)S(1)}, bf16[1,16,64,256]{3,2,1,0:T(8,128)(2,1)}, u32[]{:S(2)}) copy-start(bf16[1,16,64,256]{3,2,1,0:T(8,128)(2,1)} %param.4) | copy-start | bytes 1572868
  1.1 5.5 %copy-start.2 = (s32[2,256]{1,0:T(2,128)S(1)}, s32[2,256]{1,0:T(2,128)}, u32[]{:S(2)}) copy-start(s32[2,256]{1,0:T(2,128)} %rest_0_.5) | copy-start | bytes 6148
  1.1 8.6 %collective-permute-start.3 = (bf16[128,256]{1,0:T(8,128)(2,1)S(1)}, bf16[128,256]{1,0:T(8,128)(2,1)S(1)}, u32[]{:S(2)}, u32[]{:S(2)}) collective-permute-start(bf16[128,256]{1,0:T(8,128)(2,1)S(1)} %shard_map.50.rest_1_), channel_id=1, source_target_pairs={{0,8},{1,9},{4,12},{5,13},{8,0},{9,1},{12,4},{13,5},{2,10},{3,11},... | collective-permute-start | bytes 196616 | tf_op jit(solution)/shard_map/ppermute | solution.py:613
  5.2 6.5 %collective-permute-start.5 = (bf16[128,256]{1,0:T(8,128)(2,1)S(1)}, bf16[128,256]{1,0:T(8,128)(2,1)S(1)}, u32[]{:S(2)}, u32[]{:S(2)}) collective-permute-start(bf16[128,256]{1,0:T(8,128)(2,1)S(1)} %shard_map.49.rest_0_), channel_id=1, source_target_pairs={{0,12},{1,13},{4,8},{5,9},{8,4},{9,5},{12,0},{13,1},{2,14},{3,15},... | collective-permute-start | bytes 196616 | tf_op jit(solution)/shard_map/ppermute | solution.py:613
  6.7 5.1 %copy-start.3 = (bf16[64,108]{1,0:T(8,128)(2,1)S(1)}, bf16[64,108]{1,0:T(8,128)(2,1)}, u32[]{:S(2)}) copy-start(bf16[64,108]{1,0:T(8,128)(2,1)} %guide.1) | copy-start | bytes 41476
  6.7 5.1 %copy-start.4 = (s32[16]{0:T(128)S(1)}, s32[16]{0:T(128)}, u32[]{:S(2)}) copy-start(s32[16]{0:T(128)} %offsets.3) | copy-start | bytes 196
  6.7 9.4 %collective-permute-start.2 = (bf16[136,256]{1,0:T(8,128)(2,1)S(1)}, bf16[136,256]{1,0:T(8,128)(2,1)S(1)}, u32[]{:S(2)}, u32[]{:S(2)}) collective-permute-start(bf16[136,256]{1,0:T(8,128)(2,1)S(1)} %shard_map.53.rest_0_), channel_id=1, source_target_pairs={{0,5},{1,4},{4,1},{5,0},{8,13},{9,12},{12,9},{13,8},{2,7},{3,6},{6... | collective-permute-start | bytes 208904 | tf_op jit(solution)/shard_map/ppermute | solution.py:613
  6.8 9.3 %collective-permute-start.4 = (bf16[136,256]{1,0:T(8,128)(2,1)S(1)}, bf16[136,256]{1,0:T(8,128)(2,1)S(1)}, u32[]{:S(2)}, u32[]{:S(2)}) collective-permute-start(bf16[136,256]{1,0:T(8,128)(2,1)S(1)} %shard_map.52.rest_1_), channel_id=1, source_target_pairs={{0,9},{1,8},{4,13},{5,12},{8,1},{9,0},{12,5},{13,4},{2,11},{3,10},... | collective-permute-start | bytes 208904 | tf_op jit(solution)/shard_map/ppermute | solution.py:613
  9.5 6.5 %collective-permute-start.6 = (bf16[136,256]{1,0:T(8,128)(2,1)S(1)}, bf16[136,256]{1,0:T(8,128)(2,1)S(1)}, u32[]{:S(2)}, u32[]{:S(2)}) collective-permute-start(bf16[136,256]{1,0:T(8,128)(2,1)S(1)} %shard_map.51.rest_1_), channel_id=1, source_target_pairs={{0,13},{1,12},{4,9},{5,8},{8,5},{9,4},{12,1},{13,0},{2,15},{3,14},... | collective-permute-start | bytes 208904 | tf_op jit(solution)/shard_map/ppermute | solution.py:613
  9.8 6.3 %collective-permute-start.1 = (bf16[128,256]{1,0:T(8,128)(2,1)S(1)}, bf16[128,256]{1,0:T(8,128)(2,1)S(1)}, u32[]{:S(2)}, u32[]{:S(2)}) collective-permute-start(bf16[128,256]{1,0:T(8,128)(2,1)S(1)} %shard_map.48.rest_0_), channel_id=1, source_target_pairs={{0,4},{1,5},{4,0},{5,1},{8,12},{9,13},{12,8},{13,9},{2,6},{3,7},{6... | collective-permute-start | bytes 196616 | tf_op jit(solution)/shard_map/ppermute | solution.py:613
  11.7 4.3 %collective-permute-start = (bf16[128,256]{1,0:T(8,128)(2,1)S(1)}, bf16[128,256]{1,0:T(8,128)(2,1)S(1)}, u32[]{:S(2)}, u32[]{:S(2)}) collective-permute-start(bf16[128,256]{1,0:T(8,128)(2,1)S(1)} %shard_map.47.rest_0_), channel_id=1, source_target_pairs={{0,1},{1,0},{4,5},{5,4},{8,9},{9,8},{12,13},{13,12},{2,3},{3,2},{6... | collective-permute-start | bytes 196616 | tf_op jit(solution)/shard_map/ppermute | solution.py:613
  20.0 1.2 %collective-permute-start.7 = (f32[2,1024]{1,0:T(2,128)S(1)}, f32[2,1024]{1,0:T(2,128)S(1)}, u32[]{:S(2)}, u32[]{:S(2)}) collective-permute-start(f32[2,1024]{1,0:T(2,128)S(1)} %shard_map.55), channel_id=1, source_target_pairs={{0,1},{1,0},{2,3},{3,2},{4,5},{5,4},{6,7},{7,6},{8,9},{9,8},{10,11... | collective-permute-start | bytes 24584 | tf_op jit(solution)/shard_map/ppermute | solution.py:636

commit v24 on v20

--- a/solution.py
+++ b/solution.py
@@ -515,6 +515,7 @@
                 for m in range(3):
                     wts[i, t, m * KEYS : (m + 1) * KEYS, :] = taps[m]
 
+    peaks = [[None] * LINE_RUN for _ in range(PAIR)]
     for group in range(GROUPS):
         starts = [group * DGROUP + 8 * half for half in range(2)]
         for i in range(PAIR):
@@ -535,6 +536,9 @@
             for half, at_row in enumerate(starts):
                 for t in range(LINE_RUN):
                     done[i, t, at_row : at_row + 8, :] = v[half][t]
+            for t in range(LINE_RUN):
+                peak = jnp.maximum(v[0][t], v[1][t])
+                peaks[i][t] = peak if group == 0 else jnp.maximum(peaks[i][t], peak)
 
     sub = iota((8, LANES), 0)
     results = []
@@ -544,10 +548,7 @@
         for s in range(LINE_RUN):
             t = LINE_RUN - 1 - s
             v = [done[i, t, 8 * j : 8 * j + 8, :] for j in range(DISP // 8)]
-            top = v
-            while len(top) > 1:
-                top = [jnp.maximum(a, b) for a, b in zip(top[::2], top[1::2])] + top[len(top) & ~1 :]
-            top = jnp.max(top[0], axis=0, keepdims=True)
+            top = jnp.max(peaks[i][t], axis=0, keepdims=True)
             total = jnp.exp2(v[-1] - top)
             moment = total
             for j in range(DISP // 8 - 2, -1, -1):

time: 21.9 us -> 21.9 us (level)
  no operation moved by 1% of the time
where the time goes in v24:
time: 21.9 us; the launch traced here: 21.7 us
  starting transfers between devices  10.5 us (48%)
  Pallas kernels  4.73 us (22%)
  waiting for transfers between devices  4.65 us (21%)
  local copies, waits for them, and re-layouts  1.07 us (5%)
  other arithmetic  0.62 us (3%)
    ppermute x7, starting transfers between devices, lines_plan(): pieces[key] = lax.ppermute(piece, ('cols', 'view'), moves) if key else piece  10.1 us
    pallas_call x10, Pallas kernels, call(): pl.pallas_call(kernel, out_shape=[jax.ShapeDtypeStruct(shape, dtype) for...  4.73 us
    ppermute x7, waiting for transfers between devices, lines_plan(): pieces[key] = lax.ppermute(piece, ('cols', 'view'), moves) if key else piece  3.79 us
    unnamed x10, local copies, waits for them, and re-layouts  1.07 us
    ppermute x1, waiting for transfers between devices, lines_plan(): others = lax.ppermute(rows, 'view', [(0, 1), (1, 0)])  0.87 us
    select_n x1, other arithmetic, lines_plan(): jnp.where(first, jnp.concatenate([rows, others]), jnp.concatenate([others...  0.62 us
  transfers between devices with their start and end apart: 8, of which 3 were waited for; matrix products, arithmetic and copies ran while one was open for 0% of the time, Pallas kernels for 4%

profile of v24, /device:TPU:0, one launch (start us, length us, event | category | flops | bytes accessed | tf_op | source)
XLA Modules:
  0.0 21.7 jit_solution(9889068322820663167)
XLA Ops:
  0.0 1.0 %copy-done = bf16[1,16,64,256]{3,2,1,0:T(8,128)(2,1)S(1)} copy-done((bf16[1,16,64,256]{3,2,1,0:T(8,128)(2,1)S(1)}, bf16[1,16,64,256]{3,2,1,0:T(8,128)(2,1)}, u32[]{:S(2)}) %copy-start) | copy-done | bytes 524312
  1.1 0.0 copy-start.1
  1.1 0.0 copy-start.2
  1.1 4.1 %collective-permute-start.3 = (bf16[128,256]{1,0:T(8,128)(2,1)S(1)}, bf16[128,256]{1,0:T(8,128)(2,1)S(1)}, u32[]{:S(2)}, u32[]{:S(2)}) collective-permute-start(bf16[128,256]{1,0:T(8,128)(2,1)S(1)} %shard_map.50.rest_1_), channel_id=1, source_target_pairs={{0,8},{1,9},{4,12},{5,13},{8,0},{9,1},{12,4},{13,5},{2,10},{3,11},... | collective-permute-start | bytes 196616 | tf_op jit(solution)/shard_map/ppermute | solution.py:597
  5.2 1.3 %collective-permute-start.5 = (bf16[128,256]{1,0:T(8,128)(2,1)S(1)}, bf16[128,256]{1,0:T(8,128)(2,1)S(1)}, u32[]{:S(2)}, u32[]{:S(2)}) collective-permute-start(bf16[128,256]{1,0:T(8,128)(2,1)S(1)} %shard_map.49.rest_0_), channel_id=1, source_target_pairs={{0,12},{1,13},{4,8},{5,9},{8,4},{9,5},{12,0},{13,1},{2,14},{3,15},... | collective-permute-start | bytes 196616 | tf_op jit(solution)/shard_map/ppermute | solution.py:597
  6.7 0.0 copy-start.3
  6.7 0.0 copy-start.4
  6.7 0.1 collective-permute-start.2
  6.8 2.7 %collective-permute-start.4 = (bf16[136,256]{1,0:T(8,128)(2,1)S(1)}, bf16[136,256]{1,0:T(8,128)(2,1)S(1)}, u32[]{:S(2)}, u32[]{:S(2)}) collective-permute-start(bf16[136,256]{1,0:T(8,128)(2,1)S(1)} %shard_map.52.rest_1_), channel_id=1, source_target_pairs={{0,9},{1,8},{4,13},{5,12},{8,1},{9,0},{12,5},{13,4},{2,11},{3,10},... | collective-permute-start | bytes 208904 | tf_op jit(solution)/shard_map/ppermute | solution.py:597
  9.5 0.2 %collective-permute-start.6 = (bf16[136,256]{1,0:T(8,128)(2,1)S(1)}, bf16[136,256]{1,0:T(8,128)(2,1)S(1)}, u32[]{:S(2)}, u32[]{:S(2)}) collective-permute-start(bf16[136,256]{1,0:T(8,128)(2,1)S(1)} %shard_map.51.rest_1_), channel_id=1, source_target_pairs={{0,13},{1,12},{4,9},{5,8},{8,5},{9,4},{12,1},{13,0},{2,15},{3,14},... | collective-permute-start | bytes 208904 | tf_op jit(solution)/shard_map/ppermute | solution.py:597
  9.8 0.0 collective-permute-done.3.rest_5_
  9.8 1.6 %collective-permute-start.1 = (bf16[128,256]{1,0:T(8,128)(2,1)S(1)}, bf16[128,256]{1,0:T(8,128)(2,1)S(1)}, u32[]{:S(2)}, u32[]{:S(2)}) collective-permute-start(bf16[128,256]{1,0:T(8,128)(2,1)S(1)} %shard_map.48.rest_0_), channel_id=1, source_target_pairs={{0,4},{1,5},{4,0},{5,1},{8,12},{9,13},{12,8},{13,9},{2,6},{3,7},{6... | collective-permute-start | bytes 196616 | tf_op jit(solution)/shard_map/ppermute | solution.py:597
  11.4 0.3 %collective-permute-done.5.rest_7_ = bf16[128,256]{1,0:T(8,128)(2,1)S(1)} collective-permute-done((bf16[128,256]{1,0:T(8,128)(2,1)S(1)}, bf16[128,256]{1,0:T(8,128)(2,1)S(1)}, u32[]{:S(2)}, u32[]{:S(2)}) %collective-permute-start.5) | collective-permute-done | bytes 65568 | tf_op jit(solution)/shard_map/ppermute | solution.py:597
  11.7 0.0 collective-permute-start
  11.8 0.8 %shard_map.46 = (bf16[128,128]{1,0:T(8,128)(2,1)S(1)}, bf16[128,128]{1,0:T(8,128)(2,1)S(1)}, bf16[192,256]{1,0:T(8,128)(2,1)S(1)}, bf16[120,128]{1,0:T(8,128)(2,...) custom-call(s32[16]{0:T(128)S(1)} %copy-done.4, bf16[64,108]{1,0:T(8,128)(2,1)S(1)} %copy-done.3, ...), custom_call_target="tpu_custom_call" | custom-call | flops 1000000 | bytes 1000000 | tf_op jit(solution)/shard_map/pallas_call | solution.py:50
  12.6 3.4 %collective-permute-done.1.rest_3_ = bf16[128,256]{1,0:T(8,128)(2,1)S(1)} collective-permute-done((bf16[128,256]{1,0:T(8,128)(2,1)S(1)}, bf16[128,256]{1,0:T(8,128)(2,1)S(1)}, u32[]{:S(2)}, u32[]{:S(2)}) %collective-permute-start.1) | collective-permute-done | bytes 65568 | tf_op jit(solution)/shard_map/ppermute | solution.py:597
  16.0 0.0 collective-permute-done.rest_2_
  16.0 0.0 collective-permute-done.2.rest_4_
  16.1 0.0 collective-permute-done.4.rest_6_
  16.1 0.0 collective-permute-done.6.rest_8_
  16.1 3.8 %shard_map.55 = f32[2,1024]{1,0:T(2,128)S(1)} custom-call(s32[16]{0:T(128)S(1)} %copy-done.4, bf16[128,128]{1,0:T(8,128)(2,1)S(1)} %get-tuple-element.11.order, bf16[128,128]{1,0:T(8,128)(2,1)S(1)} %get-tuple-element.12.order_band, bf16[192,256]{1,0:T(8,128)(2,1)S(1)} %get-tuple-element.13.flip, bf16[120,128]{1,0:T(8,128)(2,1)S(1)} %get-tuple-element.14.guide, ...), custom_call_target="tpu_custom_call" | custom-call | flops 1000000000 | bytes 1000000 | tf_op jit(solution)/shard_map/pallas_call | solution.py:50
  19.9 0.4 %collective-permute-start.7 = (f32[2,1024]{1,0:T(2,128)S(1)}, f32[2,1024]{1,0:T(2,128)S(1)}, u32[]{:S(2)}, u32[]{:S(2)}) collective-permute-start(f32[2,1024]{1,0:T(2,128)S(1)} %shard_map.55), channel_id=1, source_target_pairs={{0,1},{1,0},{2,3},{3,2},{4,5},{5,4},{6,7},{7,6},{8,9},{9,8},{10,11... | collective-permute-start | bytes 24584 | tf_op jit(solution)/shard_map/ppermute | solution.py:620
  20.2 0.9 %collective-permute-done.7 = f32[2,1024]{1,0:T(2,128)S(1)} collective-permute-done((f32[2,1024]{1,0:T(2,128)S(1)}, f32[2,1024]{1,0:T(2,128)S(1)}, u32[]{:S(2)}, u32[]{:S(2)}) %collective-permute-start.7) | collective-permute-done | bytes 8224 | tf_op jit(solution)/shard_map/ppermute | solution.py:620
  21.1 0.6 %maximum_select_fusion = f32[1,4,1024]{2,1,0:T(4,128)} fusion(f32[1,2,1024]{2,1,0:T(2,128)S(1)} %bitcast.12, f32[1,2,1024]{2,1,0:T(2,128)S(1)} %bitcast.11, pred[]{:T(512)S(6)} %eq.3), kind=kLoop, calls=%fused_computation | loop fusion | flops 12288 | bytes 32769 | tf_op jit(solution)/shard_map/jit(_where)/select_n | solution.py:622
  (13 shorter events, 0.1 us)
Async XLA Ops:
  0.0 1.0 %copy-start = (bf16[1,16,64,256]{3,2,1,0:T(8,128)(2,1)S(1)}, bf16[1,16,64,256]{3,2,1,0:T(8,128)(2,1)}, u32[]{:S(2)}) copy-start(bf16[1,16,64,256]{3,2,1,0:T(8,128)(2,1)} %param.4) | copy-start | bytes 1572868
  1.1 5.5 %copy-start.1 = (bf16[1,16,64,256]{3,2,1,0:T(8,128)(2,1)S(1)}, bf16[1,16,64,256]{3,2,1,0:T(8,128)(2,1)}, u32[]{:S(2)}) copy-start(bf16[1,16,64,256]{3,2,1,0:T(8,128)(2,1)} %param.4) | copy-start | bytes 1572868
  1.1 5.5 %copy-start.2 = (s32[2,256]{1,0:T(2,128)S(1)}, s32[2,256]{1,0:T(2,128)}, u32[]{:S(2)}) copy-start(s32[2,256]{1,0:T(2,128)} %rest_0_.5) | copy-start | bytes 6148
  1.1 8.6 %collective-permute-start.3 = (bf16[128,256]{1,0:T(8,128)(2,1)S(1)}, bf16[128,256]{1,0:T(8,128)(2,1)S(1)}, u32[]{:S(2)}, u32[]{:S(2)}) collective-permute-start(bf16[128,256]{1,0:T(8,128)(2,1)S(1)} %shard_map.50.rest_1_), channel_id=1, source_target_pairs={{0,8},{1,9},{4,12},{5,13},{8,0},{9,1},{12,4},{13,5},{2,10},{3,11},... | collective-permute-start | bytes 196616 | tf_op jit(solution)/shard_map/ppermute | solution.py:597
  5.2 6.5 %collective-permute-start.5 = (bf16[128,256]{1,0:T(8,128)(2,1)S(1)}, bf16[128,256]{1,0:T(8,128)(2,1)S(1)}, u32[]{:S(2)}, u32[]{:S(2)}) collective-permute-start(bf16[128,256]{1,0:T(8,128)(2,1)S(1)} %shard_map.49.rest_0_), channel_id=1, source_target_pairs={{0,12},{1,13},{4,8},{5,9},{8,4},{9,5},{12,0},{13,1},{2,14},{3,15},... | collective-permute-start | bytes 196616 | tf_op jit(solution)/shard_map/ppermute | solution.py:597
  6.7 5.1 %copy-start.3 = (bf16[64,108]{1,0:T(8,128)(2,1)S(1)}, bf16[64,108]{1,0:T(8,128)(2,1)}, u32[]{:S(2)}) copy-start(bf16[64,108]{1,0:T(8,128)(2,1)} %guide.1) | copy-start | bytes 41476
  6.7 5.1 %copy-start.4 = (s32[16]{0:T(128)S(1)}, s32[16]{0:T(128)}, u32[]{:S(2)}) copy-start(s32[16]{0:T(128)} %offsets.3) | copy-start | bytes 196
  6.7 9.4 %collective-permute-start.2 = (bf16[136,256]{1,0:T(8,128)(2,1)S(1)}, bf16[136,256]{1,0:T(8,128)(2,1)S(1)}, u32[]{:S(2)}, u32[]{:S(2)}) collective-permute-start(bf16[136,256]{1,0:T(8,128)(2,1)S(1)} %shard_map.53.rest_0_), channel_id=1, source_target_pairs={{0,5},{1,4},{4,1},{5,0},{8,13},{9,12},{12,9},{13,8},{2,7},{3,6},{6... | collective-permute-start | bytes 208904 | tf_op jit(solution)/shard_map/ppermute | solution.py:597
  6.8 9.3 %collective-permute-start.4 = (bf16[136,256]{1,0:T(8,128)(2,1)S(1)}, bf16[136,256]{1,0:T(8,128)(2,1)S(1)}, u32[]{:S(2)}, u32[]{:S(2)}) collective-permute-start(bf16[136,256]{1,0:T(8,128)(2,1)S(1)} %shard_map.52.rest_1_), channel_id=1, source_target_pairs={{0,9},{1,8},{4,13},{5,12},{8,1},{9,0},{12,5},{13,4},{2,11},{3,10},... | collective-permute-start | bytes 208904 | tf_op jit(solution)/shard_map/ppermute | solution.py:597
  9.5 6.5 %collective-permute-start.6 = (bf16[136,256]{1,0:T(8,128)(2,1)S(1)}, bf16[136,256]{1,0:T(8,128)(2,1)S(1)}, u32[]{:S(2)}, u32[]{:S(2)}) collective-permute-start(bf16[136,256]{1,0:T(8,128)(2,1)S(1)} %shard_map.51.rest_1_), channel_id=1, source_target_pairs={{0,13},{1,12},{4,9},{5,8},{8,5},{9,4},{12,1},{13,0},{2,15},{3,14},... | collective-permute-start | bytes 208904 | tf_op jit(solution)/shard_map/ppermute | solution.py:597
  9.8 6.3 %collective-permute-start.1 = (bf16[128,256]{1,0:T(8,128)(2,1)S(1)}, bf16[128,256]{1,0:T(8,128)(2,1)S(1)}, u32[]{:S(2)}, u32[]{:S(2)}) collective-permute-start(bf16[128,256]{1,0:T(8,128)(2,1)S(1)} %shard_map.48.rest_0_), channel_id=1, source_target_pairs={{0,4},{1,5},{4,0},{5,1},{8,12},{9,13},{12,8},{13,9},{2,6},{3,7},{6... | collective-permute-start | bytes 196616 | tf_op jit(solution)/shard_map/ppermute | solution.py:597
  11.7 4.3 %collective-permute-start = (bf16[128,256]{1,0:T(8,128)(2,1)S(1)}, bf16[128,256]{1,0:T(8,128)(2,1)S(1)}, u32[]{:S(2)}, u32[]{:S(2)}) collective-permute-start(bf16[128,256]{1,0:T(8,128)(2,1)S(1)} %shard_map.47.rest_0_), channel_id=1, source_target_pairs={{0,1},{1,0},{4,5},{5,4},{8,9},{9,8},{12,13},{13,12},{2,3},{3,2},{6... | collective-permute-start | bytes 196616 | tf_op jit(solution)/shard_map/ppermute | solution.py:597
  19.9 1.2 %collective-permute-start.7 = (f32[2,1024]{1,0:T(2,128)S(1)}, f32[2,1024]{1,0:T(2,128)S(1)}, u32[]{:S(2)}, u32[]{:S(2)}) collective-permute-start(f32[2,1024]{1,0:T(2,128)S(1)} %shard_map.55), channel_id=1, source_target_pairs={{0,1},{1,0},{2,3},{3,2},{4,5},{5,4},{6,7},{7,6},{8,9},{9,8},{10,11... | collective-permute-start | bytes 24584 | tf_op jit(solution)/shard_map/ppermute | solution.py:620

commit v25 on v20

--- a/solution.py
+++ b/solution.py
@@ -515,9 +515,9 @@
                 for m in range(3):
                     wts[i, t, m * KEYS : (m + 1) * KEYS, :] = taps[m]
 
-    for group in range(GROUPS):
-        starts = [group * DGROUP + 8 * half for half in range(2)]
-        for i in range(PAIR):
+    for i in range(PAIR):
+        for group in range(GROUPS):
+            starts = [group * DGROUP + 8 * half for half in range(2)]
             v = [[vol[i, t, at : at + 8, :] for t in range(LINE_RUN)] for at in starts]
             for layer in range(LAYERS):
                 s = 3**layer

time: 21.9 us -> 21.9 us (level)
  no operation moved by 1% of the time
where the time goes in v25:
time: 21.9 us; the launch traced here: 21.6 us
  starting transfers between devices  10.5 us (48%)
  Pallas kernels  4.65 us (21%)
  waiting for transfers between devices  4.65 us (21%)
  local copies, waits for them, and re-layouts  1.07 us (5%)
  other arithmetic  0.62 us (3%)
    ppermute x7, starting transfers between devices, lines_plan(): pieces[key] = lax.ppermute(piece, ('cols', 'view'), moves) if key else piece  10.1 us
    pallas_call x10, Pallas kernels, call(): pl.pallas_call(kernel, out_shape=[jax.ShapeDtypeStruct(shape, dtype) for...  4.65 us
    ppermute x7, waiting for transfers between devices, lines_plan(): pieces[key] = lax.ppermute(piece, ('cols', 'view'), moves) if key else piece  3.79 us
    unnamed x10, local copies, waits for them, and re-layouts  1.07 us
    ppermute x1, waiting for transfers between devices, lines_plan(): others = lax.ppermute(rows, 'view', [(0, 1), (1, 0)])  0.86 us
    select_n x1, other arithmetic, lines_plan(): jnp.where(first, jnp.concatenate([rows, others]), jnp.concatenate([others...  0.62 us
  transfers between devices with their start and end apart: 8, of which 3 were waited for; matrix products, arithmetic and copies ran while one was open for 0% of the time, Pallas kernels for 4%

profile of v25, /device:TPU:0, one launch (start us, length us, event | category | flops | bytes accessed | tf_op | source)
XLA Modules:
  0.0 21.6 jit_solution(828898015474002254)
XLA Ops:
  0.0 1.0 %copy-done = bf16[1,16,64,256]{3,2,1,0:T(8,128)(2,1)S(1)} copy-done((bf16[1,16,64,256]{3,2,1,0:T(8,128)(2,1)S(1)}, bf16[1,16,64,256]{3,2,1,0:T(8,128)(2,1)}, u32[]{:S(2)}) %copy-start) | copy-done | bytes 524312
  1.1 0.0 copy-start.1
  1.1 0.0 copy-start.2
  1.1 4.1 %collective-permute-start.3 = (bf16[128,256]{1,0:T(8,128)(2,1)S(1)}, bf16[128,256]{1,0:T(8,128)(2,1)S(1)}, u32[]{:S(2)}, u32[]{:S(2)}) collective-permute-start(bf16[128,256]{1,0:T(8,128)(2,1)S(1)} %shard_map.50.rest_1_), channel_id=1, source_target_pairs={{0,8},{1,9},{4,12},{5,13},{8,0},{9,1},{12,4},{13,5},{2,10},{3,11},... | collective-permute-start | bytes 196616 | tf_op jit(solution)/shard_map/ppermute | solution.py:596
  5.2 1.3 %collective-permute-start.5 = (bf16[128,256]{1,0:T(8,128)(2,1)S(1)}, bf16[128,256]{1,0:T(8,128)(2,1)S(1)}, u32[]{:S(2)}, u32[]{:S(2)}) collective-permute-start(bf16[128,256]{1,0:T(8,128)(2,1)S(1)} %shard_map.49.rest_0_), channel_id=1, source_target_pairs={{0,12},{1,13},{4,8},{5,9},{8,4},{9,5},{12,0},{13,1},{2,14},{3,15},... | collective-permute-start | bytes 196616 | tf_op jit(solution)/shard_map/ppermute | solution.py:596
  6.7 0.0 copy-start.3
  6.7 0.0 copy-start.4
  6.7 0.1 collective-permute-start.2
  6.8 2.7 %collective-permute-start.4 = (bf16[136,256]{1,0:T(8,128)(2,1)S(1)}, bf16[136,256]{1,0:T(8,128)(2,1)S(1)}, u32[]{:S(2)}, u32[]{:S(2)}) collective-permute-start(bf16[136,256]{1,0:T(8,128)(2,1)S(1)} %shard_map.52.rest_1_), channel_id=1, source_target_pairs={{0,9},{1,8},{4,13},{5,12},{8,1},{9,0},{12,5},{13,4},{2,11},{3,10},... | collective-permute-start | bytes 208904 | tf_op jit(solution)/shard_map/ppermute | solution.py:596
  9.5 0.2 %collective-permute-start.6 = (bf16[136,256]{1,0:T(8,128)(2,1)S(1)}, bf16[136,256]{1,0:T(8,128)(2,1)S(1)}, u32[]{:S(2)}, u32[]{:S(2)}) collective-permute-start(bf16[136,256]{1,0:T(8,128)(2,1)S(1)} %shard_map.51.rest_1_), channel_id=1, source_target_pairs={{0,13},{1,12},{4,9},{5,8},{8,5},{9,4},{12,1},{13,0},{2,15},{3,14},... | collective-permute-start | bytes 208904 | tf_op jit(solution)/shard_map/ppermute | solution.py:596
  9.8 0.0 collective-permute-done.3.rest_5_
  9.8 1.6 %collective-permute-start.1 = (bf16[128,256]{1,0:T(8,128)(2,1)S(1)}, bf16[128,256]{1,0:T(8,128)(2,1)S(1)}, u32[]{:S(2)}, u32[]{:S(2)}) collective-permute-start(bf16[128,256]{1,0:T(8,128)(2,1)S(1)} %shard_map.48.rest_0_), channel_id=1, source_target_pairs={{0,4},{1,5},{4,0},{5,1},{8,12},{9,13},{12,8},{13,9},{2,6},{3,7},{6... | collective-permute-start | bytes 196616 | tf_op jit(solution)/shard_map/ppermute | solution.py:596
  11.4 0.3 %collective-permute-done.5.rest_7_ = bf16[128,256]{1,0:T(8,128)(2,1)S(1)} collective-permute-done((bf16[128,256]{1,0:T(8,128)(2,1)S(1)}, bf16[128,256]{1,0:T(8,128)(2,1)S(1)}, u32[]{:S(2)}, u32[]{:S(2)}) %collective-permute-start.5) | collective-permute-done | bytes 65568 | tf_op jit(solution)/shard_map/ppermute | solution.py:596
  11.7 0.0 collective-permute-start
  11.8 0.8 %shard_map.46 = (bf16[128,128]{1,0:T(8,128)(2,1)S(1)}, bf16[128,128]{1,0:T(8,128)(2,1)S(1)}, bf16[192,256]{1,0:T(8,128)(2,1)S(1)}, bf16[120,128]{1,0:T(8,128)(2,...) custom-call(s32[16]{0:T(128)S(1)} %copy-done.4, bf16[64,108]{1,0:T(8,128)(2,1)S(1)} %copy-done.3, ...), custom_call_target="tpu_custom_call" | custom-call | flops 1000000 | bytes 1000000 | tf_op jit(solution)/shard_map/pallas_call | solution.py:50
  12.6 3.4 %collective-permute-done.1.rest_3_ = bf16[128,256]{1,0:T(8,128)(2,1)S(1)} collective-permute-done((bf16[128,256]{1,0:T(8,128)(2,1)S(1)}, bf16[128,256]{1,0:T(8,128)(2,1)S(1)}, u32[]{:S(2)}, u32[]{:S(2)}) %collective-permute-start.1) | collective-permute-done | bytes 65568 | tf_op jit(solution)/shard_map/ppermute | solution.py:596
  16.0 0.0 collective-permute-done.rest_2_
  16.0 0.0 collective-permute-done.2.rest_4_
  16.1 0.0 collective-permute-done.4.rest_6_
  16.1 0.0 collective-permute-done.6.rest_8_
  16.1 3.7 %shard_map.55 = f32[2,1024]{1,0:T(2,128)S(1)} custom-call(s32[16]{0:T(128)S(1)} %copy-done.4, bf16[128,128]{1,0:T(8,128)(2,1)S(1)} %get-tuple-element.11.order, bf16[128,128]{1,0:T(8,128)(2,1)S(1)} %get-tuple-element.12.order_band, bf16[192,256]{1,0:T(8,128)(2,1)S(1)} %get-tuple-element.13.flip, bf16[120,128]{1,0:T(8,128)(2,1)S(1)} %get-tuple-element.14.guide, ...), custom_call_target="tpu_custom_call" | custom-call | flops 1000000000 | bytes 1000000 | tf_op jit(solution)/shard_map/pallas_call | solution.py:50
  19.8 0.4 %collective-permute-start.7 = (f32[2,1024]{1,0:T(2,128)S(1)}, f32[2,1024]{1,0:T(2,128)S(1)}, u32[]{:S(2)}, u32[]{:S(2)}) collective-permute-start(f32[2,1024]{1,0:T(2,128)S(1)} %shard_map.55), channel_id=1, source_target_pairs={{0,1},{1,0},{2,3},{3,2},{4,5},{5,4},{6,7},{7,6},{8,9},{9,8},{10,11... | collective-permute-start | bytes 24584 | tf_op jit(solution)/shard_map/ppermute | solution.py:619
  20.2 0.9 %collective-permute-done.7 = f32[2,1024]{1,0:T(2,128)S(1)} collective-permute-done((f32[2,1024]{1,0:T(2,128)S(1)}, f32[2,1024]{1,0:T(2,128)S(1)}, u32[]{:S(2)}, u32[]{:S(2)}) %collective-permute-start.7) | collective-permute-done | bytes 8224 | tf_op jit(solution)/shard_map/ppermute | solution.py:619
  21.0 0.6 %maximum_select_fusion = f32[1,4,1024]{2,1,0:T(4,128)} fusion(f32[1,2,1024]{2,1,0:T(2,128)S(1)} %bitcast.12, f32[1,2,1024]{2,1,0:T(2,128)S(1)} %bitcast.11, pred[]{:T(512)S(6)} %eq.3), kind=kLoop, calls=%fused_computation | loop fusion | flops 12288 | bytes 32769 | tf_op jit(solution)/shard_map/jit(_where)/select_n | solution.py:621
  (13 shorter events, 0.1 us)
Async XLA Ops:
  0.0 1.0 %copy-start = (bf16[1,16,64,256]{3,2,1,0:T(8,128)(2,1)S(1)}, bf16[1,16,64,256]{3,2,1,0:T(8,128)(2,1)}, u32[]{:S(2)}) copy-start(bf16[1,16,64,256]{3,2,1,0:T(8,128)(2,1)} %param.4) | copy-start | bytes 1572868
  1.1 5.5 %copy-start.1 = (bf16[1,16,64,256]{3,2,1,0:T(8,128)(2,1)S(1)}, bf16[1,16,64,256]{3,2,1,0:T(8,128)(2,1)}, u32[]{:S(2)}) copy-start(bf16[1,16,64,256]{3,2,1,0:T(8,128)(2,1)} %param.4) | copy-start | bytes 1572868
  1.1 5.5 %copy-start.2 = (s32[2,256]{1,0:T(2,128)S(1)}, s32[2,256]{1,0:T(2,128)}, u32[]{:S(2)}) copy-start(s32[2,256]{1,0:T(2,128)} %rest_0_.5) | copy-start | bytes 6148
  1.1 8.6 %collective-permute-start.3 = (bf16[128,256]{1,0:T(8,128)(2,1)S(1)}, bf16[128,256]{1,0:T(8,128)(2,1)S(1)}, u32[]{:S(2)}, u32[]{:S(2)}) collective-permute-start(bf16[128,256]{1,0:T(8,128)(2,1)S(1)} %shard_map.50.rest_1_), channel_id=1, source_target_pairs={{0,8},{1,9},{4,12},{5,13},{8,0},{9,1},{12,4},{13,5},{2,10},{3,11},... | collective-permute-start | bytes 196616 | tf_op jit(solution)/shard_map/ppermute | solution.py:596
  5.2 6.5 %collective-permute-start.5 = (bf16[128,256]{1,0:T(8,128)(2,1)S(1)}, bf16[128,256]{1,0:T(8,128)(2,1)S(1)}, u32[]{:S(2)}, u32[]{:S(2)}) collective-permute-start(bf16[128,256]{1,0:T(8,128)(2,1)S(1)} %shard_map.49.rest_0_), channel_id=1, source_target_pairs={{0,12},{1,13},{4,8},{5,9},{8,4},{9,5},{12,0},{13,1},{2,14},{3,15},... | collective-permute-start | bytes 196616 | tf_op jit(solution)/shard_map/ppermute | solution.py:596
  6.7 5.1 %copy-start.3 = (bf16[64,108]{1,0:T(8,128)(2,1)S(1)}, bf16[64,108]{1,0:T(8,128)(2,1)}, u32[]{:S(2)}) copy-start(bf16[64,108]{1,0:T(8,128)(2,1)} %guide.1) | copy-start | bytes 41476
  6.7 5.1 %copy-start.4 = (s32[16]{0:T(128)S(1)}, s32[16]{0:T(128)}, u32[]{:S(2)}) copy-start(s32[16]{0:T(128)} %offsets.3) | copy-start | bytes 196
  6.7 9.4 %collective-permute-start.2 = (bf16[136,256]{1,0:T(8,128)(2,1)S(1)}, bf16[136,256]{1,0:T(8,128)(2,1)S(1)}, u32[]{:S(2)}, u32[]{:S(2)}) collective-permute-start(bf16[136,256]{1,0:T(8,128)(2,1)S(1)} %shard_map.53.rest_0_), channel_id=1, source_target_pairs={{0,5},{1,4},{4,1},{5,0},{8,13},{9,12},{12,9},{13,8},{2,7},{3,6},{6... | collective-permute-start | bytes 208904 | tf_op jit(solution)/shard_map/ppermute | solution.py:596
  6.8 9.3 %collective-permute-start.4 = (bf16[136,256]{1,0:T(8,128)(2,1)S(1)}, bf16[136,256]{1,0:T(8,128)(2,1)S(1)}, u32[]{:S(2)}, u32[]{:S(2)}) collective-permute-start(bf16[136,256]{1,0:T(8,128)(2,1)S(1)} %shard_map.52.rest_1_), channel_id=1, source_target_pairs={{0,9},{1,8},{4,13},{5,12},{8,1},{9,0},{12,5},{13,4},{2,11},{3,10},... | collective-permute-start | bytes 208904 | tf_op jit(solution)/shard_map/ppermute | solution.py:596
  9.5 6.5 %collective-permute-start.6 = (bf16[136,256]{1,0:T(8,128)(2,1)S(1)}, bf16[136,256]{1,0:T(8,128)(2,1)S(1)}, u32[]{:S(2)}, u32[]{:S(2)}) collective-permute-start(bf16[136,256]{1,0:T(8,128)(2,1)S(1)} %shard_map.51.rest_1_), channel_id=1, source_target_pairs={{0,13},{1,12},{4,9},{5,8},{8,5},{9,4},{12,1},{13,0},{2,15},{3,14},... | collective-permute-start | bytes 208904 | tf_op jit(solution)/shard_map/ppermute | solution.py:596
  9.8 6.3 %collective-permute-start.1 = (bf16[128,256]{1,0:T(8,128)(2,1)S(1)}, bf16[128,256]{1,0:T(8,128)(2,1)S(1)}, u32[]{:S(2)}, u32[]{:S(2)}) collective-permute-start(bf16[128,256]{1,0:T(8,128)(2,1)S(1)} %shard_map.48.rest_0_), channel_id=1, source_target_pairs={{0,4},{1,5},{4,0},{5,1},{8,12},{9,13},{12,8},{13,9},{2,6},{3,7},{6... | collective-permute-start | bytes 196616 | tf_op jit(solution)/shard_map/ppermute | solution.py:596
  11.7 4.3 %collective-permute-start = (bf16[128,256]{1,0:T(8,128)(2,1)S(1)}, bf16[128,256]{1,0:T(8,128)(2,1)S(1)}, u32[]{:S(2)}, u32[]{:S(2)}) collective-permute-start(bf16[128,256]{1,0:T(8,128)(2,1)S(1)} %shard_map.47.rest_0_), channel_id=1, source_target_pairs={{0,1},{1,0},{4,5},{5,4},{8,9},{9,8},{12,13},{13,12},{2,3},{3,2},{6... | collective-permute-start | bytes 196616 | tf_op jit(solution)/shard_map/ppermute | solution.py:596
  19.8 1.2 %collective-permute-start.7 = (f32[2,1024]{1,0:T(2,128)S(1)}, f32[2,1024]{1,0:T(2,128)S(1)}, u32[]{:S(2)}, u32[]{:S(2)}) collective-permute-start(f32[2,1024]{1,0:T(2,128)S(1)} %shard_map.55), channel_id=1, source_target_pairs={{0,1},{1,0},{2,3},{3,2},{4,5},{5,4},{6,7},{7,6},{8,9},{9,8},{10,11... | collective-permute-start | bytes 24584 | tf_op jit(solution)/shard_map/ppermute | solution.py:619
